TPU v7x, 32 devices: a whole 2x2x4 slice. The times are simulated.
32 devices in a mesh: seq: 8 (over z, x), head: 4 (over y, core).
Axes of the slice: x: 2, y: 2, z: 4, core: 2. Of those that a mesh axis runs over, the one named last changes fastest.
Arguments:
- tokens: bfloat16 [2, 8192, 1024], P(None, 'seq', 'head'), may hold values from -250 to 250
- cotangent: bfloat16 [2, 8192, 1024], P(None, 'seq', 'head'), may hold values from -6 to 6
- query_weight: float32 [1024, 4, 256], P('seq', 'head'), may hold values from -0.1875 to 0.1875
- query_mean: float32 [1024, 4, 256], P('seq', 'head'), may hold values from -24 to 24
- query_square: float32 [1024, 4, 256], P('seq', 'head'), may hold values from 1.47456 to 5.89824
- value_weight: float32 [1024, 4, 512], P('seq', 'head'), may hold values from -0.1875 to 0.1875
- value_mean: float32 [1024, 4, 512], P('seq', 'head'), may hold values from -32 to 32
- value_square: float32 [1024, 4, 512], P('seq', 'head'), may hold values from 2.62144 to 10.48576
- squeeze_weight: float32 [1024, 16], P('seq'), may hold values from -1 to 1
- squeeze_mean: float32 [1024, 16], P('seq'), may hold values from -24 to 24
- squeeze_square: float32 [1024, 16], P('seq'), may hold values from 1.47456 to 5.89824
- expand_weight: float32 [17, 512], replicated, may hold values from -2 to 12
- expand_mean: float32 [17, 512], replicated, may hold values from -4 to 4
- expand_square: float32 [17, 512], replicated, may hold values from 0.04096 to 0.16384
- group_weight: float32 [256], replicated, may hold values from 0.5 to 1.5
- group_mean: float32 [256], replicated, may hold values from -80 to 80
- group_square: float32 [256], replicated, may hold values from 16.384 to 65.536
- output_weight: float32 [1024, 1024], P('head', 'seq'), may hold values from -0.1875 to 0.1875
- output_mean: float32 [1024, 1024], P('head', 'seq'), may hold values from -48 to 48
- output_square: float32 [1024, 1024], P('head', 'seq'), may hold values from 5.89824 to 23.59296
- ffn_weight: float32 [1024, 2, 2816], P('seq', None, 'head'), may hold values from -0.1875 to 0.1875
- ffn_mean: float32 [1024, 2, 2816], P('seq', None, 'head'), may hold values from -24 to 24
- ffn_square: float32 [1024, 2, 2816], P('seq', None, 'head'), may hold values from 1.47456 to 5.89824
- down_weight: float32 [2816, 1024], P('head', 'seq'), may hold values from -0.109375 to 0.109375
- down_mean: float32 [2816, 1024], P('head', 'seq'), may hold values from -40 to 40
- down_square: float32 [2816, 1024], P('head', 'seq'), may hold values from 4.096 to 16.384
- norms_weight: float32 [2, 1024], P(None, 'seq'), may hold values from 0.5 to 1.5
- norms_mean: float32 [2, 1024], P(None, 'seq'), may hold values from -80 to 80
- norms_square: float32 [2, 1024], P(None, 'seq'), may hold values from 16.384 to 65.536
Outputs:
- block_out: bfloat16 [2, 8192, 1024], P(None, 'seq', 'head')
- tokens_grad: float32 [2, 8192, 1024], P(None, 'seq', 'head')
- query_new: float32 [1024, 4, 256], P('seq', 'head')
- query_newmean: float32 [1024, 4, 256], P('seq', 'head')
- query_newsquare: float32 [1024, 4, 256], P('seq', 'head')
- value_new: float32 [1024, 4, 512], P('seq', 'head')
- value_newmean: float32 [1024, 4, 512], P('seq', 'head')
- value_newsquare: float32 [1024, 4, 512], P('seq', 'head')
- squeeze_new: float32 [1024, 16], P('seq')
- squeeze_newmean: float32 [1024, 16], P('seq')
- squeeze_newsquare: float32 [1024, 16], P('seq')
- expand_new: float32 [17, 512], replicated
- expand_newmean: float32 [17, 512], replicated
- expand_newsquare: float32 [17, 512], replicated
- group_new: float32 [256], replicated
- group_newmean: float32 [256], replicated
- group_newsquare: float32 [256], replicated
- output_new: float32 [1024, 1024], P('head', 'seq')
- output_newmean: float32 [1024, 1024], P('head', 'seq')
- output_newsquare: float32 [1024, 1024], P('head', 'seq')
- ffn_new: float32 [1024, 2, 2816], P('seq', None, 'head')
- ffn_newmean: float32 [1024, 2, 2816], P('seq', None, 'head')
- ffn_newsquare: float32 [1024, 2, 2816], P('seq', None, 'head')
- down_new: float32 [2816, 1024], P('head', 'seq')
- down_newmean: float32 [2816, 1024], P('head', 'seq')
- down_newsquare: float32 [2816, 1024], P('head', 'seq')
- norms_new: float32 [2, 1024], P(None, 'seq')
- norms_newmean: float32 [2, 1024], P(None, 'seq')
- norms_newsquare: float32 [2, 1024], P(None, 'seq')
All inputs are finite; a program needn't handle non-finite values.
Results may differ from a plain program's by a relative error of at most 0.012.
The roundings to bfloat16 on the way count: a program that leaves them out, or rounds other values in their place, can miss the bound.
Values may be sent and summed in bfloat16 or wider, within the bound.
No kernel may reach another device: no remote copies, remote signals or barrier semaphores. Data moves between devices by JAX's collectives and lax.ppermute only.
A program may use at most 192 MiB of HBM per device.

v0:
```python
import jax
import jax.numpy as jnp
from jax import lax
from jax.sharding import PartitionSpec as P

SPAN = 64
STEP = 10


eps_norm = 1e-06
gate_scale = 16.0
beta_one = 0.9
beta_two = 0.999
eps_adam = 1e-06
decay_rate = 0.01
learn_rate = 0.5
highest = lax.Precision.HIGHEST


def prefix(value, axis, combine, identity, reverse):
    peers, position = (lax.axis_size(axis), lax.axis_index(axis))
    everything = jax.tree.map(lambda part: lax.all_gather(part, axis), value)
    start = jax.tree.map(
        lambda part, zero: jnp.broadcast_to(jnp.asarray(zero, part.dtype), part.shape),
        value,
        identity,
    )

    def step(k, before):
        at = peers - 1 - k if reverse else k
        reached = at > position if reverse else at < position
        new = combine(before, jax.tree.map(lambda part: part[at], everything))
        return jax.tree.map(lambda a, b: jnp.where(reached, a, b), new, before)

    return lax.fori_loop(0, peers, step, start)


def to_half(value_entries):
    return value_entries.astype(jnp.bfloat16)


def norm_piece(value_entries, gain_vector):
    return (
        value_entries
        * lax.rsqrt(jnp.mean(value_entries * value_entries, axis=-1, keepdims=True) + eps_norm)
        * gain_vector
    )


def gate_piece(recurrent, gate_values, gain_vector):
    return norm_piece(recurrent, gain_vector) * jax.nn.silu(gate_values)


def swish_product(gate_part, up_part):
    return jax.nn.silu(gate_part) * up_part


def head_share(value_entries):
    return lax.psum_scatter(value_entries, "head", scatter_dimension=1, tiled=True)


def row_total(value_entries):
    return lax.psum(value_entries, "head")


def row_gather(value_entries):
    return lax.all_gather(value_entries, "head", axis=1, tiled=True)


def span_local(queries, key_rows, value_entries, decay_factors):
    sequences, tokens, key_width = queries.shape
    value_width = value_entries.shape[-1]
    blocks = tokens // SPAN
    cumulate = jnp.cumsum(decay_factors.reshape(sequences, blocks, SPAN, key_width), axis=2)
    closing = cumulate[:, :, -1:, :]
    query_decayed = queries.reshape(sequences, blocks, SPAN, key_width) * jnp.exp(cumulate)
    key_blocks = key_rows.reshape(sequences, blocks, SPAN, key_width)
    key_inverse = key_blocks * jnp.exp(-cumulate)
    key_closing = key_blocks * jnp.exp(closing - cumulate)
    value_blocks = value_entries.reshape(sequences, blocks, SPAN, value_width)
    scores = jnp.einsum("sbic,sbjc->sbij", query_decayed, key_inverse, precision=highest)
    causal = jnp.arange(SPAN)[:, None] >= jnp.arange(SPAN)[None, :]
    scores = jnp.where(causal, scores, 0.0)
    within = jnp.einsum("sbij,sbjv->sbiv", scores, value_blocks, precision=highest)
    block_states = jnp.einsum("sbjc,sbjv->sbcv", key_closing, value_blocks, precision=highest)

    def advance(running, element):
        decay_item, state_item = element
        return (decay_item[:, :, None] * running + state_item, running)

    start_state = jnp.zeros((sequences, key_width, value_width), jnp.float32)
    final_state, starting = lax.scan(
        advance,
        start_state,
        (jnp.moveaxis(jnp.exp(closing[:, :, 0, :]), 1, 0), jnp.moveaxis(block_states, 1, 0)),
    )
    starting = jnp.moveaxis(starting, 0, 1)
    across = jnp.einsum("sbic,sbcv->sbiv", query_decayed, starting, precision=highest)
    outputs = (within + across).reshape(sequences, tokens, value_width) * key_width ** (-0.5)
    return (outputs, final_state)


def carried(queries, decay_factors, incoming):
    sequences, tokens, key_width = queries.shape
    blocks = tokens // SPAN
    cumulate = jnp.cumsum(decay_factors.reshape(sequences, blocks, SPAN, key_width), axis=2)
    totals = cumulate[:, :, -1, :]
    offsets = jnp.cumsum(totals, axis=1) - totals
    through = (cumulate + offsets[:, :, None, :]).reshape(sequences, tokens, key_width)
    decayed = queries * jnp.exp(through)
    return jnp.einsum("stc,scv->stv", decayed, incoming, precision=highest) * key_width ** (-0.5)


def compose(before_part, after_part):
    return (
        before_part[0] * after_part[0],
        after_part[0][:, :, None] * before_part[1] + after_part[1],
    )


def adam_direction(master, gradient, first_moment, second_moment, fix_one, second_correction):
    new_first = beta_one * first_moment + (1.0 - beta_one) * gradient
    new_second = beta_two * second_moment + (1.0 - beta_two) * gradient * gradient
    update_direction = (
        new_first / fix_one / (jnp.sqrt(new_second / second_correction) + eps_adam)
        + decay_rate * master
    )
    return (new_first, new_second, update_direction)


def per_device(
    tokens,
    cotangent,
    query_weight,
    query_mean,
    query_square,
    value_weight,
    value_mean,
    value_square,
    squeeze_weight,
    squeeze_mean,
    squeeze_square,
    expand_weight,
    expand_mean,
    expand_square,
    group_weight,
    group_mean,
    group_square,
    output_weight,
    output_mean,
    output_square,
    ffn_weight,
    ffn_mean,
    ffn_square,
    down_weight,
    down_mean,
    down_square,
    norms_weight,
    norms_mean,
    norms_square,
):
    sequences, segment, column_count = tokens.shape
    head_index = lax.axis_index("head")
    halves = (
        lax.all_gather(to_half(query_weight), "seq", axis=0, tiled=True),
        lax.all_gather(to_half(value_weight), "seq", axis=0, tiled=True),
        lax.all_gather(to_half(squeeze_weight), "seq", axis=0, tiled=True),
        lax.all_gather(to_half(output_weight), "seq", axis=1, tiled=True),
        lax.all_gather(to_half(ffn_weight), "seq", axis=0, tiled=True),
        lax.all_gather(to_half(down_weight), "seq", axis=1, tiled=True),
        lax.all_gather(to_half(norms_weight), "seq", axis=1, tiled=True),
    )
    query_full, value_full, squeeze_full, output_full, ffn_full, down_full, norms_full = halves
    model_width = query_full.shape[0]
    key_width = query_full.shape[2] // 2
    value_width = value_full.shape[2] // 2
    ffn_width = ffn_full.shape[2]
    row_count = sequences * segment
    column_start = head_index * column_count
    query_matrix = query_full.reshape(model_width, 2 * key_width)
    value_matrix = value_full.reshape(model_width, 2 * value_width)
    ffn_matrix = ffn_full.reshape(model_width, 2 * ffn_width)
    gain_one = norms_full[0].astype(jnp.float32)
    gain_two = norms_full[1].astype(jnp.float32)
    rows_full = lax.all_gather(tokens, "head", axis=2, tiled=True)
    inputs = rows_full.reshape(row_count, model_width).astype(jnp.float32)
    normed_value, pull_one = jax.vjp(norm_piece, inputs, gain_one)
    normed = to_half(normed_value)
    query_key = jnp.dot(normed, query_matrix, preferred_element_type=jnp.float32)
    queries = to_half(query_key[:, :key_width])
    key_rows = to_half(query_key[:, key_width:])
    value_gate = jnp.dot(normed, value_matrix, preferred_element_type=jnp.float32)
    value_entries = to_half(value_gate[:, :value_width])
    gate_values = value_gate[:, value_width:]
    rank_values = jnp.dot(normed, squeeze_full, preferred_element_type=jnp.float32)
    expand_columns = lax.dynamic_slice_in_dim(expand_weight, head_index * key_width, key_width, 1)
    rank_count = expand_columns.shape[0] - 1
    logits = (
        jnp.dot(rank_values, expand_columns[:rank_count], precision=highest)
        + expand_columns[rank_count]
    )
    decay_factors = (jax.nn.log_sigmoid(logits) / gate_scale).reshape(sequences, segment, key_width)
    query_float = queries.astype(jnp.float32).reshape(sequences, segment, key_width)
    key_float = key_rows.astype(jnp.float32).reshape(sequences, segment, key_width)
    value_float = value_entries.astype(jnp.float32).reshape(sequences, segment, value_width)
    (local_out, block_state), pull_local = jax.vjp(
        span_local, query_float, key_float, value_float, decay_factors
    )
    log_block = jnp.sum(decay_factors, axis=1)
    block_decay = jnp.exp(log_block)
    identity_pair = (jnp.ones_like(block_decay), jnp.zeros_like(block_state))
    decay_before, state_in = prefix(
        (block_decay, block_state), "seq", compose, identity_pair, False
    )
    carried_out, pull_carried = jax.vjp(carried, query_float, decay_factors, state_in)
    recurrent = (local_out + carried_out).reshape(row_count, value_width)
    mixed_value, pull_gate = jax.vjp(gate_piece, recurrent, gate_values, group_weight)
    mixed_half = to_half(mixed_value)
    attention_part = jnp.dot(mixed_half, output_full, preferred_element_type=jnp.float32)
    input_cols = tokens.reshape(row_count, column_count).astype(jnp.float32)
    gain_one_cols = lax.dynamic_slice_in_dim(gain_one, column_start, column_count, 0)
    gain_two_cols = lax.dynamic_slice_in_dim(gain_two, column_start, column_count, 0)
    residual_cols = input_cols + head_share(attention_part)
    scale_two = lax.rsqrt(
        row_total(jnp.sum(residual_cols * residual_cols, axis=1)) / model_width + eps_norm
    )
    normed_two = row_gather(to_half(residual_cols * scale_two[:, None] * gain_two_cols))
    ffn_in = jnp.dot(normed_two, ffn_matrix, preferred_element_type=jnp.float32)
    hidden_value, pull_hidden = jax.vjp(swish_product, ffn_in[:, :ffn_width], ffn_in[:, ffn_width:])
    hidden = to_half(hidden_value)
    ffn_out = jnp.dot(hidden, down_full, preferred_element_type=jnp.float32).reshape(
        sequences, segment, model_width
    )
    ffn_cols = lax.psum_scatter(ffn_out, "head", scatter_dimension=2, tiled=True)
    block_out = to_half(residual_cols.reshape(sequences, segment, column_count) + ffn_cols)
    cot_full = lax.all_gather(cotangent, "head", axis=2, tiled=True).reshape(row_count, model_width)
    down_grad = jnp.einsum("nf,nd->fd", hidden, cot_full, preferred_element_type=jnp.float32)
    hidden_grad = jnp.einsum("nd,fd->nf", cot_full, down_full, preferred_element_type=jnp.float32)
    gate_part_grad, up_part_grad = pull_hidden(hidden_grad)
    ffn_in_grad = to_half(jnp.concatenate([gate_part_grad, up_part_grad], axis=1))
    ffn_grad = jnp.einsum(
        "nd,nf->df", normed_two, ffn_in_grad, preferred_element_type=jnp.float32
    ).reshape(model_width, 2, ffn_width)
    normed_two_part = jnp.einsum(
        "nf,df->nd", ffn_in_grad, ffn_matrix, preferred_element_type=jnp.float32
    )
    grad_cols = head_share(normed_two_part)
    weighted_two = grad_cols * gain_two_cols
    inner_two = row_total(jnp.sum(weighted_two * residual_cols, axis=1))
    residual_grad_cols = (
        cotangent.reshape(row_count, column_count).astype(jnp.float32)
        + scale_two[:, None] * weighted_two
        - residual_cols * (scale_two * scale_two * scale_two * inner_two / model_width)[:, None]
    )
    gain_two_cols_grad = jnp.sum(grad_cols * residual_cols * scale_two[:, None], axis=0)
    residual_half = row_gather(to_half(residual_grad_cols))
    output_grad = jnp.einsum(
        "nv,nd->vd", mixed_half, residual_half, preferred_element_type=jnp.float32
    )
    mixed_grad = jnp.einsum(
        "nd,vd->nv", residual_half, output_full, preferred_element_type=jnp.float32
    )
    recurrent_grad, gate_values_grad, group_grad = pull_gate(mixed_grad)
    recurrent_grad = recurrent_grad.reshape(sequences, segment, value_width)
    query_grad_carried, decays_grad_carried, state_in_grad = pull_carried(recurrent_grad)
    later_decay, later_grad = prefix(
        (block_decay, state_in_grad), "seq", compose, identity_pair, True
    )
    log_block_grad = jnp.sum(state_in * later_grad, axis=2) * block_decay
    query_grad_local, key_grad, value_grad, decays_grad_local = pull_local(
        (recurrent_grad, later_grad)
    )
    query_grad = query_grad_carried + query_grad_local
    decays_grad = decays_grad_carried + decays_grad_local + log_block_grad[:, None, :]
    logit_grad = decays_grad.reshape(row_count, key_width) * jax.nn.sigmoid(-logits) / gate_scale
    expand_grad = jnp.concatenate(
        [
            jnp.einsum("nr,nc->rc", rank_values, logit_grad, precision=highest),
            jnp.sum(logit_grad, axis=0)[None, :],
        ],
        axis=0,
    )
    rank_grad_part = jnp.einsum(
        "nc,rc->nr", logit_grad, expand_columns[:rank_count], precision=highest
    )
    query_key_grad = to_half(
        jnp.concatenate(
            [query_grad.reshape(row_count, key_width), key_grad.reshape(row_count, key_width)],
            axis=1,
        )
    )
    value_gate_grad = to_half(
        jnp.concatenate([value_grad.reshape(row_count, value_width), gate_values_grad], axis=1)
    )
    query_weight_grad = jnp.einsum(
        "nd,nc->dc", normed, query_key_grad, preferred_element_type=jnp.float32
    ).reshape(model_width, 1, 2 * key_width)
    value_weight_grad = jnp.einsum(
        "nd,nc->dc", normed, value_gate_grad, preferred_element_type=jnp.float32
    ).reshape(model_width, 1, 2 * value_width)
    normed_part = jnp.einsum(
        "nc,dc->nd", query_key_grad, query_matrix, preferred_element_type=jnp.float32
    ) + jnp.einsum("nc,dc->nd", value_gate_grad, value_matrix, preferred_element_type=jnp.float32)
    normed_cols = head_share(normed_part)
    rank_sum = lax.psum(rank_grad_part, "head")
    rank_half = to_half(rank_sum)
    squeeze_grad = jnp.einsum("nd,nr->dr", normed, rank_half, preferred_element_type=jnp.float32)
    squeeze_cols = lax.dynamic_slice_in_dim(squeeze_full, column_start, column_count, 0)
    normed_grad_cols = normed_cols + jnp.einsum(
        "nr,dr->nd", rank_half, squeeze_cols, preferred_element_type=jnp.float32
    )
    scale_one = lax.rsqrt(jnp.mean(inputs * inputs, axis=1) + eps_norm)
    weighted_one = normed_grad_cols * gain_one_cols
    inner_one = row_total(jnp.sum(weighted_one * input_cols, axis=1))
    tokens_cols_grad = (
        residual_grad_cols
        + scale_one[:, None] * weighted_one
        - input_cols * (scale_one * scale_one * scale_one * inner_one / model_width)[:, None]
    )
    tokens_grad = tokens_cols_grad.reshape(sequences, segment, column_count)
    gain_one_cols_grad = jnp.sum(normed_grad_cols * input_cols * scale_one[:, None], axis=0)
    gain_pad = lax.dynamic_update_slice_in_dim(
        jnp.zeros((2, model_width), jnp.float32),
        jnp.stack([gain_one_cols_grad, gain_two_cols_grad]),
        column_start,
        1,
    )
    norms_grad = lax.psum(gain_pad, "head")
    (
        query_sum_grad,
        value_sum_grad,
        squeeze_sum_grad,
        output_sum_grad,
        ffn_sum_grad,
        down_sum_grad,
        norms_sum_grad,
    ) = (
        lax.psum_scatter(query_weight_grad, "seq", scatter_dimension=0, tiled=True),
        lax.psum_scatter(value_weight_grad, "seq", scatter_dimension=0, tiled=True),
        lax.psum_scatter(squeeze_grad, "seq", scatter_dimension=0, tiled=True),
        lax.psum_scatter(output_grad, "seq", scatter_dimension=1, tiled=True),
        lax.psum_scatter(ffn_grad, "seq", scatter_dimension=0, tiled=True),
        lax.psum_scatter(down_grad, "seq", scatter_dimension=1, tiled=True),
        lax.psum_scatter(norms_grad, "seq", scatter_dimension=1, tiled=True),
    )
    step_float = jnp.asarray(STEP, jnp.float32)
    fix_one = 1.0 - jnp.power(beta_one, step_float)
    second_correction = 1.0 - jnp.power(beta_two, step_float)
    owner_share = (head_index == 0).astype(jnp.float32)
    sharded = [
        (query_weight, query_sum_grad, query_mean, query_square, 1.0),
        (value_weight, value_sum_grad, value_mean, value_square, 1.0),
        (squeeze_weight, squeeze_sum_grad, squeeze_mean, squeeze_square, owner_share),
        (output_weight, output_sum_grad, output_mean, output_square, 1.0),
        (ffn_weight, ffn_sum_grad, ffn_mean, ffn_square, 1.0),
        (down_weight, down_sum_grad, down_mean, down_square, 1.0),
        (norms_weight, norms_sum_grad, norms_mean, norms_square, owner_share),
    ]
    updates = []
    weight_squares = []
    direction_squares = []
    for master, gradient, first_moment, second_moment, weighting in sharded:
        new_first, new_second, update_direction = adam_direction(
            master, gradient, first_moment, second_moment, fix_one, second_correction
        )
        updates.append((master, new_first, new_second, update_direction))
        weight_squares.append(jnp.sum(master * master) * weighting)
        direction_squares.append(jnp.sum(update_direction * update_direction) * weighting)
    squares = jnp.stack([jnp.stack(weight_squares), jnp.stack(direction_squares)])
    expand_pad = lax.dynamic_update_slice_in_dim(
        jnp.zeros_like(expand_weight), expand_grad, head_index * key_width, 1
    )
    total_squares, expand_total, group_total = lax.psum(
        (squares, expand_pad, group_grad), ("seq", "head")
    )
    results = []
    for token_position, packed in enumerate(updates):
        master, new_first, new_second, update_direction = packed
        trust_ratio = jnp.sqrt(total_squares[0, token_position]) / (
            jnp.sqrt(total_squares[1, token_position]) + eps_adam
        )
        results.append(
            (master - learn_rate * trust_ratio * update_direction, new_first, new_second)
        )
    replicated = []
    for master, gradient, first_moment, second_moment in (
        (expand_weight, expand_total, expand_mean, expand_square),
        (group_weight, group_total, group_mean, group_square),
    ):
        new_first, new_second, update_direction = adam_direction(
            master, gradient, first_moment, second_moment, fix_one, second_correction
        )
        trust_ratio = jnp.sqrt(jnp.sum(master * master)) / (
            jnp.sqrt(jnp.sum(update_direction * update_direction)) + eps_adam
        )
        replicated.append(
            (master - learn_rate * trust_ratio * update_direction, new_first, new_second)
        )
    return (
        block_out,
        tokens_grad,
        results[0][0],
        results[0][1],
        results[0][2],
        results[1][0],
        results[1][1],
        results[1][2],
        results[2][0],
        results[2][1],
        results[2][2],
        replicated[0][0],
        replicated[0][1],
        replicated[0][2],
        replicated[1][0],
        replicated[1][1],
        replicated[1][2],
        results[3][0],
        results[3][1],
        results[3][2],
        results[4][0],
        results[4][1],
        results[4][2],
        results[5][0],
        results[5][1],
        results[5][2],
        results[6][0],
        results[6][1],
        results[6][2],
    )


def solution(mesh):
    in_specs = (
        P(None, "seq", "head"),
        P(None, "seq", "head"),
        P("seq", "head", None),
        P("seq", "head", None),
        P("seq", "head", None),
        P("seq", "head", None),
        P("seq", "head", None),
        P("seq", "head", None),
        P("seq", None),
        P("seq", None),
        P("seq", None),
        P(),
        P(),
        P(),
        P(),
        P(),
        P(),
        P("head", "seq"),
        P("head", "seq"),
        P("head", "seq"),
        P("seq", None, "head"),
        P("seq", None, "head"),
        P("seq", None, "head"),
        P("head", "seq"),
        P("head", "seq"),
        P("head", "seq"),
        P(None, "seq"),
        P(None, "seq"),
        P(None, "seq"),
    )
    out_specs = (
        P(None, "seq", "head"),
        P(None, "seq", "head"),
        P("seq", "head", None),
        P("seq", "head", None),
        P("seq", "head", None),
        P("seq", "head", None),
        P("seq", "head", None),
        P("seq", "head", None),
        P("seq", None),
        P("seq", None),
        P("seq", None),
        P(),
        P(),
        P(),
        P(),
        P(),
        P(),
        P("head", "seq"),
        P("head", "seq"),
        P("head", "seq"),
        P("seq", None, "head"),
        P("seq", None, "head"),
        P("seq", None, "head"),
        P("head", "seq"),
        P("head", "seq"),
        P("head", "seq"),
        P(None, "seq"),
        P(None, "seq"),
        P(None, "seq"),
    )
    return jax.shard_map(
        per_device, mesh=mesh, in_specs=in_specs, out_specs=out_specs, check_vma=False
    )
```

profile of v0, /device:TPU:0, one launch (start us, length us, event | category | flops | bytes accessed | tf_op | source)
XLA Modules:
  0.0 1444.6 jit_solution(7260644089413603618)
XLA Ops:
  11.1 22.1 %all_gather.52 = bf16[2,1024]{1,0:T(2,128)(2,1)S(1)} all-gather(bf16[2,128]{1,0:T(2,128)(2,1)S(1)} %get-tuple-element.735), channel_id=1, replica_groups=mesh['seq'=8,'head'=4] {'seq'}, dimensions={1}, use_global_device_ids=true | all-gather | bytes 4608 | tf_op jit(solution)/shard_map/all_gather | solution.py:171
  34.1 31.5 %all_gather.53 = bf16[1024,1,256]{2,0,1:T(8,128)(2,1)S(1)} all-gather(bf16[128,1,256]{2,0,1:T(8,128)(2,1)S(1)} %copy.311), channel_id=1, replica_groups=mesh['seq'=8,'head'=4] {'seq'}, dimensions={0}, use_global_device_ids=true | all-gather | bytes 589824 | tf_op jit(solution)/shard_map/all_gather | solution.py:165
  65.7 26.1 %all_gather.54 = bf16[1024,16]{0,1:T(8,128)(2,1)S(1)} all-gather(bf16[128,16]{0,1:T(8,128)(2,1)S(1)} %convert_element_type.103), channel_id=1, replica_groups=mesh['seq'=8,'head'=4] {'seq'}, dimensions={0}, use_global_device_ids=true | all-gather | bytes 36864 | tf_op jit(solution)/shard_map/all_gather | solution.py:167
  92.4 3.2 multiply_reduce_fusion
  99.5 3.9 bitcast_reduce_fusion.1
  108.6 4.9 fusion.51
  113.7 4.1 convolution_bitcast_fusion
  120.3 29.4 %while.64 = (s32[]{:T(128)}, f32[2,128,256]{2,1,0:T(8,128)S(1)}, f32[16,2,128,256]{3,2,1,0:T(8,128)}, f32[16,2,128,1]{2,1,3,0:T(2,128)S(1)}, f32[16,2,128]{2,0,1...) while((s32[]{:T(128)}, f32[2,128,256]{2,1,0:T(8,128)S(1)}, ...), condition=%wide.region_3.4_spmd.clone, body=%wide.region_2.3_spmd.clone.sunk | while | flops 262147 | bytes 1315960 | solution.py:92
  150.5 29.4 %all_gather.59 = bf16[256,1024]{1,0:T(8,128)(2,1)} all-gather(bf16[256,128]{1,0:T(8,128)(2,1)S(1)} %convert_element_type.106), channel_id=1, replica_groups=mesh['seq'=8,'head'=4] {'seq'}, dimensions={1}, use_global_device_ids=true | all-gather | bytes 589824 | tf_op jit(solution)/shard_map/all_gather | solution.py:168
  180.5 16.6 %all-gather.3 = f32[8,2,128]{2,1,0:T(2,128)S(1)} all-gather(f32[1,2,128]{2,1,0:T(2,128)S(1)} %exponential_bitcast_fusion.1), channel_id=2, replica_groups=mesh['seq'=8,'head'=4] {'seq'}, dimensions={0}, use_global_device_ids=true | all-gather | bytes 9216 | tf_op jit(solution)/shard_map/all_gather | solution.py:22
  205.8 9.0 while.65
  214.8 4.2 multiply_reduce_fusion.5
  221.4 4.5 fusion.129
  227.9 68.8 %reduce-scatter.14.cloned.1.call-done = f32[2048,256]{1,0:T(8,128)} async-done(((f32[2048,1024]{1,0:T(8,128)}), f32[2048,256]{1,0:T(8,128)}) %reduce-scatter.14.cloned.1.call-update) | async-done | bytes 2097168 | tf_op jit(solution)/shard_map/reduce_scatter | solution.py:59
  298.9 6.0 psum.56
  308.9 50.5 %all-gather.20.cloned.1.call-done = bf16[1024,2,704]{0,2,1:T(8,128)(2,1)} async-done(((bf16[128,2,704]{0,2,1:T(8,128)(2,1)}), bf16[1024,2,704]{0,2,1:T(8,128)(2,1)}) %all-gather.20.cloned.1.call-update) | async-done | bytes 2883600 | tf_op jit(solution)/shard_map/all_gather | solution.py:169
  359.4 34.7 %all-gather.18.cloned.1.call-done = bf16[2048,1024]{1,0:T(8,128)(2,1)} async-done(((bf16[2048,256]{1,0:T(8,128)(2,1)}), bf16[2048,1024]{1,0:T(8,128)(2,1)}) %all-gather.18.cloned.1.call-update) | async-done | bytes 4194320 | tf_op jit(solution)/shard_map/all_gather | solution.py:67
  394.1 11.4 fusion.130
  405.5 35.2 %all-gather.22.cloned.1.call-done = bf16[704,1024]{1,0:T(8,128)(2,1)} async-done(((bf16[704,128]{1,0:T(8,128)(2,1)}), bf16[704,1024]{1,0:T(8,128)(2,1)}) %all-gather.22.cloned.1.call-update) | async-done | bytes 1441808 | tf_op jit(solution)/shard_map/all_gather | solution.py:170
  440.8 35.1 %all-gather.24.cloned.1.call-done = bf16[2,1024,1024]{2,1,0:T(8,128)(2,1)} async-done(((bf16[2,1024,256]{2,1,0:T(8,128)(2,1)}), bf16[2,1024,1024]{2,1,0:T(8,128)(2,1)}) %all-gather.24.cloned.1.call-update) | async-done | bytes 4194320 | tf_op jit(solution)/shard_map/all_gather | solution.py:236
  475.9 11.3 fusion.7
  489.6 8.9 fusion.18
  498.6 71.8 %reduce-scatter.18.cloned.1.call-done = f32[2048,256]{1,0:T(8,128)} async-done(((f32[2048,1024]{1,0:T(8,128)}), f32[2048,256]{1,0:T(8,128)}) %reduce-scatter.18.cloned.1.call-update) | async-done | bytes 2097168 | tf_op jit(solution)/shard_map/reduce_scatter | solution.py:59
  570.4 2.8 multiply_reduce_fusion.2
  573.3 5.8 psum.57
  579.1 3.0 fusion.107
  582.4 36.1 %all-gather.26.cloned.1.call-done = bf16[2048,1024]{1,0:T(8,128)(2,1)} async-done(((bf16[2048,256]{1,0:T(8,128)(2,1)}), bf16[2048,1024]{1,0:T(8,128)(2,1)}) %all-gather.26.cloned.1.call-update) | async-done | bytes 4194320 | tf_op jit(solution)/shard_map/all_gather | solution.py:67
  618.5 6.3 multiply_reduce_fusion.1
  624.8 3.7 fusion.19
  631.3 7.9 fusion.135
  639.2 11.4 fusion.17
  650.7 9.0 fusion.131
  660.2 4.5 bitcast_reduce_fusion
  668.5 5.2 fusion.29
  676.0 7.9 fusion.35
  684.2 9.1 while.66
  697.4 31.7 %while.63 = (s32[]{:T(128)}, f32[2,128,256]{2,1,0:T(8,128)S(1)}, f32[16,2,128]{2,0,1:T(8,128)S(1)}, f32[16,2,128,256]{3,2,1,0:T(8,128)}, f32[16,2,128,256]{3,2,1...) while((s32[]{:T(128)}, f32[2,128,256]{2,1,0:T(8,128)S(1)}, ...), condition=%wide.region_21.22_spmd, body=%wide.region_19.21_spmd.sunk | while | flops 261891 | bytes 1579145 | solution.py:92
  729.2 6.4 fusion.63
  735.7 3.9 fusion.44
  747.4 12.1 all-reduce.5
  759.5 2.8 fusion.49
  762.3 3.5 fusion.137
  765.9 4.7 convolution_bitcast_fusion.2
  770.9 3.3 fusion.133
  774.3 2.8 add_convert_fusion
  779.6 4.6 convolution_add_fusion
  784.2 6.0 convolution_bitcast_fusion.1
  797.5 70.6 %reduce-scatter.30.cloned.1.call-done = f32[128,2,704]{0,2,1:T(8,128)} async-done(((f32[1024,2,704]{0,2,1:T(8,128)}), f32[128,2,704]{0,2,1:T(8,128)}) %reduce-scatter.30.cloned.1.call-update) | async-done | bytes 720912 | tf_op jit(solution)/shard_map/reduce_scatter | solution.py:342
  868.1 3.8 multiply_reduce_fusion.7
  871.9 70.1 %reduce-scatter.16.cloned.1.call-done = f32[2,1024,256]{2,1,0:T(8,128)} async-done(((f32[2,1024,1024]{2,1,0:T(8,128)}), f32[2,1024,256]{2,1,0:T(8,128)}) %reduce-scatter.16.cloned.1.call-update) | async-done | bytes 2097168 | tf_op jit(solution)/shard_map/reduce_scatter | solution.py:234
  942.0 2.8 add_convert_fusion.1
  944.8 64.9 %reduce-scatter.28.cloned.1.call-done = f32[256,128]{1,0:T(8,128)} async-done(((f32[256,1024]{1,0:T(8,128)}), f32[256,128]{1,0:T(8,128)}) %reduce-scatter.28.cloned.1.call-update) | async-done | bytes 131088 | tf_op jit(solution)/shard_map/reduce_scatter | solution.py:341
  1016.0 49.9 %reduce-scatter.26.cloned.1.call-done = f32[128,16]{0,1:T(8,128)} async-done(((f32[1024,16]{0,1:T(8,128)}), f32[128,16]{0,1:T(8,128)}) %reduce-scatter.26.cloned.1.call-update) | async-done | bytes 8208 | tf_op jit(solution)/shard_map/reduce_scatter | solution.py:340
  1069.2 3.8 stack.73
  1073.0 58.6 %reduce-scatter.22.cloned.1.call-done = f32[128,1,256]{2,0,1:T(8,128)} async-done(((f32[1024,1,256]{2,0,1:T(8,128)}), f32[128,1,256]{2,0,1:T(8,128)}) %reduce-scatter.22.cloned.1.call-update) | async-done | bytes 131088 | tf_op jit(solution)/shard_map/reduce_scatter | solution.py:338
  1135.5 69.4 %reduce-scatter.20.cloned.1.call-done = f32[2048,256]{1,0:T(8,128)} async-done(((f32[2048,1024]{1,0:T(8,128)}), f32[2048,256]{1,0:T(8,128)}) %reduce-scatter.20.cloned.1.call-update) | async-done | bytes 2097168 | tf_op jit(solution)/shard_map/reduce_scatter | solution.py:59
  1205.0 4.5 fusion.26
  1212.4 63.8 %reduce-scatter.24.cloned.1.call-done = f32[128,1,512]{2,0,1:T(8,128)} async-done(((f32[1024,1,512]{2,0,1:T(8,128)}), f32[128,1,512]{2,0,1:T(8,128)}) %reduce-scatter.24.cloned.1.call-update) | async-done | bytes 262160 | tf_op jit(solution)/shard_map/reduce_scatter | solution.py:339
  1280.7 60.1 %reduce-scatter.34.cloned.1.call-done = f32[128,2]{1,0:T(8,128)} async-done(((f32[1024,2]{1,0:T(8,128)}), f32[128,2]{1,0:T(8,128)}) %reduce-scatter.34.cloned.1.call-update) | async-done | bytes 1040
  1342.4 6.6 all-reduce.3
  1352.8 3.8 stack.85
  1357.8 41.4 %all-reduce.2 = (f32[2,7]{1,0:T(2,128)}, f32[17,512]{1,0:T(8,128)}, f32[256]{0:T(256)}) all-reduce(f32[2,7]{1,0:T(2,128)} %pad_maximum_fusion.9, f32[17,512]{1,0:T(8,128)} %maximum_dynamic-update-slice_fusion, f32[256]{0:T(256)} %get-tuple-element.600), channel_id=1, replica_groups=mesh['seq'=8,'head'=4] {'seq','head'}, use_global_device_ids=true, to_apply=%region_56.57 | all-reduce | flops 8974 | bytes 71792 | tf_op jit(solution)/shard_map/psum | solution.py:373
  1428.7 2.9 multiply_subtract_fusion
  1432.7 4.6 fusion.24
  (464 shorter events, 191.9 us)
Async XLA Ops:
  7.2 58.4 %copy-start.66 = (f32[128,16]{0,1:T(8,128)S(1)}, f32[128,16]{0,1:T(8,128)}, u32[]{:S(2)}) copy-start(f32[128,16]{0,1:T(8,128)} %param.45) | copy-start | bytes 24580
  7.2 85.2 %all-gather.14.cloned.1.call-start = ((), (), s32[]{:S(2)}) async-start(), calls=%async_computation.11 | async-start | bytes 5242880 | tf_op jit(solution)/shard_map/all_gather | solution.py:185
  7.9 100.6 %all-gather.16.cloned.1.call-start = ((), (), s32[]{:S(2)}) async-start(), calls=%async_computation.12 | async-start | bytes 1179648 | tf_op jit(solution)/shard_map/all_gather | solution.py:166
  9.6 196.2 %all-gather.28.cloned.1.call-start = ((), (), s32[]{:S(2)}) async-start(), calls=%async_computation.28 | async-start | bytes 2359296 | tf_op jit(solution)/shard_map/all_gather | solution.py:22
  33.2 70.9 %copy-start.69 = (f32[1,1024]{1,0:T(1,128)}, f32[1,1024]{1,0:T(1,128)S(1)}, u32[]{:S(2)}) copy-start(f32[1,1024]{1,0:T(1,128)S(1)} %get-tuple-element.718) | copy-start | bytes 12292
  65.6 39.6 %copy-start.49 = (bf16[1024,1,256]{2,0,1:T(8,128)(2,1)}, bf16[1024,1,256]{2,0,1:T(8,128)(2,1)S(1)}, u32[]{:S(2)}) copy-start(bf16[1024,1,256]{2,0,1:T(8,128)(2,1)S(1)} %all_gather.53) | copy-start | bytes 1572868
  91.7 5.7 copy-start.62
  99.5 4.6 copy-start.58
  108.5 90.1 %copy-start.14 = (bf16[2048,128]{1,0:T(8,128)(2,1)}, bf16[2048,128]{1,0:T(8,128)(2,1)S(1)}, u32[]{:S(2)}) copy-start(bf16[2048,128]{1,0:T(8,128)(2,1)S(1)} %get-tuple-element.713) | copy-start | bytes 1572868
  113.5 4.2 copy-start.33
  113.7 89.6 %copy-start.11 = (bf16[2048,256]{1,0:T(8,128)(2,1)}, bf16[2048,256]{1,0:T(8,128)(2,1)S(1)}, u32[]{:S(2)}) copy-start(bf16[2048,256]{1,0:T(8,128)(2,1)S(1)} %slice.146) | copy-start | bytes 3145732
  120.3 30.2 %copy-start.55 = (f32[256,128]{1,0:T(8,128)S(1)}, f32[256,128]{1,0:T(8,128)}, u32[]{:S(2)}) copy-start(f32[256,128]{1,0:T(8,128)} %param.54) | copy-start | bytes 393220
  150.4 146.2 %reduce-scatter.14.cloned.1.call-start = ((), (), s32[]{:S(2)}) async-start(), calls=%async_computation.13 | async-start | bytes 10485760 | tf_op jit(solution)/shard_map/reduce_scatter | solution.py:59
  180.0 17.1 %copy-start.44 = (bf16[2048,256]{1,0:T(8,128)(2,1)S(1)}, bf16[2048,256]{1,0:T(8,128)(2,1)}, u32[]{:S(2)}) copy-start(bf16[2048,256]{1,0:T(8,128)(2,1)} %copy-done.43) | copy-start | bytes 3145732
  180.2 18.0 %copy-start.20 = (f32[2048,128]{1,0:T(8,128)S(1)}, f32[2048,128]{1,0:T(8,128)}, u32[]{:S(2)}) copy-start(f32[2048,128]{1,0:T(8,128)} %get-tuple-element.714) | copy-start | bytes 3145732
  180.5 17.7 %copy-start.10 = (f32[2,16,64,128]{3,2,1,0:T(8,128)}, f32[2,16,64,128]{3,2,1,0:T(8,128)S(1)}, u32[]{:S(2)}) copy-start(f32[2,16,64,128]{3,2,1,0:T(8,128)S(1)} %copy.146) | copy-start | bytes 3145732
  198.7 4.6 copy-start.7
  214.8 445.4 %copy-start.22 = (f32[2,128,256]{2,1,0:T(8,128)}, f32[2,128,256]{2,1,0:T(8,128)S(1)}, u32[]{:S(2)}) copy-start(f32[2,128,256]{2,1,0:T(8,128)S(1)} %get-tuple-element.433) | copy-start | bytes 786436
  214.8 4.2 copy-start.34
  214.8 4.2 copy-start.73
  225.9 133.5 %all-gather.20.cloned.1.call-start = ((), (), s32[]{:S(2)}) async-start(), calls=%async_computation.15 | async-start | bytes 3244032 | tf_op jit(solution)/shard_map/all_gather | solution.py:169
  227.8 166.3 %all-gather.18.cloned.1.call-start = ((), (), s32[]{:S(2)}) async-start(), calls=%async_computation.14 | async-start | bytes 5242880 | tf_op jit(solution)/shard_map/all_gather | solution.py:67
  227.9 351.2 %copy-start.71 = (f32[1,256]{1,0:T(1,128)}, f32[1,256]{1,0:T(1,128)S(1)}, u32[]{:S(2)}) copy-start(f32[1,256]{1,0:T(1,128)S(1)} %fusion.97) | copy-start | bytes 3076
  298.9 280.2 %copy-start = (f32[2048,256]{1,0:T(8,128)}, f32[2048,256]{1,0:T(8,128)S(1)}, u32[]{:S(2)}) copy-start(f32[2048,256]{1,0:T(8,128)S(1)} %get-tuple-element.696) | copy-start | bytes 6291460
  306.3 134.5 %all-gather.22.cloned.1.call-start = ((), (), s32[]{:S(2)}) async-start(), calls=%async_computation.16 | async-start | bytes 1622016 | tf_op jit(solution)/shard_map/all_gather | solution.py:170
  308.1 167.8 %all-gather.24.cloned.1.call-start = ((), (), s32[]{:S(2)}) async-start(), calls=%async_computation.18 | async-start | bytes 5242880 | tf_op jit(solution)/shard_map/all_gather | solution.py:236
  308.8 261.6 %reduce-scatter.18.cloned.1.call-start = ((), (), s32[]{:S(2)}) async-start(), calls=%async_computation.19 | async-start | bytes 10485760 | tf_op jit(solution)/shard_map/reduce_scatter | solution.py:59
  475.9 13.7 copy-start.77
  498.5 119.9 %all-gather.26.cloned.1.call-start = ((), (), s32[]{:S(2)}) async-start(), calls=%async_computation.20 | async-start | bytes 5242880 | tf_op jit(solution)/shard_map/all_gather | solution.py:67
  582.2 102.0 %all-gather.30.cloned.1.call-start = ((), (), s32[]{:S(2)}) async-start(), calls=%async_computation.29 | async-start | bytes 2359296 | tf_op jit(solution)/shard_map/all_gather | solution.py:22
  618.5 6.3 copy-start.35
  631.3 163.4 %reduce-scatter.32.cloned.1.call-start = ((), (), s32[]{:S(2)}) async-start(), calls=%async_computation.27 | async-start | bytes 3244032 | tf_op jit(solution)/shard_map/reduce_scatter | solution.py:343
  639.2 228.9 %reduce-scatter.30.cloned.1.call-start = ((), (), s32[]{:S(2)}) async-start(), calls=%async_computation.26 | async-start | bytes 6488064 | tf_op jit(solution)/shard_map/reduce_scatter | solution.py:342
  650.7 291.3 %reduce-scatter.16.cloned.1.call-start = ((), (), s32[]{:S(2)}) async-start(), calls=%async_computation.17 | async-start | bytes 10485760 | tf_op jit(solution)/shard_map/reduce_scatter | solution.py:234
  659.7 349.9 %reduce-scatter.28.cloned.1.call-start = ((), (), s32[]{:S(2)}) async-start(), calls=%async_computation.25 | async-start | bytes 1179648 | tf_op jit(solution)/shard_map/reduce_scatter | solution.py:341
  660.2 4.6 copy-start.12
  666.0 7.7 copy-start.28
  668.5 5.2 copy-start.39
  668.5 5.2 copy-start.76
  676.0 8.2 copy-start.24
  684.0 381.9 %reduce-scatter.26.cloned.1.call-start = ((), (), s32[]{:S(2)}) async-start(), calls=%async_computation.24 | async-start | bytes 73728 | tf_op jit(solution)/shard_map/reduce_scatter | solution.py:340
  729.1 6.5 copy-start.9
  729.2 6.5 copy-start.16
  729.2 6.5 copy-start.21
  729.2 6.5 copy-start.29
  729.2 6.5 copy-start.42
  759.5 6.3 copy-start.59
  765.8 365.7 %reduce-scatter.22.cloned.1.call-start = ((), (), s32[]{:S(2)}) async-start(), calls=%async_computation.22 | async-start | bytes 1179648 | tf_op jit(solution)/shard_map/reduce_scatter | solution.py:338
  770.6 434.3 %reduce-scatter.20.cloned.1.call-start = ((), (), s32[]{:S(2)}) async-start(), calls=%async_computation.21 | async-start | bytes 10485760 | tf_op jit(solution)/shard_map/reduce_scatter | solution.py:59
  784.2 492.0 %reduce-scatter.24.cloned.1.call-start = ((), (), s32[]{:S(2)}) async-start(), calls=%async_computation.23 | async-start | bytes 2359296 | tf_op jit(solution)/shard_map/reduce_scatter | solution.py:339
  790.2 4.5 copy-start.45
  790.2 4.5 copy-start.60
  790.2 4.5 copy-start.61
  790.2 77.8 %copy-start.37 = (f32[128,2,704]{0,2,1:T(8,128)S(1)}, f32[128,2,704]{0,2,1:T(8,128)}, u32[]{:S(2)}) copy-start(f32[128,2,704]{0,2,1:T(8,128)} %param.57) | copy-start | bytes 2162692
  790.3 550.6 %reduce-scatter.34.cloned.1.call-start = ((), (), s32[]{:S(2)}) async-start(), calls=%async_computation.30 | async-start | bytes 589824
  797.5 144.5 %copy-start.1 = (f32[2048,256]{1,0:T(8,128)S(1)}, f32[2048,256]{1,0:T(8,128)}, u32[]{:S(2)}) copy-start(f32[2048,256]{1,0:T(8,128)} %copy-done) | copy-start | bytes 6291460
  944.8 260.2 %copy-start.19 = (bf16[2,1024,256]{2,1,0:T(8,128)(2,1)S(1)}, bf16[2,1024,256]{2,1,0:T(8,128)(2,1)}, u32[]{:S(2)}) copy-start(bf16[2,1024,256]{2,1,0:T(8,128)(2,1)} %param.37) | copy-start | bytes 3145732
  944.8 260.2 %copy-start.64 = (f32[1,8,2,128]{3,1,2,0:T(8,128)S(1)}, f32[1,8,2,128]{3,1,2,0:T(8,128)}, u32[]{:S(2)}) copy-start(f32[1,8,2,128]{3,1,2,0:T(8,128)} %copy-done.63) | copy-start | bytes 24580
  1205.0 5.1 copy-start.75
  1407.6 24.1 %copy-start.46 = (f32[704,128]{1,0:T(8,128)S(1)}, f32[704,128]{1,0:T(8,128)}, u32[]{:S(2)}) copy-start(f32[704,128]{1,0:T(8,128)} %param.60) | copy-start | bytes 1081348
  1415.9 15.7 %copy-start.53 = (f32[704,128]{1,0:T(8,128)S(1)}, f32[704,128]{1,0:T(8,128)}, u32[]{:S(2)}) copy-start(f32[704,128]{1,0:T(8,128)} %get-tuple-element.679) | copy-start | bytes 1081348
  1416.0 15.7 %copy-start.54 = (f32[704,128]{1,0:T(8,128)S(1)}, f32[704,128]{1,0:T(8,128)}, u32[]{:S(2)}) copy-start(f32[704,128]{1,0:T(8,128)} %get-tuple-element.680) | copy-start | bytes 1081348
  1428.7 3.9 copy-start.70
  1428.7 3.9 copy-start.72
  (37 other events, 84.8 us)
Sparse Core Ops, SparseCore 0:
  9.6 37.7 all-gather.13
  50.1 40.5 all-gather.15
  150.6 48.3 all-gather.27
  226.0 70.5 reduce-scatter.13
  299.3 60.0 all-gather.19
  360.9 33.2 all-gather.17
  396.9 43.8 all-gather.21
  442.4 33.4 all-gather.23
  498.7 71.6 reduce-scatter.17
  582.3 36.1 all-gather.25
  631.4 49.2 all-gather.29
  684.1 70.6 reduce-scatter.31
  758.5 109.5 reduce-scatter.29
  870.5 71.4 reduce-scatter.15
  945.6 63.9 reduce-scatter.27
  1013.2 52.6 reduce-scatter.25
  1069.2 62.3 reduce-scatter.21
  1134.2 70.7 reduce-scatter.19
  1208.5 67.6 reduce-scatter.23
  1279.9 60.8 reduce-scatter.33
where the time goes:
time: 1460 us; the launch traced here: 1440 us
  waiting for transfers between devices  841 us (58%)
  blocking collectives  198 us (14%)
  matrix products  169 us (12%)
  other arithmetic  147 us (10%)
  local copies, waits for them, and re-layouts  53.9 us (4%)
  between operations  31.6 us (2%)
    reduce_scatter x3, waiting for transfers between devices, head_share(): lax.psum_scatter(value_entries, 'head', scatter_dimension=1, tiled=True)  210 us
    all_gather x2, waiting for transfers between devices, row_gather(): return lax.all_gather(value_entries, 'head', axis=1, tiled=True)  70.8 us
    reduce_scatter x1, waiting for transfers between devices, per_device(): lax.psum_scatter(ffn_grad, 'seq', scatter_dimension=0, tiled=True)  70.6 us
    reduce_scatter x1, waiting for transfers between devices, per_device(): lax.psum_scatter(ffn_out, 'head', scatter_dimension=2, tiled=True)  70.1 us
    reduce_scatter x1, waiting for transfers between devices, per_device(): lax.psum_scatter(output_grad, 'seq', scatter_dimension=1, tiled=True)  64.9 us
    reduce_scatter x1, waiting for transfers between devices, per_device(): lax.psum_scatter(value_weight_grad, 'seq', scatter_dimension=0, tiled=True)  63.8 us
    unnamed x21, waiting for transfers between devices  61.8 us
    reduce_scatter x1, waiting for transfers between devices, per_device(): lax.psum_scatter(query_weight_grad, 'seq', scatter_dimension=0, tiled=True)  58.6 us
  transfers between devices with their start and end apart: 20, of which 15 were waited for; matrix products, arithmetic and copies ran while one was open for 16% of the time, Pallas kernels for 0%

commit v1 on v0

v1 whole, which is shorter than its diff:
```python
import jax
import jax.numpy as jnp
from jax import lax
from jax.sharding import PartitionSpec as P

SPAN = 64
STEP = 10


eps_norm = 1e-06
gate_scale = 16.0
beta_one = 0.9
beta_two = 0.999
eps_adam = 1e-06
decay_rate = 0.01
learn_rate = 0.5
highest = lax.Precision.HIGHEST


def to_half(value_entries):
    return value_entries.astype(jnp.bfloat16)


def to_float(value_entries):
    return value_entries.astype(jnp.float32)


def mm(pattern, left, right):
    return jnp.einsum(pattern, left, right, preferred_element_type=jnp.float32)


def exact(pattern, left, right):
    return jnp.einsum(pattern, left, right, precision=highest)


def swap(value_entries, axis, bit):
    peers = lax.axis_size(axis)
    return lax.ppermute(value_entries, axis, [(i, i ^ bit) for i in range(peers)])


def bit_of(axis, bit):
    return (lax.axis_index(axis) // bit) % 2


def pick(value_entries, at, axis=0):
    return lax.dynamic_index_in_dim(value_entries, at, axis, keepdims=False)


def ordered(mine, other, upper):
    return (jnp.where(upper == 0, mine, other), jnp.where(upper == 0, other, mine))


def seq_bits():
    bits, bit = [], lax.axis_size("seq") // 2
    while bit:
        bits.append(("seq", bit))
        bit //= 2
    return bits


def gather_cube(part, stages):
    held = []
    rank = [("head", 2)] + seq_bits()
    for axis, bit in stages:
        low, high = ordered(part, swap(part, axis, bit), bit_of(axis, bit))
        held = sorted(held + [(axis, bit)], key=rank.index)
        part = jnp.stack([low, high], axis=held.index((axis, bit)))
    return part.reshape((2, lax.axis_size("seq")) + part.shape[len(held) :])


def scatter_cube(part, stages):
    held = [("head", 2)] + seq_bits()
    part = part.reshape((2,) * len(held) + part.shape[2:])
    for axis, bit in stages:
        at = held.index((axis, bit))
        held.pop(at)
        upper = bit_of(axis, bit)
        moved = swap(to_half(pick(part, 1 - upper, at)), axis, bit)
        part = to_float(pick(part, upper, at)) + to_float(moved)
    return part


def sum_everywhere(value_entries):
    for axis, bit in [("head", 1), ("head", 2)] + seq_bits()[::-1]:
        value_entries = value_entries + swap(value_entries, axis, bit)
    return value_entries


def scan_blocks(decay, state, reverse):
    before_decay, before_state = (jnp.ones_like(decay), jnp.zeros_like(state))
    for axis, bit in seq_bits()[::-1]:
        upper = bit_of(axis, bit) == (0 if reverse else 1)
        other_decay, other_state = (swap(decay, axis, bit), swap(state, axis, bit))
        before_state = jnp.where(
            upper, before_decay[:, :, None] * other_state + before_state, before_state
        )
        before_decay = jnp.where(upper, before_decay * other_decay, before_decay)
        state = jnp.where(
            upper,
            decay[:, :, None] * other_state + state,
            other_decay[:, :, None] * state + other_state,
        )
        decay = decay * other_decay
    return before_state


def norm_piece(value_entries, gain_vector):
    return (
        value_entries
        * lax.rsqrt(jnp.mean(value_entries * value_entries, axis=-1, keepdims=True) + eps_norm)
        * gain_vector
    )


def gate_piece(recurrent, gate_values, gain_vector):
    return norm_piece(recurrent, gain_vector) * jax.nn.silu(gate_values)


def swish_product(gate_part, up_part):
    return jax.nn.silu(gate_part) * up_part


def span_local(queries, key_rows, value_entries, decay_factors):
    sequences, tokens, key_width = queries.shape
    value_width = value_entries.shape[-1]
    blocks = tokens // SPAN
    cumulate = jnp.cumsum(decay_factors.reshape(sequences, blocks, SPAN, key_width), axis=2)
    closing = cumulate[:, :, -1:, :]
    query_decayed = queries.reshape(sequences, blocks, SPAN, key_width) * jnp.exp(cumulate)
    key_blocks = key_rows.reshape(sequences, blocks, SPAN, key_width)
    key_inverse = key_blocks * jnp.exp(-cumulate)
    key_closing = key_blocks * jnp.exp(closing - cumulate)
    value_blocks = value_entries.reshape(sequences, blocks, SPAN, value_width)
    scores = jnp.einsum("sbic,sbjc->sbij", query_decayed, key_inverse, precision=highest)
    causal = jnp.arange(SPAN)[:, None] >= jnp.arange(SPAN)[None, :]
    scores = jnp.where(causal, scores, 0.0)
    within = jnp.einsum("sbij,sbjv->sbiv", scores, value_blocks, precision=highest)
    block_states = jnp.einsum("sbjc,sbjv->sbcv", key_closing, value_blocks, precision=highest)

    def advance(running, element):
        decay_item, state_item = element
        return (decay_item[:, :, None] * running + state_item, running)

    start_state = jnp.zeros((sequences, key_width, value_width), jnp.float32)
    final_state, starting = lax.scan(
        advance,
        start_state,
        (jnp.moveaxis(jnp.exp(closing[:, :, 0, :]), 1, 0), jnp.moveaxis(block_states, 1, 0)),
    )
    starting = jnp.moveaxis(starting, 0, 1)
    across = jnp.einsum("sbic,sbcv->sbiv", query_decayed, starting, precision=highest)
    outputs = (within + across).reshape(sequences, tokens, value_width) * key_width ** (-0.5)
    return (outputs, final_state)


def carried(queries, decay_factors, incoming):
    sequences, tokens, key_width = queries.shape
    blocks = tokens // SPAN
    cumulate = jnp.cumsum(decay_factors.reshape(sequences, blocks, SPAN, key_width), axis=2)
    totals = cumulate[:, :, -1, :]
    offsets = jnp.cumsum(totals, axis=1) - totals
    through = (cumulate + offsets[:, :, None, :]).reshape(sequences, tokens, key_width)
    decayed = queries * jnp.exp(through)
    return jnp.einsum("stc,scv->stv", decayed, incoming, precision=highest) * key_width ** (-0.5)


def adam_direction(master, gradient, first_moment, second_moment, fix_one, second_correction):
    new_first = beta_one * first_moment + (1.0 - beta_one) * gradient
    new_second = beta_two * second_moment + (1.0 - beta_two) * gradient * gradient
    update_direction = (
        new_first / fix_one / (jnp.sqrt(new_second / second_correction) + eps_adam)
        + decay_rate * master
    )
    return (new_first, new_second, update_direction)


def per_device(
    tokens,
    cotangent,
    query_weight,
    query_mean,
    query_square,
    value_weight,
    value_mean,
    value_square,
    squeeze_weight,
    squeeze_mean,
    squeeze_square,
    expand_weight,
    expand_mean,
    expand_square,
    group_weight,
    group_mean,
    group_square,
    output_weight,
    output_mean,
    output_square,
    ffn_weight,
    ffn_mean,
    ffn_square,
    down_weight,
    down_mean,
    down_square,
    norms_weight,
    norms_mean,
    norms_square,
):
    sequences, segment, column_count = tokens.shape
    head_index = lax.axis_index("head")
    chip, core = (head_index // 2, head_index % 2)
    rows = query_weight.shape[0]
    peers = lax.axis_size("seq")
    model_width = rows * peers
    key_width = query_weight.shape[2] // 2
    value_width = value_weight.shape[2] // 2
    half_segment = segment // 2
    seq_stages = seq_bits()

    small = jnp.concatenate([squeeze_weight, norms_weight.T], axis=1)
    rank_count = squeeze_weight.shape[1]
    small = jnp.pad(small, ((0, 0), (0, 128 - small.shape[1])))
    first = gather_cube(
        to_half(jnp.concatenate([query_weight[:, 0, :], small], axis=1)),
        [("head", 2), ("seq", 1)] + seq_stages[:-1],
    ).reshape(2, model_width, 2 * key_width + 128)
    value_full = gather_cube(
        to_half(value_weight[:, 0, :]), seq_stages + [("head", 2)]
    ).reshape(2, model_width, 2 * value_width)
    query_full = first[:, :, : 2 * key_width]
    small_full = first[0, :, 2 * key_width :]
    squeeze_full = small_full[:, :rank_count]
    gains = to_float(small_full[:, rank_count : rank_count + 2])
    gain_one, gain_two = (gains[:, 0], gains[:, 1])
    output_mine = to_half(output_weight.T)
    output_pair = jnp.stack(ordered(output_mine, swap(output_mine, "head", 2), chip))
    output_full = jnp.moveaxis(lax.all_gather(output_pair, "seq", axis=0), 0, 1).reshape(
        2, model_width, value_width
    )
    ffn_mine = to_half(jnp.stack([ffn_weight[:, 0, :], ffn_weight[:, 1, :], down_weight.T]))
    ffn_full = jnp.moveaxis(lax.all_gather(ffn_mine, "seq", axis=0), 0, 1).reshape(
        3, model_width, ffn_weight.shape[2]
    )

    def full_rows(mine, other):
        pair = jnp.stack(ordered(mine, other, chip))
        low, high = ordered(pair, swap(pair, "head", 1), core)
        return jnp.concatenate([low[0], high[0], low[1], high[1]], axis=-1)

    input_half = full_rows(pick(tokens, chip), swap(pick(tokens, 1 - chip), "head", 2))
    cot_full = full_rows(cotangent, swap(cotangent, "head", 2))
    cot_own, cot_other = (pick(cot_full, chip), pick(cot_full, 1 - chip))
    inputs = to_float(input_half)
    scale_one = lax.rsqrt(jnp.mean(inputs * inputs, axis=1, keepdims=True) + eps_norm)
    normed = to_half(inputs * scale_one * gain_one)

    query_key = mm("td,hdc->htc", normed, query_full)
    queries = to_half(query_key[:, :, :key_width])
    key_rows = to_half(query_key[:, :, key_width:])
    value_gate = mm("td,hdc->htc", normed, value_full)
    value_entries = to_half(value_gate[:, :, :value_width])
    gate_values = value_gate[:, :, value_width:]
    rank_values = mm("td,dr->tr", normed, squeeze_full)
    expand_columns = pick(expand_weight.reshape(rank_count + 1, 2, 2, key_width), core, 2)
    logits = (
        exact("tr,rhc->htc", rank_values, expand_columns[:rank_count])
        + expand_columns[rank_count][:, None, :]
    )
    decay_factors = jax.nn.log_sigmoid(logits) / gate_scale
    (local_out, block_state), pull_local = jax.vjp(
        span_local, to_float(queries), to_float(key_rows), to_float(value_entries), decay_factors
    )
    block_decay = jnp.exp(jnp.sum(decay_factors, axis=1))
    state_in = scan_blocks(block_decay, block_state, False)
    carried_out, pull_carried = jax.vjp(carried, to_float(queries), decay_factors, state_in)
    recurrent = local_out + carried_out
    mixed_value, pull_gate = jax.vjp(gate_piece, recurrent, gate_values, group_weight)
    mixed_half = to_half(mixed_value)
    mixer_part = to_half(mm("htv,hdv->td", mixed_half, output_full))
    residual = inputs + (to_float(mixer_part) + to_float(swap(mixer_part, "head", 1)))
    scale_two = lax.rsqrt(jnp.mean(residual * residual, axis=1, keepdims=True) + eps_norm)
    normed_two = to_half(residual * scale_two * gain_two)

    moved = swap(lax.dynamic_slice_in_dim(normed_two, core * half_segment, half_segment, 0), "head", 2)
    normed_two_other = jnp.concatenate(ordered(moved, swap(moved, "head", 1), core), axis=0)

    def feed_forward(normed_rows, cot_rows):
        gate_part = mm("td,df->tf", normed_rows, ffn_full[0])
        up_part = mm("td,df->tf", normed_rows, ffn_full[1])
        hidden_value, pull_hidden = jax.vjp(swish_product, gate_part, up_part)
        hidden = to_half(hidden_value)
        out_part = mm("tf,df->td", hidden, ffn_full[2])
        hidden_grad = mm("td,df->tf", cot_rows, ffn_full[2])
        gate_grad, up_grad = map(to_half, pull_hidden(hidden_grad))
        rows_grad = mm("tf,df->td", gate_grad, ffn_full[0]) + mm("tf,df->td", up_grad, ffn_full[1])
        return out_part, rows_grad, hidden, gate_grad, up_grad

    own = feed_forward(normed_two, cot_own)
    other = feed_forward(normed_two_other, cot_other)
    other_rows = other[1].reshape(2, half_segment, model_width)
    other_sum = pick(other_rows, core) + to_float(
        swap(to_half(pick(other_rows, 1 - core)), "head", 1)
    )
    home = to_float(swap(to_half(other_sum), "head", 2))
    own_grad = to_half(
        own[1]
        + lax.dynamic_update_slice_in_dim(jnp.zeros_like(own[1]), home, core * half_segment, 0)
    )
    normed_two_grad = to_float(own_grad) + to_float(swap(own_grad, "head", 1))
    out_rows = jnp.stack([own[0], other[0]]).reshape(2, segment, 2, 2, column_count)
    out_rows = pick(out_rows, core, 3) + to_float(
        swap(to_half(pick(out_rows, 1 - core, 3)), "head", 1)
    )
    residual_cols = pick(residual.reshape(segment, 2, 2, column_count), core, 2)
    out_rows = out_rows + jnp.stack([residual_cols, jnp.zeros_like(residual_cols)])
    out_home = to_float(swap(to_half(pick(out_rows, 1 - chip, 2)), "head", 2))
    block_out = to_half(
        jnp.stack(ordered(*(pick(out_rows, chip, 2) + out_home[::-1]), chip))
    )

    normed_two_both = jnp.concatenate([normed_two, normed_two_other])
    ffn_grad = jnp.stack(
        [
            mm("td,tf->df", normed_two_both, jnp.concatenate([own[3], other[3]])),
            mm("td,tf->df", normed_two_both, jnp.concatenate([own[4], other[4]])),
            mm("td,tf->df", jnp.concatenate([cot_own, cot_other]), jnp.concatenate([own[2], other[2]])),
        ]
    )
    ffn_sum = to_float(
        lax.psum_scatter(
            jnp.moveaxis(to_half(ffn_grad).reshape(3, peers, rows, -1), 1, 0),
            "seq",
            scatter_dimension=0,
            tiled=False,
        )
    )
    ffn_sum_grad = jnp.stack([ffn_sum[0], ffn_sum[1]], axis=1)
    down_sum_grad = ffn_sum[2].T

    weighted_two = normed_two_grad * gain_two
    inner_two = jnp.mean(weighted_two * residual, axis=1, keepdims=True)
    residual_grad = (
        to_float(cot_own)
        + scale_two * weighted_two
        - residual * (scale_two * scale_two * scale_two * inner_two)
    )
    gain_two_grad = jnp.sum(normed_two_grad * residual * scale_two, axis=0)
    residual_half = to_half(residual_grad)
    output_grad = mm("td,htv->hdv", residual_half, mixed_half).reshape(2, peers, rows, value_width)
    mixed_grad = mm("td,hdv->htv", residual_half, output_full)
    recurrent_grad, gate_values_grad, group_grad = pull_gate(mixed_grad)
    query_grad_carried, decays_grad_carried, state_in_grad = pull_carried(recurrent_grad)
    later_grad = scan_blocks(block_decay, state_in_grad, True)
    log_block_grad = jnp.sum(state_in * later_grad, axis=2) * block_decay
    query_grad_local, key_grad, value_grad, decays_grad_local = pull_local(
        (recurrent_grad, later_grad)
    )
    query_grad = query_grad_carried + query_grad_local
    decays_grad = decays_grad_carried + decays_grad_local + log_block_grad[:, None, :]
    logit_grad = decays_grad * jax.nn.sigmoid(-logits) / gate_scale
    expand_grad = jnp.concatenate(
        [exact("tr,htc->rhc", rank_values, logit_grad), jnp.sum(logit_grad, axis=1)[None]], axis=0
    )
    rank_grad_part = exact("htc,rhc->rt", logit_grad, expand_columns[:rank_count])
    query_key_grad = to_half(jnp.concatenate([query_grad, key_grad], axis=2))
    value_gate_grad = to_half(jnp.concatenate([value_grad, gate_values_grad], axis=2))
    query_weight_grad = mm("td,htc->hdc", normed, query_key_grad)
    value_weight_grad = mm("td,htc->hdc", normed, value_gate_grad)
    normed_part = to_half(
        mm("htc,hdc->td", query_key_grad, query_full) + mm("htc,hdc->td", value_gate_grad, value_full)
    )
    rank_half = to_half(rank_grad_part + swap(rank_grad_part, "head", 1))
    squeeze_grad = mm("td,rt->dr", normed, rank_half)
    normed_grad = (
        to_float(normed_part)
        + to_float(swap(normed_part, "head", 1))
        + mm("rt,dr->td", rank_half, squeeze_full)
    )
    weighted_one = normed_grad * gain_one
    inner_one = jnp.mean(weighted_one * inputs, axis=1, keepdims=True)
    inputs_grad = (
        residual_grad
        + scale_one * weighted_one
        - inputs * (scale_one * scale_one * scale_one * inner_one)
    )
    gain_one_grad = jnp.sum(normed_grad * inputs * scale_one, axis=0)
    grad_cols = pick(inputs_grad.reshape(segment, 2, 2, column_count), core, 2)
    grad_home = to_float(swap(to_half(pick(grad_cols, 1 - chip, 1)), "head", 2))
    tokens_grad = jnp.stack(ordered(pick(grad_cols, chip, 1), grad_home, chip))

    late_stages = seq_stages[:-1][::-1]
    small_grad = jnp.concatenate([squeeze_grad, gain_one_grad[:, None], gain_two_grad[:, None]], axis=1)
    small_grad = jnp.pad(small_grad, ((0, 0), (0, 128 - small_grad.shape[1])))
    first_grad = jnp.concatenate(
        [query_weight_grad, jnp.broadcast_to(small_grad[None], (2,) + small_grad.shape)], axis=2
    ).reshape(2, peers, rows, -1)
    first_sum = scatter_cube(first_grad, [("seq", 1), ("head", 2)] + late_stages)
    value_sum_grad = scatter_cube(
        value_weight_grad.reshape(2, peers, rows, -1), [("head", 2), ("seq", 1)] + late_stages
    )[:, None, :]
    query_sum_grad = first_sum[:, None, : 2 * key_width]
    squeeze_sum_grad = first_sum[:, 2 * key_width : 2 * key_width + rank_count]
    norms_sum_grad = first_sum[:, 2 * key_width + rank_count : 2 * key_width + rank_count + 2].T
    output_give = to_half(pick(output_grad, 1 - chip))
    output_two = pick(output_grad, chip) + to_float(swap(output_give, "head", 2))
    output_sum_grad = to_float(
        lax.psum_scatter(to_half(output_two), "seq", scatter_dimension=0, tiled=False)
    ).T

    step_float = jnp.asarray(STEP, jnp.float32)
    fix_one = 1.0 - jnp.power(beta_one, step_float)
    second_correction = 1.0 - jnp.power(beta_two, step_float)
    owner_share = (head_index == 0).astype(jnp.float32)
    sharded = [
        (query_weight, query_sum_grad, query_mean, query_square, 1.0),
        (value_weight, value_sum_grad, value_mean, value_square, 1.0),
        (squeeze_weight, squeeze_sum_grad, squeeze_mean, squeeze_square, owner_share),
        (output_weight, output_sum_grad, output_mean, output_square, 1.0),
        (ffn_weight, ffn_sum_grad, ffn_mean, ffn_square, 1.0),
        (down_weight, down_sum_grad, down_mean, down_square, 1.0),
        (norms_weight, norms_sum_grad, norms_mean, norms_square, owner_share),
    ]
    updates = []
    squares = []
    for master, gradient, first_moment, second_moment, weighting in sharded:
        new_first, new_second, update_direction = adam_direction(
            master, gradient, first_moment, second_moment, fix_one, second_correction
        )
        updates.append((master, new_first, new_second, update_direction))
        squares.append(jnp.sum(master * master) * weighting)
        squares.append(jnp.sum(update_direction * update_direction) * weighting)
    total_squares = sum_everywhere(jnp.stack(squares)[None, :])[0]
    expand_pad = jnp.zeros((rank_count + 1, 2, 2, key_width), jnp.float32)
    expand_pad = lax.dynamic_update_index_in_dim(expand_pad, expand_grad, core, 2)
    replicas = jnp.concatenate(
        [expand_pad.reshape(rank_count + 1, -1), jnp.pad(group_grad[None, :], ((0, 0), (0, 4 * key_width - value_width)))]
    )
    replicas = sum_everywhere(replicas)
    expand_total = replicas[: rank_count + 1]
    group_total = replicas[rank_count + 1, :value_width]
    results = []
    for position, packed in enumerate(updates):
        master, new_first, new_second, update_direction = packed
        trust_ratio = jnp.sqrt(total_squares[2 * position]) / (
            jnp.sqrt(total_squares[2 * position + 1]) + eps_adam
        )
        results.append(
            (master - learn_rate * trust_ratio * update_direction, new_first, new_second)
        )
    replicated = []
    for master, gradient, first_moment, second_moment in (
        (expand_weight, expand_total, expand_mean, expand_square),
        (group_weight, group_total, group_mean, group_square),
    ):
        new_first, new_second, update_direction = adam_direction(
            master, gradient, first_moment, second_moment, fix_one, second_correction
        )
        trust_ratio = jnp.sqrt(jnp.sum(master * master)) / (
            jnp.sqrt(jnp.sum(update_direction * update_direction)) + eps_adam
        )
        replicated.append(
            (master - learn_rate * trust_ratio * update_direction, new_first, new_second)
        )
    return (
        block_out,
        tokens_grad,
        results[0][0],
        results[0][1],
        results[0][2],
        results[1][0],
        results[1][1],
        results[1][2],
        results[2][0],
        results[2][1],
        results[2][2],
        replicated[0][0],
        replicated[0][1],
        replicated[0][2],
        replicated[1][0],
        replicated[1][1],
        replicated[1][2],
        results[3][0],
        results[3][1],
        results[3][2],
        results[4][0],
        results[4][1],
        results[4][2],
        results[5][0],
        results[5][1],
        results[5][2],
        results[6][0],
        results[6][1],
        results[6][2],
    )


def solution(mesh):
    in_specs = (
        P(None, "seq", "head"),
        P(None, "seq", "head"),
        P("seq", "head", None),
        P("seq", "head", None),
        P("seq", "head", None),
        P("seq", "head", None),
        P("seq", "head", None),
        P("seq", "head", None),
        P("seq", None),
        P("seq", None),
        P("seq", None),
        P(),
        P(),
        P(),
        P(),
        P(),
        P(),
        P("head", "seq"),
        P("head", "seq"),
        P("head", "seq"),
        P("seq", None, "head"),
        P("seq", None, "head"),
        P("seq", None, "head"),
        P("head", "seq"),
        P("head", "seq"),
        P("head", "seq"),
        P(None, "seq"),
        P(None, "seq"),
        P(None, "seq"),
    )
    out_specs = (
        P(None, "seq", "head"),
        P(None, "seq", "head"),
        P("seq", "head", None),
        P("seq", "head", None),
        P("seq", "head", None),
        P("seq", "head", None),
        P("seq", "head", None),
        P("seq", "head", None),
        P("seq", None),
        P("seq", None),
        P("seq", None),
        P(),
        P(),
        P(),
        P(),
        P(),
        P(),
        P("head", "seq"),
        P("head", "seq"),
        P("head", "seq"),
        P("seq", None, "head"),
        P("seq", None, "head"),
        P("seq", None, "head"),
        P("head", "seq"),
        P("head", "seq"),
        P("head", "seq"),
        P(None, "seq"),
        P(None, "seq"),
        P(None, "seq"),
    )
    return jax.shard_map(
        per_device, mesh=mesh, in_specs=in_specs, out_specs=out_specs, check_vma=False
    )
```

time: 1460 us -> 813 us (0.56)
  waiting for transfers between devices: 841 us -> 218 us
  blocking collectives: 198 us -> 0 us
  local copies, waits for them, and re-layouts: 53.9 us -> 190 us
  starting transfers between devices: 2.08 us -> 63.9 us
  matrix products: 169 us -> 146 us
    reduce_scatter x10 -> x2, waiting for transfers between devices: 588 us -> 0.01 us  [the longest x1 0.01 us: per_device(): lax.psum_scatter(to_half(output_two), 'seq', scatter_dimension=0, tiled=F...]
    ppermute x0 -> x51, waiting for transfers between devices: none -> 218 us  [swap(): lax.ppermute(value_entries, axis, [(i, i ^ bit) for i in range(peers)])]
    all_gather x9 -> x2, waiting for transfers between devices: 192 us -> 0.01 us  [the longest x1 0.01 us: per_device(): lax.all_gather(output_pair, 'seq', axis=0)]
    all_gather x5 -> x0, blocking collectives: 126 us -> none  [the longest x1 31.5 us: per_device(): lax.all_gather(to_half(query_weight), 'seq', axis=0, tiled=True)]
    psum x5 -> x0, blocking collectives: 71.9 us -> none  [the longest x1 41.4 us: per_device(): lax.psum((squares, expand_pad, group_grad), ('seq', 'head'))]
    ppermute x0 -> x51, starting transfers between devices: none -> 63.2 us  [swap(): lax.ppermute(value_entries, axis, [(i, i ^ bit) for i in range(peers)])]
    unnamed x21 -> x4, waiting for transfers between devices: 61.8 us -> 0.07 us
    dynamic_slice x1 -> x19, local copies, waits for them, and re-layouts: 1.2 us -> 35 us  [the longest x18 33.9 us: pick(): return lax.dynamic_index_in_dim(value_entries, at, axis, keepdims=False)]
  transfers between devices with their start and end apart: 20 -> 55, of which waited for: 15 -> 29; matrix products, arithmetic and copies ran while one was open for 16% -> 54% of each run, Pallas kernels for 0% -> 0%
where the time goes in v1:
time: 813 us; the launch traced here: 805 us
  waiting for transfers between devices  218 us (27%)
  local copies, waits for them, and re-layouts  190 us (23%)
  other arithmetic  155 us (19%)
  matrix products  146 us (18%)
  starting transfers between devices  63.9 us (8%)
  between operations  32.4 us (4%)
    ppermute x51, waiting for transfers between devices, swap(): lax.ppermute(value_entries, axis, [(i, i ^ bit) for i in range(peers)])  218 us
    dot_general x27, matrix products, mm(): return jnp.einsum(pattern, left, right, preferred_element_type=jnp.float32)  85.6 us
    ppermute x51, starting transfers between devices, swap(): lax.ppermute(value_entries, axis, [(i, i ^ bit) for i in range(peers)])  63.2 us
    unnamed x416, local copies, waits for them, and re-layouts  44.5 us
    dynamic_slice x18, local copies, waits for them, and re-layouts, pick(): return lax.dynamic_index_in_dim(value_entries, at, axis, keepdims=False)  33.9 us
    dynamic_update_slice x48, local copies, waits for them, and re-layouts, span_local(): lax.scan(advance, start_state, (jnp.moveaxis(jnp.exp(closing[:, :, 0, :])...  21.3 us
    reduce_sum x16, other arithmetic, advance(): return (decay_item[:, :, None] * running + state_item, running)  19.2 us
    add x16, other arithmetic, advance(): return (decay_item[:, :, None] * running + state_item, running)  17 us
  transfers between devices with their start and end apart: 55, of which 29 were waited for; matrix products, arithmetic and copies ran while one was open for 54% of the time, Pallas kernels for 0%

profile of v1, /device:TPU:0, one launch (start us, length us, event | category | flops | bytes accessed | tf_op | source)
XLA Modules:
  0.0 805.5 jit_solution(16387484011089985226)
XLA Ops:
  8.3 3.0 collective-permute-start.15
  21.4 3.1 collective-permute-start.6
  25.7 6.2 collective-permute-done.2
  41.9 7.6 collective-permute-done.7
  50.6 14.2 %collective-permute-done.4 = bf16[2,2,128,384]{3,2,0,1:T(8,128)(2,1)S(1)} collective-permute-done((bf16[2,2,128,384]{3,2,0,1:T(8,128)(2,1)S(1)}, bf16[2,2,128,384]{3,2,0,1:T(8,128)(2,1)S(1)}, u32[]{:S(2)}, u32[]{:S(2)}) %collective-permute-start.4) | collective-permute-done | bytes 393248 | tf_op jit(solution)/shard_map/ppermute | solution.py:38
  70.4 22.9 %collective-permute-done.5 = bf16[2,2,2,128,384]{4,3,0,2,1:T(8,128)(2,1)S(1)} collective-permute-done((bf16[2,2,2,128,384]{4,3,0,2,1:T(8,128)(2,1)S(1)}, bf16[2,2,2,128,384]{4,3,0,2,1:T(8,128)(2,1)S(1)}, u32[]{:S(2)}, u32[]{:S(2)}) %collective-permute-start.5) | collective-permute-done | bytes 786464 | tf_op jit(solution)/shard_map/ppermute | solution.py:38
  93.7 3.2 copy.244
  116.7 3.0 convolution_select_fusion.1
  122.6 3.7 copy.253
  131.2 3.7 copy.254
  139.7 4.6 convolution_bitcast_fusion.4
  150.0 5.3 convolution_bitcast_fusion.3
  157.8 38.0 %while.34 = (s32[]{:T(128)}, f32[2,128,256]{2,1,0:T(8,128)S(1)}, f32[16,2,128,256]{3,2,1,0:T(8,128)}, f32[16,2,128,1]{2,1,3,0:T(2,128)}, f32[16,2,128]{2,0,1:T(8...) while((s32[]{:T(128)}, f32[2,128,256]{2,1,0:T(8,128)S(1)}, ...), condition=%wide.region_3.4_spmd.clone, body=%wide.region_2.3_spmd.clone.sunk | while | flops 262147 | bytes 1316968 | solution.py:145
  205.4 4.3 fusion.26
  212.2 9.0 %collective-permute-start.14 = (f32[2,128,256]{2,1,0:T(8,128)}, f32[2,128,256]{2,1,0:T(8,128)}, u32[]{:S(2)}, u32[]{:S(2)}) collective-permute-start(f32[2,128,256]{2,1,0:T(8,128)} %add_select_fusion.6), channel_id=1, source_target_pairs={{0,16},{4,20},{8,24},{12,28},{16,0},{20,4},{24,8},{28,12},{1,17},{... | collective-permute-start | bytes 786440 | tf_op jit(solution)/shard_map/ppermute | solution.py:38
  229.3 3.3 multiply_reduce_fusion.5
  238.7 24.1 %collective-permute-done.21 = bf16[2,1024,256]{2,1,0:T(8,128)(2,1)} collective-permute-done((bf16[2,1024,256]{2,1,0:T(8,128)(2,1)S(1)}, bf16[2,1024,256]{2,1,0:T(8,128)(2,1)}, u32[]{:S(2)}, u32[]{:S(2)}) %collective-permute-start.21) | collective-permute-done | bytes 1048608 | tf_op jit(solution)/shard_map/ppermute | solution.py:38
  266.4 3.1 multiply_reduce_fusion.2
  274.8 23.6 %collective-permute-done.17 = bf16[512,1024]{0,1:T(8,128)(2,1)S(1)} collective-permute-done((bf16[512,1024]{0,1:T(8,128)(2,1)}, bf16[512,1024]{0,1:T(8,128)(2,1)S(1)}, u32[]{:S(2)}, u32[]{:S(2)}) %collective-permute-start.17) | collective-permute-done | bytes 1048608 | tf_op jit(solution)/shard_map/ppermute | solution.py:38
  313.5 4.5 multiply_convert_fusion.1
  327.8 3.1 constant_dynamic-slice_fusion.9
  330.9 2.9 copy.281
  333.8 3.8 fusion.110
  342.7 4.1 multiply_convert_fusion.2
  351.1 15.2 %collective-permute-done.24 = bf16[512,1024]{0,1:T(8,128)(2,1)S(1)} collective-permute-done((bf16[512,1024]{0,1:T(8,128)(2,1)S(1)}, bf16[512,1024]{0,1:T(8,128)(2,1)S(1)}, u32[]{:S(2)}, u32[]{:S(2)}) %collective-permute-start.24) | collective-permute-done | bytes 1048608 | tf_op jit(solution)/shard_map/ppermute | solution.py:38
  374.4 4.0 copy.278
  385.7 3.8 convolution_bitcast_fusion
  389.5 3.2 convolution_bitcast_fusion.1
  396.5 4.3 fusion.94
  400.8 3.7 multiply_reduce_fusion
  404.6 3.7 multiply_subtract_fusion
  417.4 8.3 %collective-permute-done.40 = bf16[8,128,256]{1,2,0:T(8,128)(2,1)S(1)} collective-permute-done((bf16[8,128,256]{1,2,0:T(8,128)(2,1)S(1)}, bf16[8,128,256]{1,2,0:T(8,128)(2,1)S(1)}, u32[]{:S(2)}, u32[]{:S(2)}) %collective-permute-start.40) | collective-permute-done | bytes 524320 | tf_op jit(solution)/shard_map/ppermute | solution.py:38
  427.3 5.6 fusion.97
  436.6 3.2 fusion.89
  442.9 5.1 collective-permute-done.20
  454.3 3.5 multiply_reduce_fusion.3
  462.2 3.3 fusion.244
  465.5 5.4 fusion.67
  475.1 6.9 collective-permute-done.26
  484.8 5.3 collective-permute-done.27
  492.0 2.9 fusion.243
  494.9 13.4 %collective-permute-done.28 = f32[2,128,256]{2,1,0:T(8,128)S(1)} collective-permute-done((f32[2,128,256]{2,1,0:T(8,128)S(1)}, f32[2,128,256]{2,1,0:T(8,128)S(1)}, u32[]{:S(2)}, u32[]{:S(2)}) %collective-permute-start.28) | collective-permute-done | bytes 262176 | tf_op jit(solution)/shard_map/ppermute | solution.py:38
  511.0 43.0 %while.33 = (s32[]{:T(128)}, f32[2,128,256]{2,1,0:T(8,128)S(1)}, f32[16,2,128]{2,0,1:T(8,128)S(1)}, f32[16,2,128,256]{3,2,1,0:T(8,128)}, f32[16,2,128,256]{3,2,1...) while((s32[]{:T(128)}, f32[2,128,256]{2,1,0:T(8,128)S(1)}, ...), condition=%wide.region_12.13_spmd, body=%wide.region_10.12_spmd.sunk | while | flops 261891 | bytes 1579137 | solution.py:145
  554.0 5.7 fusion.166
  559.8 6.0 pad_add_fusion
  566.0 4.5 fusion.135
  573.3 3.5 fusion.157
  595.6 3.8 add_convert_fusion
  601.1 5.6 convolution_bitcast_fusion.2
  606.8 6.6 reshape_reshape.12
  621.0 7.2 fusion.18
  628.2 17.3 %collective-permute-done.47 = f32[18,512]{1,0:T(8,128)S(1)} collective-permute-done((f32[18,512]{1,0:T(8,128)S(1)}, f32[18,512]{1,0:T(8,128)S(1)}, u32[]{:S(2)}, u32[]{:S(2)}) %collective-permute-start.47) | collective-permute-done | bytes 36896 | tf_op jit(solution)/shard_map/ppermute | solution.py:38
  655.7 3.7 collective-permute-start.50
  667.9 7.1 collective-permute-done.37
  687.0 6.1 fusion.7
  695.1 4.0 reshape_reshape.11
  699.1 3.4 constant_dynamic-slice_fusion.6
  711.1 10.3 %collective-permute-done.32 = bf16[2,2,2,128,384]{3,4,1,2,0:T(8,128)(2,1)} collective-permute-done((bf16[2,2,2,128,384]{3,4,1,2,0:T(8,128)(2,1)}, bf16[2,2,2,128,384]{3,4,1,2,0:T(8,128)(2,1)}, u32[]{:S(2)}, u32[]{:S(2)}) %collective-permute-start.32) | collective-permute-done | bytes 786464 | tf_op jit(solution)/shard_map/ppermute | solution.py:38
  724.1 3.1 multiply_reduce_fusion.10
  727.3 4.0 collective-permute-done.33
  732.3 4.4 fusion.5
  741.1 3.7 collective-permute-done.35
  752.0 2.9 multiply_reduce_fusion.8
  757.3 6.4 stack.258
  (854 shorter events, 386.0 us)
Async XLA Ops:
  7.2 190.4 %all-gather.6.cloned.1.call-start = ((), (), s32[]{:S(2)}) async-start(), calls=%async_computation.5 | async-start | bytes 1179648 | tf_op jit(solution)/shard_map/all_gather | solution.py:236
  8.3 5.3 collective-permute-start.15
  14.3 290.1 %all-gather.4.cloned.1.call-start = ((), (), s32[]{:S(2)}) async-start(), calls=%async_computation.2 | async-start | bytes 4866048 | tf_op jit(solution)/shard_map/all_gather | solution.py:240
  16.7 49.0 %collective-permute-start = (bf16[1024,256]{0,1:T(8,128)(2,1)}, bf16[1024,256]{0,1:T(8,128)(2,1)S(1)}, u32[]{:S(2)}, u32[]{:S(2)}) collective-permute-start(bf16[1024,256]{0,1:T(8,128)(2,1)} %bitcast.632), channel_id=1, source_target_pairs={{0,2},{1,3},{2,0},{3,1},{4,6},{5,7},{6,4},{7,5},{8,10},{9,11},{10,... | collective-permute-start | bytes 1572872 | tf_op jit(solution)/shard_map/ppermute | solution.py:38
  20.5 11.5 %collective-permute-start.2 = (bf16[128,384]{1,0:T(8,128)(2,1)}, bf16[128,384]{1,0:T(8,128)(2,1)}, u32[]{:S(2)}, u32[]{:S(2)}) collective-permute-start(bf16[128,384]{1,0:T(8,128)(2,1)} %fusion.192), channel_id=1, source_target_pairs={{0,2},{1,3},{2,0},{3,1},{4,6},{5,7},{6,4},{7,5},{8,10},{9,11},{10,... | collective-permute-start | bytes 294920 | tf_op jit(solution)/shard_map/ppermute | solution.py:38
  21.4 13.3 %collective-permute-start.6 = (bf16[128,512]{1,0:T(8,128)(2,1)}, bf16[128,512]{1,0:T(8,128)(2,1)}, u32[]{:S(2)}, u32[]{:S(2)}) collective-permute-start(bf16[128,512]{1,0:T(8,128)(2,1)} %bitcast.559), channel_id=1, source_target_pairs={{0,16},{4,20},{8,24},{12,28},{16,0},{20,4},{24,8},{28,12},{1,17},{... | collective-permute-start | bytes 393224 | tf_op jit(solution)/shard_map/ppermute | solution.py:38
  25.5 679.5 %reduce-scatter.3.cloned.1.call-start = ((), (), s32[]{:S(2)}) async-start(), calls=%async_computation.3 | async-start | bytes 589824 | tf_op jit(solution)/shard_map/reduce_scatter | solution.py:406
  25.7 79.8 %copy-start.147 = (f32[16,2,1,128]{3,2,1,0:T(1,128)}, f32[16,2,1,128]{3,2,1,0:T(1,128)S(1)}, u32[]{:S(2)}) copy-start(f32[16,2,1,128]{3,2,1,0:T(1,128)S(1)} %constant_dynamic-slice_fusion.1) | copy-start | bytes 49156
  25.7 91.0 %copy-start.139 = (pred[64,64]{1,0:T(8,128)(4,1)}, pred[64,64]{1,0:T(8,128)(4,1)S(1)}, u32[]{:S(2)}) copy-start(pred[64,64]{1,0:T(8,128)(4,1)S(1)} %iota_compare_fusion.3) | copy-start | bytes 12292
  32.9 5.7 collective-permute-start.3
  36.4 13.1 %collective-permute-start.7 = (bf16[2,128,512]{2,1,0:T(8,128)(2,1)}, bf16[2,128,512]{2,1,0:T(8,128)(2,1)}, u32[]{:S(2)}, u32[]{:S(2)}) collective-permute-start(bf16[2,128,512]{2,1,0:T(8,128)(2,1)} %pad_maximum_fusion.34), channel_id=1, source_target_pairs={{0,8},{4,12},{8,0},{12,4},{16,24},{20,28},{24,16},{28,20},{1,9},{5... | collective-permute-start | bytes 786440 | tf_op jit(solution)/shard_map/ppermute | solution.py:38
  38.8 26.1 %collective-permute-start.4 = (bf16[2,2,128,384]{3,2,0,1:T(8,128)(2,1)S(1)}, bf16[2,2,128,384]{3,2,0,1:T(8,128)(2,1)S(1)}, u32[]{:S(2)}, u32[]{:S(2)}) collective-permute-start(bf16[2,2,128,384]{3,2,0,1:T(8,128)(2,1)S(1)} %pad_maximum_fusion.33), channel_id=1, source_target_pairs={{0,16},{4,20},{8,24},{12,28},{16,0},{20,4},{24,8},{28,12},{1,17},{... | collective-permute-start | bytes 1179656 | tf_op jit(solution)/shard_map/ppermute | solution.py:38
  50.5 16.4 %collective-permute-start.8 = (bf16[2,2,128,512]{3,2,0,1:T(8,128)(2,1)S(1)}, bf16[2,2,128,512]{3,2,0,1:T(8,128)(2,1)S(1)}, u32[]{:S(2)}, u32[]{:S(2)}) collective-permute-start(bf16[2,2,128,512]{3,2,0,1:T(8,128)(2,1)S(1)} %pad_maximum_fusion.32), channel_id=1, source_target_pairs={{0,4},{4,0},{8,12},{12,8},{16,20},{20,16},{24,28},{28,24},{1,5},{5... | collective-permute-start | bytes 1572872 | tf_op jit(solution)/shard_map/ppermute | solution.py:38
  65.0 28.2 %collective-permute-start.5 = (bf16[2,2,2,128,384]{4,3,0,2,1:T(8,128)(2,1)S(1)}, bf16[2,2,2,128,384]{4,3,0,2,1:T(8,128)(2,1)S(1)}, u32[]{:S(2)}, u32[]{:S(2)}) collective-permute-start(bf16[2,2,2,128,384]{4,3,0,2,1:T(8,128)(2,1)S(1)} %pad_maximum_fusion.27), channel_id=1, source_target_pairs={{0,8},{4,12},{8,0},{12,4},{16,24},{20,28},{24,16},{28,20},{1,9},{5... | collective-permute-start | bytes 2359304 | tf_op jit(solution)/shard_map/ppermute | solution.py:38
  66.9 32.9 %collective-permute-start.1 = (bf16[2,1024,256]{1,2,0:T(8,128)(2,1)}, bf16[2,1024,256]{1,2,0:T(8,128)(2,1)}, u32[]{:S(2)}, u32[]{:S(2)}) collective-permute-start(bf16[2,1024,256]{1,2,0:T(8,128)(2,1)} %pad_maximum_fusion.23), channel_id=1, source_target_pairs={{0,1},{1,0},{2,3},{3,2},{4,5},{5,4},{6,7},{7,6},{8,9},{9,8},{10,11... | collective-permute-start | bytes 3145736 | tf_op jit(solution)/shard_map/ppermute | solution.py:38
  68.9 51.0 %collective-permute-start.9 = (bf16[2,2,2,128,512]{4,3,0,1,2:T(8,128)(2,1)}, bf16[2,2,2,128,512]{4,3,0,1,2:T(8,128)(2,1)}, u32[]{:S(2)}, u32[]{:S(2)}) collective-permute-start(bf16[2,2,2,128,512]{4,3,0,1,2:T(8,128)(2,1)} %pad_maximum_fusion.24), channel_id=1, source_target_pairs={{0,2},{1,3},{2,0},{3,1},{4,6},{5,7},{6,4},{7,5},{8,10},{9,11},{10,... | collective-permute-start | bytes 3145736 | tf_op jit(solution)/shard_map/ppermute | solution.py:38
  109.1 87.0 %copy-start = (f32[2,16,64,128]{3,1,2,0:T(8,128)}, f32[2,16,64,128]{3,1,2,0:T(8,128)S(1)}, u32[]{:S(2)}) copy-start(f32[2,16,64,128]{3,1,2,0:T(8,128)S(1)} %fusion.145) | copy-start | bytes 3145732
  109.2 93.0 %copy-start.172 = (f32[2,128]{1,0:T(2,128)}, f32[2,128]{1,0:T(2,128)S(1)}, u32[]{:S(2)}) copy-start(f32[2,128]{1,0:T(2,128)S(1)} %exp.56) | copy-start | bytes 3076
  109.2 10.5 %collective-permute-start.10 = (f32[2,128]{1,0:T(2,128)S(1)}, f32[2,128]{1,0:T(2,128)S(1)}, u32[]{:S(2)}, u32[]{:S(2)}) collective-permute-start(f32[2,128]{1,0:T(2,128)S(1)} %exp.56), channel_id=1, source_target_pairs={{0,4},{4,0},{8,12},{12,8},{16,20},{20,16},{24,28},{28,24},{1,5},{5... | collective-permute-start | bytes 3080 | tf_op jit(solution)/shard_map/ppermute | solution.py:38
  116.7 88.7 %copy-start.17 = (f32[2,16,64,128]{3,2,1,0:T(8,128)}, f32[2,16,64,128]{3,2,1,0:T(8,128)S(1)}, u32[]{:S(2)}) copy-start(f32[2,16,64,128]{3,2,1,0:T(8,128)S(1)} %fusion.161) | copy-start | bytes 3145732
  119.8 82.4 %copy-start.160 = (f32[2,128]{1,0:T(2,128)}, f32[2,128]{1,0:T(2,128)S(1)}, u32[]{:S(2)}) copy-start(f32[2,128]{1,0:T(2,128)S(1)} %collective-permute-done.10) | copy-start | bytes 3076
  119.8 91.5 %copy-start.170 = (f32[2,128]{1,0:T(2,128)}, f32[2,128]{1,0:T(2,128)S(1)}, u32[]{:S(2)}) copy-start(f32[2,128]{1,0:T(2,128)S(1)} %exponential_multiply_fusion.1) | copy-start | bytes 3076
  119.8 77.2 %collective-permute-start.11 = (f32[2,128]{1,0:T(2,128)S(1)}, f32[2,128]{1,0:T(2,128)S(1)}, u32[]{:S(2)}, u32[]{:S(2)}) collective-permute-start(f32[2,128]{1,0:T(2,128)S(1)} %exponential_multiply_fusion.1), channel_id=1, source_target_pairs={{0,8},{4,12},{8,0},{12,4},{16,24},{20,28},{24,16},{28,20},{1,9},{5... | collective-permute-start | bytes 3080 | tf_op jit(solution)/shard_map/ppermute | solution.py:38
  195.8 6.5 collective-permute-start.12
  203.3 8.0 collective-permute-start.13
  212.2 16.0 %collective-permute-start.14 = (f32[2,128,256]{2,1,0:T(8,128)}, f32[2,128,256]{2,1,0:T(8,128)}, u32[]{:S(2)}, u32[]{:S(2)}) collective-permute-start(f32[2,128,256]{2,1,0:T(8,128)} %add_select_fusion.6), channel_id=1, source_target_pairs={{0,16},{4,20},{8,24},{12,28},{16,0},{20,4},{24,8},{28,12},{1,17},{... | collective-permute-start | bytes 786440 | tf_op jit(solution)/shard_map/ppermute | solution.py:38
  237.1 28.6 %collective-permute-start.16 = (bf16[1024,1024]{0,1:T(8,128)(2,1)}, bf16[1024,1024]{0,1:T(8,128)(2,1)}, u32[]{:S(2)}, u32[]{:S(2)}) collective-permute-start(bf16[1024,1024]{0,1:T(8,128)(2,1)} %bitcast_convert_fusion), channel_id=1, source_target_pairs={{0,1},{1,0},{2,3},{3,2},{4,5},{5,4},{6,7},{7,6},{8,9},{9,8},{10,11... | collective-permute-start | bytes 6291464 | tf_op jit(solution)/shard_map/ppermute | solution.py:38
  237.1 25.7 %collective-permute-start.21 = (bf16[2,1024,256]{2,1,0:T(8,128)(2,1)S(1)}, bf16[2,1024,256]{2,1,0:T(8,128)(2,1)}, u32[]{:S(2)}, u32[]{:S(2)}) collective-permute-start(bf16[2,1024,256]{2,1,0:T(8,128)(2,1)S(1)} %copy-done.112), channel_id=1, source_target_pairs={{0,2},{1,3},{2,0},{3,1},{4,6},{5,7},{6,4},{7,5},{8,10},{9,11},{10,... | collective-permute-start | bytes 3145736 | tf_op jit(solution)/shard_map/ppermute | solution.py:38
  265.7 32.7 %collective-permute-start.22 = (bf16[2,2,1024,256]{3,2,1,0:T(8,128)(2,1)}, bf16[2,2,1024,256]{3,2,1,0:T(8,128)(2,1)}, u32[]{:S(2)}, u32[]{:S(2)}) collective-permute-start(bf16[2,2,1024,256]{3,2,1,0:T(8,128)(2,1)} %pad_maximum_fusion.5), channel_id=1, source_target_pairs={{0,1},{1,0},{2,3},{3,2},{4,5},{5,4},{6,7},{7,6},{8,9},{9,8},{10,11... | collective-permute-start | bytes 6291464 | tf_op jit(solution)/shard_map/ppermute | solution.py:38
  273.3 25.1 %collective-permute-start.17 = (bf16[512,1024]{0,1:T(8,128)(2,1)}, bf16[512,1024]{0,1:T(8,128)(2,1)S(1)}, u32[]{:S(2)}, u32[]{:S(2)}) collective-permute-start(bf16[512,1024]{0,1:T(8,128)(2,1)} %constant_dynamic-slice_fusion.13), channel_id=1, source_target_pairs={{0,2},{1,3},{2,0},{3,1},{4,6},{5,7},{6,4},{7,5},{8,10},{9,11},{10,... | collective-permute-start | bytes 3145736 | tf_op jit(solution)/shard_map/ppermute | solution.py:38
  298.4 4.5 collective-permute-start.18
  327.3 12.1 %collective-permute-start.23 = (bf16[512,1024]{0,1:T(8,128)(2,1)}, bf16[512,1024]{0,1:T(8,128)(2,1)}, u32[]{:S(2)}, u32[]{:S(2)}) collective-permute-start(bf16[512,1024]{0,1:T(8,128)(2,1)} %bitcast.628), channel_id=1, source_target_pairs={{0,1},{1,0},{2,3},{3,2},{4,5},{5,4},{6,7},{7,6},{8,9},{9,8},{10,11... | collective-permute-start | bytes 3145736 | tf_op jit(solution)/shard_map/ppermute | solution.py:38
  341.2 25.1 %collective-permute-start.24 = (bf16[512,1024]{0,1:T(8,128)(2,1)S(1)}, bf16[512,1024]{0,1:T(8,128)(2,1)S(1)}, u32[]{:S(2)}, u32[]{:S(2)}) collective-permute-start(bf16[512,1024]{0,1:T(8,128)(2,1)S(1)} %fusion.60), channel_id=1, source_target_pairs={{0,2},{1,3},{2,0},{3,1},{4,6},{5,7},{6,4},{7,5},{8,10},{9,11},{10,... | collective-permute-start | bytes 3145736 | tf_op jit(solution)/shard_map/ppermute | solution.py:38
  369.4 31.4 %collective-permute-start.25 = (bf16[1024,1024]{0,1:T(8,128)(2,1)}, bf16[1024,1024]{0,1:T(8,128)(2,1)}, u32[]{:S(2)}, u32[]{:S(2)}) collective-permute-start(bf16[1024,1024]{0,1:T(8,128)(2,1)} %convert_element_type.276), channel_id=1, source_target_pairs={{0,1},{1,0},{2,3},{3,2},{4,5},{5,4},{6,7},{7,6},{8,9},{9,8},{10,11... | collective-permute-start | bytes 6291464 | tf_op jit(solution)/shard_map/ppermute | solution.py:38
  394.4 18.1 %collective-permute-start.19 = (bf16[2,1024,2,256]{3,1,2,0:T(8,128)(2,1)}, bf16[2,1024,2,256]{3,1,2,0:T(8,128)(2,1)}, u32[]{:S(2)}, u32[]{:S(2)}) collective-permute-start(bf16[2,1024,2,256]{3,1,2,0:T(8,128)(2,1)} %fusion.51), channel_id=1, source_target_pairs={{0,1},{1,0},{2,3},{3,2},{4,5},{5,4},{6,7},{7,6},{8,9},{9,8},{10,11... | collective-permute-start | bytes 6291464 | tf_op jit(solution)/shard_map/ppermute | solution.py:38
  410.9 14.8 %collective-permute-start.40 = (bf16[8,128,256]{1,2,0:T(8,128)(2,1)S(1)}, bf16[8,128,256]{1,2,0:T(8,128)(2,1)S(1)}, u32[]{:S(2)}, u32[]{:S(2)}) collective-permute-start(bf16[8,128,256]{1,2,0:T(8,128)(2,1)S(1)} %bitcast.633), channel_id=1, source_target_pairs={{0,2},{1,3},{2,0},{3,1},{4,6},{5,7},{6,4},{7,5},{8,10},{9,11},{10,... | collective-permute-start | bytes 1572872 | tf_op jit(solution)/shard_map/ppermute | solution.py:38
  416.0 31.9 %collective-permute-start.20 = (bf16[2,1024,256]{2,1,0:T(8,128)(2,1)}, bf16[2,1024,256]{2,1,0:T(8,128)(2,1)}, u32[]{:S(2)}, u32[]{:S(2)}) collective-permute-start(bf16[2,1024,256]{2,1,0:T(8,128)(2,1)} %fusion.130), channel_id=1, source_target_pairs={{0,2},{1,3},{2,0},{3,1},{4,6},{5,7},{6,4},{7,5},{8,10},{9,11},{10,... | collective-permute-start | bytes 3145736 | tf_op jit(solution)/shard_map/ppermute | solution.py:38
  426.8 324.0 %reduce-scatter.5.cloned.1.call-start = ((), (), s32[]{:S(2)}) async-start(), calls=%async_computation.4 | async-start | bytes 4866048 | tf_op jit(solution)/shard_map/reduce_scatter | solution.py:329
  473.3 8.7 %collective-permute-start.26 = (f32[2,128,256]{2,1,0:T(8,128)S(1)}, f32[2,128,256]{2,1,0:T(8,128)S(1)}, u32[]{:S(2)}, u32[]{:S(2)}) collective-permute-start(f32[2,128,256]{2,1,0:T(8,128)S(1)} %fusion.173), channel_id=1, source_target_pairs={{0,4},{4,0},{8,12},{12,8},{16,20},{20,16},{24,28},{28,24},{1,5},{5... | collective-permute-start | bytes 786440 | tf_op jit(solution)/shard_map/ppermute | solution.py:38
  482.2 8.0 collective-permute-start.27
  490.3 18.0 %collective-permute-start.28 = (f32[2,128,256]{2,1,0:T(8,128)S(1)}, f32[2,128,256]{2,1,0:T(8,128)S(1)}, u32[]{:S(2)}, u32[]{:S(2)}) collective-permute-start(f32[2,128,256]{2,1,0:T(8,128)S(1)} %add_select_fusion.4), channel_id=1, source_target_pairs={{0,16},{4,20},{8,24},{12,28},{16,0},{20,4},{24,8},{28,12},{1,17},{... | collective-permute-start | bytes 786440 | tf_op jit(solution)/shard_map/ppermute | solution.py:38
  613.6 6.7 collective-permute-start.46
  618.7 40.7 %collective-permute-start.36 = (bf16[2,2,2,128,512]{4,3,0,1,2:T(8,128)(2,1)}, bf16[2,2,2,128,512]{4,3,0,1,2:T(8,128)(2,1)}, u32[]{:S(2)}, u32[]{:S(2)}) collective-permute-start(bf16[2,2,2,128,512]{4,3,0,1,2:T(8,128)(2,1)} %bitcast.481), channel_id=1, source_target_pairs={{0,2},{1,3},{2,0},{3,1},{4,6},{5,7},{6,4},{7,5},{8,10},{9,11},{10,... | collective-permute-start | bytes 3145736 | tf_op jit(solution)/shard_map/ppermute | solution.py:38
  620.0 33.2 %collective-permute-start.30 = (f32[16,1024]{1,0:T(8,128)S(1)}, f32[16,1024]{1,0:T(8,128)S(1)}, u32[]{:S(2)}, u32[]{:S(2)}) collective-permute-start(f32[16,1024]{1,0:T(8,128)S(1)} %convolution_bitcast_fusion.6), channel_id=1, source_target_pairs={{0,1},{1,0},{2,3},{3,2},{4,5},{5,4},{6,7},{7,6},{8,9},{9,8},{10,11... | collective-permute-start | bytes 196616 | tf_op jit(solution)/shard_map/ppermute | solution.py:38
  620.3 25.2 %collective-permute-start.47 = (f32[18,512]{1,0:T(8,128)S(1)}, f32[18,512]{1,0:T(8,128)S(1)}, u32[]{:S(2)}, u32[]{:S(2)}) collective-permute-start(f32[18,512]{1,0:T(8,128)S(1)} %fusion.284), channel_id=1, source_target_pairs={{0,2},{1,3},{2,0},{3,1},{4,6},{5,7},{6,4},{7,5},{8,10},{9,11},{10,... | collective-permute-start | bytes 110600 | tf_op jit(solution)/shard_map/ppermute | solution.py:38
  645.5 5.1 collective-permute-start.48
  650.5 36.4 %collective-permute-start.29 = (bf16[1024,1024]{0,1:T(8,128)(2,1)}, bf16[1024,1024]{0,1:T(8,128)(2,1)}, u32[]{:S(2)}, u32[]{:S(2)}) collective-permute-start(bf16[1024,1024]{0,1:T(8,128)(2,1)} %fusion.18), channel_id=1, source_target_pairs={{0,1},{1,0},{2,3},{3,2},{4,5},{5,4},{6,7},{7,6},{8,9},{9,8},{10,11... | collective-permute-start | bytes 6291464 | tf_op jit(solution)/shard_map/ppermute | solution.py:38
  650.7 5.0 collective-permute-start.49
  655.7 8.8 %collective-permute-start.50 = (f32[18,512]{1,0:T(8,128)S(1)}, f32[18,512]{1,0:T(8,128)S(1)}, u32[]{:S(2)}, u32[]{:S(2)}) collective-permute-start(f32[18,512]{1,0:T(8,128)S(1)} %add.708), channel_id=1, source_target_pairs={{0,16},{4,20},{8,24},{12,28},{16,0},{20,4},{24,8},{28,12},{1,17},{... | collective-permute-start | bytes 110600 | tf_op jit(solution)/shard_map/ppermute | solution.py:38
  661.1 13.9 %collective-permute-start.37 = (bf16[2,2,128,512]{3,2,0,1:T(8,128)(2,1)S(1)}, bf16[2,2,128,512]{3,2,0,1:T(8,128)(2,1)}, u32[]{:S(2)}, u32[]{:S(2)}) collective-permute-start(bf16[2,2,128,512]{3,2,0,1:T(8,128)(2,1)S(1)} %fusion.168), channel_id=1, source_target_pairs={{0,4},{4,0},{8,12},{12,8},{16,20},{20,16},{24,28},{28,24},{1,5},{5... | collective-permute-start | bytes 1572872 | tf_op jit(solution)/shard_map/ppermute | solution.py:38
  677.3 7.4 collective-permute-start.38
  686.3 21.0 %collective-permute-start.39 = (bf16[128,512]{1,0:T(8,128)(2,1)}, bf16[128,512]{1,0:T(8,128)(2,1)S(1)}, u32[]{:S(2)}, u32[]{:S(2)}) collective-permute-start(bf16[128,512]{1,0:T(8,128)(2,1)} %fusion.189), channel_id=1, source_target_pairs={{0,16},{4,20},{8,24},{12,28},{16,0},{20,4},{24,8},{28,12},{1,17},{... | collective-permute-start | bytes 393224 | tf_op jit(solution)/shard_map/ppermute | solution.py:38
  703.5 17.9 %collective-permute-start.32 = (bf16[2,2,2,128,384]{3,4,1,2,0:T(8,128)(2,1)}, bf16[2,2,2,128,384]{3,4,1,2,0:T(8,128)(2,1)}, u32[]{:S(2)}, u32[]{:S(2)}) collective-permute-start(bf16[2,2,2,128,384]{3,4,1,2,0:T(8,128)(2,1)} %bitcast.557), channel_id=1, source_target_pairs={{0,4},{4,0},{8,12},{12,8},{16,20},{20,16},{24,28},{28,24},{1,5},{5... | collective-permute-start | bytes 2359304 | tf_op jit(solution)/shard_map/ppermute | solution.py:38
  722.9 8.3 %collective-permute-start.33 = (bf16[2,2,128,384]{2,3,0,1:T(8,128)(2,1)S(1)}, bf16[2,2,128,384]{2,3,0,1:T(8,128)(2,1)S(1)}, u32[]{:S(2)}, u32[]{:S(2)}) collective-permute-start(bf16[2,2,128,384]{2,3,0,1:T(8,128)(2,1)S(1)} %fusion.176), channel_id=1, source_target_pairs={{0,2},{1,3},{2,0},{3,1},{4,6},{5,7},{6,4},{7,5},{8,10},{9,11},{10,... | collective-permute-start | bytes 1179656 | tf_op jit(solution)/shard_map/ppermute | solution.py:38
  731.4 6.8 collective-permute-start.34
  738.2 6.6 collective-permute-start.35
  739.9 23.8 %collective-permute-start.31 = (bf16[1024,256]{0,1:T(8,128)(2,1)S(1)}, bf16[1024,256]{0,1:T(8,128)(2,1)S(1)}, u32[]{:S(2)}, u32[]{:S(2)}) collective-permute-start(bf16[1024,256]{0,1:T(8,128)(2,1)S(1)} %fusion.167), channel_id=1, source_target_pairs={{0,2},{1,3},{2,0},{3,1},{4,6},{5,7},{6,4},{7,5},{8,10},{9,11},{10,... | collective-permute-start | bytes 1572872 | tf_op jit(solution)/shard_map/ppermute | solution.py:38
  745.6 51.6 %copy-start.157 = (f32[128,16]{0,1:T(8,128)}, f32[128,16]{0,1:T(8,128)S(1)}, u32[]{:S(2)}) copy-start(f32[128,16]{0,1:T(8,128)S(1)} %get-tuple-element.396) | copy-start | bytes 24580
  745.6 51.6 %copy-start.158 = (f32[128,16]{0,1:T(8,128)}, f32[128,16]{0,1:T(8,128)S(1)}, u32[]{:S(2)}) copy-start(f32[128,16]{0,1:T(8,128)S(1)} %get-tuple-element.397) | copy-start | bytes 24580
  763.6 1.6 collective-permute-start.41
  765.2 3.6 collective-permute-start.42
  768.8 3.5 collective-permute-start.43
  772.4 3.5 collective-permute-start.44
  775.9 4.4 collective-permute-start.45
  (189 other events, 1351.7 us)
Sparse Core Ops, SparseCore 0:
  14.4 48.8 all-gather.5
  66.1 81.7 all-gather.3
  426.9 61.7 reduce-scatter.2
  492.6 91.9 reduce-scatter.4

commit v2 on v1

v2 whole, which is shorter than its diff:
```python
import jax
import jax.numpy as jnp
from jax import lax
from jax.experimental import pallas as pl
from jax.experimental.pallas import tpu as pltpu
from jax.sharding import PartitionSpec as P

SPAN = 64
STEP = 10


eps_norm = 1e-06
gate_scale = 16.0
beta_one = 0.9
beta_two = 0.999
eps_adam = 1e-06
decay_rate = 0.01
learn_rate = 0.5
highest = lax.Precision.HIGHEST


def to_half(value_entries):
    return value_entries.astype(jnp.bfloat16)


def to_float(value_entries):
    return value_entries.astype(jnp.float32)


def mm(pattern, left, right):
    return jnp.einsum(pattern, left, right, preferred_element_type=jnp.float32)


def exact(pattern, left, right):
    return jnp.einsum(pattern, left, right, precision=highest)


def swap(value_entries, axis, bit):
    peers = lax.axis_size(axis)
    return lax.ppermute(value_entries, axis, [(i, i ^ bit) for i in range(peers)])


def bit_of(axis, bit):
    return (lax.axis_index(axis) // bit) % 2


def pick(value_entries, at, axis=0):
    return lax.dynamic_index_in_dim(value_entries, at, axis, keepdims=False)


def ordered(mine, other, upper):
    return (jnp.where(upper == 0, mine, other), jnp.where(upper == 0, other, mine))


def seq_bits():
    bits, bit = [], lax.axis_size("seq") // 2
    while bit:
        bits.append(("seq", bit))
        bit //= 2
    return bits


def cube_rank():
    return [("head", 2)] + seq_bits()


def grow(part, held, stages):
    for stage in stages:
        low, high = ordered(part, swap(part, *stage), bit_of(*stage))
        held = sorted(held + [stage], key=cube_rank().index)
        part = jnp.stack([low, high], axis=held.index(stage))
    return part, held


def grown(part, held):
    return part.reshape((2, lax.axis_size("seq")) + part.shape[len(held) :])


def gather_cube(part, stages):
    return grown(*grow(part, [], stages))


def split(part, held, stage):
    if held is None:
        held = cube_rank()
        part = part.reshape((2,) * len(held) + part.shape[2:])
    at = held.index(stage)
    return pick(part, bit_of(*stage), at), to_half(pick(part, 1 - bit_of(*stage), at))


def shrink(part, held, stages, pin=lambda at, moved: moved):
    if held is None:
        held = cube_rank()
        part = part.reshape((2,) * len(held) + part.shape[2:])
    held = list(held)
    for number, (axis, bit) in enumerate(stages):
        at = held.index((axis, bit))
        held.pop(at)
        upper = bit_of(axis, bit)
        moved = pin(number, swap(to_half(pick(part, 1 - upper, at)), axis, bit))
        part = to_float(pick(part, upper, at)) + to_float(moved)
    return [part, held]


def scatter_cube(part, stages, pin=lambda at, moved: moved):
    return shrink(part, None, stages, pin)[0]


def sum_everywhere(value_entries):
    for axis, bit in [("head", 1), ("head", 2)] + seq_bits()[::-1]:
        value_entries = value_entries + swap(value_entries, axis, bit)
    return value_entries


def after(value_entries, *others):
    return lax.optimization_barrier((value_entries, others))[0]


def scan_blocks(decay, state, reverse):
    before_decay, before_state = (jnp.ones_like(decay), jnp.zeros_like(state))
    heard = []
    for axis, bit in seq_bits()[::-1]:
        upper = bit_of(axis, bit) == (0 if reverse else 1)
        other_decay = swap(decay, axis, bit)
        heard.append(swap(to_half(state), axis, bit))
        other_state = to_float(heard[-1])
        before_state = jnp.where(upper, before_decay * other_state + before_state, before_state)
        before_decay = jnp.where(upper, before_decay * other_decay, before_decay)
        state = jnp.where(
            upper,
            decay * other_state + state,
            other_decay * state + other_state,
        )
        decay = decay * other_decay
    return before_state, heard


TILE = 256
LANES = 128
VALUES = 256
VMEM_LIMIT = 50 * 1024 * 1024


def mul(left, right, left_dim=1, right_dim=0):
    return lax.dot_general(
        to_half(left),
        to_half(right),
        (((left_dim,), (right_dim,)), ((), ())),
        preferred_element_type=jnp.float32,
    )


def mul_exact(left, right, left_dim=1, right_dim=0):
    return lax.dot_general(
        left,
        right,
        (((left_dim,), (right_dim,)), ((), ())),
        precision=highest,
        preferred_element_type=jnp.float32,
    )


def mul_ones(ones, right):
    total = None
    for _ in range(3):
        part = to_half(right)
        right = right - to_float(part)
        product = mul(ones, part)
        total = product if total is None else total + product
    return total


def at_or_after(size):
    row = lax.broadcasted_iota(jnp.int32, (size, size), 0)
    column = lax.broadcasted_iota(jnp.int32, (size, size), 1)
    return row >= column


def ones_where(mask):
    return jnp.where(mask, 1.0, 0.0).astype(jnp.bfloat16)


def log_sigmoid(z):
    decay = jnp.exp(-jnp.abs(z))
    ratio = decay / (2.0 + decay)
    square = ratio * ratio
    series = 1.0 / 15.0
    for odd in (13.0, 11.0, 9.0, 7.0, 5.0, 3.0, 1.0):
        series = series * square + 1.0 / odd
    return jnp.minimum(z, 0.0) - 2.0 * ratio * series


def call(body, steps, ins, outs, reverse=False, scratch=(), cost=0):
    def spec(shape, axis):
        block = tuple(n // steps if d == axis else n for d, n in enumerate(shape))

        def where(i):
            return tuple((steps - 1 - i if reverse else i) if d == axis else 0 for d in range(len(shape)))

        return pl.BlockSpec(block, where)

    return pl.pallas_call(
        body,
        grid=(steps,),
        in_specs=[spec(array.shape, axis) for array, axis in ins],
        out_specs=[spec(shape, axis) for shape, _, axis in outs],
        out_shape=[jax.ShapeDtypeStruct(shape, dtype) for shape, dtype, _ in outs],
        scratch_shapes=list(scratch),
        compiler_params=pltpu.CompilerParams(vmem_limit_bytes=VMEM_LIMIT),
        cost_estimate=pl.CostEstimate(flops=1, bytes_accessed=0, transcendentals=0) if cost else None,
    )(*[array for array, _ in ins])


def heads(width):
    return [slice(h * width, (h + 1) * width) for h in range(2)]


def whole_tile(within):
    spans, offset = [], jnp.zeros_like(within[:1])
    for j in range(TILE // SPAN):
        spans.append(within[j * SPAN : (j + 1) * SPAN] + offset)
        offset = spans[-1][SPAN - 1 :]
    return jnp.concatenate(spans, axis=0)


def first_step(body):
    pl.when(pl.program_id(0) == 0)(body)


def model_rows(ref, h, first, blocks=1):
    parts = [
        ref[h, :, first + LANES * b : first + LANES * (b + 1), :].reshape(-1, LANES)
        for b in range(blocks)
    ]
    return parts[0] if blocks == 1 else jnp.concatenate(parts, axis=1)


def project_kernel(
    x_ref, key_ref, value_ref, expand_ref,
    normed_ref, key_out_ref, value_out_ref, rank_ref, within_ref, slope_ref, state_ref, log_ref, gain_ref, small_ref,
):
    @first_step
    def _():
        state_ref[...] = jnp.zeros_like(state_ref)
        log_ref[...] = jnp.zeros_like(log_ref)
        small_ref[32:] = jnp.zeros_like(small_ref[32:])
        for s in range(key_ref.shape[1]):
            small_ref[:32, s * LANES : (s + 1) * LANES] = key_ref[0, s, LANES : LANES + 32]
        gain_ref[...] = to_float(small_ref[16:24])

    x = to_float(x_ref[...])
    scale = lax.rsqrt(jnp.mean(x * x, axis=1, keepdims=True) + eps_norm)
    normed = to_half(x * scale * gain_ref[0:1])
    normed_ref[...] = normed
    rank_values = mul(normed, small_ref[...], 1, 1)
    column = lax.broadcasted_iota(jnp.int32, rank_values.shape, 1)
    rank_values = jnp.where(column < 16, rank_values, jnp.where(column == 16, 1.0, 0.0))
    rank_ref[...] = rank_values
    logits = mul_exact(rank_values, expand_ref[...])
    decays = log_sigmoid(logits) * (1.0 / gate_scale)
    slope_ref[...] = 1.0 / (gate_scale * (1.0 + jnp.exp(logits)))
    sums = mul_ones(ones_where(at_or_after(TILE)), decays)
    log_ref[...] += sums[TILE - 1 :]
    for j in range(TILE // SPAN):
        part = sums[j * SPAN : (j + 1) * SPAN]
        within_ref[j * SPAN : (j + 1) * SPAN, :] = part - sums[j * SPAN - 1 : j * SPAN] if j else part
    closing = sums[TILE - 1 :]
    rest = jnp.exp(closing - sums)
    decay = jnp.exp(closing)
    for h, (k, v) in enumerate(zip(heads(LANES), heads(VALUES))):
        keys = to_half(mul(normed, model_rows(key_ref, h, 0)))
        key_out_ref[:, k] = keys
        values = to_half(mul(normed, value_ref[h]))
        value_out_ref[:, v] = values
        state_ref[h] = state_ref[h] * decay[:, k] + mul(values, to_float(keys) * rest[:, k], 0, 0)


def project_late_kernel(normed_ref, weight_ref, query_ref, gate_ref):
    normed = normed_ref[...]
    for h, (k, v) in enumerate(zip(heads(LANES), heads(VALUES))):
        query_ref[:, k] = to_half(mul(normed, model_rows(weight_ref, h, 0)))
        gate_ref[:, v] = mul(normed, model_rows(weight_ref, h, LANES, 2))


def load_output(late_ref, output_ref):
    for s in range(late_ref.shape[1]):
        output_ref[:, :, s * LANES : (s + 1) * LANES] = late_ref[:, s, 3 * LANES :]


def forward_kernel(
    query_ref, key_ref, value_ref, gate_ref, within_ref, incoming_ref, group_ref, late_ref,
    recurrent_ref, start_ref, mixed_ref, part_ref, state_ref, output_ref,
):
    @first_step
    def _():
        state_ref[...] = incoming_ref[...]
        load_output(late_ref, output_ref)

    causal = at_or_after(SPAN)
    total = None
    for h, (k, v) in enumerate(zip(heads(LANES), heads(VALUES))):
        state = state_ref[h]
        outs = []
        for j in range(TILE // SPAN):
            span = pl.ds(j * SPAN, SPAN)
            within = within_ref[span, k]
            closing = within[SPAN - 1 :]
            values = value_ref[span, v]
            queries = to_half(to_float(query_ref[span, k]) * jnp.exp(within))
            keys = to_float(key_ref[span, k])
            start = to_half(state)
            start_ref[j, h] = start
            scores = jnp.where(causal, mul(queries, keys * jnp.exp(-within), 1, 1), 0.0)
            outs.append(mul(scores, values) + mul(queries, start, 1, 1))
            state = state * jnp.exp(closing) + mul(values, keys * jnp.exp(closing - within), 0, 0)
        state_ref[h] = state
        recurrent = jnp.concatenate(outs, axis=0) * LANES ** (-0.5)
        recurrent_ref[:, v] = recurrent
        scale = lax.rsqrt(jnp.mean(recurrent * recurrent, axis=1, keepdims=True) + eps_norm)
        gate = gate_ref[:, v]
        mixed = to_half(recurrent * scale * group_ref[...] * (gate * jax.nn.sigmoid(gate)))
        mixed_ref[:, v] = mixed
        part = mul(mixed, output_ref[h])
        total = part if total is None else total + part
    part_ref[...] = to_half(total)


def residual_kernel(x_ref, mine_ref, other_ref, gain_ref, residual_ref, normed_ref):
    residual = to_float(x_ref[...]) + (to_float(mine_ref[...]) + to_float(other_ref[...]))
    scale = lax.rsqrt(jnp.mean(residual * residual, axis=1, keepdims=True) + eps_norm)
    residual_ref[...] = residual
    normed_ref[...] = to_half(residual * scale * gain_ref[1:2])


def feed_forward_kernel(
    normed_ref, cot_ref, weight_ref,
    hidden_ref, gate_grad_ref, up_grad_ref, out_ref, rows_grad_ref, all_ref,
):
    width = weight_ref.shape[2]

    @first_step
    def _():
        all_ref[:, width:] = jnp.zeros_like(all_ref[:, width:])
        for s in range(weight_ref.shape[0]):
            all_ref[:, :width, s * LANES : (s + 1) * LANES] = weight_ref[s]

    normed = normed_ref[...]
    gate = mul(normed, all_ref[0], 1, 1)
    up = mul(normed, all_ref[1], 1, 1)
    hidden_grad = mul(cot_ref[...], all_ref[2], 1, 1)
    sigmoid = jax.nn.sigmoid(gate)
    silu = gate * sigmoid
    hidden = to_half(silu * up)
    hidden_ref[...] = hidden.T
    gate_grad = to_half(hidden_grad * up * sigmoid * (1.0 + gate * (1.0 - sigmoid)))
    gate_grad_ref[...] = gate_grad.T
    up_grad = to_half(hidden_grad * silu)
    up_grad_ref[...] = up_grad.T
    rows_grad_ref[...] = to_half(mul(gate_grad, all_ref[0]) + mul(up_grad, all_ref[1]))
    out_ref[...] = to_half(mul(hidden, all_ref[2]))


def feed_forward_weights_kernel(
    own_ref, other_ref, cot_own_ref, cot_other_ref,
    gate_own_ref, gate_other_ref, up_own_ref, up_other_ref, hidden_own_ref, hidden_other_ref,
    out_ref,
):
    width = out_ref.shape[2]
    for i, (left, left_other, right, right_other) in enumerate(
        [
            (gate_own_ref, gate_other_ref, own_ref, other_ref),
            (up_own_ref, up_other_ref, own_ref, other_ref),
            (hidden_own_ref, hidden_other_ref, cot_own_ref, cot_other_ref),
        ]
    ):
        total = to_half(mul(left[...], right[...]) + mul(left_other[...], right_other[...]))
        for s in range(out_ref.shape[0]):
            out_ref[s, i] = total[:width, s * LANES : (s + 1) * LANES]


def residual_backward_kernel(
    residual_ref, cot_ref, mine_ref, other_ref, home_ref, gain_ref,
    grad_ref, half_ref, gain_grad_ref,
):
    @first_step
    def _():
        gain_grad_ref[...] = jnp.zeros_like(gain_grad_ref)

    residual = residual_ref[...]
    scale = lax.rsqrt(jnp.mean(residual * residual, axis=1, keepdims=True) + eps_norm)
    normed = residual * scale
    pulled = to_float(mine_ref[...]) + to_float(other_ref[...]) + to_float(home_ref[...])
    gain_grad_ref[...] += jnp.sum(pulled * normed, axis=0, keepdims=True)
    weighted = pulled * gain_ref[1:2]
    grad = to_float(cot_ref[...]) + scale * (
        weighted - normed * jnp.mean(weighted * normed, axis=1, keepdims=True)
    )
    grad_ref[...] = grad
    half_ref[...] = to_half(grad)


def gate_backward_kernel(
    grad_ref, late_ref, recurrent_ref, gate_ref, query_ref, within_ref, group_ref,
    recurrent_grad_ref, gate_grad_ref, group_grad_ref, state_grad_ref, output_ref,
):
    @first_step
    def _():
        load_output(late_ref, output_ref)
        group_grad_ref[...] = jnp.zeros_like(group_grad_ref)
        state_grad_ref[...] = jnp.zeros_like(state_grad_ref)

    for h, (k, v) in enumerate(zip(heads(LANES), heads(VALUES))):
        mixed_grad = mul(grad_ref[...], output_ref[h], 1, 1)
        recurrent = recurrent_ref[:, v]
        gate = gate_ref[:, v]
        scale = lax.rsqrt(jnp.mean(recurrent * recurrent, axis=1, keepdims=True) + eps_norm)
        sigmoid = jax.nn.sigmoid(gate)
        silu = gate * sigmoid
        normed = recurrent * scale
        group = group_ref[...]
        pulled = mixed_grad * normed
        group_grad_ref[...] += jnp.sum(pulled * silu, axis=0, keepdims=True)
        gate_grad_ref[:, v] = to_half(pulled * group * sigmoid * (1.0 + gate * (1.0 - sigmoid)))
        weighted = mixed_grad * group * silu
        recurrent_grad = scale * (weighted - normed * jnp.mean(weighted * normed, axis=1, keepdims=True))
        recurrent_grad = to_half(recurrent_grad * LANES ** (-0.5))
        recurrent_grad_ref[:, v] = recurrent_grad
        sums = whole_tile(within_ref[:, k])
        queries = to_float(query_ref[:, k]) * jnp.exp(sums)
        state_grad_ref[h] = state_grad_ref[h] * jnp.exp(sums[TILE - 1 :]) + mul(recurrent_grad, queries, 0, 0)


def query_backward_kernel(
    query_ref, key_ref, value_ref, within_ref, recurrent_grad_ref, start_ref, gate_grad_ref, weight_ref,
    query_grad_ref, kept_ref, normed_grad_ref,
):
    causal = at_or_after(SPAN)
    total = None
    for h, (k, v) in enumerate(zip(heads(LANES), heads(VALUES))):
        for j in range(TILE // SPAN):
            span = pl.ds(j * SPAN, SPAN)
            within = within_ref[span, k]
            pulled = recurrent_grad_ref[span, v]
            keys_in = to_float(key_ref[span, k]) * jnp.exp(-within)
            scores_grad = jnp.where(causal, mul(pulled, value_ref[span, v], 1, 1), 0.0)
            query_grad = (mul(scores_grad, keys_in) + mul(pulled, start_ref[j, h])) * jnp.exp(within)
            query_grad_ref[span, k] = to_half(query_grad)
            kept_ref[span, k] = query_grad * to_float(query_ref[span, k])
        part = mul(query_grad_ref[:, k], model_rows(weight_ref, h, 0), 1, 1) + mul(
            gate_grad_ref[:, v], model_rows(weight_ref, h, LANES, 2), 1, 1
        )
        total = part if total is None else total + part
    normed_grad_ref[...] = total


def backward_kernel(
    query_ref, key_ref, value_ref, within_ref, recurrent_grad_ref, start_ref, slope_ref, rank_ref, kept_ref,
    normed_grad_ref, key_weight_ref, value_weight_ref, expand_ref, later_ref,
    key_grad_ref, value_grad_ref, rank_grad_ref, expand_grad_ref, part_ref, state_grad_ref,
):
    @first_step
    def _():
        state_grad_ref[...] = later_ref[...]
        expand_grad_ref[...] = jnp.zeros_like(expand_grad_ref)

    causal = at_or_after(SPAN)
    last = lax.broadcasted_iota(jnp.int32, (SPAN, LANES), 0) == SPAN - 1
    until = ones_where(
        lax.broadcasted_iota(jnp.int32, (SPAN, SPAN), 0) <= lax.broadcasted_iota(jnp.int32, (SPAN, SPAN), 1)
    )
    total = normed_grad_ref[...]
    logit_grads = []
    for h, (k, v) in enumerate(zip(heads(LANES), heads(VALUES))):
        later = state_grad_ref[h]
        spans = []
        for j in reversed(range(TILE // SPAN)):
            span = pl.ds(j * SPAN, SPAN)
            within = within_ref[span, k]
            closing = within[SPAN - 1 :]
            values = value_ref[span, v]
            pulled = recurrent_grad_ref[span, v]
            keys = to_float(key_ref[span, k])
            shrink, rest = (jnp.exp(-within), jnp.exp(closing - within))
            queries = to_half(to_float(query_ref[span, k]) * jnp.exp(within))
            keys_in = keys * shrink
            keys_out = keys * rest
            later_half = to_half(later)
            scores = jnp.where(causal, mul(queries, keys_in, 1, 1), 0.0)
            scores_grad = jnp.where(causal, mul(pulled, values, 1, 1), 0.0)
            keys_in_grad = mul(scores_grad, queries, 0, 0)
            keys_out_grad = mul(values, later_half)
            value_grad_ref[span, v] = to_half(mul(scores, pulled, 0, 0) + mul(keys_out, later_half, 1, 1))
            key_grad_ref[span, k] = to_half(keys_in_grad * shrink + keys_out_grad * rest)
            kept = keys_out_grad * keys_out
            sums_grad = kept_ref[span, k] - keys_in_grad * keys_in - kept
            closing_grad = jnp.sum(kept, axis=0, keepdims=True) + jnp.sum(
                later * to_float(start_ref[j, h]), axis=0, keepdims=True
            ) * jnp.exp(closing)
            spans.append(mul_ones(until, sums_grad + jnp.where(last, closing_grad, 0.0)))
            later = later * jnp.exp(closing) + mul(pulled, queries, 0, 0)
        state_grad_ref[h] = later
        logit_grads.append(jnp.concatenate(spans[::-1], axis=0) * slope_ref[:, k])
        total = total + (
            mul(key_grad_ref[:, k], model_rows(key_weight_ref, h, 0), 1, 1)
            + mul(value_grad_ref[:, v], value_weight_ref[h], 1, 1)
        )
    part_ref[...] = to_half(total)
    logit_grad = jnp.concatenate(logit_grads, axis=1)
    rank_grad_ref[...] = mul_exact(expand_ref[:16], logit_grad, 1, 1)
    expand_grad_ref[...] += mul_exact(rank_ref[...], logit_grad, 0, 0)[:24]


def store_rows(out_ref, h, first, total):
    for s in range(out_ref.shape[1]):
        for b in range(total.shape[1] // LANES):
            out_ref[h, s, first + LANES * b : first + LANES * (b + 1)] = to_half(
                total[s * LANES : (s + 1) * LANES, b * LANES : (b + 1) * LANES]
            )


def weights_kernel(rows_ref, first_ref, second_ref, out_ref):
    rows = rows_ref[...]
    for h, (k, v) in enumerate(zip(heads(LANES), heads(VALUES))):
        store_rows(out_ref, h, 0, mul(rows, first_ref[:, k]))
        store_rows(out_ref, h, LANES, mul(rows, second_ref[:, v]))


def late_weights_kernel(rows_ref, query_ref, gate_ref, mixed_ref, grad_ref, out_ref):
    weights_kernel(rows_ref, query_ref, gate_ref, out_ref)
    for h, v in enumerate(heads(VALUES)):
        total = mul(mixed_ref[v, :], grad_ref[...])
        for s in range(out_ref.shape[1]):
            out_ref[h, s, 3 * LANES :] = to_half(total[:, s * LANES : (s + 1) * LANES])


def inputs_backward_kernel(
    core_ref, x_ref, grad_ref, mine_ref, other_ref, rank_grad_ref, small_ref, gain_ref, normed_ref,
    out_ref, gain_grad_ref, squeeze_grad_ref,
):
    @first_step
    def _():
        gain_grad_ref[...] = jnp.zeros_like(gain_grad_ref)
        squeeze_grad_ref[...] = jnp.zeros_like(squeeze_grad_ref)

    rank_grad = to_half(rank_grad_ref[...])
    x = to_float(x_ref[...])
    scale = lax.rsqrt(jnp.mean(x * x, axis=1, keepdims=True) + eps_norm)
    normed = x * scale
    pulled = (
        to_float(mine_ref[...])
        + to_float(other_ref[...])
        + mul(rank_grad, small_ref[:16], 0, 0)
    )
    squeeze_grad_ref[...] += mul(rank_grad, normed_ref[...])
    gain_grad_ref[...] += jnp.sum(pulled * normed, axis=0, keepdims=True)
    weighted = pulled * gain_ref[0:1]
    grad = grad_ref[...] + scale * (weighted - normed * jnp.mean(weighted * normed, axis=1, keepdims=True))
    columns = out_ref.shape[2]
    for b in range(2):
        low, high = (grad[:, (2 * b + i) * columns : (2 * b + i + 1) * columns] for i in range(2))
        out_ref[b] = jnp.where(core_ref[0, 0] == 0, low, high)


def adam_kernel(count, joins, *refs):
    grads = refs[: len(refs) - 6 * count - 2]
    refs = refs[len(grads) :]
    share, ins, outs = refs[0], refs[1 : 1 + 3 * count], refs[1 + 3 * count :]
    squares = outs[3 * count]
    squares[...] = jnp.zeros_like(squares)
    for p, (join, shared) in enumerate(joins):
        gradient = to_float(join(*grads))
        master, first, second = (ref[...].reshape(gradient.shape) for ref in ins[3 * p : 3 * p + 3])
        new_first, new_second, direction = adam_direction(master, gradient, first, second)
        for ref, value in zip(outs[3 * p : 3 * p + 3], (new_first, new_second, direction)):
            ref[...] = value.reshape(ref.shape)
        for row, value in ((p, master), (8 + p, direction)):
            total = value * value
            while total.ndim > 2:
                total = jnp.sum(total, axis=0)
            total = jnp.sum(jnp.sum(total, axis=0, keepdims=True), axis=1, keepdims=True)
            if shared:
                total = total * share[0:1, 0:1]
            squares[row : row + 1] = jnp.broadcast_to(total, (1, LANES))


def trust_kernel(rows, squares_ref, *refs):
    count = len(rows)
    for p, row in enumerate(rows):
        master, direction, out = refs[p], refs[count + p], refs[2 * count + p]
        norm = jnp.sqrt(squares_ref[row : row + 1, 0:1])
        ratio = norm / (jnp.sqrt(squares_ref[row + 8 : row + 9, 0:1]) + eps_adam)
        shape = (1,) * len(master.shape)
        out[...] = master[...] - (learn_rate * ratio).reshape(shape) * direction[...]


def whole_call(body, ins, outs):
    return pl.pallas_call(
        body,
        out_shape=[jax.ShapeDtypeStruct(shape, jnp.float32) for shape in outs],
        compiler_params=pltpu.CompilerParams(vmem_limit_bytes=VMEM_LIMIT),
        cost_estimate=pl.CostEstimate(flops=1, bytes_accessed=0, transcendentals=0),
    )(*ins)


def adam_group(share, grads, joins, params):
    count = len(params)
    outs = []
    for param in params:
        outs += [param[0].shape] * 3
    results = whole_call(
        lambda *refs: adam_kernel(count, joins, *refs),
        list(grads) + [share] + [array for param in params for array in param],
        outs + [(16, LANES)],
    )
    return [tuple(results[3 * p : 3 * p + 3]) for p in range(count)], results[-1]


def adam_direction(master, gradient, first_moment, second_moment):
    fix_one = 1.0 - beta_one**STEP
    second_correction = 1.0 - beta_two**STEP
    new_first = beta_one * first_moment + (1.0 - beta_one) * gradient
    new_second = beta_two * second_moment + (1.0 - beta_two) * gradient * gradient
    update_direction = (
        new_first * (1.0 / fix_one) / (jnp.sqrt(new_second * (1.0 / second_correction)) + eps_adam)
        + decay_rate * master
    )
    return (new_first, new_second, update_direction)


def per_device(
    tokens,
    cotangent,
    query_weight,
    query_mean,
    query_square,
    value_weight,
    value_mean,
    value_square,
    squeeze_weight,
    squeeze_mean,
    squeeze_square,
    expand_weight,
    expand_mean,
    expand_square,
    group_weight,
    group_mean,
    group_square,
    output_weight,
    output_mean,
    output_square,
    ffn_weight,
    ffn_mean,
    ffn_square,
    down_weight,
    down_mean,
    down_square,
    norms_weight,
    norms_mean,
    norms_square,
):
    sequences, segment, column_count = tokens.shape
    head_index = lax.axis_index("head")
    chip, core = (head_index // 2, head_index % 2)
    rows = query_weight.shape[0]
    peers = lax.axis_size("seq")
    seq_index = lax.axis_index("seq")
    model_width = rows * peers
    key_width = query_weight.shape[2] // 2
    value_width = value_weight.shape[2] // 2
    ffn_width = ffn_weight.shape[2]
    ffn_padded = -(-ffn_width // 256) * 256
    rank_count = squeeze_weight.shape[1]
    half_segment = segment // 2
    steps = segment // TILE
    half, full = (jnp.bfloat16, jnp.float32)
    aligned = rows % LANES == 0
    blocks = model_width // LANES
    along = seq_bits()[:-1]
    beside = ("seq", 1)
    across = ("head", 2)

    def column_pair(a):
        parts = [a[:, i * column_count : (i + 1) * column_count] for i in range(4)]
        return [jnp.where(core == 0, parts[2 * b], parts[2 * b + 1]) for b in range(2)]

    def other_pair(a):
        parts = [a[:, i * column_count : (i + 1) * column_count] for i in range(4)]
        return [jnp.where(core == 0, parts[2 * b + 1], parts[2 * b]) for b in range(2)]

    def full_rows(mine, other):
        pair = jnp.stack(ordered(mine, other, chip))
        low, high = ordered(pair, swap(pair, "head", 1), core)
        return jnp.concatenate([low[0], high[0], low[1], high[1]], axis=-1)

    ffn_mine = jnp.concatenate([jnp.moveaxis(ffn_weight, 0, 2), down_weight[None]])
    ffn_mine = to_half(ffn_mine if aligned else jnp.moveaxis(ffn_mine, 2, 1))
    small_mine = jnp.concatenate(
        [
            squeeze_weight.T,
            jnp.zeros((16 - rank_count, rows), jnp.float32),
            norms_weight,
            jnp.zeros((14, rows), jnp.float32),
        ]
    )
    key_mine = query_weight[:, 0, key_width:]
    value_mine = to_half(value_weight[:, 0, :value_width])
    late_mine = jnp.concatenate(
        [
            query_weight[:, 0, :key_width],
            value_weight[:, 0, value_width : value_width + LANES],
            value_weight[:, 0, value_width + LANES :],
        ]
    )
    tokens_moved = swap(pick(tokens, 1 - chip), *across)
    value_mine, ffn_mine = lax.optimization_barrier((value_mine, ffn_mine))
    ffn_all = lax.all_gather(ffn_mine, "seq", axis=0)
    if not aligned:
        ffn_all = ffn_all.reshape(blocks, LANES // rows, 3, rows, ffn_width)
        ffn_all = ffn_all.transpose(0, 2, 4, 1, 3).reshape(blocks, 3, ffn_width, LANES)

    input_half = full_rows(pick(tokens, chip), tokens_moved)
    value_part, held = grow(value_mine, [], along)
    if aligned:
        key_part, held = grow(to_half(jnp.concatenate([key_mine, small_mine])), [], along)
        late_mine = to_half(jnp.concatenate([late_mine, output_weight]))
        late_part, late_held = grow(after(late_mine, key_part, value_part), [], along[:1])
        key_all = grown(*grow(key_part, held, [across, beside]))
        value_part, value_held = grow(value_part, held, [beside])
        late_part, _ = grow(after(late_part, value_part), late_held, along[1:])
        value_part = after(value_part, input_half)
        value_full = grown(*grow(value_part, value_held, [across])).reshape(
            2, model_width, value_width
        )
        late_part, key_all, value_full = lax.optimization_barrier((late_part, key_all, value_full))
        cut = 5 * LANES // 2
        late_halves = [
            grow(late_part[..., :cut, :], held, [across]),
            grow(late_part[..., cut:, :], held, [beside]),
        ]
    else:
        value_full = grown(*grow(value_part, held, [beside, across])).reshape(
            2, model_width, value_width
        )
        stages = along + [across, beside]
        small_all = gather_cube(to_half(small_mine.T), stages)
        small_all = jnp.moveaxis(small_all.reshape(2, blocks, LANES, 32), 3, 2)
        key_all = gather_cube(to_half(key_mine), stages).reshape(2, blocks, LANES, key_width)
        key_all = jnp.concatenate([key_all, small_all], axis=2)
        late_all = gather_cube(to_half(late_mine), stages).reshape(2, peers, 3, rows, LANES)
        late_all = jnp.moveaxis(late_all, 2, 1).reshape(2, 3, blocks, LANES, LANES)
        late_all = jnp.moveaxis(late_all, 1, 2).reshape(2, blocks, 3 * LANES, LANES)
        output_all = gather_cube(to_half(output_weight.T), stages)
        output_all = jnp.moveaxis(output_all.reshape(2, blocks, LANES, value_width), 3, 2)
        late_all = jnp.concatenate([late_all, output_all], axis=2)

    expand_columns = pick(expand_weight.reshape(rank_count + 1, 2, 2, key_width), core, 2)
    expand_columns = jnp.pad(
        expand_columns.reshape(rank_count + 1, 2 * key_width), ((0, LANES - 1 - rank_count), (0, 0))
    )
    (
        normed, keys, value_entries, rank_values, within, slope, block_state, log_block, gains, small_full,
    ) = call(
        project_kernel,
        steps,
        [(input_half, 0), (key_all, None), (value_full, None), (expand_columns, None)],
        [
            ((segment, model_width), half, 0),
            ((segment, 2 * key_width), half, 0),
            ((segment, 2 * value_width), half, 0),
            ((segment, LANES), full, 0),
            ((segment, 2 * key_width), full, 0),
            ((segment, 2 * key_width), full, 0),
            ((2, value_width, key_width), full, None),
            ((1, 2 * key_width), full, None),
            ((8, model_width), full, None),
            ((LANES, model_width), half, None),
        ],
        cost=4,
    )
    block_decay = jnp.exp(log_block).reshape(2, 1, key_width)
    if aligned:
        block_state, late_halves = lax.optimization_barrier((block_state, [a for a, _ in late_halves]))
        late_helds = [sorted(held + [link], key=cube_rank().index) for link in (across, beside)]
    state_in, heard = scan_blocks(block_decay, block_state, False)
    if aligned:
        late_halves = [(after(late_halves[0], heard[0]), late_helds[0]), (late_halves[1], late_helds[1])]
        late_all = jnp.concatenate(
            [
                grown(*grow(*late_halves[0], [beside])),
                grown(*grow(*late_halves[1], [across])),
            ],
            axis=2,
        )
    queries, gate_values = call(
        project_late_kernel,
        steps,
        [(normed, 0), (late_all, None)],
        [((segment, 2 * key_width), half, 0), ((segment, 2 * value_width), full, 0)],
        cost=4,
    )
    cot_moved = swap(after(cotangent, late_all), *across)
    recurrent, starts, mixed_half, mixer_part = call(
        forward_kernel,
        steps,
        [
            (queries, 0),
            (keys, 0),
            (value_entries, 0),
            (gate_values, 0),
            (within, 0),
            (state_in, None),
            (group_weight[None, :], None),
            (late_all, None),
        ],
        [
            ((segment, 2 * value_width), full, 0),
            ((segment // SPAN, 2, value_width, key_width), half, 0),
            ((segment, 2 * value_width), half, 0),
            ((segment, model_width), half, 0),
        ],
        scratch=[
            pltpu.VMEM((2, value_width, key_width), jnp.float32),
            pltpu.VMEM((2, value_width, model_width), jnp.bfloat16),
        ],
        cost=4,
    )
    cot_moved = after(cot_moved, mixer_part)
    cot_own = full_rows(pick(cotangent, chip), pick(cot_moved, chip))
    cot_other = full_rows(pick(cotangent, 1 - chip), pick(cot_moved, 1 - chip))
    residual, normed_two = call(
        residual_kernel,
        steps,
        [(input_half, 0), (mixer_part, 0), (swap(mixer_part, "head", 1), 0), (gains, None)],
        [((segment, model_width), full, 0), ((segment, model_width), half, 0)],
        cost=2,
    )

    moved = swap(lax.dynamic_slice_in_dim(normed_two, core * half_segment, half_segment, 0), *across)

    def feed_forward(normed_rows, cot_rows):
        return call(
            feed_forward_kernel,
            steps,
            [(normed_rows, 0), (cot_rows, 0), (ffn_all, None)],
            [((ffn_padded, segment), half, 1)] * 3 + [((segment, model_width), half, 0)] * 2,
            scratch=[pltpu.VMEM((3, ffn_padded, model_width), jnp.bfloat16)],
            cost=12,
        )

    own = feed_forward(normed_two, cot_own)
    normed_t, mixed_t = (after(normed, own[0]).T, after(mixed_half, own[0]).T)
    moved, own, normed_t, mixed_t = lax.optimization_barrier((moved, own, normed_t, mixed_t))
    normed_two_other = jnp.concatenate(ordered(moved, swap(moved, "head", 1), core), axis=0)
    other = feed_forward(normed_two_other, cot_other)
    other_rows = other[4].reshape(2, half_segment, model_width)
    other_sum = to_half(
        to_float(pick(other_rows, core)) + to_float(swap(pick(other_rows, 1 - core), "head", 1))
    )
    home = swap(other_sum, *across)
    (ffn_grad,) = call(
        feed_forward_weights_kernel,
        4,
        [
            (normed_two, 1),
            (normed_two_other, 1),
            (cot_own, 1),
            (cot_other, 1),
            (own[1], None),
            (other[1], None),
            (own[2], None),
            (other[2], None),
            (own[0], None),
            (other[0], None),
        ],
        [((blocks, 3, ffn_width, LANES), half, 0)],
        cost=12,
    )
    own_grad = after(own[4], other_sum)
    own_beside = swap(own_grad, "head", 1)
    home, ffn_grad, own_beside = lax.optimization_barrier((home, ffn_grad, own_beside))
    home_full = jnp.concatenate(ordered(home, swap(home, "head", 1), core), axis=0)
    residual_grad, residual_half, gain_two_grad = call(
        residual_backward_kernel,
        steps,
        [
            (residual, 0),
            (cot_own, 0),
            (own_grad, 0),
            (own_beside, 0),
            (home_full, 0),
            (gains, None),
        ],
        [
            ((segment, model_width), full, 0),
            ((segment, model_width), half, 0),
            ((1, model_width), full, None),
        ],
        cost=2,
    )
    if not aligned:
        ffn_grad = ffn_grad.reshape(blocks, 3, ffn_width, LANES // rows, rows)
        ffn_grad = ffn_grad.transpose(0, 3, 1, 4, 2).reshape(peers, 3, rows, ffn_width)
    ffn_sum = lax.psum_scatter(ffn_grad, "seq", scatter_dimension=0, tiled=False)
    if not aligned:
        ffn_sum = jnp.moveaxis(ffn_sum, 1, 2)

    recurrent_grad, gate_grad, group_grad, state_in_grad = call(
        gate_backward_kernel,
        steps,
        [
            (residual_half, 0),
            (late_all, None),
            (recurrent, 0),
            (gate_values, 0),
            (queries, 0),
            (within, 0),
            (group_weight[None, :], None),
        ],
        [
            ((segment, 2 * value_width), half, 0),
            ((segment, 2 * value_width), half, 0),
            ((1, value_width), full, None),
            ((2, value_width, key_width), full, None),
        ],
        reverse=True,
        scratch=[pltpu.VMEM((2, value_width, model_width), jnp.bfloat16)],
        cost=3,
    )
    later_grad, heard = scan_blocks(block_decay, state_in_grad, True)
    own_out, other_out, residual_cols = after((own[3], other[3], residual), residual_half)
    give = jnp.stack([jnp.stack(other_pair(a)) for a in (own_out, other_out)])
    out_beside = swap(give, "head", 1)
    own_out, other_out, residual_cols = after((own_out, other_out, residual_cols), state_in_grad)
    keep = jnp.stack([jnp.stack(column_pair(a)) for a in (own_out, other_out)])
    out_rows = to_float(keep) + to_float(out_beside)
    residual_cols = jnp.stack(column_pair(residual_cols))
    out_rows = out_rows + jnp.stack([residual_cols, jnp.zeros_like(residual_cols)])
    out_give = to_half(pick(out_rows, 1 - chip, 1))
    out_mine = pick(out_rows, chip, 1)
    gate_grad, out_give, out_mine = lax.optimization_barrier((gate_grad, out_give, out_mine))
    out_moved = swap(out_give, *across)
    query_grad, kept, normed_grad = call(
        query_backward_kernel,
        steps,
        [
            (queries, 0),
            (keys, 0),
            (value_entries, 0),
            (within, 0),
            (recurrent_grad, 0),
            (starts, 0),
            (gate_grad, 0),
            (late_all, None),
        ],
        [
            ((segment, 2 * key_width), half, 0),
            ((segment, 2 * key_width), full, 0),
            ((segment, model_width), full, 0),
        ],
        cost=4,
    )
    (late_grad,) = call(
        late_weights_kernel,
        4,
        [(normed_t, 0), (query_grad, None), (gate_grad, None), (mixed_t, None), (residual_half, 1)],
        [((2, blocks, 5 * LANES, LANES), half, 1)],
        cost=4,
    )
    late_grad, later_grad, out_moved = lax.optimization_barrier((late_grad, later_grad, out_moved))
    back = along[::-1]
    if aligned:
        cut = 5 * LANES // 2
        late_splits = [
            split(late_grad[:, :, :cut], None, beside),
            split(late_grad[:, :, cut:], None, across),
        ]
        later_grad, late_splits = lax.optimization_barrier((later_grad, late_splits))
        late_moved = [swap(late_splits[0][1], *beside), swap(late_splits[1][1], *across)]
    key_grad, value_grad, rank_grad_part, expand_grad, normed_part = call(
        backward_kernel,
        steps,
        [
            (queries, 0),
            (keys, 0),
            (value_entries, 0),
            (within, 0),
            (recurrent_grad, 0),
            (starts, 0),
            (slope, 0),
            (rank_values, 0),
            (kept, 0),
            (normed_grad, 0),
            (key_all, None),
            (value_full, None),
            (expand_columns, None),
            (later_grad, None),
        ],
        [
            ((segment, 2 * key_width), half, 0),
            ((segment, 2 * value_width), half, 0),
            ((rank_count, segment), full, 1),
            ((24, 2 * key_width), full, None),
            ((segment, model_width), half, 0),
        ],
        reverse=True,
        scratch=[pltpu.VMEM((2, value_width, key_width), jnp.float32)],
        cost=5,
    )
    if aligned:
        key_grad, value_grad, normed_part, rank_grad_part, late_moved = lax.optimization_barrier(
            (key_grad, value_grad, normed_part, rank_grad_part, late_moved)
        )
        late_held = [[link for link in cube_rank() if link != gone] for gone in (beside, across)]
        late_splits = [
            split(to_float(splits[0]) + to_float(moved), held, link)
            for splits, moved, held, link in zip(
                late_splits, late_moved, late_held, (across, beside)
            )
        ]
    normed_beside, rank_beside = (swap(normed_part, "head", 1), swap(rank_grad_part, "head", 1))
    (state_weight_grad,) = call(
        weights_kernel,
        4,
        [(normed_t, 0), (key_grad, None), (value_grad, None)],
        [((2, blocks, 3 * LANES, LANES), half, 1)],
        cost=3,
    )
    normed_beside, rank_beside, state_weight_grad = lax.optimization_barrier(
        (normed_beside, rank_beside, state_weight_grad)
    )
    rank_grad = rank_grad_part + rank_beside
    grad_cols, gain_one_grad, squeeze_grad = call(
        inputs_backward_kernel,
        steps,
        [
            (core.reshape(1, 1), None),
            (input_half, 0),
            (residual_grad, 0),
            (normed_part, 0),
            (normed_beside, 0),
            (rank_grad, 1),
            (small_full, None),
            (gains, None),
            (normed, 0),
        ],
        [
            ((2, segment, column_count), full, 1),
            ((1, model_width), full, None),
            ((rank_count, model_width), full, None),
        ],
        cost=2,
    )
    if aligned:
        heard = []

        def listen(number, moved):
            if number == 0:
                moved = after(moved, gain_one_grad)
            heard.append(moved)
            return moved

        state_sum = scatter_cube(state_weight_grad, [across, beside] + back, listen)
        late_moved = [swap(late_splits[0][1], *across), swap(late_splits[1][1], *beside)]
        late_part = jnp.concatenate(
            [to_float(splits[0]) + to_float(moved) for splits, moved in zip(late_splits, late_moved)],
            axis=-2,
        )
        late_part = after(late_part, gain_one_grad)
        late_sum = shrink(late_part, along, back)[0]
        output_sum_grad = late_sum[3 * LANES :]
        grad_give = after(pick(grad_cols, 1 - chip), heard[0])
    else:

        def split_rows(a):
            a = a.reshape(2, blocks, 3, LANES // rows, rows, LANES)
            return jnp.moveaxis(a, 3, 2).reshape(2, peers, 3 * rows, LANES)

        late_sum = scatter_cube(split_rows(late_grad[:, :, : 3 * LANES]), [beside, across] + back)
        state_sum = scatter_cube(split_rows(state_weight_grad), [across, beside] + back)
        output_grad = late_grad[:, :, 3 * LANES :].reshape(2, blocks, value_width, LANES // rows, rows)
        output_grad = output_grad.transpose(0, 1, 3, 4, 2).reshape(2, peers, rows, value_width)
        output_sum_grad = scatter_cube(output_grad, [beside, across] + back).T
        grad_give = pick(grad_cols, 1 - chip)
    grad_home = to_float(swap(to_half(grad_give), *across))
    tokens_grad = jnp.stack(ordered(pick(grad_cols, chip), grad_home, chip))
    out_home = to_float(out_moved)
    block_out = to_half(jnp.stack(ordered(out_mine[0] + out_home[1], out_mine[1] + out_home[0], chip)))

    expand_pad = jnp.zeros((rank_count + 1, 2, 2, key_width), jnp.float32)
    expand_pad = lax.dynamic_update_index_in_dim(
        expand_pad, expand_grad[: rank_count + 1].reshape(rank_count + 1, 2, key_width), core, 2
    ).reshape(rank_count + 1, 4 * key_width)
    group_rows = jnp.pad(group_grad, ((0, rank_count), (0, model_width - 4 * key_width - value_width)))
    small_grad = jnp.concatenate(
        [
            0.5 * squeeze_grad,
            0.5 * gain_one_grad,
            0.5 * gain_two_grad,
            jnp.concatenate([expand_pad, group_rows], axis=1),
        ]
    )
    small_grad = sum_everywhere(small_grad)
    mine_grad = lax.dynamic_slice_in_dim(small_grad[: rank_count + 2], seq_index * rows, rows, 1)
    expand_total = small_grad[rank_count + 2 :, : 4 * key_width]
    group_total = small_grad[rank_count + 2 : rank_count + 3, 4 * key_width : 4 * key_width + value_width]

    share = jnp.broadcast_to((head_index == 0).astype(jnp.float32), (8, LANES))
    by_width = lambda a: jnp.moveaxis(a, 0, 2)
    early, early_squares = adam_group(
        share,
        [ffn_sum],
        [(lambda g: g[:2], False), (lambda g: g[2], False)],
        [
            tuple(map(by_width, (ffn_weight, ffn_mean, ffn_square))),
            (down_weight, down_mean, down_square),
        ],
    )
    late, late_squares = adam_group(
        share,
        [late_sum, state_sum, output_sum_grad, mine_grad],
        [
            (lambda l, s, o, m: jnp.concatenate([l[:rows], s[:rows]], axis=1), False),
            (
                lambda l, s, o, m: jnp.concatenate(
                    [s[rows : 2 * rows], s[2 * rows : 3 * rows], l[rows : 2 * rows], l[2 * rows : 3 * rows]],
                    axis=1,
                ),
                False,
            ),
            (lambda l, s, o, m: o[...], False),
            (lambda l, s, o, m: m[:rank_count], True),
            (lambda l, s, o, m: m[rank_count:], True),
        ],
        [
            (query_weight, query_mean, query_square),
            (value_weight, value_mean, value_square),
            (output_weight, output_mean, output_square),
            (squeeze_weight.T, squeeze_mean.T, squeeze_square.T),
            (norms_weight, norms_mean, norms_square),
        ],
    )
    copied, copied_squares = adam_group(
        share,
        [expand_total, group_total],
        [(lambda e, g: e[...], False), (lambda e, g: g[...], False)],
        [
            (expand_weight, expand_mean, expand_square),
            tuple(a[None, :] for a in (group_weight, group_mean, group_square)),
        ],
    )
    squares = sum_everywhere(jnp.concatenate([early_squares, late_squares]))
    squares = jnp.concatenate([squares, copied_squares])
    masters = [
        by_width(ffn_weight), down_weight,
        query_weight, value_weight, output_weight, squeeze_weight.T, norms_weight,
        expand_weight, group_weight[None, :],
    ]
    moments = early + late + copied
    news = whole_call(
        lambda *refs: trust_kernel([0, 1, 16, 17, 18, 19, 20, 32, 33], *refs),
        [squares] + masters + [moment[2] for moment in moments],
        [master.shape for master in masters],
    )
    triples = [(new,) + moment[:2] for new, moment in zip(news, moments)]
    ffn_out, down_out, query_out, value_out, output_out, squeeze_out, norms_out, expand_out, group_out = triples
    ffn_out = tuple(jnp.moveaxis(a, 2, 0) for a in ffn_out)
    squeeze_out = tuple(a.T for a in squeeze_out)
    group_out = tuple(a[0] for a in group_out)
    return (block_out, tokens_grad) + tuple(
        array
        for triple in (
            query_out, value_out, squeeze_out, expand_out, group_out, output_out, ffn_out, down_out, norms_out,
        )
        for array in triple
    )


def solution(mesh):
    in_specs = (
        P(None, "seq", "head"),
        P(None, "seq", "head"),
        P("seq", "head", None),
        P("seq", "head", None),
        P("seq", "head", None),
        P("seq", "head", None),
        P("seq", "head", None),
        P("seq", "head", None),
        P("seq", None),
        P("seq", None),
        P("seq", None),
        P(),
        P(),
        P(),
        P(),
        P(),
        P(),
        P("head", "seq"),
        P("head", "seq"),
        P("head", "seq"),
        P("seq", None, "head"),
        P("seq", None, "head"),
        P("seq", None, "head"),
        P("head", "seq"),
        P("head", "seq"),
        P("head", "seq"),
        P(None, "seq"),
        P(None, "seq"),
        P(None, "seq"),
    )
    out_specs = (
        P(None, "seq", "head"),
        P(None, "seq", "head"),
        P("seq", "head", None),
        P("seq", "head", None),
        P("seq", "head", None),
        P("seq", "head", None),
        P("seq", "head", None),
        P("seq", "head", None),
        P("seq", None),
        P("seq", None),
        P("seq", None),
        P(),
        P(),
        P(),
        P(),
        P(),
        P(),
        P("head", "seq"),
        P("head", "seq"),
        P("head", "seq"),
        P("seq", None, "head"),
        P("seq", None, "head"),
        P("seq", None, "head"),
        P("head", "seq"),
        P("head", "seq"),
        P("head", "seq"),
        P(None, "seq"),
        P(None, "seq"),
        P(None, "seq"),
    )
    return jax.shard_map(
        per_device, mesh=mesh, in_specs=in_specs, out_specs=out_specs, check_vma=False
    )
```

time: 813 us -> 454 us (0.56)
  Pallas kernels: 0 us -> 155 us
  local copies, waits for them, and re-layouts: 190 us -> 37.2 us
  matrix products: 146 us -> 0 us
  other arithmetic: 155 us -> 50 us
  waiting for transfers between devices: 218 us -> 138 us
  between operations: 32.4 us -> 16.2 us
  starting transfers between devices: 63.9 us -> 53.9 us
    pallas_call x0 -> x18, Pallas kernels: none -> 155 us  [the longest x14 146 us: call(): pl.pallas_call(body, grid=(steps,), in_specs=[spec(array.shape, axis) for...]
    dot_general x45 -> x0, matrix products: 146 us -> none  [the longest x27 85.6 us: mm(): return jnp.einsum(pattern, left, right, preferred_element_type=jnp.float32)]
    ppermute x51 -> x59, waiting for transfers between devices: 218 us -> 138 us  [swap(): lax.ppermute(value_entries, axis, [(i, i ^ bit) for i in range(peers)])]
    reduce_sum x32 -> x0, other arithmetic: 45.6 us -> none  [the longest x16 19.2 us: advance(): return (decay_item[:, :, None] * running + state_item, running)]
    another operation x15 -> x2, local copies, waits for them, and re-layouts: 35.9 us -> 0.13 us  [grow(): part = jnp.stack([low, high], axis=held.index(stage))]
    dynamic_slice x18 -> x5, local copies, waits for them, and re-layouts: 33.9 us -> 0.39 us  [pick(): return lax.dynamic_index_in_dim(value_entries, at, axis, keepdims=False)]
    unnamed x416 -> x187, local copies, waits for them, and re-layouts: 44.5 us -> 16.8 us
    add x27 -> x11, other arithmetic: 25.4 us -> 3.19 us  [the longest x4 2.79 us: per_device(): to_float(splits[0]) + to_float(moved)]
  transfers between devices with their start and end apart: 55 -> 61, of which waited for: 29 -> 29; matrix products, arithmetic and copies ran while one was open for 54% -> 14% of each run, Pallas kernels for 0% -> 28%
where the time goes in v2:
time: 454 us; the launch traced here: 450 us
  Pallas kernels  155 us (34%)
  waiting for transfers between devices  138 us (30%)
  starting transfers between devices  53.9 us (12%)
  other arithmetic  50 us (11%)
  local copies, waits for them, and re-layouts  37.2 us (8%)
  between operations  16.2 us (4%)
    pallas_call x14, Pallas kernels, call(): pl.pallas_call(body, grid=(steps,), in_specs=[spec(array.shape, axis) for...  146 us
    ppermute x59, waiting for transfers between devices, swap(): lax.ppermute(value_entries, axis, [(i, i ^ bit) for i in range(peers)])  138 us
    ppermute x59, starting transfers between devices, swap(): lax.ppermute(value_entries, axis, [(i, i ^ bit) for i in range(peers)])  53.8 us
    unnamed x187, local copies, waits for them, and re-layouts  16.8 us
  transfers between devices with their start and end apart: 61, of which 29 were waited for; matrix products, arithmetic and copies ran while one was open for 14% of the time, Pallas kernels for 28%

profile of v2, /device:TPU:0, one launch (start us, length us, event | category | flops | bytes accessed | tf_op | source)
XLA Modules:
  0.0 449.8 jit_solution(10722020328089250256)
XLA Ops:
  8.4 3.0 collective-permute-start
  14.6 2.6 collective-permute-start.2
  21.3 1.6 collective-permute-start.3
  22.9 2.3 collective-permute-done.4
  25.2 2.1 collective-permute-start.5
  28.0 2.5 collective-permute-done.5
  34.4 14.8 %collective-permute-done.6 = bf16[640,128]{1,0:T(8,128)(2,1)S(1)} collective-permute-done((bf16[640,128]{1,0:T(8,128)(2,1)S(1)}, bf16[640,128]{1,0:T(8,128)(2,1)S(1)}, u32[]{:S(2)}, u32[]{:S(2)}) %collective-permute-start.6) | collective-permute-done | bytes 163872 | tf_op jit(solution)/shard_map/ppermute | solution.py:40
  49.8 1.6 pad_maximum_fusion.x_ref
  51.6 10.9 %collective-permute-done.8 = bf16[2,640,128]{2,1,0:T(8,128)(2,1)S(1)} collective-permute-done((bf16[2,640,128]{2,1,0:T(8,128)(2,1)S(1)}, bf16[2,640,128]{2,1,0:T(8,128)(2,1)S(1)}, u32[]{:S(2)}, u32[]{:S(2)}) %collective-permute-start.8) | collective-permute-done | bytes 327712 | tf_op jit(solution)/shard_map/ppermute | solution.py:40
  66.4 13.6 %shard_map.500 = (bf16[1024,1024]{1,0:T(8,128)(2,1)}, bf16[1024,256]{1,0:T(8,128)(2,1)S(1)}, bf16[1024,512]{1,0:T(8,128)(2,1)S(1)}, f32[1024,128]{1,0:T(8,128)S(...) custom-call(bf16[1024,1024]{1,0:T(8,128)(2,1)} %pad_maximum_fusion.x, ...), custom_call_target="tpu_custom_call" | custom-call | flops 1 | tf_op jit(solution)/shard_map/pallas_call | solution.py:202
  80.0 2.0 collective-permute-done.13
  87.6 6.2 %collective-permute-done.17 = f32[2,1,128]{2,0,1:T(2,128)S(1)} collective-permute-done((f32[2,1,128]{2,0,1:T(2,128)S(1)}, f32[2,1,128]{2,0,1:T(2,128)S(1)}, u32[]{:S(2)}, u32[]{:S(2)}) %collective-permute-start.17) | collective-permute-done | bytes 1056 | tf_op jit(solution)/shard_map/ppermute | solution.py:40
  93.7 1.6 fusion.25
  96.2 2.0 collective-permute-start.18
  98.2 3.0 collective-permute-done.18
  102.3 2.8 collective-permute-start.20
  106.5 7.8 %collective-permute-done.15 = bf16[2,2,2,320,128]{4,3,1,2,0:T(8,128)(2,1)} collective-permute-done((bf16[2,2,2,320,128]{4,3,1,2,0:T(8,128)(2,1)S(1)}, bf16[2,2,2,320,128]{4,3,1,2,0:T(8,128)(2,1)}, u32[]{:S(2)}, u32[]{:S(2)}) %collective-permute-start.15) | collective-permute-done | bytes 655392 | tf_op jit(solution)/shard_map/ppermute | solution.py:40
  115.8 1.7 maximum_maximum_fusion.weight_ref.late_ref
  120.3 5.1 %shard_map.501 = (bf16[1024,256]{1,0:T(8,128)(2,1)S(1)}, f32[1024,512]{1,0:T(8,128)S(1)}) custom-call(bf16[1024,1024]{1,0:T(8,128)(2,1)} %get-tuple-element.202.normed_ref, bf16[2,8,640,128]{3,2,1,0:T(8,128)(2,1)} %maximum_maximum_fusion.weight_ref.late_ref), custom_call_target="tpu_custom_call" | custom-call | flops 1 | tf_op jit(solution)/shard_map/pallas_call | solution.py:202
  126.9 9.4 %shard_map.502 = (f32[1024,512]{1,0:T(8,128)}, bf16[16,2,256,128]{3,2,1,0:T(8,128)(2,1)}, bf16[1024,512]{1,0:T(8,128)(2,1)S(1)}, bf16[1024,1024]{1,0:T(8,128)(2,1)}) custom-call(bf16[1024,256]{1,0:T(8,128)(2,1)S(1)} %get-tuple-element.184.query_ref, bf16[1024,256]{1,0:T(8,128)(2,1)S(1)} %get-tuple-element.185.key_ref, ...), custom_call_target="tpu_custom_call" | custom-call | flops 1 | tf_op jit(solution)/shard_map/pallas_call | solution.py:202
  136.4 5.4 %collective-permute-done.22 = bf16[2,1024,256]{2,1,0:T(8,128)(2,1)S(1)} collective-permute-done((bf16[2,1024,256]{2,1,0:T(8,128)(2,1)S(1)}, bf16[2,1024,256]{2,1,0:T(8,128)(2,1)S(1)}, u32[]{:S(2)}, u32[]{:S(2)}) %collective-permute-start.22) | collective-permute-done | bytes 1048608 | tf_op jit(solution)/shard_map/ppermute | solution.py:40
  144.7 5.5 %shard_map.503 = (f32[1024,1024]{1,0:T(8,128)}, bf16[1024,1024]{1,0:T(8,128)(2,1)S(1)}) custom-call(bf16[1024,1024]{1,0:T(8,128)(2,1)} %pad_maximum_fusion.x_ref, bf16[1024,1024]{1,0:T(8,128)(2,1)} %get-tuple-element.190.mine_ref, bf16[1024,1024]{1,0:T(8,128)(2,1)} %collective-permute-done.21.other_ref, f32[8,1024]{1,0:T(8,128)S(1)} %get-tuple-element.191.gain_ref), custom_call_target="tpu_custom_call" | custom-call | flops 1 | tf_op jit(solution)/shard_map/pallas_call | solution.py:202
  152.2 3.1 broadcast_select_fusion.5
  155.5 1.6 pad_maximum_fusion.1.cot_ref.cot_own_ref
  157.0 17.5 %shard_map.504 = (bf16[768,1024]{1,0:T(8,128)(2,1)S(1)}, bf16[768,1024]{1,0:T(8,128)(2,1)S(1)}, bf16[768,1024]{1,0:T(8,128)(2,1)}, bf16[1024,1024]{1,0:T(8,128)(2,1)}, bf16[1024,1024]{1,0:T(8,128)(2,1)}) custom-call(bf16[1024,1024]{1,0:T(8,128)(2,1)} %copy-done.1, bf16[1024,1024]{1,0:T(8,128)(2,1)} %pad_maximum_fusion.1.cot_ref.cot_own_ref, ...), custom_call_target="tpu_custom_call" | custom-call | flops 1 | tf_op jit(solution)/shard_map/pallas_call | solution.py:202
  175.7 3.9 copy.103
  179.6 2.5 copy.104
  183.7 1.6 pad_maximum_fusion.3.cot_ref.cot_other_ref
  185.3 1.7 broadcast_select_fusion.3
  188.5 17.4 %shard_map.505 = (bf16[768,1024]{1,0:T(8,128)(2,1)S(1)}, bf16[768,1024]{1,0:T(8,128)(2,1)S(1)}, bf16[768,1024]{1,0:T(8,128)(2,1)}, bf16[1024,1024]{1,0:T(8,128)(2,1)}, bf16[1024,1024]{1,0:T(8,128)(2,1)}) custom-call(bf16[1024,1024]{1,0:T(8,128)(2,1)} %pad_maximum_fusion.2.normed_ref.other_ref, bf16[1024,1024]{1,0:T(8,128)(2,1)} %pad_maximum_fusion.3.cot_ref.cot_other_ref, ...), custom_call_target="tpu_custom_call" | custom-call | flops 1 | tf_op jit(solution)/shard_map/pallas_call | solution.py:202
  205.9 1.9 dynamic-slice_bitcast_fusion.2
  208.4 2.3 collective-permute-done.27
  213.6 15.2 %shard_map.506 = bf16[8,3,704,128]{3,2,1,0:T(8,128)(2,1)} custom-call(bf16[1024,1024]{1,0:T(8,128)(2,1)} %copy-done.1, bf16[1024,1024]{1,0:T(8,128)(2,1)} %pad_maximum_fusion.2.normed_ref.other_ref, bf16[1024,1024]{1,0:T(8,128)(2,1)} %pad_maximum_fusion.1.cot_ref.cot_own_ref, bf16[1024,1024]{1,0:T(8,128)(2,1)} %pad_maximum_fusion.3.cot_ref.cot_other_ref, ...), custom_call_target="tpu_custom_call" | custom-call | flops 1 | tf_op jit(solution)/shard_map/pallas_call | solution.py:202
  228.7 9.2 %collective-permute-done.28 = bf16[512,1024]{1,0:T(8,128)(2,1)} collective-permute-done((bf16[512,1024]{1,0:T(8,128)(2,1)}, bf16[512,1024]{1,0:T(8,128)(2,1)}, u32[]{:S(2)}, u32[]{:S(2)}) %collective-permute-start.28) | collective-permute-done | bytes 1048608 | tf_op jit(solution)/shard_map/ppermute | solution.py:40
  237.9 2.9 collective-permute-done.30
  243.7 7.9 %shard_map.507 = (f32[1024,1024]{1,0:T(8,128)}, bf16[1024,1024]{1,0:T(8,128)(2,1)S(1)}, f32[1,1024]{1,0:T(1,128)S(1)}) custom-call(f32[1024,1024]{1,0:T(8,128)} %get-tuple-element.228.residual_ref, bf16[1024,1024]{1,0:T(8,128)(2,1)} %pad_maximum_fusion.1.cot_ref.cot_own_ref, bf16[1024,1024]{1,0:T(8,128)(2,1)} %get-tuple-element.208.mine_ref, ...), custom_call_target="tpu_custom_call" | custom-call | flops 1 | tf_op jit(solution)/shard_map/pallas_call | solution.py:202
  251.7 2.2 copy-done.65
  257.8 9.2 %shard_map.508 = (bf16[1024,512]{1,0:T(8,128)(2,1)S(1)}, bf16[1024,512]{1,0:T(8,128)(2,1)S(1)}, f32[1,256]{1,0:T(1,128)S(1)}, f32[2,256,128]{2,1,0:T(8,128)S(1)}) custom-call(bf16[1024,1024]{1,0:T(8,128)(2,1)} %copy-done.4, bf16[2,8,640,128]{3,2,1,0:T(8,128)(2,1)} %maximum_maximum_fusion.weight_ref.late_ref, f32[1024,512]{1,0:T(8,128)} %get-tuple-element.218.recurrent_ref, ...), custom_call_target="tpu_custom_call" | custom-call | flops 1 | tf_op jit(solution)/shard_map/pallas_call | solution.py:202
  269.6 2.0 copy-done.63
  272.0 2.1 copy_add_fusion
  277.9 12.7 %collective-permute-done.33 = bf16[2,256,128]{2,1,0:T(8,128)(2,1)S(1)} collective-permute-done((bf16[2,256,128]{2,1,0:T(8,128)(2,1)S(1)}, bf16[2,256,128]{2,1,0:T(8,128)(2,1)S(1)}, u32[]{:S(2)}, u32[]{:S(2)}) %collective-permute-start.33) | collective-permute-done | bytes 131104 | tf_op jit(solution)/shard_map/ppermute | solution.py:40
  292.1 15.8 %collective-permute-done.34 = bf16[2,256,128]{2,1,0:T(8,128)(2,1)S(1)} collective-permute-done((bf16[2,256,128]{2,1,0:T(8,128)(2,1)S(1)}, bf16[2,256,128]{2,1,0:T(8,128)(2,1)S(1)}, u32[]{:S(2)}, u32[]{:S(2)}) %collective-permute-start.34) | collective-permute-done | bytes 131104 | tf_op jit(solution)/shard_map/ppermute | solution.py:40
  308.7 9.7 %shard_map.509 = (bf16[1024,256]{1,0:T(8,128)(2,1)S(1)}, f32[1024,256]{1,0:T(8,128)S(1)}, f32[1024,1024]{1,0:T(8,128)}) custom-call(bf16[1024,256]{1,0:T(8,128)(2,1)S(1)} %copy-done.6, bf16[1024,256]{1,0:T(8,128)(2,1)S(1)} %copy-done.12, bf16[1024,512]{1,0:T(8,128)(2,1)S(1)} %get-tuple-element.186.value_ref, f32[1024,256]{1,0:T(8,128)} %get-tuple-element.188.within_ref, ...), custom_call_target="tpu_custom_call" | custom-call | flops 1 | tf_op jit(solution)/shard_map/pallas_call | solution.py:202
  319.5 6.5 %shard_map.510 = bf16[2,8,640,128]{3,2,1,0:T(8,128)(2,1)} custom-call(bf16[1024,1024]{1,0:T(8,128)(2,1)} %bitcast.267, bf16[1024,256]{1,0:T(8,128)(2,1)S(1)} %get-tuple-element.234.query_ref, bf16[1024,512]{1,0:T(8,128)(2,1)S(1)} %copy-done.14, bf16[512,1024]{1,0:T(8,128)(2,1)S(1)} %bitcast.254, bf16[1024,1024]{1,0:T(8,128)(2,1)} %copy-done.4), custom_call_target="tpu_custom_call" | custom-call | flops 1 | tf_op jit(solution)/shard_map/pallas_call | solution.py:202
  326.0 1.9 fusion.32
  332.4 18.6 %shard_map.511 = (bf16[1024,256]{1,0:T(8,128)(2,1)S(1)}, bf16[1024,512]{1,0:T(8,128)(2,1)}, f32[16,1024]{1,0:T(8,128)S(1)}, f32[24,256]{1,0:T(8,128)S(1)}, bf16[1024,1024]{1,0:T(8,128)(2,1)}) custom-call(bf16[1024,256]{1,0:T(8,128)(2,1)S(1)} %copy-done.6, bf16[1024,256]{1,0:T(8,128)(2,1)S(1)} %copy-done.12, bf16[1024,512]{1,0:T(8,128)(2,1)} %copy-done.2, ...), custom_call_target="tpu_custom_call" | custom-call | flops 1 | tf_op jit(solution)/shard_map/pallas_call | solution.py:202
  356.3 2.0 collective-permute-start.42
  358.3 4.5 shard_map.512
  365.4 6.4 %shard_map.513 = (f32[2,1024,256]{2,1,0:T(8,128)S(1)}, f32[1,1024]{1,0:T(1,128)S(1)}, f32[16,1024]{1,0:T(8,128)S(1)}) custom-call(s32[1,1]{1,0:T(1,128)} %bitcast.87.core_ref, bf16[1024,1024]{1,0:T(8,128)(2,1)} %pad_maximum_fusion.x_ref, f32[1024,1024]{1,0:T(8,128)} %get-tuple-element.238.grad_ref, bf16[1024,1024]{1,0:T(8,128)(2,1)} %get-tuple-element.252.mine_ref, ...), custom_call_target="tpu_custom_call" | custom-call | flops 1 | tf_op jit(solution)/shard_map/pallas_call | solution.py:202
  375.0 11.8 %collective-permute-done.50 = f32[35,1024]{1,0:T(8,128)S(1)} collective-permute-done((f32[35,1024]{1,0:T(8,128)S(1)}, f32[35,1024]{1,0:T(8,128)S(1)}, u32[]{:S(2)}, u32[]{:S(2)}) %collective-permute-start.50) | collective-permute-done | bytes 143392 | tf_op jit(solution)/shard_map/ppermute | solution.py:40
  390.1 4.0 collective-permute-done.51
  394.3 2.7 collective-permute-start.45
  397.0 3.4 collective-permute-done.52
  403.3 4.0 collective-permute-done.45
  407.3 1.7 collective-permute-done.53
  409.8 1.9 collective-permute-start.41
  411.7 3.6 collective-permute-done.48
  415.5 2.3 shard_map.515
  418.9 3.4 shard_map.514
  423.9 1.9 collective-permute-start.55
  427.8 2.9 collective-permute-start.56
  433.8 2.5 collective-permute-done.57
  438.8 2.2 collective-permute-done.58
  440.9 1.8 shard_map.517
  (422 shorter events, 93.5 us)
Async XLA Ops:
  7.2 149.8 %all-gather.3.cloned.1.call-start = ((), (), s32[]{:S(2)}) async-start(), calls=%async_computation.2 | async-start | bytes 4866048 | tf_op jit(solution)/shard_map/all_gather | solution.py:716
  8.4 24.0 %collective-permute-start = (bf16[1024,256]{1,0:T(8,128)(2,1)S(1)}, bf16[1024,256]{1,0:T(8,128)(2,1)S(1)}, u32[]{:S(2)}, u32[]{:S(2)}) collective-permute-start(bf16[1024,256]{1,0:T(8,128)(2,1)S(1)} %dynamic-slice_bitcast_fusion.3), channel_id=1, source_target_pairs={{0,2},{1,3},{2,0},{3,1},{4,6},{5,7},{6,4},{7,5},{8,10},{9,11},{10,... | collective-permute-start | bytes 1572872 | tf_op jit(solution)/shard_map/ppermute | solution.py:40
  14.6 5.7 %collective-permute-start.2 = (bf16[160,128]{1,0:T(8,128)(2,1)}, bf16[160,128]{1,0:T(8,128)(2,1)}, u32[]{:S(2)}, u32[]{:S(2)}) collective-permute-start(bf16[160,128]{1,0:T(8,128)(2,1)} %maximum_maximum_fusion.1), channel_id=1, source_target_pairs={{0,16},{4,20},{8,24},{12,28},{16,0},{20,4},{24,8},{28,12},{1,17},{... | collective-permute-start | bytes 122888 | tf_op jit(solution)/shard_map/ppermute | solution.py:40
  19.8 5.4 %collective-permute-start.4 = (bf16[128,256]{1,0:T(8,128)(2,1)}, bf16[128,256]{1,0:T(8,128)(2,1)S(1)}, u32[]{:S(2)}, u32[]{:S(2)}) collective-permute-start(bf16[128,256]{1,0:T(8,128)(2,1)} %slice_bitcast_fusion.12), channel_id=1, source_target_pairs={{0,16},{4,20},{8,24},{12,28},{16,0},{20,4},{24,8},{28,12},{1,17},{... | collective-permute-start | bytes 196616 | tf_op jit(solution)/shard_map/ppermute | solution.py:40
  20.1 397.7 %reduce-scatter.2.cloned.1.call-start = ((), (), s32[]{:S(2)}) async-start(), calls=%async_computation.1 | async-start | bytes 4866048 | tf_op jit(solution)/shard_map/reduce_scatter | solution.py:903
  21.3 6.1 %collective-permute-start.3 = (bf16[2,160,128]{2,1,0:T(8,128)(2,1)S(1)}, bf16[2,160,128]{2,1,0:T(8,128)(2,1)S(1)}, u32[]{:S(2)}, u32[]{:S(2)}) collective-permute-start(bf16[2,160,128]{2,1,0:T(8,128)(2,1)S(1)} %pad_maximum_fusion.26), channel_id=1, source_target_pairs={{0,8},{4,12},{8,0},{12,4},{16,24},{20,28},{24,16},{28,20},{1,9},{5... | collective-permute-start | bytes 245768 | tf_op jit(solution)/shard_map/ppermute | solution.py:40
  25.2 5.3 %collective-permute-start.5 = (bf16[2,128,256]{2,1,0:T(8,128)(2,1)S(1)}, bf16[2,128,256]{2,1,0:T(8,128)(2,1)S(1)}, u32[]{:S(2)}, u32[]{:S(2)}) collective-permute-start(bf16[2,128,256]{2,1,0:T(8,128)(2,1)S(1)} %pad_maximum_fusion.25), channel_id=1, source_target_pairs={{0,8},{4,12},{8,0},{12,4},{16,24},{20,28},{24,16},{28,20},{1,9},{5... | collective-permute-start | bytes 393224 | tf_op jit(solution)/shard_map/ppermute | solution.py:40
  27.4 5.4 %collective-permute-start.9 = (bf16[2,2,160,128]{3,2,0,1:T(8,128)(2,1)S(1)}, bf16[2,2,160,128]{3,2,0,1:T(8,128)(2,1)S(1)}, u32[]{:S(2)}, u32[]{:S(2)}) collective-permute-start(bf16[2,2,160,128]{3,2,0,1:T(8,128)(2,1)S(1)} %pad_maximum_fusion.24), channel_id=1, source_target_pairs={{0,2},{1,3},{2,0},{3,1},{4,6},{5,7},{6,4},{7,5},{8,10},{9,11},{10,... | collective-permute-start | bytes 491528 | tf_op jit(solution)/shard_map/ppermute | solution.py:40
  30.6 18.7 %collective-permute-start.7 = (bf16[2,2,128,256]{3,2,0,1:T(8,128)(2,1)S(1)}, bf16[2,2,128,256]{3,2,0,1:T(8,128)(2,1)S(1)}, u32[]{:S(2)}, u32[]{:S(2)}) collective-permute-start(bf16[2,2,128,256]{3,2,0,1:T(8,128)(2,1)S(1)} %pad_maximum_fusion.22), channel_id=1, source_target_pairs={{0,4},{4,0},{8,12},{12,8},{16,20},{20,16},{24,28},{28,24},{1,5},{5... | collective-permute-start | bytes 786440 | tf_op jit(solution)/shard_map/ppermute | solution.py:40
  31.9 17.3 %collective-permute-start.6 = (bf16[640,128]{1,0:T(8,128)(2,1)S(1)}, bf16[640,128]{1,0:T(8,128)(2,1)S(1)}, u32[]{:S(2)}, u32[]{:S(2)}) collective-permute-start(bf16[640,128]{1,0:T(8,128)(2,1)S(1)} %pad_maximum_fusion.23), channel_id=1, source_target_pairs={{0,16},{4,20},{8,24},{12,28},{16,0},{20,4},{24,8},{28,12},{1,17},{... | collective-permute-start | bytes 491528 | tf_op jit(solution)/shard_map/ppermute | solution.py:40
  32.6 16.9 %collective-permute-start.1 = (bf16[2,1024,256]{2,1,0:T(8,128)(2,1)S(1)}, bf16[2,1024,256]{2,1,0:T(8,128)(2,1)S(1)}, u32[]{:S(2)}, u32[]{:S(2)}) collective-permute-start(bf16[2,1024,256]{2,1,0:T(8,128)(2,1)S(1)} %pad_maximum_fusion.9), channel_id=1, source_target_pairs={{0,1},{1,0},{2,3},{3,2},{4,5},{5,4},{6,7},{7,6},{8,9},{9,8},{10,11... | collective-permute-start | bytes 3145736 | tf_op jit(solution)/shard_map/ppermute | solution.py:40
  32.9 18.5 %collective-permute-start.10 = (bf16[2,2,2,160,128]{4,3,1,2,0:T(8,128)(2,1)S(1)}, bf16[2,2,2,160,128]{4,3,1,2,0:T(8,128)(2,1)S(1)}, u32[]{:S(2)}, u32[]{:S(2)}) collective-permute-start(bf16[2,2,2,160,128]{4,3,1,2,0:T(8,128)(2,1)S(1)} %pad_maximum_fusion.21), channel_id=1, source_target_pairs={{0,4},{4,0},{8,12},{12,8},{16,20},{20,16},{24,28},{28,24},{1,5},{5... | collective-permute-start | bytes 983048 | tf_op jit(solution)/shard_map/ppermute | solution.py:40
  49.4 13.1 %collective-permute-start.8 = (bf16[2,640,128]{2,1,0:T(8,128)(2,1)S(1)}, bf16[2,640,128]{2,1,0:T(8,128)(2,1)S(1)}, u32[]{:S(2)}, u32[]{:S(2)}) collective-permute-start(bf16[2,640,128]{2,1,0:T(8,128)(2,1)S(1)} %pad_maximum_fusion.20), channel_id=1, source_target_pairs={{0,8},{4,12},{8,0},{12,4},{16,24},{20,28},{24,16},{28,20},{1,9},{5... | collective-permute-start | bytes 983048 | tf_op jit(solution)/shard_map/ppermute | solution.py:40
  51.4 11.3 %collective-permute-start.11 = (bf16[2,2,2,128,256]{4,3,0,1,2:T(8,128)(2,1)S(1)}, bf16[2,2,2,128,256]{4,3,0,1,2:T(8,128)(2,1)S(1)}, u32[]{:S(2)}, u32[]{:S(2)}) collective-permute-start(bf16[2,2,2,128,256]{4,3,0,1,2:T(8,128)(2,1)S(1)} %pad_maximum_fusion.19), channel_id=1, source_target_pairs={{0,2},{1,3},{2,0},{3,1},{4,6},{5,7},{6,4},{7,5},{8,10},{9,11},{10,... | collective-permute-start | bytes 1572872 | tf_op jit(solution)/shard_map/ppermute | solution.py:40
  64.8 17.2 %collective-permute-start.13 = (bf16[2,2,320,128]{3,2,0,1:T(8,128)(2,1)}, bf16[2,2,320,128]{3,2,0,1:T(8,128)(2,1)}, u32[]{:S(2)}, u32[]{:S(2)}) collective-permute-start(bf16[2,2,320,128]{3,2,0,1:T(8,128)(2,1)} %get-tuple-element.375), channel_id=1, source_target_pairs={{0,4},{4,0},{8,12},{12,8},{16,20},{20,16},{24,28},{28,24},{1,5},{5... | collective-permute-start | bytes 983048 | tf_op jit(solution)/shard_map/ppermute | solution.py:40
  66.0 16.1 %collective-permute-start.12 = (bf16[2,2,320,128]{3,2,0,1:T(8,128)(2,1)}, bf16[2,2,320,128]{3,2,0,1:T(8,128)(2,1)}, u32[]{:S(2)}, u32[]{:S(2)}) collective-permute-start(bf16[2,2,320,128]{3,2,0,1:T(8,128)(2,1)} %get-tuple-element.376), channel_id=1, source_target_pairs={{0,2},{1,3},{2,0},{3,1},{4,6},{5,7},{6,4},{7,5},{8,10},{9,11},{10,... | collective-permute-start | bytes 983048 | tf_op jit(solution)/shard_map/ppermute | solution.py:40
  80.0 46.9 %copy-start.11 = (bf16[1024,256]{1,0:T(8,128)(2,1)}, bf16[1024,256]{1,0:T(8,128)(2,1)S(1)}, u32[]{:S(2)}) copy-start(bf16[1024,256]{1,0:T(8,128)(2,1)S(1)} %get-tuple-element.185.key_ref) | copy-start | bytes 1572868
  80.0 64.7 %copy-start.35 = (f32[8,1024]{1,0:T(8,128)}, f32[8,1024]{1,0:T(8,128)S(1)}, u32[]{:S(2)}) copy-start(f32[8,1024]{1,0:T(8,128)S(1)} %get-tuple-element.191.gain_ref) | copy-start | bytes 98308
  80.0 228.7 %copy-start.2 = (bf16[1024,512]{1,0:T(8,128)(2,1)}, bf16[1024,512]{1,0:T(8,128)(2,1)S(1)}, u32[]{:S(2)}) copy-start(bf16[1024,512]{1,0:T(8,128)(2,1)S(1)} %get-tuple-element.186.value_ref) | copy-start | bytes 3145732
  84.9 8.8 %collective-permute-start.14 = (bf16[2,256,128]{2,1,0:T(8,128)(2,1)}, bf16[2,256,128]{2,1,0:T(8,128)(2,1)}, u32[]{:S(2)}, u32[]{:S(2)}) collective-permute-start(bf16[2,256,128]{2,1,0:T(8,128)(2,1)} %convert_element_type.169), channel_id=1, source_target_pairs={{0,4},{4,0},{8,12},{12,8},{16,20},{20,16},{24,28},{28,24},{1,5},{5... | collective-permute-start | bytes 393224 | tf_op jit(solution)/shard_map/ppermute | solution.py:40
  86.0 19.1 %collective-permute-start.16 = (bf16[2,2,2,320,128]{4,3,0,1,2:T(8,128)(2,1)}, bf16[2,2,2,320,128]{4,3,0,1,2:T(8,128)(2,1)}, u32[]{:S(2)}, u32[]{:S(2)}) collective-permute-start(bf16[2,2,2,320,128]{4,3,0,1,2:T(8,128)(2,1)} %pad_maximum_fusion.17), channel_id=1, source_target_pairs={{0,2},{1,3},{2,0},{3,1},{4,6},{5,7},{6,4},{7,5},{8,10},{9,11},{10,... | collective-permute-start | bytes 1966088 | tf_op jit(solution)/shard_map/ppermute | solution.py:40
  86.1 7.6 %collective-permute-start.17 = (f32[2,1,128]{2,0,1:T(2,128)S(1)}, f32[2,1,128]{2,0,1:T(2,128)S(1)}, u32[]{:S(2)}, u32[]{:S(2)}) collective-permute-start(f32[2,1,128]{2,0,1:T(2,128)S(1)} %bitcast.291), channel_id=1, source_target_pairs={{0,4},{4,0},{8,12},{12,8},{16,20},{20,16},{24,28},{28,24},{1,5},{5... | collective-permute-start | bytes 3080 | tf_op jit(solution)/shard_map/ppermute | solution.py:40
  95.4 5.8 %collective-permute-start.19 = (bf16[2,256,128]{2,1,0:T(8,128)(2,1)}, bf16[2,256,128]{2,1,0:T(8,128)(2,1)}, u32[]{:S(2)}, u32[]{:S(2)}) collective-permute-start(bf16[2,256,128]{2,1,0:T(8,128)(2,1)} %fusion.25), channel_id=1, source_target_pairs={{0,8},{4,12},{8,0},{12,4},{16,24},{20,28},{24,16},{28,20},{1,9},{5... | collective-permute-start | bytes 393224 | tf_op jit(solution)/shard_map/ppermute | solution.py:40
  95.4 19.0 %collective-permute-start.15 = (bf16[2,2,2,320,128]{4,3,1,2,0:T(8,128)(2,1)S(1)}, bf16[2,2,2,320,128]{4,3,1,2,0:T(8,128)(2,1)}, u32[]{:S(2)}, u32[]{:S(2)}) collective-permute-start(bf16[2,2,2,320,128]{4,3,1,2,0:T(8,128)(2,1)S(1)} %pad_maximum_fusion.16), channel_id=1, source_target_pairs={{0,4},{4,0},{8,12},{12,8},{16,20},{20,16},{24,28},{28,24},{1,5},{5... | collective-permute-start | bytes 1966088 | tf_op jit(solution)/shard_map/ppermute | solution.py:40
  96.2 5.0 %collective-permute-start.18 = (f32[2,1,128]{2,0,1:T(2,128)S(1)}, f32[2,1,128]{2,0,1:T(2,128)S(1)}, u32[]{:S(2)}, u32[]{:S(2)}) collective-permute-start(f32[2,1,128]{2,0,1:T(2,128)S(1)} %mul.132), channel_id=1, source_target_pairs={{0,8},{4,12},{8,0},{12,4},{16,24},{20,28},{24,16},{28,20},{1,9},{5... | collective-permute-start | bytes 3080 | tf_op jit(solution)/shard_map/ppermute | solution.py:40
  102.3 17.0 %collective-permute-start.20 = (bf16[2,256,128]{2,1,0:T(8,128)(2,1)S(1)}, bf16[2,256,128]{2,1,0:T(8,128)(2,1)S(1)}, u32[]{:S(2)}, u32[]{:S(2)}) collective-permute-start(bf16[2,256,128]{2,1,0:T(8,128)(2,1)S(1)} %fusion.14), channel_id=1, source_target_pairs={{0,16},{4,20},{8,24},{12,28},{16,0},{20,4},{24,8},{28,12},{1,17},{... | collective-permute-start | bytes 393224 | tf_op jit(solution)/shard_map/ppermute | solution.py:40
  117.5 24.3 %collective-permute-start.22 = (bf16[2,1024,256]{2,1,0:T(8,128)(2,1)S(1)}, bf16[2,1024,256]{2,1,0:T(8,128)(2,1)S(1)}, u32[]{:S(2)}, u32[]{:S(2)}) collective-permute-start(bf16[2,1024,256]{2,1,0:T(8,128)(2,1)S(1)} %copy-done.78), channel_id=1, source_target_pairs={{0,2},{1,3},{2,0},{3,1},{4,6},{5,7},{6,4},{7,5},{8,10},{9,11},{10,... | collective-permute-start | bytes 3145736 | tf_op jit(solution)/shard_map/ppermute | solution.py:40
  136.3 8.4 %collective-permute-start.21 = (bf16[1024,1024]{1,0:T(8,128)(2,1)}, bf16[1024,1024]{1,0:T(8,128)(2,1)}, u32[]{:S(2)}, u32[]{:S(2)}) collective-permute-start(bf16[1024,1024]{1,0:T(8,128)(2,1)} %get-tuple-element.190.mine_ref), channel_id=1, source_target_pairs={{0,1},{1,0},{2,3},{3,2},{4,5},{5,4},{6,7},{7,6},{8,9},{9,8},{10,11... | collective-permute-start | bytes 6291464 | tf_op jit(solution)/shard_map/ppermute | solution.py:40
  143.1 8.7 %collective-permute-start.26 = (bf16[2,1024,256]{2,1,0:T(8,128)(2,1)}, bf16[2,1024,256]{2,1,0:T(8,128)(2,1)}, u32[]{:S(2)}, u32[]{:S(2)}) collective-permute-start(bf16[2,1024,256]{2,1,0:T(8,128)(2,1)} %pad_maximum_fusion.12), channel_id=1, source_target_pairs={{0,1},{1,0},{2,3},{3,2},{4,5},{5,4},{6,7},{7,6},{8,9},{9,8},{10,11... | collective-permute-start | bytes 3145736 | tf_op jit(solution)/shard_map/ppermute | solution.py:40
  144.2 7.7 %collective-permute-start.23 = (bf16[2,1024,256]{2,1,0:T(8,128)(2,1)}, bf16[2,1024,256]{2,1,0:T(8,128)(2,1)}, u32[]{:S(2)}, u32[]{:S(2)}) collective-permute-start(bf16[2,1024,256]{2,1,0:T(8,128)(2,1)} %pad_maximum_fusion.11), channel_id=1, source_target_pairs={{0,1},{1,0},{2,3},{3,2},{4,5},{5,4},{6,7},{7,6},{8,9},{9,8},{10,11... | collective-permute-start | bytes 3145736 | tf_op jit(solution)/shard_map/ppermute | solution.py:40
  151.3 30.8 %collective-permute-start.24 = (bf16[512,1024]{1,0:T(8,128)(2,1)}, bf16[512,1024]{1,0:T(8,128)(2,1)}, u32[]{:S(2)}, u32[]{:S(2)}) collective-permute-start(bf16[512,1024]{1,0:T(8,128)(2,1)} %constant_dynamic-slice_fusion.7), channel_id=1, source_target_pairs={{0,2},{1,3},{2,0},{3,1},{4,6},{5,7},{6,4},{7,5},{8,10},{9,11},{10,... | collective-permute-start | bytes 3145736 | tf_op jit(solution)/shard_map/ppermute | solution.py:40
  182.1 3.3 collective-permute-start.25
  207.8 2.8 collective-permute-start.27
  212.0 25.9 %collective-permute-start.29 = (bf16[1024,1024]{1,0:T(8,128)(2,1)}, bf16[1024,1024]{1,0:T(8,128)(2,1)}, u32[]{:S(2)}, u32[]{:S(2)}) collective-permute-start(bf16[1024,1024]{1,0:T(8,128)(2,1)} %get-tuple-element.208.mine_ref), channel_id=1, source_target_pairs={{0,1},{1,0},{2,3},{3,2},{4,5},{5,4},{6,7},{7,6},{8,9},{9,8},{10,11... | collective-permute-start | bytes 6291464 | tf_op jit(solution)/shard_map/ppermute | solution.py:40
  212.4 25.5 %collective-permute-start.28 = (bf16[512,1024]{1,0:T(8,128)(2,1)}, bf16[512,1024]{1,0:T(8,128)(2,1)}, u32[]{:S(2)}, u32[]{:S(2)}) collective-permute-start(bf16[512,1024]{1,0:T(8,128)(2,1)} %fusion), channel_id=1, source_target_pairs={{0,2},{1,3},{2,0},{3,1},{4,6},{5,7},{6,4},{7,5},{8,10},{9,11},{10,... | collective-permute-start | bytes 3145736 | tf_op jit(solution)/shard_map/ppermute | solution.py:40
  237.9 2.9 collective-permute-start.30
  255.8 16.2 %collective-permute-start.31 = (bf16[2,2,1024,256]{3,2,1,0:T(8,128)(2,1)}, bf16[2,2,1024,256]{3,2,1,0:T(8,128)(2,1)}, u32[]{:S(2)}, u32[]{:S(2)}) collective-permute-start(bf16[2,2,1024,256]{3,2,1,0:T(8,128)(2,1)} %pad_maximum_fusion.5), channel_id=1, source_target_pairs={{0,1},{1,0},{2,3},{3,2},{4,5},{5,4},{6,7},{7,6},{8,9},{9,8},{10,11... | collective-permute-start | bytes 6291464 | tf_op jit(solution)/shard_map/ppermute | solution.py:40
  267.0 10.7 %collective-permute-start.32 = (bf16[2,256,128]{2,1,0:T(8,128)(2,1)S(1)}, bf16[2,256,128]{2,1,0:T(8,128)(2,1)S(1)}, u32[]{:S(2)}, u32[]{:S(2)}) collective-permute-start(bf16[2,256,128]{2,1,0:T(8,128)(2,1)S(1)} %convert_element_type.183), channel_id=1, source_target_pairs={{0,4},{4,0},{8,12},{12,8},{16,20},{20,16},{24,28},{28,24},{1,5},{5... | collective-permute-start | bytes 393224 | tf_op jit(solution)/shard_map/ppermute | solution.py:40
  276.8 49.3 %collective-permute-start.35 = (bf16[2,1024,256]{2,1,0:T(8,128)(2,1)}, bf16[2,1024,256]{2,1,0:T(8,128)(2,1)}, u32[]{:S(2)}, u32[]{:S(2)}) collective-permute-start(bf16[2,1024,256]{2,1,0:T(8,128)(2,1)} %fusion.3), channel_id=1, source_target_pairs={{0,2},{1,3},{2,0},{3,1},{4,6},{5,7},{6,4},{7,5},{8,10},{9,11},{10,... | collective-permute-start | bytes 3145736 | tf_op jit(solution)/shard_map/ppermute | solution.py:40
  277.8 12.8 %collective-permute-start.33 = (bf16[2,256,128]{2,1,0:T(8,128)(2,1)S(1)}, bf16[2,256,128]{2,1,0:T(8,128)(2,1)S(1)}, u32[]{:S(2)}, u32[]{:S(2)}) collective-permute-start(bf16[2,256,128]{2,1,0:T(8,128)(2,1)S(1)} %fusion.24), channel_id=1, source_target_pairs={{0,8},{4,12},{8,0},{12,4},{16,24},{20,28},{24,16},{28,20},{1,9},{5... | collective-permute-start | bytes 393224 | tf_op jit(solution)/shard_map/ppermute | solution.py:40
  290.8 17.1 %collective-permute-start.34 = (bf16[2,256,128]{2,1,0:T(8,128)(2,1)S(1)}, bf16[2,256,128]{2,1,0:T(8,128)(2,1)S(1)}, u32[]{:S(2)}, u32[]{:S(2)}) collective-permute-start(bf16[2,256,128]{2,1,0:T(8,128)(2,1)S(1)} %fusion.19), channel_id=1, source_target_pairs={{0,16},{4,20},{8,24},{12,28},{16,0},{20,4},{24,8},{28,12},{1,17},{... | collective-permute-start | bytes 393224 | tf_op jit(solution)/shard_map/ppermute | solution.py:40
  330.1 22.3 %collective-permute-start.36 = (bf16[2,2,2,320,128]{4,3,1,2,0:T(8,128)(2,1)S(1)}, bf16[2,2,2,320,128]{4,3,1,2,0:T(8,128)(2,1)}, u32[]{:S(2)}, u32[]{:S(2)}) collective-permute-start(bf16[2,2,2,320,128]{4,3,1,2,0:T(8,128)(2,1)S(1)} %bitcast.285), channel_id=1, source_target_pairs={{0,4},{4,0},{8,12},{12,8},{16,20},{20,16},{24,28},{28,24},{1,5},{5... | collective-permute-start | bytes 1966088 | tf_op jit(solution)/shard_map/ppermute | solution.py:40
  330.9 21.5 %collective-permute-start.37 = (bf16[2,2,2,320,128]{4,3,0,1,2:T(8,128)(2,1)S(1)}, bf16[2,2,2,320,128]{4,3,0,1,2:T(8,128)(2,1)}, u32[]{:S(2)}, u32[]{:S(2)}) collective-permute-start(bf16[2,2,2,320,128]{4,3,0,1,2:T(8,128)(2,1)S(1)} %bitcast.286), channel_id=1, source_target_pairs={{0,2},{1,3},{2,0},{3,1},{4,6},{5,7},{6,4},{7,5},{8,10},{9,11},{10,... | collective-permute-start | bytes 1966088 | tf_op jit(solution)/shard_map/ppermute | solution.py:40
  352.4 12.0 %collective-permute-start.38 = (bf16[1024,1024]{1,0:T(8,128)(2,1)}, bf16[1024,1024]{1,0:T(8,128)(2,1)}, u32[]{:S(2)}, u32[]{:S(2)}) collective-permute-start(bf16[1024,1024]{1,0:T(8,128)(2,1)} %get-tuple-element.252.mine_ref), channel_id=1, source_target_pairs={{0,1},{1,0},{2,3},{3,2},{4,5},{5,4},{6,7},{7,6},{8,9},{9,8},{10,11... | collective-permute-start | bytes 6291464 | tf_op jit(solution)/shard_map/ppermute | solution.py:40
  352.6 11.8 %collective-permute-start.39 = (f32[16,1024]{1,0:T(8,128)S(1)}, f32[16,1024]{1,0:T(8,128)S(1)}, u32[]{:S(2)}, u32[]{:S(2)}) collective-permute-start(f32[16,1024]{1,0:T(8,128)S(1)} %get-tuple-element.253), channel_id=1, source_target_pairs={{0,1},{1,0},{2,3},{3,2},{4,5},{5,4},{6,7},{7,6},{8,9},{9,8},{10,11... | collective-permute-start | bytes 196616 | tf_op jit(solution)/shard_map/ppermute | solution.py:40
  354.6 9.7 %collective-permute-start.43 = (bf16[2,2,320,128]{3,2,0,1:T(8,128)(2,1)S(1)}, bf16[2,2,320,128]{3,2,0,1:T(8,128)(2,1)S(1)}, u32[]{:S(2)}, u32[]{:S(2)}) collective-permute-start(bf16[2,2,320,128]{3,2,0,1:T(8,128)(2,1)S(1)} %fusion.8), channel_id=1, source_target_pairs={{0,4},{4,0},{8,12},{12,8},{16,20},{20,16},{24,28},{28,24},{1,5},{5... | collective-permute-start | bytes 983048 | tf_op jit(solution)/shard_map/ppermute | solution.py:40
  356.3 15.7 %collective-permute-start.42 = (bf16[2,2,320,128]{3,2,0,1:T(8,128)(2,1)S(1)}, bf16[2,2,320,128]{3,2,0,1:T(8,128)(2,1)S(1)}, u32[]{:S(2)}, u32[]{:S(2)}) collective-permute-start(bf16[2,2,320,128]{3,2,0,1:T(8,128)(2,1)S(1)} %fusion.7), channel_id=1, source_target_pairs={{0,2},{1,3},{2,0},{3,1},{4,6},{5,7},{6,4},{7,5},{8,10},{9,11},{10,... | collective-permute-start | bytes 983048 | tf_op jit(solution)/shard_map/ppermute | solution.py:40
  364.7 23.2 %collective-permute-start.40 = (bf16[2,2,2,384,128]{4,3,0,1,2:T(8,128)(2,1)S(1)}, bf16[2,2,2,384,128]{4,3,0,1,2:T(8,128)(2,1)S(1)}, u32[]{:S(2)}, u32[]{:S(2)}) collective-permute-start(bf16[2,2,2,384,128]{4,3,0,1,2:T(8,128)(2,1)S(1)} %bitcast.282), channel_id=1, source_target_pairs={{0,2},{1,3},{2,0},{3,1},{4,6},{5,7},{6,4},{7,5},{8,10},{9,11},{10,... | collective-permute-start | bytes 2359304 | tf_op jit(solution)/shard_map/ppermute | solution.py:40
  371.9 1.5 collective-permute-start.49
  373.4 13.4 %collective-permute-start.50 = (f32[35,1024]{1,0:T(8,128)S(1)}, f32[35,1024]{1,0:T(8,128)S(1)}, u32[]{:S(2)}, u32[]{:S(2)}) collective-permute-start(f32[35,1024]{1,0:T(8,128)S(1)} %fusion.31), channel_id=1, source_target_pairs={{0,2},{1,3},{2,0},{3,1},{4,6},{5,7},{6,4},{7,5},{8,10},{9,11},{10,... | collective-permute-start | bytes 430088 | tf_op jit(solution)/shard_map/ppermute | solution.py:40
  375.0 19.2 %collective-permute-start.44 = (bf16[2,640,128]{2,1,0:T(8,128)(2,1)S(1)}, bf16[2,640,128]{2,1,0:T(8,128)(2,1)S(1)}, u32[]{:S(2)}, u32[]{:S(2)}) collective-permute-start(bf16[2,640,128]{2,1,0:T(8,128)(2,1)S(1)} %fusion.9), channel_id=1, source_target_pairs={{0,8},{4,12},{8,0},{12,4},{16,24},{20,28},{24,16},{28,20},{1,9},{5... | collective-permute-start | bytes 983048 | tf_op jit(solution)/shard_map/ppermute | solution.py:40
  386.9 7.2 %collective-permute-start.51 = (f32[35,1024]{1,0:T(8,128)S(1)}, f32[35,1024]{1,0:T(8,128)S(1)}, u32[]{:S(2)}, u32[]{:S(2)}) collective-permute-start(f32[35,1024]{1,0:T(8,128)S(1)} %add.309), channel_id=1, source_target_pairs={{0,4},{4,0},{8,12},{12,8},{16,20},{20,16},{24,28},{28,24},{1,5},{5... | collective-permute-start | bytes 430088 | tf_op jit(solution)/shard_map/ppermute | solution.py:40
  388.1 13.5 %collective-permute-start.46 = (bf16[2,2,384,128]{3,2,0,1:T(8,128)(2,1)S(1)}, bf16[2,2,384,128]{3,2,0,1:T(8,128)(2,1)S(1)}, u32[]{:S(2)}, u32[]{:S(2)}) collective-permute-start(bf16[2,2,384,128]{3,2,0,1:T(8,128)(2,1)S(1)} %fusion.6), channel_id=1, source_target_pairs={{0,4},{4,0},{8,12},{12,8},{16,20},{20,16},{24,28},{28,24},{1,5},{5... | collective-permute-start | bytes 1179656 | tf_op jit(solution)/shard_map/ppermute | solution.py:40
  394.1 6.3 %collective-permute-start.52 = (f32[35,1024]{1,0:T(8,128)S(1)}, f32[35,1024]{1,0:T(8,128)S(1)}, u32[]{:S(2)}, u32[]{:S(2)}) collective-permute-start(f32[35,1024]{1,0:T(8,128)S(1)} %add.310), channel_id=1, source_target_pairs={{0,8},{4,12},{8,0},{12,4},{16,24},{20,28},{24,16},{28,20},{1,9},{5... | collective-permute-start | bytes 430088 | tf_op jit(solution)/shard_map/ppermute | solution.py:40
  394.3 13.0 %collective-permute-start.45 = (bf16[640,128]{1,0:T(8,128)(2,1)S(1)}, bf16[640,128]{1,0:T(8,128)(2,1)S(1)}, u32[]{:S(2)}, u32[]{:S(2)}) collective-permute-start(bf16[640,128]{1,0:T(8,128)(2,1)S(1)} %fusion.21), channel_id=1, source_target_pairs={{0,16},{4,20},{8,24},{12,28},{16,0},{20,4},{24,8},{28,12},{1,17},{... | collective-permute-start | bytes 491528 | tf_op jit(solution)/shard_map/ppermute | solution.py:40
  400.4 8.6 %collective-permute-start.53 = (f32[35,1024]{1,0:T(8,128)S(1)}, f32[35,1024]{1,0:T(8,128)S(1)}, u32[]{:S(2)}, u32[]{:S(2)}) collective-permute-start(f32[35,1024]{1,0:T(8,128)S(1)} %add.311), channel_id=1, source_target_pairs={{0,16},{4,20},{8,24},{12,28},{16,0},{20,4},{24,8},{28,12},{1,17},{... | collective-permute-start | bytes 430088 | tf_op jit(solution)/shard_map/ppermute | solution.py:40
  401.9 7.7 %collective-permute-start.47 = (bf16[2,384,128]{2,1,0:T(8,128)(2,1)S(1)}, bf16[2,384,128]{2,1,0:T(8,128)(2,1)S(1)}, u32[]{:S(2)}, u32[]{:S(2)}) collective-permute-start(bf16[2,384,128]{2,1,0:T(8,128)(2,1)S(1)} %fusion.20), channel_id=1, source_target_pairs={{0,8},{4,12},{8,0},{12,4},{16,24},{20,28},{24,16},{28,20},{1,9},{5... | collective-permute-start | bytes 589832 | tf_op jit(solution)/shard_map/ppermute | solution.py:40
  409.7 5.6 %collective-permute-start.48 = (bf16[384,128]{1,0:T(8,128)(2,1)S(1)}, bf16[384,128]{1,0:T(8,128)(2,1)S(1)}, u32[]{:S(2)}, u32[]{:S(2)}) collective-permute-start(bf16[384,128]{1,0:T(8,128)(2,1)S(1)} %fusion.26), channel_id=1, source_target_pairs={{0,16},{4,20},{8,24},{12,28},{16,0},{20,4},{24,8},{28,12},{1,17},{... | collective-permute-start | bytes 294920 | tf_op jit(solution)/shard_map/ppermute | solution.py:40
  409.8 22.8 %collective-permute-start.41 = (bf16[1024,256]{1,0:T(8,128)(2,1)}, bf16[1024,256]{1,0:T(8,128)(2,1)}, u32[]{:S(2)}, u32[]{:S(2)}) collective-permute-start(bf16[1024,256]{1,0:T(8,128)(2,1)} %dynamic-slice_bitcast_fusion.1), channel_id=1, source_target_pairs={{0,2},{1,3},{2,0},{3,1},{4,6},{5,7},{6,4},{7,5},{8,10},{9,11},{10,... | collective-permute-start | bytes 1572872 | tf_op jit(solution)/shard_map/ppermute | solution.py:40
  422.3 1.6 collective-permute-start.54
  423.9 3.8 collective-permute-start.55
  427.8 4.7 %collective-permute-start.56 = (f32[32,128]{1,0:T(8,128)S(1)}, f32[32,128]{1,0:T(8,128)S(1)}, u32[]{:S(2)}, u32[]{:S(2)}) collective-permute-start(f32[32,128]{1,0:T(8,128)S(1)} %add.315), channel_id=1, source_target_pairs={{0,4},{4,0},{8,12},{12,8},{16,20},{20,16},{24,28},{28,24},{1,5},{5... | collective-permute-start | bytes 49160 | tf_op jit(solution)/shard_map/ppermute | solution.py:40
  432.5 3.8 collective-permute-start.57
  436.3 4.6 %collective-permute-start.58 = (f32[32,128]{1,0:T(8,128)S(1)}, f32[32,128]{1,0:T(8,128)S(1)}, u32[]{:S(2)}, u32[]{:S(2)}) collective-permute-start(f32[32,128]{1,0:T(8,128)S(1)} %add.317), channel_id=1, source_target_pairs={{0,16},{4,20},{8,24},{12,28},{16,0},{20,4},{24,8},{28,12},{1,17},{... | collective-permute-start | bytes 49160 | tf_op jit(solution)/shard_map/ppermute | solution.py:40
  (86 other events, 688.3 us)
Sparse Core Ops, SparseCore 0:
  20.3 101.7 all-gather.2
  256.0 102.6 reduce-scatter.1

commit v3 on v2

v3 whole, which is shorter than its diff:
```python
import jax
import jax.numpy as jnp
from jax import lax
from jax.experimental import pallas as pl
from jax.experimental.pallas import tpu as pltpu
from jax.sharding import PartitionSpec as P

SPAN = 64
STEP = 10


eps_norm = 1e-06
gate_scale = 16.0
beta_one = 0.9
beta_two = 0.999
eps_adam = 1e-06
decay_rate = 0.01
learn_rate = 0.5
highest = lax.Precision.HIGHEST


def to_half(value_entries):
    return value_entries.astype(jnp.bfloat16)


def to_float(value_entries):
    return value_entries.astype(jnp.float32)


def mm(pattern, left, right):
    return jnp.einsum(pattern, left, right, preferred_element_type=jnp.float32)


def exact(pattern, left, right):
    return jnp.einsum(pattern, left, right, precision=highest)


def swap(value_entries, axis, bit):
    peers = lax.axis_size(axis)
    return lax.ppermute(value_entries, axis, [(i, i ^ bit) for i in range(peers)])


def bit_of(axis, bit):
    return (lax.axis_index(axis) // bit) % 2


def pick(value_entries, at, axis=0):
    return lax.dynamic_index_in_dim(value_entries, at, axis, keepdims=False)


def ordered(mine, other, upper):
    return (jnp.where(upper == 0, mine, other), jnp.where(upper == 0, other, mine))


def seq_bits():
    bits, bit = [], lax.axis_size("seq") // 2
    while bit:
        bits.append(("seq", bit))
        bit //= 2
    return bits


def cube_rank():
    return [("head", 2)] + seq_bits()


def beside_each_other(part, moved, held, stage):
    low, high = ordered(part, moved, bit_of(*stage))
    held = sorted(held + [stage], key=cube_rank().index)
    return jnp.stack([low, high], axis=held.index(stage)), held


def grow(part, held, stages):
    for stage in stages:
        part, held = beside_each_other(part, swap(part, *stage), held, stage)
    return part, held


def grown(part, held):
    return part.reshape((2, lax.axis_size("seq")) + part.shape[len(held) :])


def gather_cube(part, stages):
    return grown(*grow(part, [], stages))


def split(part, held, stage):
    if held is None:
        held = cube_rank()
        part = part.reshape((2,) * len(held) + part.shape[2:])
    at = held.index(stage)
    return pick(part, bit_of(*stage), at), to_half(pick(part, 1 - bit_of(*stage), at))


def shrink(part, held, stages, pin=lambda at, moved: moved):
    if held is None:
        held = cube_rank()
        part = part.reshape((2,) * len(held) + part.shape[2:])
    held = list(held)
    for number, (axis, bit) in enumerate(stages):
        at = held.index((axis, bit))
        held.pop(at)
        upper = bit_of(axis, bit)
        moved = pin(number, swap(to_half(pick(part, 1 - upper, at)), axis, bit))
        part = to_float(pick(part, upper, at)) + to_float(moved)
    return [part, held]


def scatter_cube(part, stages, pin=lambda at, moved: moved):
    return shrink(part, None, stages, pin)[0]


def sum_everywhere(value_entries):
    for axis, bit in [("head", 1), ("head", 2)] + seq_bits()[::-1]:
        value_entries = value_entries + swap(value_entries, axis, bit)
    return value_entries


tie = lax.optimization_barrier


def scan_blocks(decay, state, reverse, hook):
    before_decay, before_state = (jnp.ones_like(decay), jnp.zeros_like(state))
    size = state.shape[1]
    for number, (axis, bit) in enumerate(seq_bits()[::-1]):
        upper = bit_of(axis, bit) == (0 if reverse else 1)
        high = to_half(decay)
        low = to_half(decay - to_float(high))
        blank = jnp.zeros_like(state[:, :14], jnp.bfloat16)
        message = jnp.concatenate([to_half(state), high, low, blank], axis=1)
        message = to_float(hook(number, swap(message, axis, bit)))
        other_state = message[:, :size]
        other_decay = message[:, size : size + 1] + message[:, size + 1 : size + 2]
        before_state = jnp.where(upper, before_decay * other_state + before_state, before_state)
        before_decay = jnp.where(upper, before_decay * other_decay, before_decay)
        state = jnp.where(
            upper,
            decay * other_state + state,
            other_decay * state + other_state,
        )
        decay = decay * other_decay
    return before_state


TILE = 256
LANES = 128
VALUES = 256
VMEM_LIMIT = 50 * 1024 * 1024
WHOLE_LIMIT = 60 * 1024 * 1024


def mul(left, right, left_dim=1, right_dim=0):
    return lax.dot_general(
        to_half(left),
        to_half(right),
        (((left_dim,), (right_dim,)), ((), ())),
        preferred_element_type=jnp.float32,
    )


def mul_exact(left, right, left_dim=1, right_dim=0):
    return lax.dot_general(
        left,
        right,
        (((left_dim,), (right_dim,)), ((), ())),
        precision=highest,
        preferred_element_type=jnp.float32,
    )


def halves(value_entries):
    high = to_half(value_entries)
    return high, to_half(value_entries - to_float(high))


def mul_ones(ones, right):
    high, low = halves(right)
    return mul(ones, high) + mul(ones, low)


def span_masks():
    row = lax.broadcasted_iota(jnp.int32, (TILE, TILE), 0)
    column = lax.broadcasted_iota(jnp.int32, (TILE, TILE), 1)
    same = (row // SPAN) == (column // SPAN)
    return same & (row >= column), same & (row <= column), row >= column


def ones_where(mask):
    return jnp.where(mask, 1.0, 0.0).astype(jnp.bfloat16)


def log_sigmoid(z):
    decay = jnp.exp(-jnp.abs(z))
    ratio = decay / (2.0 + decay)
    square = ratio * ratio
    series = 1.0 / 15.0
    for odd in (13.0, 11.0, 9.0, 7.0, 5.0, 3.0, 1.0):
        series = series * square + 1.0 / odd
    return jnp.minimum(z, 0.0) - 2.0 * ratio * series


def call(body, steps, ins, outs, reverse=False, scratch=()):
    def spec(shape, axis, period=steps):
        if axis == "smem":
            return pl.BlockSpec(memory_space=pltpu.SMEM)
        block = tuple(n // period if d == axis else n for d, n in enumerate(shape))

        def where(i):
            at = (steps - 1 - i if reverse else i) % period
            return tuple(at if d == axis else 0 for d in range(len(shape)))

        return pl.BlockSpec(block, where)

    return pl.pallas_call(
        body,
        grid=(steps,),
        in_specs=[spec(entry[0].shape, *entry[1:]) for entry in ins],
        out_specs=[spec(shape, axis) for shape, _, axis in outs],
        out_shape=[jax.ShapeDtypeStruct(shape, dtype) for shape, dtype, _ in outs],
        scratch_shapes=list(scratch),
        compiler_params=pltpu.CompilerParams(vmem_limit_bytes=VMEM_LIMIT),
        cost_estimate=pl.CostEstimate(flops=1, bytes_accessed=0, transcendentals=0),
    )(*[entry[0] for entry in ins])


def heads(width):
    return [slice(h * width, (h + 1) * width) for h in range(2)]


def span_rows(j):
    return slice(j * SPAN, (j + 1) * SPAN)


def ends(within):
    return [within[(j + 1) * SPAN - 1 : (j + 1) * SPAN] for j in range(TILE // SPAN)]


def stacked(parts):
    return jnp.concatenate(parts, axis=0)


def spread(rows):
    return stacked([jnp.broadcast_to(row, (SPAN, row.shape[1])) for row in rows])


def whole_tile(within):
    offset, offsets = jnp.zeros_like(within[:1]), []
    for row in ends(within):
        offsets.append(offset)
        offset = offset + row
    return within + spread(offsets)


def four_blocks(place_ref, mine, moved, beside_mine, beside_moved):
    chip, core = (place_ref[0], place_ref[1])
    own = [jnp.where(chip == b, mine, moved) for b in range(2)]
    beside = [jnp.where(chip == b, beside_mine, beside_moved) for b in range(2)]
    return jnp.concatenate(
        [jnp.where(core == l, own[b], beside[b]) for b in range(2) for l in range(2)], axis=1
    )


def two_halves(place_ref, number, mine, beside):
    return jnp.where(place_ref[1] == number // 2, mine, beside)


def first_step(body):
    pl.when(pl.program_id(0) == 0)(body)


def model_rows(ref, h, first, blocks=1):
    parts = [
        ref[h, :, first + LANES * b : first + LANES * (b + 1), :].reshape(-1, LANES)
        for b in range(blocks)
    ]
    return parts[0] if blocks == 1 else jnp.concatenate(parts, axis=1)


def project_kernel(
    place_ref, tokens_ref, moved_ref, beside_ref, beside_moved_ref, first_ref, expand_ref,
    x_ref, normed_ref, key_out_ref, value_out_ref, rank_ref, within_ref, slope_ref, state_ref, log_ref, gain_ref, small_ref,
):
    @first_step
    def _():
        state_ref[...] = jnp.zeros_like(state_ref)
        log_ref[...] = jnp.zeros_like(log_ref)
        small_ref[32:] = jnp.zeros_like(small_ref[32:])
        for s in range(first_ref.shape[1]):
            small_ref[:32, s * LANES : (s + 1) * LANES] = first_ref[0, s, LANES : LANES + 32]
        gain_ref[...] = to_float(small_ref[16:24])

    chip = place_ref[0]
    x = four_blocks(
        place_ref, tokens_ref[chip], moved_ref[0], beside_ref[chip], beside_moved_ref[0]
    )
    x_ref[...] = x
    x = to_float(x)
    scale = lax.rsqrt(jnp.mean(x * x, axis=1, keepdims=True) + eps_norm)
    normed = to_half(x * scale * gain_ref[0:1])
    normed_ref[...] = normed
    key_weight = jnp.concatenate([model_rows(first_ref, h, 0) for h in range(2)], axis=1)
    keys = to_half(mul(normed, key_weight))
    key_out_ref[...] = keys
    values = [to_half(mul(normed, model_rows(first_ref, h, LANES + 32, 2))) for h in range(2)]
    for h, v in enumerate(heads(VALUES)):
        value_out_ref[:, v] = values[h]
    rank_values = mul(normed, small_ref[...], 1, 1)
    column = lax.broadcasted_iota(jnp.int32, rank_values.shape, 1)
    rank_values = jnp.where(column < 16, rank_values, jnp.where(column == 16, 1.0, 0.0))
    rank_ref[...] = rank_values
    rank_high, rank_low = halves(rank_values)
    expand_high, expand_low = halves(expand_ref[...])
    logits = mul(rank_high, expand_high) + (mul(rank_low, expand_high) + mul(rank_high, expand_low))
    decays = log_sigmoid(logits) * (1.0 / gate_scale)
    slope_ref[...] = 1.0 / (gate_scale * (1.0 + jnp.exp(logits)))
    sums = mul_ones(ones_where(span_masks()[2]), decays)
    log_ref[...] += sums[TILE - 1 :]
    for j in range(TILE // SPAN):
        part = sums[span_rows(j)]
        within_ref[span_rows(j), :] = part - sums[j * SPAN - 1 : j * SPAN] if j else part
    closing = sums[TILE - 1 :]
    rest = to_half(to_float(keys) * jnp.exp(closing - sums))
    decay = jnp.exp(closing)
    for h, k in enumerate(heads(LANES)):
        state_ref[h] = state_ref[h] * decay[:, k] + mul(values[h], rest[:, k], 0, 0)


def project_late_kernel(normed_ref, weight_ref, query_ref, gate_ref):
    normed = normed_ref[...]
    for h, (k, v) in enumerate(zip(heads(LANES), heads(VALUES))):
        query_ref[:, k] = to_half(mul(normed, model_rows(weight_ref, h, 0)))
        gate_ref[:, v] = mul(normed, model_rows(weight_ref, h, LANES, 2))


def load_output(late_ref, output_ref):
    for s in range(late_ref.shape[1]):
        output_ref[:, :, s * LANES : (s + 1) * LANES] = late_ref[:, s]


def forward_kernel(
    query_ref, key_ref, value_ref, gate_ref, within_ref, incoming_ref, group_ref,
    recurrent_ref, start_ref, mixed_ref, state_ref,
):
    @first_step
    def _():
        state_ref[...] = incoming_ref[...]

    causal = span_masks()[0]
    for h, (k, v) in enumerate(zip(heads(LANES), heads(VALUES))):
        within = within_ref[:, k]
        closings = ends(within)
        values = value_ref[:, v]
        keys = to_float(key_ref[:, k])
        queries = to_half(to_float(query_ref[:, k]) * jnp.exp(within))
        scores = jnp.where(causal, mul(queries, keys * jnp.exp(-within), 1, 1), 0.0)
        inside = mul(scores, values)
        keys_out = to_half(keys * jnp.exp(spread(closings) - within))
        state = state_ref[h]
        across = []
        for j, closing in enumerate(closings):
            start = to_half(state)
            start_ref[j, h] = start
            across.append(mul(queries[span_rows(j)], start, 1, 1))
            state = state * jnp.exp(closing) + mul(values[span_rows(j)], keys_out[span_rows(j)], 0, 0)
        state_ref[h] = state
        recurrent = (inside + stacked(across)) * LANES ** (-0.5)
        recurrent_ref[:, v] = recurrent
        scale = lax.rsqrt(jnp.mean(recurrent * recurrent, axis=1, keepdims=True) + eps_norm)
        gate = gate_ref[:, v]
        mixed = to_half(recurrent * scale * group_ref[...] * (gate * jax.nn.sigmoid(gate)))
        mixed_ref[:, v] = mixed


def mix_kernel(mixed_ref, weight_ref, part_ref, output_ref):
    @first_step
    def _():
        load_output(weight_ref, output_ref)

    part_ref[...] = to_half(mul(mixed_ref[...], output_ref[...].reshape(2 * VALUES, -1)))


def residual_kernel(x_ref, mine_ref, other_ref, gain_ref, residual_ref, normed_ref):
    residual = to_float(x_ref[...]) + (to_float(mine_ref[...]) + to_float(other_ref[...]))
    scale = lax.rsqrt(jnp.mean(residual * residual, axis=1, keepdims=True) + eps_norm)
    residual_ref[...] = residual
    normed_ref[...] = to_half(residual * scale * gain_ref[1:2])


def feed_forward_kernel(
    other, place_ref, normed_ref, beside_normed_ref, cot_ref, moved_ref, beside_ref, beside_moved_ref, weight_ref,
    hidden_ref, gate_grad_ref, up_grad_ref, keep_ref, give_ref, rows_grad_ref, cot_out_ref, normed_out_ref, all_ref,
):
    width = weight_ref.shape[2]

    @first_step
    def _():
        all_ref[:, width:] = jnp.zeros_like(all_ref[:, width:])
        for s in range(weight_ref.shape[0]):
            all_ref[:, :width, s * LANES : (s + 1) * LANES] = weight_ref[s]

    normed = normed_ref[...]
    if other:
        normed = two_halves(place_ref, pl.program_id(0), normed, beside_normed_ref[...])
        normed_out_ref[...] = normed
    chip = place_ref[0]
    sequence = 1 - chip if other else chip
    moved, beside_moved = (moved_ref[...], beside_moved_ref[...])
    cot = four_blocks(place_ref, cot_ref[sequence], moved, beside_ref[sequence], beside_moved)
    cot_out_ref[...] = cot
    gate = mul(normed, all_ref[0], 1, 1)
    up = mul(normed, all_ref[1], 1, 1)
    hidden_grad = mul(cot, all_ref[2], 1, 1)
    sigmoid = jax.nn.sigmoid(gate)
    silu = gate * sigmoid
    hidden = to_half(silu * up)
    hidden_ref[...] = hidden.T
    gate_grad = to_half(hidden_grad * up * sigmoid * (1.0 + gate * (1.0 - sigmoid)))
    gate_grad_ref[...] = gate_grad.T
    up_grad = to_half(hidden_grad * silu)
    up_grad_ref[...] = up_grad.T
    rows_grad_ref[...] = to_half(mul(gate_grad, all_ref[0]) + mul(up_grad, all_ref[1]))
    out = to_half(mul(hidden, all_ref[2]))
    columns = keep_ref.shape[2]
    for b in range(2):
        low, high = (out[:, (2 * b + l) * columns : (2 * b + l + 1) * columns] for l in range(2))
        keep_ref[b] = jnp.where(place_ref[1] == 0, low, high)
        give_ref[b] = jnp.where(place_ref[1] == 0, high, low)


def feed_forward_weights_kernel(
    own_ref, other_ref, cot_own_ref, cot_other_ref,
    gate_own_ref, gate_other_ref, up_own_ref, up_other_ref, hidden_own_ref, hidden_other_ref,
    out_ref,
):
    width = out_ref.shape[2]
    for i, (left, left_other, right, right_other) in enumerate(
        [
            (gate_own_ref, gate_other_ref, own_ref, other_ref),
            (up_own_ref, up_other_ref, own_ref, other_ref),
            (hidden_own_ref, hidden_other_ref, cot_own_ref, cot_other_ref),
        ]
    ):
        total = to_half(mul(left[...], right[...]) + mul(left_other[...], right_other[...]))
        for s in range(out_ref.shape[0]):
            out_ref[s, i] = total[:width, s * LANES : (s + 1) * LANES]


def mixer_backward_kernel(
    place_ref, residual_ref, cot_ref, mine_ref, other_ref, home_ref, beside_home_ref, gain_ref,
    late_ref, recurrent_ref, gate_ref, query_ref, within_ref, group_ref,
    keep_own_ref, beside_own_ref, keep_other_ref, beside_other_ref,
    grad_ref, half_ref, gain_grad_ref, recurrent_grad_ref, gate_grad_ref, group_grad_ref, state_grad_ref,
    send_ref, stay_ref, output_ref,
):
    @first_step
    def _():
        load_output(late_ref, output_ref)
        gain_grad_ref[...] = jnp.zeros_like(gain_grad_ref)
        group_grad_ref[...] = jnp.zeros_like(group_grad_ref)
        state_grad_ref[...] = jnp.zeros_like(state_grad_ref)

    residual = residual_ref[...]
    scale = lax.rsqrt(jnp.mean(residual * residual, axis=1, keepdims=True) + eps_norm)
    normed = residual * scale
    number = pl.num_programs(0) - 1 - pl.program_id(0)
    home = two_halves(place_ref, number, home_ref[...], beside_home_ref[...])
    pulled = to_float(mine_ref[...]) + to_float(other_ref[...]) + to_float(home)
    gain_grad_ref[...] += jnp.sum(pulled * normed, axis=0, keepdims=True)
    weighted = pulled * gain_ref[1:2]
    grad = to_float(cot_ref[...]) + scale * (
        weighted - normed * jnp.mean(weighted * normed, axis=1, keepdims=True)
    )
    grad_ref[...] = grad
    grad = to_half(grad)
    half_ref[...] = grad

    chip, core = (place_ref[0], place_ref[1])
    columns = keep_own_ref.shape[2]
    own, other = [], []
    for b in range(2):
        low, high = (residual[:, (2 * b + l) * columns : (2 * b + l + 1) * columns] for l in range(2))
        own.append(to_float(keep_own_ref[b]) + to_float(beside_own_ref[b]) + jnp.where(core == 0, low, high))
        other.append(to_float(keep_other_ref[b]) + to_float(beside_other_ref[b]))
    for at, rows in enumerate((own, other)):
        send_ref[at] = to_half(jnp.where(chip == 0, rows[1], rows[0]))
        stay_ref[at] = jnp.where(chip == 0, rows[0], rows[1])

    for h, (k, v) in enumerate(zip(heads(LANES), heads(VALUES))):
        mixed_grad = mul(grad, output_ref[h], 1, 1)
        recurrent = recurrent_ref[:, v]
        gate = gate_ref[:, v]
        scale = lax.rsqrt(jnp.mean(recurrent * recurrent, axis=1, keepdims=True) + eps_norm)
        sigmoid = jax.nn.sigmoid(gate)
        silu = gate * sigmoid
        normed = recurrent * scale
        group = group_ref[...]
        pulled = mixed_grad * normed
        group_grad_ref[...] += jnp.sum(pulled * silu, axis=0, keepdims=True)
        gate_grad_ref[:, v] = to_half(pulled * group * sigmoid * (1.0 + gate * (1.0 - sigmoid)))
        weighted = mixed_grad * group * silu
        recurrent_grad = scale * (weighted - normed * jnp.mean(weighted * normed, axis=1, keepdims=True))
        recurrent_grad = to_half(recurrent_grad * LANES ** (-0.5))
        recurrent_grad_ref[:, v] = recurrent_grad
        sums = whole_tile(within_ref[:, k])
        queries = to_float(query_ref[:, k]) * jnp.exp(sums)
        state_grad_ref[h] = state_grad_ref[h] * jnp.exp(sums[TILE - 1 :]) + mul(recurrent_grad, queries, 0, 0)


def query_backward_kernel(
    query_ref, key_ref, value_ref, within_ref, recurrent_grad_ref, start_ref, gate_grad_ref, weight_ref,
    query_grad_ref, kept_ref, normed_grad_ref,
):
    causal = span_masks()[0]
    total = None
    for h, (k, v) in enumerate(zip(heads(LANES), heads(VALUES))):
        within = within_ref[:, k]
        pulled = recurrent_grad_ref[:, v]
        keys_in = to_float(key_ref[:, k]) * jnp.exp(-within)
        scores_grad = jnp.where(causal, mul(pulled, value_ref[:, v], 1, 1), 0.0)
        across = stacked([mul(pulled[span_rows(j)], start_ref[j, h]) for j in range(TILE // SPAN)])
        query_grad = (mul(scores_grad, keys_in) + across) * jnp.exp(within)
        query_half = to_half(query_grad)
        query_grad_ref[:, k] = query_half
        kept_ref[:, k] = query_grad * to_float(query_ref[:, k])
        part = mul(query_half, model_rows(weight_ref, h, 0), 1, 1) + mul(
            gate_grad_ref[:, v], model_rows(weight_ref, h, LANES, 2), 1, 1
        )
        total = part if total is None else total + part
    normed_grad_ref[...] = to_half(total)


def backward_kernel(
    query_ref, key_ref, value_ref, within_ref, recurrent_grad_ref, start_ref, slope_ref, rank_ref, kept_ref,
    normed_grad_ref, first_ref, expand_ref, later_ref,
    key_grad_ref, value_grad_ref, rank_grad_ref, expand_grad_ref, part_ref, state_grad_ref,
):
    @first_step
    def _():
        state_grad_ref[...] = later_ref[...]
        expand_grad_ref[...] = jnp.zeros_like(expand_grad_ref)

    causal, until, _ = span_masks()
    last = lax.broadcasted_iota(jnp.int32, (TILE, LANES), 0) % SPAN == SPAN - 1
    total = to_float(normed_grad_ref[...])
    sums_grads = []
    for h, (k, v) in enumerate(zip(heads(LANES), heads(VALUES))):
        within = within_ref[:, k]
        closings = ends(within)
        values = value_ref[:, v]
        pulled = recurrent_grad_ref[:, v]
        keys = to_float(key_ref[:, k])
        shrink = jnp.exp(-within)
        rest = jnp.exp(spread(closings) - within)
        queries = to_half(to_float(query_ref[:, k]) * jnp.exp(within))
        keys_in = keys * shrink
        keys_out = keys * rest
        keys_half = to_half(keys_out)
        scores = jnp.where(causal, mul(queries, keys_in, 1, 1), 0.0)
        scores_grad = jnp.where(causal, mul(pulled, values, 1, 1), 0.0)
        keys_in_grad = mul(scores_grad, queries, 0, 0)
        value_in_grad = mul(scores, pulled, 0, 0)
        later = state_grad_ref[h]
        keys_out_grads, value_out_grads, bounds = [], [], []
        for j in reversed(range(TILE // SPAN)):
            at = span_rows(j)
            later_half = to_half(later)
            decay = jnp.exp(closings[j])
            keys_out_grads.insert(0, mul(values[at], later_half))
            value_out_grads.insert(0, mul(keys_half[at], later_half, 1, 1))
            bounds.insert(0, jnp.sum(later * to_float(start_ref[j, h]), axis=0, keepdims=True) * decay)
            later = later * decay + mul(pulled[at], queries[at], 0, 0)
        state_grad_ref[h] = later
        keys_out_grad = stacked(keys_out_grads)
        value_grad = to_half(value_in_grad + stacked(value_out_grads))
        value_grad_ref[:, v] = value_grad
        key_grad = to_half(keys_in_grad * shrink + keys_out_grad * rest)
        key_grad_ref[:, k] = key_grad
        kept = keys_out_grad * keys_out
        bounds = [
            bound + jnp.sum(kept[span_rows(j)], axis=0, keepdims=True) for j, bound in enumerate(bounds)
        ]
        sums_grads.append(
            kept_ref[:, k] - keys_in_grad * keys_in - kept + jnp.where(last, spread(bounds), 0.0)
        )
        total = total + (
            mul(key_grad, model_rows(first_ref, h, 0), 1, 1)
            + mul(value_grad, model_rows(first_ref, h, LANES + 32, 2), 1, 1)
        )
    part_ref[...] = to_half(total)
    logit_grad = mul_ones(ones_where(until), jnp.concatenate(sums_grads, axis=1)) * slope_ref[...]
    rank_grad_ref[...] = mul(expand_ref[:16], logit_grad, 1, 1)
    expand_grad_ref[...] += mul(rank_ref[...], logit_grad, 0, 0)[:24]


def store_whole(place_ref, refs, packs):
    for h in range(2):
        for s in range(2):
            refs[0][h, s] = packs[h][s]


def store_sides(place_ref, refs, packs):
    keep_first, give_first, keep_second, give_second = refs
    cut = keep_first.shape[1]
    chip, side = (place_ref[0], place_ref[2])
    for s in range(2):
        low, high = (packs[h][s][:cut] for h in range(2))
        keep_first[s] = jnp.where(chip == 0, low, high)
        give_first[s] = jnp.where(chip == 0, high, low)
    for h in range(2):
        low, high = (packs[h][s][cut:] for s in range(2))
        keep_second[h, 0] = jnp.where(side == 0, low, high)
        give_second[h, 0] = jnp.where(side == 0, high, low)


def block_rows(total, s):
    rows = to_half(total[s * LANES : (s + 1) * LANES])
    return [rows[:, b * LANES : (b + 1) * LANES] for b in range(total.shape[1] // LANES)]


def weights_kernel(store, place_ref, rows_ref, first_ref, second_ref, *refs):
    rows = rows_ref[...]
    packs = []
    for k, v in zip(heads(LANES), heads(VALUES)):
        first, second = (mul(rows, first_ref[:, k]), mul(rows, second_ref[:, v]))
        packs.append([stacked(block_rows(first, s) + block_rows(second, s)) for s in range(2)])
    store(place_ref, refs, packs)


def late_weights_kernel(store, place_ref, rows_ref, query_ref, gate_ref, mixed_ref, grad_ref, *refs):
    rows = rows_ref[...]
    packs = []
    for k, v in zip(heads(LANES), heads(VALUES)):
        first, second = (mul(rows, query_ref[:, k]), mul(rows, gate_ref[:, v]))
        output = to_half(mul(mixed_ref[v, :], grad_ref[...]))
        packs.append(
            [
                stacked(block_rows(first, s) + block_rows(second, s) + [output[:, s * LANES : (s + 1) * LANES]])
                for s in range(2)
            ]
        )
    store(place_ref, refs, packs)


def inputs_backward_kernel(
    place_ref, x_ref, grad_ref, mine_ref, other_ref, rank_grad_ref, small_ref, gain_ref, normed_ref,
    out_ref, gain_grad_ref, squeeze_grad_ref,
):
    @first_step
    def _():
        gain_grad_ref[...] = jnp.zeros_like(gain_grad_ref)
        squeeze_grad_ref[...] = jnp.zeros_like(squeeze_grad_ref)

    rank_grad = to_half(rank_grad_ref[...])
    x = to_float(x_ref[...])
    scale = lax.rsqrt(jnp.mean(x * x, axis=1, keepdims=True) + eps_norm)
    normed = x * scale
    pulled = (
        to_float(mine_ref[...])
        + to_float(other_ref[...])
        + mul(rank_grad, small_ref[:16], 0, 0)
    )
    squeeze_grad_ref[...] += mul(rank_grad, normed_ref[...])
    gain_grad_ref[...] += jnp.sum(pulled * normed, axis=0, keepdims=True)
    weighted = pulled * gain_ref[0:1]
    grad = grad_ref[...] + scale * (weighted - normed * jnp.mean(weighted * normed, axis=1, keepdims=True))
    columns = out_ref.shape[2]
    for b in range(2):
        low, high = (grad[:, (2 * b + i) * columns : (2 * b + i + 1) * columns] for i in range(2))
        out_ref[b] = jnp.where(place_ref[1] == 0, low, high)


def adam_kernel(count, joins, *refs):
    grads = refs[: len(refs) - 6 * count - 2]
    refs = refs[len(grads) :]
    share, ins, outs = refs[0], refs[1 : 1 + 3 * count], refs[1 + 3 * count :]
    squares = outs[3 * count]
    squares[...] = jnp.zeros_like(squares)
    for p, (join, shared) in enumerate(joins):
        gradient = to_float(join(*grads))
        master, first, second = (ref[...].reshape(gradient.shape) for ref in ins[3 * p : 3 * p + 3])
        new_first, new_second, direction = adam_direction(master, gradient, first, second)
        for ref, value in zip(outs[3 * p : 3 * p + 3], (new_first, new_second, direction)):
            ref[...] = value.reshape(ref.shape)
        for row, value in ((p, master), (8 + p, direction)):
            total = value * value
            while total.ndim > 2:
                total = jnp.sum(total, axis=0)
            total = jnp.sum(jnp.sum(total, axis=0, keepdims=True), axis=1, keepdims=True)
            if shared:
                total = total * share[0:1, 0:1]
            squares[row : row + 1] = jnp.broadcast_to(total, (1, LANES))


def trust_kernel(rows, squares_ref, *refs):
    count = len(rows)
    for p, row in enumerate(rows):
        master, direction, out = refs[p], refs[count + p], refs[2 * count + p]
        norm = jnp.sqrt(squares_ref[row : row + 1, 0:1])
        ratio = norm / (jnp.sqrt(squares_ref[row + 8 : row + 9, 0:1]) + eps_adam)
        shape = (1,) * len(master.shape)
        out[...] = master[...] - (learn_rate * ratio).reshape(shape) * direction[...]


def whole_call(body, ins, outs):
    return pl.pallas_call(
        body,
        out_shape=[jax.ShapeDtypeStruct(shape, jnp.float32) for shape in outs],
        compiler_params=pltpu.CompilerParams(vmem_limit_bytes=WHOLE_LIMIT),
        cost_estimate=pl.CostEstimate(flops=1, bytes_accessed=0, transcendentals=0),
    )(*ins)


def adam_group(share, grads, joins, params):
    count = len(params)
    outs = []
    for param in params:
        outs += [param[0].shape] * 3
    results = whole_call(
        lambda *refs: adam_kernel(count, joins, *refs),
        list(grads) + [share] + [array for param in params for array in param],
        outs + [(16, LANES)],
    )
    return [tuple(results[3 * p : 3 * p + 3]) for p in range(count)], results[-1]


def adam_direction(master, gradient, first_moment, second_moment):
    fix_one = 1.0 - beta_one**STEP
    second_correction = 1.0 - beta_two**STEP
    new_first = beta_one * first_moment + (1.0 - beta_one) * gradient
    new_second = beta_two * second_moment + (1.0 - beta_two) * gradient * gradient
    update_direction = (
        new_first * (1.0 / fix_one) / (jnp.sqrt(new_second * (1.0 / second_correction)) + eps_adam)
        + decay_rate * master
    )
    return (new_first, new_second, update_direction)


def per_device(
    tokens,
    cotangent,
    query_weight,
    query_mean,
    query_square,
    value_weight,
    value_mean,
    value_square,
    squeeze_weight,
    squeeze_mean,
    squeeze_square,
    expand_weight,
    expand_mean,
    expand_square,
    group_weight,
    group_mean,
    group_square,
    output_weight,
    output_mean,
    output_square,
    ffn_weight,
    ffn_mean,
    ffn_square,
    down_weight,
    down_mean,
    down_square,
    norms_weight,
    norms_mean,
    norms_square,
):
    sequences, segment, column_count = tokens.shape
    head_index = lax.axis_index("head")
    chip, core = (head_index // 2, head_index % 2)
    rows = query_weight.shape[0]
    peers = lax.axis_size("seq")
    seq_index = lax.axis_index("seq")
    model_width = rows * peers
    key_width = query_weight.shape[2] // 2
    value_width = value_weight.shape[2] // 2
    ffn_width = ffn_weight.shape[2]
    ffn_padded = -(-ffn_width // 256) * 256
    rank_count = squeeze_weight.shape[1]
    half_segment = segment // 2
    steps = segment // TILE
    half, full = (jnp.bfloat16, jnp.float32)
    aligned = rows % LANES == 0
    blocks = model_width // LANES
    along = seq_bits()[:-1]
    beside = ("seq", 1)
    across = ("head", 2)

    side = bit_of("seq", 1)
    place = jnp.stack([chip, core, side]).astype(jnp.int32)

    ffn_mine = jnp.concatenate([jnp.moveaxis(ffn_weight, 0, 2), down_weight[None]])
    ffn_mine = to_half(ffn_mine if aligned else jnp.moveaxis(ffn_mine, 2, 1))
    small_mine = jnp.concatenate(
        [
            squeeze_weight.T,
            jnp.zeros((16 - rank_count, rows), jnp.float32),
            norms_weight,
            jnp.zeros((14, rows), jnp.float32),
        ]
    )
    key_mine = query_weight[:, 0, key_width:]
    value_mine = value_weight[:, 0, :value_width]
    late_mine = jnp.concatenate(
        [
            query_weight[:, 0, :key_width],
            value_weight[:, 0, value_width : value_width + LANES],
            value_weight[:, 0, value_width + LANES :],
        ]
    )
    rows_moved = swap(pick(tokens, 1 - chip)[None], *across)
    tokens_beside, cot_beside = (swap(tokens, "head", 1), swap(cotangent, "head", 1))
    moved_beside = swap(rows_moved, "head", 1)
    if aligned:
        lines = [[x + 2 * z for z in range(peers // 2)] for x in range(2)]
        value_mine, ffn_mine = tie((to_half(value_mine), ffn_mine))
        ffn_all = lax.all_gather(ffn_mine, "seq", axis=0)
        key_part, held = grow(to_half(jnp.concatenate([key_mine, small_mine])), [], along)
        value_part, held = grow(jnp.concatenate([value_mine[:, :LANES], value_mine[:, LANES:]]), [], along)
        late_mine = to_half(jnp.concatenate([late_mine, output_weight]))
        late_mine, key_part, value_part = tie((late_mine, key_part, value_part))
        late_part, late_held = grow(late_mine, [], along[:1])
        key_all = grown(*grow(key_part, held, [across, beside]))
        value_part, value_held = grow(value_part, held, [beside])
        late_part, key_all = tie((late_part, key_all))
        late_moved = swap(late_part, *along[1])
        value_all = grown(*grow(value_part, value_held, [across]))
        first_all = jnp.concatenate([key_all, value_all], axis=2)

        def next_links(halves, moved):
            grown_halves = [
                beside_each_other(a, other, held, link) for a, other, link in zip(halves, moved, (across, beside))
            ]
            return jnp.concatenate(
                [
                    grown(*grow(*grown_halves[0], [beside])),
                    grown(*grow(*grown_halves[1], [across])),
                ],
                axis=2,
            )

    else:
        ffn_all = lax.all_gather(ffn_mine, "seq", axis=0)
        ffn_all = ffn_all.reshape(blocks, LANES // rows, 3, rows, ffn_width)
        ffn_all = ffn_all.transpose(0, 2, 4, 1, 3).reshape(blocks, 3, ffn_width, LANES)
        stages = along + [across, beside]

        def gather_columns(part):
            part = gather_cube(to_half(part), stages)
            return jnp.moveaxis(part.reshape(2, blocks, LANES, part.shape[-1]), 3, 2)

        def gather_blocks(part):
            count = part.shape[0] // rows
            part = gather_cube(to_half(part), stages).reshape(2, peers, count, rows, LANES)
            part = jnp.moveaxis(part, 2, 1).reshape(2, count, blocks, LANES, LANES)
            return jnp.moveaxis(part, 1, 2).reshape(2, blocks, count * LANES, LANES)

        value_blocks = jnp.concatenate([value_mine[:, :LANES], value_mine[:, LANES:]])
        first_all = jnp.concatenate(
            [gather_blocks(key_mine), gather_columns(small_mine.T), gather_blocks(value_blocks)], axis=2
        )
        late_all = jnp.concatenate([gather_blocks(late_mine), gather_columns(output_weight.T)], axis=2)

    expand_columns = pick(expand_weight.reshape(rank_count + 1, 2, 2, key_width), core, 2)
    expand_columns = jnp.pad(
        expand_columns.reshape(rank_count + 1, 2 * key_width), ((0, LANES - 1 - rank_count), (0, 0))
    )
    (
        input_half, normed, keys, value_entries, rank_values, within, slope, block_state, log_block, gains, small_full,
    ) = call(
        project_kernel,
        steps,
        [
            (place, "smem"),
            (tokens, 1),
            (rows_moved, 1),
            (tokens_beside, 1),
            (moved_beside, 1),
            (first_all, None),
            (expand_columns, None),
        ],
        [
            ((segment, model_width), half, 0),
            ((segment, model_width), half, 0),
            ((segment, 2 * key_width), half, 0),
            ((segment, 2 * value_width), half, 0),
            ((segment, LANES), full, 0),
            ((segment, 2 * key_width), full, 0),
            ((segment, 2 * key_width), full, 0),
            ((2, value_width, key_width), full, None),
            ((1, 2 * key_width), full, None),
            ((8, model_width), full, None),
            ((LANES, model_width), half, None),
        ],
    )
    if aligned:
        late_moved, block_state, log_block = tie((late_moved, block_state, log_block))
        late_part, _ = beside_each_other(late_part, late_moved, late_held, along[1])
        links = {}
        for name, low, cut, high in (
            ("gate", 0, 10 * LANES // 8, 3 * LANES),
            ("output", 3 * LANES, 3 * LANES + 7 * LANES // 8, 5 * LANES),
        ):
            links[name] = [late_part[..., low:cut, :], late_part[..., cut:high, :]]

        def first_links(halves):
            return [swap(halves[0], *across), swap(halves[1], *beside)]

        def second_links(halves, moved):
            sides = [
                beside_each_other(a, other, held, link) for a, other, link in zip(halves, moved, (across, beside))
            ]
            return sides, [swap(sides[0][0], *beside), swap(sides[1][0], *across)]

        def whole_links(sides, moved):
            ends = [
                grown(*beside_each_other(*(a, other, a_held, link)))
                for (a, a_held), other, link in zip(sides, moved, (beside, across))
            ]
            return jnp.concatenate(ends, axis=2)

        gate_moved = first_links(links["gate"])
    cot_given = [pick(cotangent, 1 - chip), pick(cotangent, chip)]

    def project_late(gate_all):
        return call(
            project_late_kernel,
            steps,
            [(normed, 0), (gate_all, None)],
            [((segment, 2 * key_width), half, 0), ((segment, 2 * value_width), full, 0)],
        )

    beside_scan = {}

    def beside_forward(number, message):
        if not aligned:
            return message
        if number == 1:
            message, moved, cot_given[0] = tie((message, gate_moved, cot_given[0]))
            beside_scan["gate"] = second_links(links["gate"], moved)
            beside_scan["output"] = first_links(links["output"])
            beside_scan["cot"] = swap(cot_given[0], *across)
        if number == 2:
            gate_all = whole_links(*beside_scan["gate"])
            out = project_late(gate_all)
            message, out, output_moved, cot_given[1] = tie(
                (message, out, beside_scan["output"], cot_given[1])
            )
            beside_scan.update(gate=gate_all, out=out)
            beside_scan["output"] = second_links(links["output"], output_moved)
        return message

    block_decay = jnp.exp(log_block).reshape(2, 1, key_width)
    state_in = scan_blocks(block_decay, block_state, False, beside_forward)
    if aligned:
        gate_all = beside_scan["gate"]
        queries, gate_values = beside_scan["out"]
        cot_own_moved = beside_scan["cot"]
    else:
        gate_all, output_all = (late_all[:, :, : 3 * LANES], late_all[:, :, 3 * LANES :])
        queries, gate_values = project_late(gate_all)
        cot_own_moved = swap(cot_given[0], *across)
    cot_other_moved = swap(cot_given[1], *across)
    recurrent, starts, mixed_half = call(
        forward_kernel,
        steps,
        [
            (queries, 0),
            (keys, 0),
            (value_entries, 0),
            (gate_values, 0),
            (within, 0),
            (state_in, None),
            (group_weight[None, :], None),
        ],
        [
            ((segment, 2 * value_width), full, 0),
            ((segment // SPAN, 2, value_width, key_width), half, 0),
            ((segment, 2 * value_width), half, 0),
        ],
        scratch=[pltpu.VMEM((2, value_width, key_width), jnp.float32)],
    )
    if aligned:
        output_sides, output_moved = beside_scan["output"]
        recurrent, mixed_half, output_moved, cot_own_moved = tie(
            (recurrent, mixed_half, output_moved, cot_own_moved)
        )
        output_all = whole_links(output_sides, output_moved)
    (mixer_part,) = call(
        mix_kernel,
        steps,
        [(mixed_half, 0), (output_all, None)],
        [((segment, model_width), half, 0)],
        scratch=[pltpu.VMEM((2, value_width, model_width), jnp.bfloat16)],
    )
    mixer_part, cot_other_moved = tie((mixer_part, cot_other_moved))
    mixer_beside = swap(mixer_part, "head", 1)
    cot_others = (cot_own_moved, cot_other_moved)
    cot_others_beside = [swap(a, "head", 1) for a in cot_others]
    mixer_beside, cot_others_beside = tie((mixer_beside, cot_others_beside))
    residual, normed_two = call(
        residual_kernel,
        steps,
        [(input_half, 0), (mixer_part, 0), (mixer_beside, 0), (gains, None)],
        [((segment, model_width), full, 0), ((segment, model_width), half, 0)],
    )

    moved = swap(lax.dynamic_slice_in_dim(normed_two, core * half_segment, half_segment, 0), *across)

    def feed_forward(other, mine, beside_mine):
        return call(
            lambda *refs: feed_forward_kernel(other, *refs),
            steps,
            [(place, "smem"), mine, beside_mine, (cotangent, 1)]
            + [(cot_others[other], 0), (cot_beside, 1), (cot_others_beside[other], 0)]
            + [(ffn_all, None)],
            [((ffn_padded, segment), half, 1)] * 3
            + [((2, segment, column_count), half, 1)] * 2
            + [((segment, model_width), half, 0)] * 2
            + ([((segment, model_width), half, 0)] if other else [((TILE, model_width), half, None)]),
            scratch=[pltpu.VMEM((3, ffn_padded, model_width), jnp.bfloat16)],
        )

    dummy = (place, "smem")
    own = feed_forward(False, (normed_two, 0), dummy)
    moved, own = tie((moved, own))
    other = feed_forward(True, (moved, 0, 2), (swap(moved, "head", 1), 0, 2))
    cot_own, cot_other, normed_two_other = (own[6], other[6], other[7])
    other_rows = other[5].reshape(2, half_segment, model_width)
    other_sum = to_half(
        to_float(pick(other_rows, core)) + to_float(swap(pick(other_rows, 1 - core), "head", 1))
    )
    home = swap(other_sum, *across)
    (ffn_grad,) = call(
        feed_forward_weights_kernel,
        4,
        [
            (normed_two, 1),
            (normed_two_other, 1),
            (cot_own, 1),
            (cot_other, 1),
            (own[1], None),
            (other[1], None),
            (own[2], None),
            (other[2], None),
            (own[0], None),
            (other[0], None),
        ],
        [((blocks, 3, ffn_width, LANES), half, 0)],
    )
    own_grad = own[5]
    own_beside = swap(own_grad, "head", 1)
    ffn_grad, normed, mixed_half = tie((ffn_grad, normed, mixed_half))
    home, ffn_grad, own_beside, normed_t, mixed_t = tie(
        (home, ffn_grad, own_beside, normed.T, mixed_half.T)
    )
    out_beside = [swap(give, "head", 1) for give in (own[4], other[4])]
    (
        residual_grad, residual_half, gain_two_grad, recurrent_grad, gate_grad, group_grad, state_in_grad,
        out_give, out_mine,
    ) = call(
        mixer_backward_kernel,
        steps,
        [
            (place, "smem"),
            (residual, 0),
            (cot_own, 0),
            (own_grad, 0),
            (own_beside, 0),
            (home, 0, 2),
            (swap(home, "head", 1), 0, 2),
            (gains, None),
            (output_all, None),
            (recurrent, 0),
            (gate_values, 0),
            (queries, 0),
            (within, 0),
            (group_weight[None, :], None),
            (own[3], 1),
            (out_beside[0], 1),
            (other[3], 1),
            (out_beside[1], 1),
        ],
        [
            ((segment, model_width), full, 0),
            ((segment, model_width), half, 0),
            ((1, model_width), full, None),
            ((segment, 2 * value_width), half, 0),
            ((segment, 2 * value_width), half, 0),
            ((1, value_width), full, None),
            ((2, value_width, key_width), full, None),
            ((2, segment, column_count), half, 1),
            ((2, segment, column_count), full, 1),
        ],
        reverse=True,
        scratch=[pltpu.VMEM((2, value_width, model_width), jnp.bfloat16)],
    )
    if not aligned:
        ffn_grad = ffn_grad.reshape(blocks, 3, ffn_width, LANES // rows, rows)
        ffn_grad = ffn_grad.transpose(0, 3, 1, 4, 2).reshape(peers, 3, rows, ffn_width)
    if aligned:
        ffn_pair = lax.psum_scatter(
            ffn_grad.reshape((peers // 2, 2) + ffn_grad.shape[1:]),
            "seq",
            scatter_dimension=0,
            tiled=False,
            axis_index_groups=lines,
        )
    else:
        ffn_sum = lax.psum_scatter(ffn_grad, "seq", scatter_dimension=0, tiled=False)
        ffn_sum = jnp.moveaxis(ffn_sum, 1, 2)

    out_moved = swap(out_give, *across)
    query_grad, kept, normed_grad = call(
        query_backward_kernel,
        steps,
        [
            (queries, 0),
            (keys, 0),
            (value_entries, 0),
            (within, 0),
            (recurrent_grad, 0),
            (starts, 0),
            (gate_grad, 0),
            (gate_all, None),
        ],
        [
            ((segment, 2 * key_width), half, 0),
            ((segment, 2 * key_width), full, 0),
            ((segment, model_width), half, 0),
        ],
    )
    def weights_call(body, count, ins):
        height = count * LANES
        if not aligned:
            outs = [((2, blocks, height, LANES), half, 1)]
        else:
            outs = [((blocks, height // 2, LANES), half, 0)] * 2
            outs += [((2, blocks // 2, height // 2, LANES), half, 1)] * 2
        store = store_sides if aligned else store_whole
        return call(lambda *refs: body(store, *refs), 4, [(place, "smem")] + ins, outs)

    late_grads = weights_call(
        late_weights_kernel,
        5,
        [(normed_t, 0), (query_grad, None), (gate_grad, None), (mixed_t, None), (residual_half, 1)],
    )
    beside_scan = {"first": (query_grad, kept, normed_grad), "second": late_grads}

    def beside_backward(number, message):
        which = {1: "first", 2: "second"}.get(number)
        if which and aligned:
            message, beside_scan[which] = tie((message, beside_scan[which]))
        return message

    later_grad = scan_blocks(block_decay, state_in_grad, True, beside_backward)
    (query_grad, kept, normed_grad), late_grads = (beside_scan["first"], beside_scan["second"])
    late_grads, later_grad, out_moved = tie((late_grads, later_grad, out_moved))
    back = along[::-1]
    if aligned:
        first_held = seq_bits()
        second_held = [across] + along

        def sides(grads):
            keep_first, give_first, keep_second, give_second = grads
            links = (2,) * len(first_held)
            return (
                [keep_first.reshape(links + keep_first.shape[1:]), keep_second.reshape(links + keep_second.shape[2:])],
                [swap(give_first.reshape(links + give_first.shape[1:]), *across),
                 swap(give_second.reshape(links + give_second.shape[2:]), *beside)],
            )

        def next_sides(kept, moved):
            splits = [
                split(to_float(a) + to_float(other), held, link)
                for a, other, held, link in zip(kept, moved, (first_held, second_held), (beside, across))
            ]
            return [a for a, _ in splits], [a for _, a in splits]

        def next_moved(gives):
            return [swap(gives[0], *beside), swap(gives[1], *across)]

        def joined(kept, moved):
            return jnp.concatenate([to_float(a) + to_float(b) for a, b in zip(kept, moved)], axis=-2)

        late_kept, late_moved = sides(late_grads)
    key_grad, value_grad, rank_grad_part, expand_grad, normed_part = call(
        backward_kernel,
        steps,
        [
            (queries, 0),
            (keys, 0),
            (value_entries, 0),
            (within, 0),
            (recurrent_grad, 0),
            (starts, 0),
            (slope, 0),
            (rank_values, 0),
            (kept, 0),
            (normed_grad, 0),
            (first_all, None),
            (expand_columns, None),
            (later_grad, None),
        ],
        [
            ((segment, 2 * key_width), half, 0),
            ((segment, 2 * value_width), half, 0),
            ((rank_count, segment), full, 1),
            ((24, 2 * key_width), full, None),
            ((segment, model_width), half, 0),
        ],
        reverse=True,
        scratch=[pltpu.VMEM((2, value_width, key_width), jnp.float32)],
    )
    if aligned:
        key_grad, value_grad, normed_part, rank_grad_part, late_moved = tie(
            (key_grad, value_grad, normed_part, rank_grad_part, late_moved)
        )
    normed_beside, rank_beside = (swap(normed_part, "head", 1), swap(rank_grad_part, "head", 1))
    state_grads = weights_call(
        weights_kernel, 3, [(normed_t, 0), (key_grad, None), (value_grad, None)]
    )
    normed_beside, rank_beside, state_grads = tie(
        (normed_beside, rank_beside, state_grads)
    )
    if aligned:
        state_kept, state_moved = sides(state_grads)
    rank_grad = rank_grad_part + rank_beside
    grad_cols, gain_one_grad, squeeze_grad = call(
        inputs_backward_kernel,
        steps,
        [
            (place, "smem"),
            (input_half, 0),
            (residual_grad, 0),
            (normed_part, 0),
            (normed_beside, 0),
            (rank_grad, 1),
            (small_full, None),
            (gains, None),
            (normed, 0),
        ],
        [
            ((2, segment, column_count), full, 1),
            ((1, model_width), full, None),
            ((rank_count, model_width), full, None),
        ],
    )
    if aligned:
        state_moved, late_moved, gain_one_grad, squeeze_grad, grad_cols = tie(
            (state_moved, late_moved, gain_one_grad, squeeze_grad, grad_cols)
        )
    expand_pad = jnp.zeros((rank_count + 1, 2, 2, key_width), jnp.float32)
    expand_pad = lax.dynamic_update_index_in_dim(
        expand_pad, expand_grad[: rank_count + 1].reshape(rank_count + 1, 2, key_width), core, 2
    ).reshape(rank_count + 1, 4 * key_width)
    group_rows = jnp.pad(group_grad, ((0, rank_count), (0, model_width - 4 * key_width - value_width)))
    small_grad = jnp.concatenate(
        [
            0.5 * squeeze_grad,
            0.5 * gain_one_grad,
            0.5 * gain_two_grad,
            jnp.concatenate([expand_pad, group_rows], axis=1),
        ]
    )
    if aligned:
        small_grad = small_grad + swap(small_grad, "head", 1)
        state_kept, state_gives = next_sides(state_kept, state_moved)
        state_moved = next_moved(state_gives)
        small_moved = swap(small_grad, *across)
        late_kept, late_gives = next_sides(late_kept, late_moved)
        late_moved = next_moved(late_gives)
        grad_give = to_half(pick(grad_cols, 1 - chip))
        state_moved, small_moved, grad_give, ffn_pair = tie((state_moved, small_moved, grad_give, ffn_pair))
        state_kept, state_give = split(joined(state_kept, state_moved), along, back[0])
        state_moved = swap(state_give, *back[0])
        small_grad = small_grad + small_moved
        small_moved = swap(small_grad, *beside)
        ffn_moved = swap(pick(ffn_pair, 1 - side), *beside)
        state_moved, small_moved, late_moved = tie((state_moved, small_moved, late_moved))
        state_kept, state_give = split(to_float(state_kept) + to_float(state_moved), along[:-1], back[1])
        state_moved = swap(state_give, *back[1])
        small_grad = small_grad + small_moved
        small_moved = swap(small_grad, *back[0])
        late_kept, late_give = split(joined(late_kept, late_moved), along, back[0])
        late_moved = swap(late_give, *back[0])
        state_moved, small_moved, late_moved, ffn_moved = tie((state_moved, small_moved, late_moved, ffn_moved))
        state_sum = to_float(state_kept) + to_float(state_moved)
        small_grad = small_grad + small_moved
        small_grad = small_grad + swap(small_grad, *back[1])
        late_sum = shrink(to_float(late_kept) + to_float(late_moved), along[:-1], back[1:])[0]
        ffn_sum = to_float(pick(ffn_pair, side)) + to_float(ffn_moved)
        output_sum_grad = late_sum[3 * LANES :]
    else:

        def split_rows(a):
            a = a.reshape(2, blocks, 3, LANES // rows, rows, LANES)
            return jnp.moveaxis(a, 3, 2).reshape(2, peers, 3 * rows, LANES)

        late_sum = scatter_cube(split_rows(late_grads[0][:, :, : 3 * LANES]), [beside, across] + back)
        state_sum = scatter_cube(split_rows(state_grads[0]), [across, beside] + back)
        output_grad = late_grads[0][:, :, 3 * LANES :].reshape(2, blocks, value_width, LANES // rows, rows)
        output_grad = output_grad.transpose(0, 1, 3, 4, 2).reshape(2, peers, rows, value_width)
        output_sum_grad = scatter_cube(output_grad, [beside, across] + back).T
        grad_give = to_half(pick(grad_cols, 1 - chip))
        small_grad = sum_everywhere(small_grad)
    grad_home = to_float(swap(grad_give, *across))
    tokens_grad = jnp.stack(ordered(pick(grad_cols, chip), grad_home, chip))
    out_home = to_float(out_moved)
    block_out = to_half(jnp.stack(ordered(out_mine[0] + out_home[1], out_mine[1] + out_home[0], chip)))

    mine_grad = lax.dynamic_slice_in_dim(small_grad[: rank_count + 2], seq_index * rows, rows, 1)
    expand_total = small_grad[rank_count + 2 :, : 4 * key_width]
    group_total = small_grad[rank_count + 2 : rank_count + 3, 4 * key_width : 4 * key_width + value_width]

    share = jnp.broadcast_to((head_index == 0).astype(jnp.float32), (8, LANES))
    by_width = lambda a: jnp.moveaxis(a, 0, 2)
    early, early_squares = adam_group(
        share,
        [ffn_sum],
        [(lambda g: g[:2], False), (lambda g: g[2], False)],
        [
            tuple(map(by_width, (ffn_weight, ffn_mean, ffn_square))),
            (down_weight, down_mean, down_square),
        ],
    )
    early_squares, late_sum = tie((early_squares, late_sum))
    late, late_squares = adam_group(
        share,
        [late_sum, state_sum, output_sum_grad, mine_grad],
        [
            (lambda l, s, o, m: jnp.concatenate([l[:rows], s[:rows]], axis=1), False),
            (
                lambda l, s, o, m: jnp.concatenate(
                    [s[rows : 2 * rows], s[2 * rows : 3 * rows], l[rows : 2 * rows], l[2 * rows : 3 * rows]],
                    axis=1,
                ),
                False,
            ),
            (lambda l, s, o, m: o[...], False),
            (lambda l, s, o, m: m[:rank_count], True),
            (lambda l, s, o, m: m[rank_count:], True),
        ],
        [
            (query_weight, query_mean, query_square),
            (value_weight, value_mean, value_square),
            (output_weight, output_mean, output_square),
            (squeeze_weight.T, squeeze_mean.T, squeeze_square.T),
            (norms_weight, norms_mean, norms_square),
        ],
    )
    copied, copied_squares = adam_group(
        share,
        [expand_total, group_total],
        [(lambda e, g: e[...], False), (lambda e, g: g[...], False)],
        [
            (expand_weight, expand_mean, expand_square),
            tuple(a[None, :] for a in (group_weight, group_mean, group_square)),
        ],
    )
    squares = sum_everywhere(jnp.concatenate([early_squares, late_squares]))
    squares = jnp.concatenate([squares, copied_squares])
    masters = [
        by_width(ffn_weight), down_weight,
        query_weight, value_weight, output_weight, squeeze_weight.T, norms_weight,
        expand_weight, group_weight[None, :],
    ]
    moments = early + late + copied
    news = whole_call(
        lambda *refs: trust_kernel([0, 1, 16, 17, 18, 19, 20, 32, 33], *refs),
        [squares] + masters + [moment[2] for moment in moments],
        [master.shape for master in masters],
    )
    triples = [(new,) + moment[:2] for new, moment in zip(news, moments)]
    ffn_out, down_out, query_out, value_out, output_out, squeeze_out, norms_out, expand_out, group_out = triples
    ffn_out = tuple(jnp.moveaxis(a, 2, 0) for a in ffn_out)
    squeeze_out = tuple(a.T for a in squeeze_out)
    group_out = tuple(a[0] for a in group_out)
    return (block_out, tokens_grad) + tuple(
        array
        for triple in (
            query_out, value_out, squeeze_out, expand_out, group_out, output_out, ffn_out, down_out, norms_out,
        )
        for array in triple
    )


def solution(mesh):
    in_specs = (
        P(None, "seq", "head"),
        P(None, "seq", "head"),
        P("seq", "head", None),
        P("seq", "head", None),
        P("seq", "head", None),
        P("seq", "head", None),
        P("seq", "head", None),
        P("seq", "head", None),
        P("seq", None),
        P("seq", None),
        P("seq", None),
        P(),
        P(),
        P(),
        P(),
        P(),
        P(),
        P("head", "seq"),
        P("head", "seq"),
        P("head", "seq"),
        P("seq", None, "head"),
        P("seq", None, "head"),
        P("seq", None, "head"),
        P("head", "seq"),
        P("head", "seq"),
        P("head", "seq"),
        P(None, "seq"),
        P(None, "seq"),
        P(None, "seq"),
    )
    out_specs = (
        P(None, "seq", "head"),
        P(None, "seq", "head"),
        P("seq", "head", None),
        P("seq", "head", None),
        P("seq", "head", None),
        P("seq", "head", None),
        P("seq", "head", None),
        P("seq", "head", None),
        P("seq", None),
        P("seq", None),
        P("seq", None),
        P(),
        P(),
        P(),
        P(),
        P(),
        P(),
        P("head", "seq"),
        P("head", "seq"),
        P("head", "seq"),
        P("seq", None, "head"),
        P("seq", None, "head"),
        P("seq", None, "head"),
        P("head", "seq"),
        P("head", "seq"),
        P("head", "seq"),
        P(None, "seq"),
        P(None, "seq"),
        P(None, "seq"),
    )
    return jax.shard_map(
        per_device, mesh=mesh, in_specs=in_specs, out_specs=out_specs, check_vma=False
    )
```

time: 454 us -> 425 us (0.936)
  waiting for transfers between devices: 138 us -> 112 us
  other arithmetic: 50 us -> 34.5 us
  starting transfers between devices: 53.9 us -> 66.6 us
    ppermute x59 -> x68, waiting for transfers between devices: 138 us -> 112 us  [swap(): lax.ppermute(value_entries, axis, [(i, i ^ bit) for i in range(peers)])]
    ppermute x59 -> x68, starting transfers between devices: 53.8 us -> 66.5 us  [swap(): lax.ppermute(value_entries, axis, [(i, i ^ bit) for i in range(peers)])]
    add x5 -> x17, other arithmetic: 4.92 us -> 14 us  [the longest x4 4.78 us: joined(): to_float(a) + to_float(b)]
    pallas_call x14, Pallas kernels: 146 us -> 138 us  [call(): pl.pallas_call(body, grid=(steps,), in_specs=[spec(entry[0].shape, *entry...]
    another operation x44 -> x39, other arithmetic: 12.9 us -> 4.72 us  [the longest x33 2.84 us: beside_each_other(): return (jnp.stack([low, high], axis=held.index(stage)), held)]
    select_n x7 -> x3, other arithmetic: 7.92 us -> 0.18 us  [ordered(): jnp.where(upper == 0, mine, other)]
    concatenate x7 -> x10, other arithmetic: 9.49 us -> 2.25 us  [the longest x1 1.36 us: per_device(): first_all = jnp.concatenate([key_all, value_all], axis=2)]
    pallas_call x4, Pallas kernels: 8.24 us -> 14.1 us  [whole_call(): pl.pallas_call(body, out_shape=[jax.ShapeDtypeStruct(shape, jnp.float32)...]
  transfers between devices with their start and end apart: 61 -> 70, of which waited for: 29 -> 31; matrix products, arithmetic and copies ran while one was open for 14% -> 12% of each run, Pallas kernels for 28% -> 31%
where the time goes in v3:
time: 425 us; the launch traced here: 421 us
  Pallas kernels  152 us (36%)
  waiting for transfers between devices  112 us (26%)
  starting transfers between devices  66.6 us (16%)
  local copies, waits for them, and re-layouts  39.5 us (9%)
  other arithmetic  34.5 us (8%)
  between operations  15.9 us (4%)
    pallas_call x14, Pallas kernels, call(): pl.pallas_call(body, grid=(steps,), in_specs=[spec(entry[0].shape, *entry...  138 us
    ppermute x68, waiting for transfers between devices, swap(): lax.ppermute(value_entries, axis, [(i, i ^ bit) for i in range(peers)])  112 us
    ppermute x68, starting transfers between devices, swap(): lax.ppermute(value_entries, axis, [(i, i ^ bit) for i in range(peers)])  66.5 us
    unnamed x133, local copies, waits for them, and re-layouts  19.7 us
    pallas_call x4, Pallas kernels, whole_call(): pl.pallas_call(body, out_shape=[jax.ShapeDtypeStruct(shape, jnp.float32)...  14.1 us
  transfers between devices with their start and end apart: 70, of which 31 were waited for; matrix products, arithmetic and copies ran while one was open for 12% of the time, Pallas kernels for 31%

profile of v3, /device:TPU:0, one launch (start us, length us, event | category | flops | bytes accessed | tf_op | source)
XLA Modules:
  0.0 420.9 jit_solution(14436415008721833837)
XLA Ops:
  11.5 4.0 collective-permute-start.3
  17.7 1.8 collective-permute-start
  20.7 1.6 collective-permute-start.4
  25.8 2.4 collective-permute-done.6
  28.2 1.6 collective-permute-start.8
  31.3 1.7 collective-permute-start.7
  36.7 1.8 collective-permute-start.9
  38.5 4.5 %collective-permute-done.10 = bf16[2,2,256,128]{3,2,0,1:T(8,128)(2,1)S(1)} collective-permute-done((bf16[2,2,256,128]{3,2,0,1:T(8,128)(2,1)S(1)}, bf16[2,2,256,128]{3,2,0,1:T(8,128)(2,1)S(1)}, u32[]{:S(2)}, u32[]{:S(2)}) %collective-permute-start.10) | collective-permute-done | bytes 262176 | tf_op jit(solution)/shard_map/ppermute | solution.py:40
  44.5 6.8 %collective-permute-done.7 = bf16[640,128]{1,0:T(8,128)(2,1)S(1)} collective-permute-done((bf16[640,128]{1,0:T(8,128)(2,1)S(1)}, bf16[640,128]{1,0:T(8,128)(2,1)S(1)}, u32[]{:S(2)}, u32[]{:S(2)}) %collective-permute-start.7) | collective-permute-done | bytes 163872 | tf_op jit(solution)/shard_map/ppermute | solution.py:40
  51.8 3.9 collective-permute-done.11
  57.2 10.1 %shard_map.500 = (bf16[1024,1024]{1,0:T(8,128)(2,1)}, bf16[1024,1024]{1,0:T(8,128)(2,1)}, bf16[1024,256]{1,0:T(8,128)(2,1)S(1)}, bf16[1024,512]{1,0:T(8,128)(2,1...) custom-call(s32[3]{0:T(128)S(1)} %pad_add_fusion.place_ref.refs_0_.r, ...), custom_call_target="tpu_custom_call" | custom-call | flops 1 | tf_op jit(solution)/shard_map/pallas_call | solution.py:214
  67.7 1.8 collective-permute-start.15
  69.6 1.8 collective-permute-start.16
  71.4 5.7 %collective-permute-done.13 = bf16[2,272,128]{2,1,0:T(8,128)(2,1)S(1)} collective-permute-done((bf16[2,272,128]{2,1,0:T(8,128)(2,1)S(1)}, bf16[2,272,128]{2,1,0:T(8,128)(2,1)S(1)}, u32[]{:S(2)}, u32[]{:S(2)}) %collective-permute-start.13) | collective-permute-done | bytes 139296 | tf_op jit(solution)/shard_map/ppermute | solution.py:40
  78.8 1.6 collective-permute-start.20
  80.8 6.1 %collective-permute-done.16 = bf16[2,2,224,128]{3,2,0,1:T(8,128)(2,1)S(1)} collective-permute-done((bf16[2,2,224,128]{3,2,0,1:T(8,128)(2,1)S(1)}, bf16[2,2,224,128]{3,2,0,1:T(8,128)(2,1)S(1)}, u32[]{:S(2)}, u32[]{:S(2)}) %collective-permute-start.16) | collective-permute-done | bytes 229408 | tf_op jit(solution)/shard_map/ppermute | solution.py:40
  87.0 1.6 collective-permute-start.19
  90.3 1.7 collective-permute-start.17
  92.0 14.2 %collective-permute-done.18 = bf16[2,2,2,160,128]{4,3,1,2,0:T(8,128)(2,1)S(1)} collective-permute-done((bf16[2,2,2,160,128]{4,3,1,2,0:T(8,128)(2,1)S(1)}, bf16[2,2,2,160,128]{4,3,1,2,0:T(8,128)(2,1)S(1)}, u32[]{:S(2)}, u32[]{:S(2)}) %collective-permute-start.18) | collective-permute-done | bytes 327712 | tf_op jit(solution)/shard_map/ppermute | solution.py:40
  106.2 1.6 collective-permute-start.24
  108.3 5.6 %shard_map.501 = (bf16[1024,256]{1,0:T(8,128)(2,1)S(1)}, f32[1024,512]{1,0:T(8,128)}) custom-call(bf16[1024,1024]{1,0:T(8,128)(2,1)} %get-tuple-element.286.normed_ref, bf16[2,8,384,128]{3,2,1,0:T(8,128)(2,1)S(1)} %maximum_maximum_fusion.1.weight_ref), custom_call_target="tpu_custom_call" | custom-call | flops 1 | tf_op jit(solution)/shard_map/pallas_call | solution.py:214
  116.7 5.9 %shard_map.502 = (f32[1024,512]{1,0:T(8,128)}, bf16[16,2,256,128]{3,2,1,0:T(8,128)(2,1)}, bf16[1024,512]{1,0:T(8,128)(2,1)S(1)}) custom-call(bf16[1024,256]{1,0:T(8,128)(2,1)S(1)} %get-tuple-element.241.query_ref, bf16[1024,256]{1,0:T(8,128)(2,1)S(1)} %get-tuple-element.242.key_ref, bf16[1024,512]{1,0:T(8,128)(2,1)S(1)} %get-tuple-element.243.value_ref, ...), custom_call_target="tpu_custom_call" | custom-call | flops 1 | tf_op jit(solution)/shard_map/pallas_call | solution.py:214
  122.6 4.8 %collective-permute-done.23 = bf16[2,2,2,144,128]{4,3,0,1,2:T(8,128)(2,1)S(1)} collective-permute-done((bf16[2,2,2,144,128]{4,3,0,1,2:T(8,128)(2,1)S(1)}, bf16[2,2,2,144,128]{4,3,0,1,2:T(8,128)(2,1)S(1)}, u32[]{:S(2)}, u32[]{:S(2)}) %collective-permute-start.23) | collective-permute-done | bytes 294944 | tf_op jit(solution)/shard_map/ppermute | solution.py:40
  127.8 3.3 shard_map.503.mine_ref
  131.0 5.0 %collective-permute-done.25.refs_4_ = bf16[1024,256]{1,0:T(8,128)(2,1)S(1)} collective-permute-done((bf16[1024,256]{1,0:T(8,128)(2,1)S(1)}, bf16[1024,256]{1,0:T(8,128)(2,1)S(1)}, u32[]{:S(2)}, u32[]{:S(2)}) %collective-permute-start.25) | collective-permute-done | bytes 524320 | tf_op jit(solution)/shard_map/ppermute | solution.py:40
  137.9 4.4 %collective-permute-done.27.refs_6_ = bf16[1024,256]{1,0:T(8,128)(2,1)S(1)} collective-permute-done((bf16[1024,256]{1,0:T(8,128)(2,1)}, bf16[1024,256]{1,0:T(8,128)(2,1)S(1)}, u32[]{:S(2)}, u32[]{:S(2)}) %collective-permute-start.27) | collective-permute-done | bytes 524320 | tf_op jit(solution)/shard_map/ppermute | solution.py:40
  143.9 5.5 %shard_map.504 = (f32[1024,1024]{1,0:T(8,128)}, bf16[1024,1024]{1,0:T(8,128)(2,1)S(1)}) custom-call(bf16[1024,1024]{1,0:T(8,128)(2,1)} %get-tuple-element.228.x_ref, bf16[1024,1024]{1,0:T(8,128)(2,1)} %shard_map.503.mine_ref, bf16[1024,1024]{1,0:T(8,128)(2,1)} %collective-permute-done.26.other_ref, f32[8,1024]{1,0:T(8,128)S(1)} %get-tuple-element.260.gain_ref), custom_call_target="tpu_custom_call" | custom-call | flops 1 | tf_op jit(solution)/shard_map/pallas_call | solution.py:214
  152.1 17.9 %shard_map.505 = (bf16[768,1024]{1,0:T(8,128)(2,1)}, bf16[768,1024]{1,0:T(8,128)(2,1)}, bf16[768,1024]{1,0:T(8,128)(2,1)}, bf16[2,1024,256]{2,1,0:T(8,128)(2,1)S...) custom-call(s32[3]{0:T(128)S(1)} %pad_add_fusion.place_ref.refs_0_.r, ...), custom_call_target="tpu_custom_call" | custom-call | flops 1 | tf_op jit(solution)/shard_map/pallas_call | solution.py:214
  172.0 4.4 %collective-permute-done.29.refs_1_ = bf16[512,1024]{1,0:T(8,128)(2,1)} collective-permute-done((bf16[512,1024]{1,0:T(8,128)(2,1)}, bf16[512,1024]{1,0:T(8,128)(2,1)}, u32[]{:S(2)}, u32[]{:S(2)}) %collective-permute-start.29) | collective-permute-done | bytes 1048608 | tf_op jit(solution)/shard_map/ppermute | solution.py:40
  176.3 2.9 collective-permute-done.31.refs_2_
  182.3 18.6 %shard_map.506 = (bf16[768,1024]{1,0:T(8,128)(2,1)}, bf16[768,1024]{1,0:T(8,128)(2,1)}, bf16[768,1024]{1,0:T(8,128)(2,1)}, bf16[2,1024,256]{2,1,0:T(8,128)(2,1)S...) custom-call(s32[3]{0:T(128)S(1)} %pad_add_fusion.place_ref.refs_0_.r, ...), custom_call_target="tpu_custom_call" | custom-call | flops 1 | tf_op jit(solution)/shard_map/pallas_call | solution.py:214
  204.8 2.1 collective-permute-done.32
  207.0 2.6 fusion
  210.3 15.2 %shard_map.507 = bf16[8,3,704,128]{3,2,1,0:T(8,128)(2,1)} custom-call(bf16[1024,1024]{1,0:T(8,128)(2,1)} %copy-done.1, bf16[1024,1024]{1,0:T(8,128)(2,1)} %get-tuple-element.277.other_ref, bf16[1024,1024]{1,0:T(8,128)(2,1)} %get-tuple-element.272.cot_own_ref.cot_ref, bf16[1024,1024]{1,0:T(8,128)(2,1)} %get-tuple-element.278.cot_other_ref, ...), custom_call_target="tpu_custom_call" | custom-call | flops 1 | tf_op jit(solution)/shard_map/pallas_call | solution.py:214
  225.5 4.0 copy.106
  231.4 3.7 collective-permute-done.33.home_ref
  235.2 3.0 collective-permute-done.35.beside_home_ref
  238.1 15.7 %shard_map.508 = (f32[1024,1024]{1,0:T(8,128)}, bf16[1024,1024]{1,0:T(8,128)(2,1)}, f32[1,1024]{1,0:T(1,128)S(1)}, bf16[1024,512]{1,0:T(8,128)(2,1)S(1)}, bf16[1...) custom-call(s32[3]{0:T(128)S(1)} %pad_add_fusion.place_ref.refs_0_.r, ...), custom_call_target="tpu_custom_call" | custom-call | flops 1 | tf_op jit(solution)/shard_map/pallas_call | solution.py:214
  255.0 5.6 %collective-permute-done.38 = bf16[2,272,128]{2,1,0:T(8,128)(2,1)S(1)} collective-permute-done((bf16[2,272,128]{2,1,0:T(8,128)(2,1)S(1)}, bf16[2,272,128]{2,1,0:T(8,128)(2,1)S(1)}, u32[]{:S(2)}, u32[]{:S(2)}) %collective-permute-start.38) | collective-permute-done | bytes 139296 | tf_op jit(solution)/shard_map/ppermute | solution.py:40
  261.6 7.6 %shard_map.509 = (bf16[1024,256]{1,0:T(8,128)(2,1)S(1)}, f32[1024,256]{1,0:T(8,128)S(1)}, bf16[1024,1024]{1,0:T(8,128)(2,1)}) custom-call(bf16[1024,256]{1,0:T(8,128)(2,1)S(1)} %copy-done.5, bf16[1024,256]{1,0:T(8,128)(2,1)S(1)} %copy-done.7, bf16[1024,512]{1,0:T(8,128)(2,1)S(1)} %get-tuple-element.243.value_ref, f32[1024,256]{1,0:T(8,128)} %get-tuple-element.245.within_ref, ...), custom_call_target="tpu_custom_call" | custom-call | flops 1 | tf_op jit(solution)/shard_map/pallas_call | solution.py:214
  269.2 4.7 %collective-permute-done.39 = bf16[2,272,128]{2,1,0:T(8,128)(2,1)S(1)} collective-permute-done((bf16[2,272,128]{2,1,0:T(8,128)(2,1)S(1)}, bf16[2,272,128]{2,1,0:T(8,128)(2,1)S(1)}, u32[]{:S(2)}, u32[]{:S(2)}) %collective-permute-start.39) | collective-permute-done | bytes 139296 | tf_op jit(solution)/shard_map/ppermute | solution.py:40
  274.2 6.4 %shard_map.510 = (bf16[8,320,128]{2,1,0:T(8,128)(2,1)S(1)}, bf16[8,320,128]{2,1,0:T(8,128)(2,1)S(1)}, bf16[2,4,320,128]{3,2,1,0:T(8,128)(2,1)S(1)}, bf16[2,4,320,128]{3,2,1,0:T(8,128)(2,1)S(1)}) custom-call(s32[3]{0:T(128)S(1)} %pad_add_fusion.place_ref.refs_0_.refs_2_, bf16[1024,1024]{1,0:T(8,128)(2,1)} %bitcast.224, ...), custom_call_target="tpu_custom_call" | custom-call | flops 1 | tf_op jit(solution)/shard_map/pallas_call | solution.py:214
  280.7 10.2 %collective-permute-done.40 = bf16[2,272,128]{2,1,0:T(8,128)(2,1)S(1)} collective-permute-done((bf16[2,272,128]{2,1,0:T(8,128)(2,1)S(1)}, bf16[2,272,128]{2,1,0:T(8,128)(2,1)S(1)}, u32[]{:S(2)}, u32[]{:S(2)}) %collective-permute-start.40) | collective-permute-done | bytes 139296 | tf_op jit(solution)/shard_map/ppermute | solution.py:40
  292.3 15.2 %shard_map.511 = (bf16[1024,256]{1,0:T(8,128)(2,1)S(1)}, bf16[1024,512]{1,0:T(8,128)(2,1)S(1)}, f32[16,1024]{1,0:T(8,128)S(1)}, f32[24,256]{1,0:T(8,128)S(1)}, bf16[1024,1024]{1,0:T(8,128)(2,1)}) custom-call(bf16[1024,256]{1,0:T(8,128)(2,1)S(1)} %copy-done.5, bf16[1024,256]{1,0:T(8,128)(2,1)S(1)} %copy-done.7, bf16[1024,512]{1,0:T(8,128)(2,1)} %copy-done.2, ...), custom_call_target="tpu_custom_call" | custom-call | flops 1 | tf_op jit(solution)/shard_map/pallas_call | solution.py:214
  308.9 4.4 %shard_map.512 = (bf16[8,192,128]{2,1,0:T(8,128)(2,1)S(1)}, bf16[8,192,128]{2,1,0:T(8,128)(2,1)S(1)}, bf16[2,4,192,128]{3,2,1,0:T(8,128)(2,1)S(1)}, bf16[2,4,192,128]{3,2,1,0:T(8,128)(2,1)S(1)}) custom-call(s32[3]{0:T(128)S(1)} %pad_add_fusion.place_ref.refs_0_.refs_2_, bf16[1024,1024]{1,0:T(8,128)(2,1)} %bitcast.225, ...), custom_call_target="tpu_custom_call" | custom-call | flops 1 | tf_op jit(solution)/shard_map/pallas_call | solution.py:214
  316.3 1.6 collective-permute-start.47
  320.4 6.4 %shard_map.513 = (f32[2,1024,256]{2,1,0:T(8,128)S(1)}, f32[1,1024]{1,0:T(1,128)S(1)}, f32[16,1024]{1,0:T(8,128)S(1)}) custom-call(s32[3]{0:T(128)S(1)} %pad_add_fusion.place_ref.refs_0_.refs_2_, bf16[1024,1024]{1,0:T(8,128)(2,1)} %get-tuple-element.228.x_ref, f32[1024,1024]{1,0:T(8,128)} %get-tuple-element.341.grad_ref, ...), custom_call_target="tpu_custom_call" | custom-call | flops 1 | tf_op jit(solution)/shard_map/pallas_call | solution.py:214
  328.8 1.7 collective-permute-start.48
  337.8 3.4 collective-permute-done.51
  346.7 1.9 dynamic-slice_bitcast_fusion.1
  349.2 2.5 collective-permute-done.54
  358.6 3.5 collective-permute-start.57
  362.1 2.1 collective-permute-start.52
  364.2 1.9 collective-permute-done.57
  368.2 2.5 collective-permute-start.62
  370.7 2.3 convert_add_fusion.1.refs_0_
  377.7 4.8 %shard_map.514 = (f32[2,704,128]{2,1,0:T(8,128)}, f32[2,704,128]{2,1,0:T(8,128)}, f32[2,704,128]{2,1,0:T(8,128)}, f32[704,128]{1,0:T(8,128)}, f32[704,128]{1,0:T...) custom-call(f32[3,704,128]{2,1,0:T(8,128)} %convert_add_fusion.1.refs_0_, ...), custom_call_target="tpu_custom_call" | custom-call | flops 1 | tf_op jit(solution)/shard_map/pallas_call | solution.py:705
  384.8 4.0 shard_map.515
  392.7 2.2 collective-permute-done.64
  396.7 1.9 collective-permute-done.65
  398.6 2.0 collective-permute-start.66
  402.4 2.3 collective-permute-start.67
  407.3 1.7 shard_map.516
  410.3 3.6 shard_map.517
  (390 shorter events, 97.8 us)
Async XLA Ops:
  7.2 143.8 %all-gather.3.cloned.1.call-start = ((), (), s32[]{:S(2)}) async-start(), calls=%async_computation.2 | async-start | bytes 4866048 | tf_op jit(solution)/shard_map/all_gather | solution.py:818
  11.5 8.3 %collective-permute-start.3 = (bf16[160,128]{1,0:T(8,128)(2,1)}, bf16[160,128]{1,0:T(8,128)(2,1)}, u32[]{:S(2)}, u32[]{:S(2)}) collective-permute-start(bf16[160,128]{1,0:T(8,128)(2,1)} %maximum_maximum_fusion.7), channel_id=1, source_target_pairs={{0,16},{4,20},{8,24},{12,28},{16,0},{20,4},{24,8},{28,12},{1,17},{... | collective-permute-start | bytes 122888 | tf_op jit(solution)/shard_map/ppermute | solution.py:40
  17.5 5.5 %collective-permute-start.5 = (bf16[256,128]{1,0:T(8,128)(2,1)S(1)}, bf16[256,128]{1,0:T(8,128)(2,1)S(1)}, u32[]{:S(2)}, u32[]{:S(2)}) collective-permute-start(bf16[256,128]{1,0:T(8,128)(2,1)S(1)} %pad_maximum_fusion.23), channel_id=1, source_target_pairs={{0,16},{4,20},{8,24},{12,28},{16,0},{20,4},{24,8},{28,12},{1,17},{... | collective-permute-start | bytes 196616 | tf_op jit(solution)/shard_map/ppermute | solution.py:40
  17.6 39.6 %collective-permute-start.1 = (bf16[2,1024,256]{2,1,0:T(8,128)(2,1)S(1)}, bf16[2,1024,256]{2,1,0:T(8,128)(2,1)}, u32[]{:S(2)}, u32[]{:S(2)}) collective-permute-start(bf16[2,1024,256]{2,1,0:T(8,128)(2,1)S(1)} %copy-done.45), channel_id=1, source_target_pairs={{0,1},{1,0},{2,3},{3,2},{4,5},{5,4},{6,7},{7,6},{8,9},{9,8},{10,11... | collective-permute-start | bytes 3145736 | tf_op jit(solution)/shard_map/ppermute | solution.py:40
  17.7 33.7 %collective-permute-start = (bf16[1,1024,256]{2,1,0:T(8,128)(2,1)S(1)}, bf16[1,1024,256]{2,1,0:T(8,128)(2,1)S(1)}, u32[]{:S(2)}, u32[]{:S(2)}) collective-permute-start(bf16[1,1024,256]{2,1,0:T(8,128)(2,1)S(1)} %constant_dynamic-slice_fusion.3), channel_id=1, source_target_pairs={{0,2},{1,3},{2,0},{3,1},{4,6},{5,7},{6,4},{7,5},{8,10},{9,11},{10,... | collective-permute-start | bytes 1572872 | tf_op jit(solution)/shard_map/ppermute | solution.py:40
  19.5 321.7 %reduce-scatter.2.cloned.1.call-start = ((), (), s32[]{:S(2)}) async-start(), calls=%async_computation.1 | async-start | bytes 5406720 | tf_op jit(solution)/shard_map/reduce_scatter | solution.py:1103
  20.7 5.0 %collective-permute-start.4 = (bf16[2,160,128]{2,1,0:T(8,128)(2,1)S(1)}, bf16[2,160,128]{2,1,0:T(8,128)(2,1)S(1)}, u32[]{:S(2)}, u32[]{:S(2)}) collective-permute-start(bf16[2,160,128]{2,1,0:T(8,128)(2,1)S(1)} %pad_maximum_fusion.22), channel_id=1, source_target_pairs={{0,8},{4,12},{8,0},{12,4},{16,24},{20,28},{24,16},{28,20},{1,9},{5... | collective-permute-start | bytes 245768 | tf_op jit(solution)/shard_map/ppermute | solution.py:40
  23.1 5.1 %collective-permute-start.6 = (bf16[2,256,128]{2,1,0:T(8,128)(2,1)S(1)}, bf16[2,256,128]{2,1,0:T(8,128)(2,1)S(1)}, u32[]{:S(2)}, u32[]{:S(2)}) collective-permute-start(bf16[2,256,128]{2,1,0:T(8,128)(2,1)S(1)} %pad_maximum_fusion.21), channel_id=1, source_target_pairs={{0,8},{4,12},{8,0},{12,4},{16,24},{20,28},{24,16},{28,20},{1,9},{5... | collective-permute-start | bytes 393224 | tf_op jit(solution)/shard_map/ppermute | solution.py:40
  28.2 7.5 %collective-permute-start.8 = (bf16[2,2,160,128]{3,2,0,1:T(8,128)(2,1)S(1)}, bf16[2,2,160,128]{3,2,0,1:T(8,128)(2,1)}, u32[]{:S(2)}, u32[]{:S(2)}) collective-permute-start(bf16[2,2,160,128]{3,2,0,1:T(8,128)(2,1)S(1)} %pad_maximum_fusion.19), channel_id=1, source_target_pairs={{0,2},{1,3},{2,0},{3,1},{4,6},{5,7},{6,4},{7,5},{8,10},{9,11},{10,... | collective-permute-start | bytes 491528 | tf_op jit(solution)/shard_map/ppermute | solution.py:40
  31.3 20.0 %collective-permute-start.7 = (bf16[640,128]{1,0:T(8,128)(2,1)S(1)}, bf16[640,128]{1,0:T(8,128)(2,1)S(1)}, u32[]{:S(2)}, u32[]{:S(2)}) collective-permute-start(bf16[640,128]{1,0:T(8,128)(2,1)S(1)} %pad_maximum_fusion.18), channel_id=1, source_target_pairs={{0,16},{4,20},{8,24},{12,28},{16,0},{20,4},{24,8},{28,12},{1,17},{... | collective-permute-start | bytes 491528 | tf_op jit(solution)/shard_map/ppermute | solution.py:40
  33.0 10.0 %collective-permute-start.10 = (bf16[2,2,256,128]{3,2,0,1:T(8,128)(2,1)S(1)}, bf16[2,2,256,128]{3,2,0,1:T(8,128)(2,1)S(1)}, u32[]{:S(2)}, u32[]{:S(2)}) collective-permute-start(bf16[2,2,256,128]{3,2,0,1:T(8,128)(2,1)S(1)} %pad_maximum_fusion.12), channel_id=1, source_target_pairs={{0,4},{4,0},{8,12},{12,8},{16,20},{20,16},{24,28},{28,24},{1,5},{5... | collective-permute-start | bytes 786440 | tf_op jit(solution)/shard_map/ppermute | solution.py:40
  36.7 14.8 %collective-permute-start.9 = (bf16[2,2,2,160,128]{4,3,1,2,0:T(8,128)(2,1)S(1)}, bf16[2,2,2,160,128]{4,3,1,2,0:T(8,128)(2,1)S(1)}, u32[]{:S(2)}, u32[]{:S(2)}) collective-permute-start(bf16[2,2,2,160,128]{4,3,1,2,0:T(8,128)(2,1)S(1)} %pad_maximum_fusion.9), channel_id=1, source_target_pairs={{0,4},{4,0},{8,12},{12,8},{16,20},{20,16},{24,28},{28,24},{1,5},{5... | collective-permute-start | bytes 983048 | tf_op jit(solution)/shard_map/ppermute | solution.py:40
  43.0 12.6 %collective-permute-start.11 = (bf16[2,2,2,256,128]{4,3,0,1,2:T(8,128)(2,1)S(1)}, bf16[2,2,2,256,128]{4,3,0,1,2:T(8,128)(2,1)S(1)}, u32[]{:S(2)}, u32[]{:S(2)}) collective-permute-start(bf16[2,2,2,256,128]{4,3,0,1,2:T(8,128)(2,1)S(1)} %pad_maximum_fusion.5), channel_id=1, source_target_pairs={{0,2},{1,3},{2,0},{3,1},{4,6},{5,7},{6,4},{7,5},{8,10},{9,11},{10,... | collective-permute-start | bytes 1572872 | tf_op jit(solution)/shard_map/ppermute | solution.py:40
  51.4 5.8 %collective-permute-start.2 = (bf16[1,1024,256]{2,1,0:T(8,128)(2,1)S(1)}, bf16[1,1024,256]{2,1,0:T(8,128)(2,1)S(1)}, u32[]{:S(2)}, u32[]{:S(2)}) collective-permute-start(bf16[1,1024,256]{2,1,0:T(8,128)(2,1)S(1)} %collective-permute-done.moved_ref), channel_id=1, source_target_pairs={{0,1},{1,0},{2,3},{3,2},{4,5},{5,4},{6,7},{7,6},{8,9},{9,8},{10,11... | collective-permute-start | bytes 1572872 | tf_op jit(solution)/shard_map/ppermute | solution.py:40
  51.7 15.7 %collective-permute-start.12 = (bf16[2,640,128]{2,1,0:T(8,128)(2,1)S(1)}, bf16[2,640,128]{2,1,0:T(8,128)(2,1)S(1)}, u32[]{:S(2)}, u32[]{:S(2)}) collective-permute-start(bf16[2,640,128]{2,1,0:T(8,128)(2,1)S(1)} %pad_maximum_fusion.8), channel_id=1, source_target_pairs={{0,8},{4,12},{8,0},{12,4},{16,24},{20,28},{24,16},{28,20},{1,9},{5... | collective-permute-start | bytes 983048 | tf_op jit(solution)/shard_map/ppermute | solution.py:40
  67.5 9.6 %collective-permute-start.13 = (bf16[2,272,128]{2,1,0:T(8,128)(2,1)S(1)}, bf16[2,272,128]{2,1,0:T(8,128)(2,1)S(1)}, u32[]{:S(2)}, u32[]{:S(2)}) collective-permute-start(bf16[2,272,128]{2,1,0:T(8,128)(2,1)S(1)} %fusion.25), channel_id=1, source_target_pairs={{0,4},{4,0},{8,12},{12,8},{16,20},{20,16},{24,28},{28,24},{1,5},{5... | collective-permute-start | bytes 417800 | tf_op jit(solution)/shard_map/ppermute | solution.py:40
  67.7 13.0 %collective-permute-start.15 = (bf16[2,2,160,128]{3,2,0,1:T(8,128)(2,1)S(1)}, bf16[2,2,160,128]{3,2,0,1:T(8,128)(2,1)S(1)}, u32[]{:S(2)}, u32[]{:S(2)}) collective-permute-start(bf16[2,2,160,128]{3,2,0,1:T(8,128)(2,1)S(1)} %fusion.22), channel_id=1, source_target_pairs={{0,2},{1,3},{2,0},{3,1},{4,6},{5,7},{6,4},{7,5},{8,10},{9,11},{10,... | collective-permute-start | bytes 491528 | tf_op jit(solution)/shard_map/ppermute | solution.py:40
  69.6 17.3 %collective-permute-start.16 = (bf16[2,2,224,128]{3,2,0,1:T(8,128)(2,1)S(1)}, bf16[2,2,224,128]{3,2,0,1:T(8,128)(2,1)S(1)}, u32[]{:S(2)}, u32[]{:S(2)}) collective-permute-start(bf16[2,2,224,128]{3,2,0,1:T(8,128)(2,1)S(1)} %fusion.17), channel_id=1, source_target_pairs={{0,4},{4,0},{8,12},{12,8},{16,20},{20,16},{24,28},{28,24},{1,5},{5... | collective-permute-start | bytes 688136 | tf_op jit(solution)/shard_map/ppermute | solution.py:40
  77.3 9.6 %collective-permute-start.14 = (bf16[2,272,128]{2,1,0:T(8,128)(2,1)S(1)}, bf16[2,272,128]{2,1,0:T(8,128)(2,1)S(1)}, u32[]{:S(2)}, u32[]{:S(2)}) collective-permute-start(bf16[2,272,128]{2,1,0:T(8,128)(2,1)S(1)} %maximum_maximum_fusion.3), channel_id=1, source_target_pairs={{0,8},{4,12},{8,0},{12,4},{16,24},{20,28},{24,16},{28,20},{1,9},{5... | collective-permute-start | bytes 417800 | tf_op jit(solution)/shard_map/ppermute | solution.py:40
  78.8 35.2 %collective-permute-start.20 = (bf16[2,2,112,128]{3,2,0,1:T(8,128)(2,1)S(1)}, bf16[2,2,112,128]{3,2,0,1:T(8,128)(2,1)S(1)}, u32[]{:S(2)}, u32[]{:S(2)}) collective-permute-start(bf16[2,2,112,128]{3,2,0,1:T(8,128)(2,1)S(1)} %fusion.27), channel_id=1, source_target_pairs={{0,2},{1,3},{2,0},{3,1},{4,6},{5,7},{6,4},{7,5},{8,10},{9,11},{10,... | collective-permute-start | bytes 344072 | tf_op jit(solution)/shard_map/ppermute | solution.py:40
  80.4 33.6 %collective-permute-start.21 = (bf16[2,2,144,128]{3,2,0,1:T(8,128)(2,1)S(1)}, bf16[2,2,144,128]{3,2,0,1:T(8,128)(2,1)S(1)}, u32[]{:S(2)}, u32[]{:S(2)}) collective-permute-start(bf16[2,2,144,128]{3,2,0,1:T(8,128)(2,1)S(1)} %pad_maximum_fusion.20), channel_id=1, source_target_pairs={{0,4},{4,0},{8,12},{12,8},{16,20},{20,16},{24,28},{28,24},{1,5},{5... | collective-permute-start | bytes 442376 | tf_op jit(solution)/shard_map/ppermute | solution.py:40
  87.0 21.0 %collective-permute-start.19 = (bf16[2,2,2,224,128]{4,3,0,1,2:T(8,128)(2,1)S(1)}, bf16[2,2,2,224,128]{4,3,0,1,2:T(8,128)(2,1)S(1)}, u32[]{:S(2)}, u32[]{:S(2)}) collective-permute-start(bf16[2,2,2,224,128]{4,3,0,1,2:T(8,128)(2,1)S(1)} %pad_maximum_fusion.6), channel_id=1, source_target_pairs={{0,2},{1,3},{2,0},{3,1},{4,6},{5,7},{6,4},{7,5},{8,10},{9,11},{10,... | collective-permute-start | bytes 1376264 | tf_op jit(solution)/shard_map/ppermute | solution.py:40
  88.7 17.5 %collective-permute-start.18 = (bf16[2,2,2,160,128]{4,3,1,2,0:T(8,128)(2,1)S(1)}, bf16[2,2,2,160,128]{4,3,1,2,0:T(8,128)(2,1)S(1)}, u32[]{:S(2)}, u32[]{:S(2)}) collective-permute-start(bf16[2,2,2,160,128]{4,3,1,2,0:T(8,128)(2,1)S(1)} %pad_maximum_fusion.10), channel_id=1, source_target_pairs={{0,4},{4,0},{8,12},{12,8},{16,20},{20,16},{24,28},{28,24},{1,5},{5... | collective-permute-start | bytes 983048 | tf_op jit(solution)/shard_map/ppermute | solution.py:40
  90.3 23.6 %collective-permute-start.17 = (bf16[2,272,128]{2,1,0:T(8,128)(2,1)S(1)}, bf16[2,272,128]{2,1,0:T(8,128)(2,1)S(1)}, u32[]{:S(2)}, u32[]{:S(2)}) collective-permute-start(bf16[2,272,128]{2,1,0:T(8,128)(2,1)S(1)} %maximum_maximum_fusion.4), channel_id=1, source_target_pairs={{0,16},{4,20},{8,24},{12,28},{16,0},{20,4},{24,8},{28,12},{1,17},{... | collective-permute-start | bytes 417800 | tf_op jit(solution)/shard_map/ppermute | solution.py:40
  106.2 16.4 %collective-permute-start.24 = (bf16[1024,256]{1,0:T(8,128)(2,1)S(1)}, bf16[1024,256]{1,0:T(8,128)(2,1)}, u32[]{:S(2)}, u32[]{:S(2)}) collective-permute-start(bf16[1024,256]{1,0:T(8,128)(2,1)S(1)} %get-tuple-element.251), channel_id=1, source_target_pairs={{0,2},{1,3},{2,0},{3,1},{4,6},{5,7},{6,4},{7,5},{8,10},{9,11},{10,... | collective-permute-start | bytes 1572872 | tf_op jit(solution)/shard_map/ppermute | solution.py:40
  114.1 13.3 %collective-permute-start.23 = (bf16[2,2,2,144,128]{4,3,0,1,2:T(8,128)(2,1)S(1)}, bf16[2,2,2,144,128]{4,3,0,1,2:T(8,128)(2,1)S(1)}, u32[]{:S(2)}, u32[]{:S(2)}) collective-permute-start(bf16[2,2,2,144,128]{4,3,0,1,2:T(8,128)(2,1)S(1)} %pad_maximum_fusion.11), channel_id=1, source_target_pairs={{0,2},{1,3},{2,0},{3,1},{4,6},{5,7},{6,4},{7,5},{8,10},{9,11},{10,... | collective-permute-start | bytes 884744 | tf_op jit(solution)/shard_map/ppermute | solution.py:40
  114.6 8.0 %collective-permute-start.22 = (bf16[2,2,2,112,128]{4,3,1,2,0:T(8,128)(2,1)S(1)}, bf16[2,2,2,112,128]{4,3,1,2,0:T(8,128)(2,1)S(1)}, u32[]{:S(2)}, u32[]{:S(2)}) collective-permute-start(bf16[2,2,2,112,128]{4,3,1,2,0:T(8,128)(2,1)S(1)} %pad_maximum_fusion.13), channel_id=1, source_target_pairs={{0,4},{4,0},{8,12},{12,8},{16,20},{20,16},{24,28},{28,24},{1,5},{5... | collective-permute-start | bytes 688136 | tf_op jit(solution)/shard_map/ppermute | solution.py:40
  115.4 20.6 %collective-permute-start.25 = (bf16[1024,256]{1,0:T(8,128)(2,1)S(1)}, bf16[1024,256]{1,0:T(8,128)(2,1)S(1)}, u32[]{:S(2)}, u32[]{:S(2)}) collective-permute-start(bf16[1024,256]{1,0:T(8,128)(2,1)S(1)} %get-tuple-element.255), channel_id=1, source_target_pairs={{0,2},{1,3},{2,0},{3,1},{4,6},{5,7},{6,4},{7,5},{8,10},{9,11},{10,... | collective-permute-start | bytes 1572872 | tf_op jit(solution)/shard_map/ppermute | solution.py:40
  136.1 7.9 %collective-permute-start.26 = (bf16[1024,1024]{1,0:T(8,128)(2,1)}, bf16[1024,1024]{1,0:T(8,128)(2,1)}, u32[]{:S(2)}, u32[]{:S(2)}) collective-permute-start(bf16[1024,1024]{1,0:T(8,128)(2,1)} %shard_map.503.mine_ref), channel_id=1, source_target_pairs={{0,1},{1,0},{2,3},{3,2},{4,5},{5,4},{6,7},{7,6},{8,9},{9,8},{10,11... | collective-permute-start | bytes 6291464 | tf_op jit(solution)/shard_map/ppermute | solution.py:40
  136.1 6.2 %collective-permute-start.27 = (bf16[1024,256]{1,0:T(8,128)(2,1)}, bf16[1024,256]{1,0:T(8,128)(2,1)S(1)}, u32[]{:S(2)}, u32[]{:S(2)}) collective-permute-start(bf16[1024,256]{1,0:T(8,128)(2,1)} %collective-permute-done.24.refs_4_), channel_id=1, source_target_pairs={{0,1},{1,0},{2,3},{3,2},{4,5},{5,4},{6,7},{7,6},{8,9},{9,8},{10,11... | collective-permute-start | bytes 1572872 | tf_op jit(solution)/shard_map/ppermute | solution.py:40
  136.6 6.5 %collective-permute-start.28 = (bf16[1024,256]{1,0:T(8,128)(2,1)S(1)}, bf16[1024,256]{1,0:T(8,128)(2,1)S(1)}, u32[]{:S(2)}, u32[]{:S(2)}) collective-permute-start(bf16[1024,256]{1,0:T(8,128)(2,1)S(1)} %collective-permute-done.25.refs_4_), channel_id=1, source_target_pairs={{0,1},{1,0},{2,3},{3,2},{4,5},{5,4},{6,7},{7,6},{8,9},{9,8},{10,11... | collective-permute-start | bytes 1572872 | tf_op jit(solution)/shard_map/ppermute | solution.py:40
  137.4 13.7 %collective-permute-start.30 = (bf16[2,1024,256]{2,1,0:T(8,128)(2,1)}, bf16[2,1024,256]{2,1,0:T(8,128)(2,1)}, u32[]{:S(2)}, u32[]{:S(2)}) collective-permute-start(bf16[2,1024,256]{2,1,0:T(8,128)(2,1)} %refs_3_.5), channel_id=1, source_target_pairs={{0,1},{1,0},{2,3},{3,2},{4,5},{5,4},{6,7},{7,6},{8,9},{9,8},{10,11... | collective-permute-start | bytes 3145736 | tf_op jit(solution)/shard_map/ppermute | solution.py:40
  150.6 25.8 %collective-permute-start.29 = (bf16[512,1024]{1,0:T(8,128)(2,1)}, bf16[512,1024]{1,0:T(8,128)(2,1)}, u32[]{:S(2)}, u32[]{:S(2)}) collective-permute-start(bf16[512,1024]{1,0:T(8,128)(2,1)} %constant_dynamic-slice_fusion.1), channel_id=1, source_target_pairs={{0,2},{1,3},{2,0},{3,1},{4,6},{5,7},{6,4},{7,5},{8,10},{9,11},{10,... | collective-permute-start | bytes 3145736 | tf_op jit(solution)/shard_map/ppermute | solution.py:40
  204.5 26.9 %collective-permute-start.34 = (bf16[1024,1024]{1,0:T(8,128)(2,1)}, bf16[1024,1024]{1,0:T(8,128)(2,1)}, u32[]{:S(2)}, u32[]{:S(2)}) collective-permute-start(bf16[1024,1024]{1,0:T(8,128)(2,1)} %get-tuple-element.273.mine_ref), channel_id=1, source_target_pairs={{0,1},{1,0},{2,3},{3,2},{4,5},{5,4},{6,7},{7,6},{8,9},{9,8},{10,11... | collective-permute-start | bytes 6291464 | tf_op jit(solution)/shard_map/ppermute | solution.py:40
  209.6 25.5 %collective-permute-start.33 = (bf16[512,1024]{1,0:T(8,128)(2,1)}, bf16[512,1024]{1,0:T(8,128)(2,1)}, u32[]{:S(2)}, u32[]{:S(2)}) collective-permute-start(bf16[512,1024]{1,0:T(8,128)(2,1)} %fusion), channel_id=1, source_target_pairs={{0,2},{1,3},{2,0},{3,1},{4,6},{5,7},{6,4},{7,5},{8,10},{9,11},{10,... | collective-permute-start | bytes 3145736 | tf_op jit(solution)/shard_map/ppermute | solution.py:40
  210.3 24.9 %collective-permute-start.36 = (bf16[2,1024,256]{2,1,0:T(8,128)(2,1)S(1)}, bf16[2,1024,256]{2,1,0:T(8,128)(2,1)}, u32[]{:S(2)}, u32[]{:S(2)}) collective-permute-start(bf16[2,1024,256]{2,1,0:T(8,128)(2,1)S(1)} %copy-done.33), channel_id=1, source_target_pairs={{0,1},{1,0},{2,3},{3,2},{4,5},{5,4},{6,7},{7,6},{8,9},{9,8},{10,11... | collective-permute-start | bytes 3145736 | tf_op jit(solution)/shard_map/ppermute | solution.py:40
  230.9 4.3 %collective-permute-start.37 = (bf16[2,1024,256]{2,1,0:T(8,128)(2,1)}, bf16[2,1024,256]{2,1,0:T(8,128)(2,1)}, u32[]{:S(2)}, u32[]{:S(2)}) collective-permute-start(bf16[2,1024,256]{2,1,0:T(8,128)(2,1)} %copy-done.34), channel_id=1, source_target_pairs={{0,1},{1,0},{2,3},{3,2},{4,5},{5,4},{6,7},{7,6},{8,9},{9,8},{10,11... | collective-permute-start | bytes 3145736 | tf_op jit(solution)/shard_map/ppermute | solution.py:40
  254.9 5.6 %collective-permute-start.38 = (bf16[2,272,128]{2,1,0:T(8,128)(2,1)S(1)}, bf16[2,272,128]{2,1,0:T(8,128)(2,1)S(1)}, u32[]{:S(2)}, u32[]{:S(2)}) collective-permute-start(bf16[2,272,128]{2,1,0:T(8,128)(2,1)S(1)} %fusion.26), channel_id=1, source_target_pairs={{0,4},{4,0},{8,12},{12,8},{16,20},{20,16},{24,28},{28,24},{1,5},{5... | collective-permute-start | bytes 417800 | tf_op jit(solution)/shard_map/ppermute | solution.py:40
  260.8 13.1 %collective-permute-start.39 = (bf16[2,272,128]{2,1,0:T(8,128)(2,1)S(1)}, bf16[2,272,128]{2,1,0:T(8,128)(2,1)S(1)}, u32[]{:S(2)}, u32[]{:S(2)}) collective-permute-start(bf16[2,272,128]{2,1,0:T(8,128)(2,1)S(1)} %maximum_maximum_fusion.5), channel_id=1, source_target_pairs={{0,8},{4,12},{8,0},{12,4},{16,24},{20,28},{24,16},{28,20},{1,9},{5... | collective-permute-start | bytes 417800 | tf_op jit(solution)/shard_map/ppermute | solution.py:40
  260.8 30.2 %collective-permute-start.41 = (bf16[2,1024,256]{2,1,0:T(8,128)(2,1)S(1)}, bf16[2,1024,256]{2,1,0:T(8,128)(2,1)S(1)}, u32[]{:S(2)}, u32[]{:S(2)}) collective-permute-start(bf16[2,1024,256]{2,1,0:T(8,128)(2,1)S(1)} %get-tuple-element.316), channel_id=1, source_target_pairs={{0,2},{1,3},{2,0},{3,1},{4,6},{5,7},{6,4},{7,5},{8,10},{9,11},{10,... | collective-permute-start | bytes 3145736 | tf_op jit(solution)/shard_map/ppermute | solution.py:40
  274.2 16.8 %collective-permute-start.40 = (bf16[2,272,128]{2,1,0:T(8,128)(2,1)S(1)}, bf16[2,272,128]{2,1,0:T(8,128)(2,1)S(1)}, u32[]{:S(2)}, u32[]{:S(2)}) collective-permute-start(bf16[2,272,128]{2,1,0:T(8,128)(2,1)S(1)} %maximum_maximum_fusion.6), channel_id=1, source_target_pairs={{0,16},{4,20},{8,24},{12,28},{16,0},{20,4},{24,8},{28,12},{1,17},{... | collective-permute-start | bytes 417800 | tf_op jit(solution)/shard_map/ppermute | solution.py:40
  291.1 16.4 %collective-permute-start.42 = (bf16[2,2,2,320,128]{4,3,0,1,2:T(8,128)(2,1)S(1)}, bf16[2,2,2,320,128]{4,3,0,1,2:T(8,128)(2,1)S(1)}, u32[]{:S(2)}, u32[]{:S(2)}) collective-permute-start(bf16[2,2,2,320,128]{4,3,0,1,2:T(8,128)(2,1)S(1)} %copy.108), channel_id=1, source_target_pairs={{0,2},{1,3},{2,0},{3,1},{4,6},{5,7},{6,4},{7,5},{8,10},{9,11},{10,... | collective-permute-start | bytes 1966088 | tf_op jit(solution)/shard_map/ppermute | solution.py:40
  291.4 16.1 %collective-permute-start.43 = (bf16[2,2,2,320,128]{4,3,1,2,0:T(8,128)(2,1)S(1)}, bf16[2,2,2,320,128]{4,3,1,2,0:T(8,128)(2,1)S(1)}, u32[]{:S(2)}, u32[]{:S(2)}) collective-permute-start(bf16[2,2,2,320,128]{4,3,1,2,0:T(8,128)(2,1)S(1)} %copy.109), channel_id=1, source_target_pairs={{0,4},{4,0},{8,12},{12,8},{16,20},{20,16},{24,28},{28,24},{1,5},{5... | collective-permute-start | bytes 1966088 | tf_op jit(solution)/shard_map/ppermute | solution.py:40
  308.4 4.9 %collective-permute-start.44 = (bf16[1024,1024]{1,0:T(8,128)(2,1)}, bf16[1024,1024]{1,0:T(8,128)(2,1)S(1)}, u32[]{:S(2)}, u32[]{:S(2)}) collective-permute-start(bf16[1024,1024]{1,0:T(8,128)(2,1)} %get-tuple-element.329.mine_ref), channel_id=1, source_target_pairs={{0,1},{1,0},{2,3},{3,2},{4,5},{5,4},{6,7},{7,6},{8,9},{9,8},{10,11... | collective-permute-start | bytes 6291464 | tf_op jit(solution)/shard_map/ppermute | solution.py:40
  308.6 4.7 %collective-permute-start.45 = (f32[16,1024]{1,0:T(8,128)S(1)}, f32[16,1024]{1,0:T(8,128)S(1)}, u32[]{:S(2)}, u32[]{:S(2)}) collective-permute-start(f32[16,1024]{1,0:T(8,128)S(1)} %get-tuple-element.330), channel_id=1, source_target_pairs={{0,1},{1,0},{2,3},{3,2},{4,5},{5,4},{6,7},{7,6},{8,9},{9,8},{10,11... | collective-permute-start | bytes 196616 | tf_op jit(solution)/shard_map/ppermute | solution.py:40
  314.1 12.8 %collective-permute-start.46 = (bf16[2,2,2,192,128]{4,3,0,1,2:T(8,128)(2,1)}, bf16[2,2,2,192,128]{4,3,0,1,2:T(8,128)(2,1)}, u32[]{:S(2)}, u32[]{:S(2)}) collective-permute-start(bf16[2,2,2,192,128]{4,3,0,1,2:T(8,128)(2,1)} %copy.110), channel_id=1, source_target_pairs={{0,2},{1,3},{2,0},{3,1},{4,6},{5,7},{6,4},{7,5},{8,10},{9,11},{10,... | collective-permute-start | bytes 1179656 | tf_op jit(solution)/shard_map/ppermute | solution.py:40
  316.3 11.3 %collective-permute-start.47 = (bf16[2,2,2,192,128]{4,3,1,2,0:T(8,128)(2,1)}, bf16[2,2,2,192,128]{4,3,1,2,0:T(8,128)(2,1)}, u32[]{:S(2)}, u32[]{:S(2)}) collective-permute-start(bf16[2,2,2,192,128]{4,3,1,2,0:T(8,128)(2,1)} %copy.111), channel_id=1, source_target_pairs={{0,4},{4,0},{8,12},{12,8},{16,20},{20,16},{24,28},{28,24},{1,5},{5... | collective-permute-start | bytes 1179656 | tf_op jit(solution)/shard_map/ppermute | solution.py:40
  328.8 8.7 %collective-permute-start.48 = (bf16[2,2,192,128]{3,2,0,1:T(8,128)(2,1)S(1)}, bf16[2,2,192,128]{3,2,0,1:T(8,128)(2,1)}, u32[]{:S(2)}, u32[]{:S(2)}) collective-permute-start(bf16[2,2,192,128]{3,2,0,1:T(8,128)(2,1)S(1)} %fusion.18), channel_id=1, source_target_pairs={{0,4},{4,0},{8,12},{12,8},{16,20},{20,16},{24,28},{28,24},{1,5},{5... | collective-permute-start | bytes 589832 | tf_op jit(solution)/shard_map/ppermute | solution.py:40
  331.6 6.2 %collective-permute-start.49 = (bf16[2,2,192,128]{3,2,0,1:T(8,128)(2,1)S(1)}, bf16[2,2,192,128]{3,2,0,1:T(8,128)(2,1)}, u32[]{:S(2)}, u32[]{:S(2)}) collective-permute-start(bf16[2,2,192,128]{3,2,0,1:T(8,128)(2,1)S(1)} %fusion.19), channel_id=1, source_target_pairs={{0,2},{1,3},{2,0},{3,1},{4,6},{5,7},{6,4},{7,5},{8,10},{9,11},{10,... | collective-permute-start | bytes 589832 | tf_op jit(solution)/shard_map/ppermute | solution.py:40
  333.5 15.7 %collective-permute-start.55 = (bf16[2,2,320,128]{3,2,0,1:T(8,128)(2,1)}, bf16[2,2,320,128]{3,2,0,1:T(8,128)(2,1)}, u32[]{:S(2)}, u32[]{:S(2)}) collective-permute-start(bf16[2,2,320,128]{3,2,0,1:T(8,128)(2,1)} %fusion.14), channel_id=1, source_target_pairs={{0,4},{4,0},{8,12},{12,8},{16,20},{20,16},{24,28},{28,24},{1,5},{5... | collective-permute-start | bytes 983048 | tf_op jit(solution)/shard_map/ppermute | solution.py:40
  334.1 7.1 %collective-permute-start.51 = (f32[35,1024]{1,0:T(8,128)S(1)}, f32[35,1024]{1,0:T(8,128)S(1)}, u32[]{:S(2)}, u32[]{:S(2)}) collective-permute-start(f32[35,1024]{1,0:T(8,128)S(1)} %fusion.32), channel_id=1, source_target_pairs={{0,2},{1,3},{2,0},{3,1},{4,6},{5,7},{6,4},{7,5},{8,10},{9,11},{10,... | collective-permute-start | bytes 430088 | tf_op jit(solution)/shard_map/ppermute | solution.py:40
  335.7 13.5 %collective-permute-start.56 = (bf16[2,2,320,128]{3,2,0,1:T(8,128)(2,1)S(1)}, bf16[2,2,320,128]{3,2,0,1:T(8,128)(2,1)}, u32[]{:S(2)}, u32[]{:S(2)}) collective-permute-start(bf16[2,2,320,128]{3,2,0,1:T(8,128)(2,1)S(1)} %fusion.15), channel_id=1, source_target_pairs={{0,2},{1,3},{2,0},{3,1},{4,6},{5,7},{6,4},{7,5},{8,10},{9,11},{10,... | collective-permute-start | bytes 983048 | tf_op jit(solution)/shard_map/ppermute | solution.py:40
  344.3 7.4 %collective-permute-start.53 = (bf16[2,384,128]{2,1,0:T(8,128)(2,1)S(1)}, bf16[2,384,128]{2,1,0:T(8,128)(2,1)S(1)}, u32[]{:S(2)}, u32[]{:S(2)}) collective-permute-start(bf16[2,384,128]{2,1,0:T(8,128)(2,1)S(1)} %fusion.20), channel_id=1, source_target_pairs={{0,8},{4,12},{8,0},{12,4},{16,24},{20,28},{24,16},{28,20},{1,9},{5... | collective-permute-start | bytes 589832 | tf_op jit(solution)/shard_map/ppermute | solution.py:40
  345.2 6.5 %collective-permute-start.54 = (f32[35,1024]{1,0:T(8,128)S(1)}, f32[35,1024]{1,0:T(8,128)S(1)}, u32[]{:S(2)}, u32[]{:S(2)}) collective-permute-start(f32[35,1024]{1,0:T(8,128)S(1)} %add.313), channel_id=1, source_target_pairs={{0,4},{4,0},{8,12},{12,8},{16,20},{20,16},{24,28},{28,24},{1,5},{5... | collective-permute-start | bytes 430088 | tf_op jit(solution)/shard_map/ppermute | solution.py:40
  348.6 18.6 %collective-permute-start.60 = (bf16[3,704,128]{2,1,0:T(8,128)(2,1)}, bf16[3,704,128]{2,1,0:T(8,128)(2,1)}, u32[]{:S(2)}, u32[]{:S(2)}) collective-permute-start(bf16[3,704,128]{2,1,0:T(8,128)(2,1)} %dynamic-slice_bitcast_fusion.1), channel_id=1, source_target_pairs={{0,4},{4,0},{8,12},{12,8},{16,20},{20,16},{24,28},{28,24},{1,5},{5... | collective-permute-start | bytes 1622024 | tf_op jit(solution)/shard_map/ppermute | solution.py:40
  352.4 13.7 %collective-permute-start.58 = (f32[35,1024]{1,0:T(8,128)}, f32[35,1024]{1,0:T(8,128)}, u32[]{:S(2)}, u32[]{:S(2)}) collective-permute-start(f32[35,1024]{1,0:T(8,128)} %add.318), channel_id=1, source_target_pairs={{0,8},{4,12},{8,0},{12,4},{16,24},{20,28},{24,16},{28,20},{1,9},{5... | collective-permute-start | bytes 430088 | tf_op jit(solution)/shard_map/ppermute | solution.py:40
  357.3 10.0 %collective-permute-start.59 = (bf16[2,640,128]{2,1,0:T(8,128)(2,1)}, bf16[2,640,128]{2,1,0:T(8,128)(2,1)}, u32[]{:S(2)}, u32[]{:S(2)}) collective-permute-start(bf16[2,640,128]{2,1,0:T(8,128)(2,1)} %fusion.16), channel_id=1, source_target_pairs={{0,8},{4,12},{8,0},{12,4},{16,24},{20,28},{24,16},{28,20},{1,9},{5... | collective-permute-start | bytes 983048 | tf_op jit(solution)/shard_map/ppermute | solution.py:40
  358.6 7.5 %collective-permute-start.57 = (bf16[384,128]{1,0:T(8,128)(2,1)S(1)}, bf16[384,128]{1,0:T(8,128)(2,1)}, u32[]{:S(2)}, u32[]{:S(2)}) collective-permute-start(bf16[384,128]{1,0:T(8,128)(2,1)S(1)} %fusion.28), channel_id=1, source_target_pairs={{0,16},{4,20},{8,24},{12,28},{16,0},{20,4},{24,8},{28,12},{1,17},{... | collective-permute-start | bytes 294920 | tf_op jit(solution)/shard_map/ppermute | solution.py:40
  362.1 38.5 %collective-permute-start.52 = (bf16[1024,256]{1,0:T(8,128)(2,1)}, bf16[1024,256]{1,0:T(8,128)(2,1)}, u32[]{:S(2)}, u32[]{:S(2)}) collective-permute-start(bf16[1024,256]{1,0:T(8,128)(2,1)} %fusion.8), channel_id=1, source_target_pairs={{0,2},{1,3},{2,0},{3,1},{4,6},{5,7},{6,4},{7,5},{8,10},{9,11},{10,... | collective-permute-start | bytes 1572872 | tf_op jit(solution)/shard_map/ppermute | solution.py:40
  368.2 14.3 %collective-permute-start.62 = (f32[35,1024]{1,0:T(8,128)S(1)}, f32[35,1024]{1,0:T(8,128)S(1)}, u32[]{:S(2)}, u32[]{:S(2)}) collective-permute-start(f32[35,1024]{1,0:T(8,128)S(1)} %add.326), channel_id=1, source_target_pairs={{0,16},{4,20},{8,24},{12,28},{16,0},{20,4},{24,8},{28,12},{1,17},{... | collective-permute-start | bytes 430088 | tf_op jit(solution)/shard_map/ppermute | solution.py:40
  374.9 8.4 %collective-permute-start.61 = (bf16[640,128]{1,0:T(8,128)(2,1)S(1)}, bf16[640,128]{1,0:T(8,128)(2,1)S(1)}, u32[]{:S(2)}, u32[]{:S(2)}) collective-permute-start(bf16[640,128]{1,0:T(8,128)(2,1)S(1)} %fusion.21), channel_id=1, source_target_pairs={{0,16},{4,20},{8,24},{12,28},{16,0},{20,4},{24,8},{28,12},{1,17},{... | collective-permute-start | bytes 491528 | tf_op jit(solution)/shard_map/ppermute | solution.py:40
  391.1 3.8 collective-permute-start.64
  394.9 3.7 collective-permute-start.65
  402.4 6.6 %collective-permute-start.67 = (f32[32,128]{1,0:T(8,128)S(1)}, f32[32,128]{1,0:T(8,128)S(1)}, u32[]{:S(2)}, u32[]{:S(2)}) collective-permute-start(f32[32,128]{1,0:T(8,128)S(1)} %add.332), channel_id=1, source_target_pairs={{0,16},{4,20},{8,24},{12,28},{16,0},{20,4},{24,8},{28,12},{1,17},{... | collective-permute-start | bytes 49160 | tf_op jit(solution)/shard_map/ppermute | solution.py:40
  (70 other events, 681.4 us)
Sparse Core Ops, SparseCore 0:
  19.7 103.5 all-gather.2
  235.2 84.0 reduce-scatter.1

commit v4 on v3

--- a/solution.py
+++ b/solution.py
@@ -200,14 +200,14 @@
 
 
 def call(body, steps, ins, outs, reverse=False, scratch=()):
-    def spec(shape, axis, period=steps):
+    def spec(shape, axis, count=steps, at=lambda i: i):
         if axis == "smem":
             return pl.BlockSpec(memory_space=pltpu.SMEM)
-        block = tuple(n // period if d == axis else n for d, n in enumerate(shape))
+        block = tuple(n // count if d == axis else n for d, n in enumerate(shape))
 
         def where(i):
-            at = (steps - 1 - i if reverse else i) % period
-            return tuple(at if d == axis else 0 for d in range(len(shape)))
+            number = at(steps - 1 - i if reverse else i)
+            return tuple(number if d == axis else 0 for d in range(len(shape)))
 
         return pl.BlockSpec(block, where)
 
@@ -260,8 +260,8 @@
     )
 
 
-def two_halves(place_ref, number, mine, beside):
-    return jnp.where(place_ref[1] == number // 2, mine, beside)
+def from_core(place_ref, number, mine, beside):
+    return jnp.where(place_ref[1] == number, mine, beside)
 
 
 def first_step(body):
@@ -387,7 +387,7 @@
 
 
 def feed_forward_kernel(
-    other, place_ref, normed_ref, beside_normed_ref, cot_ref, moved_ref, beside_ref, beside_moved_ref, weight_ref,
+    ring, other, place_ref, normed_ref, beside_normed_ref, cot_ref, moved_ref, beside_ref, beside_moved_ref, weight_ref,
     hidden_ref, gate_grad_ref, up_grad_ref, keep_ref, give_ref, rows_grad_ref, cot_out_ref, normed_out_ref, all_ref,
 ):
     width = weight_ref.shape[2]
@@ -395,12 +395,12 @@
     @first_step
     def _():
         all_ref[:, width:] = jnp.zeros_like(all_ref[:, width:])
-        for s in range(weight_ref.shape[0]):
-            all_ref[:, :width, s * LANES : (s + 1) * LANES] = weight_ref[s]
+        for at, s in enumerate(ring):
+            all_ref[:, :width, s * LANES : (s + 1) * LANES] = weight_ref[at]
 
     normed = normed_ref[...]
     if other:
-        normed = two_halves(place_ref, pl.program_id(0), normed, beside_normed_ref[...])
+        normed = from_core(place_ref, pl.program_id(0), normed, beside_normed_ref[...])
         normed_out_ref[...] = normed
     chip = place_ref[0]
     sequence = 1 - chip if other else chip
@@ -427,28 +427,23 @@
         give_ref[b] = jnp.where(place_ref[1] == 0, high, low)
 
 
-def feed_forward_weights_kernel(
-    own_ref, other_ref, cot_own_ref, cot_other_ref,
-    gate_own_ref, gate_other_ref, up_own_ref, up_other_ref, hidden_own_ref, hidden_other_ref,
-    out_ref,
-):
+def feed_forward_weights_kernel(*refs):
+    sets, out_ref = [refs[7 * i : 7 * i + 7] for i in range(3)], refs[21]
     width = out_ref.shape[2]
-    for i, (left, left_other, right, right_other) in enumerate(
-        [
-            (gate_own_ref, gate_other_ref, own_ref, other_ref),
-            (up_own_ref, up_other_ref, own_ref, other_ref),
-            (hidden_own_ref, hidden_other_ref, cot_own_ref, cot_other_ref),
-        ]
-    ):
-        total = to_half(mul(left[...], right[...]) + mul(left_other[...], right_other[...]))
+    both = [
+        [jnp.concatenate([group[i][...], group[i + 1][...]], axis=1) for i in (0, 2)] for group in sets
+    ]
+    for i, (left, right) in enumerate(((4, 0), (5, 0), (6, 1))):
+        total = sum(mul(group[left][...], pair[right]) for group, pair in zip(sets, both))
+        total = to_half(total)
         for s in range(out_ref.shape[0]):
             out_ref[s, i] = total[:width, s * LANES : (s + 1) * LANES]
 
 
 def mixer_backward_kernel(
-    place_ref, residual_ref, cot_ref, mine_ref, other_ref, home_ref, beside_home_ref, gain_ref,
+    place_ref, residual_ref, cot_ref, mine_ref, other_ref, home_refs, gain_ref,
     late_ref, recurrent_ref, gate_ref, query_ref, within_ref, group_ref,
-    keep_own_ref, beside_own_ref, keep_other_ref, beside_other_ref,
+    keep_own_ref, beside_own_ref, others_refs,
     grad_ref, half_ref, gain_grad_ref, recurrent_grad_ref, gate_grad_ref, group_grad_ref, state_grad_ref,
     send_ref, stay_ref, output_ref,
 ):
@@ -463,7 +458,12 @@
     scale = lax.rsqrt(jnp.mean(residual * residual, axis=1, keepdims=True) + eps_norm)
     normed = residual * scale
     number = pl.num_programs(0) - 1 - pl.program_id(0)
-    home = two_halves(place_ref, number, home_ref[...], beside_home_ref[...])
+    piece, holder = (number % 2, number // 2)
+    home = jnp.where(
+        piece == 0,
+        from_core(place_ref, holder, home_refs[0][...], home_refs[1][...]),
+        from_core(place_ref, holder, home_refs[2][...], home_refs[3][...]),
+    )
     pulled = to_float(mine_ref[...]) + to_float(other_ref[...]) + to_float(home)
     gain_grad_ref[...] += jnp.sum(pulled * normed, axis=0, keepdims=True)
     weighted = pulled * gain_ref[1:2]
@@ -480,7 +480,10 @@
     for b in range(2):
         low, high = (residual[:, (2 * b + l) * columns : (2 * b + l + 1) * columns] for l in range(2))
         own.append(to_float(keep_own_ref[b]) + to_float(beside_own_ref[b]) + jnp.where(core == 0, low, high))
-        other.append(to_float(keep_other_ref[b]) + to_float(beside_other_ref[b]))
+        keep_other, beside_other = (
+            to_float(jnp.where(piece == 0, first[b], second[b])) for first, second in (others_refs[:2], others_refs[2:])
+        )
+        other.append(keep_other + beside_other)
     for at, rows in enumerate((own, other)):
         send_ref[at] = to_half(jnp.where(chip == 0, rows[1], rows[0]))
         stay_ref[at] = jnp.where(chip == 0, rows[0], rows[1])
@@ -687,7 +690,7 @@
                 total = jnp.sum(total, axis=0)
             total = jnp.sum(jnp.sum(total, axis=0, keepdims=True), axis=1, keepdims=True)
             if shared:
-                total = total * share[0:1, 0:1]
+                total = total * share[shared - 1 : shared, 0:1]
             squares[row : row + 1] = jnp.broadcast_to(total, (1, LANES))
 
 
@@ -790,6 +793,13 @@
     side = bit_of("seq", 1)
     place = jnp.stack([chip, core, side]).astype(jnp.int32)
 
+    ring = list(range(peers))
+    if aligned:
+        ring = ring[::2] + ring[1::2][::-1]
+
+    def ring_block(at):
+        return jnp.where(at < blocks // 2, 2 * at, 2 * blocks - 1 - 2 * at) if aligned else at
+
     ffn_mine = jnp.concatenate([jnp.moveaxis(ffn_weight, 0, 2), down_weight[None]])
     ffn_mine = to_half(ffn_mine if aligned else jnp.moveaxis(ffn_mine, 2, 1))
     small_mine = jnp.concatenate(
@@ -813,9 +823,8 @@
     tokens_beside, cot_beside = (swap(tokens, "head", 1), swap(cotangent, "head", 1))
     moved_beside = swap(rows_moved, "head", 1)
     if aligned:
-        lines = [[x + 2 * z for z in range(peers // 2)] for x in range(2)]
         value_mine, ffn_mine = tie((to_half(value_mine), ffn_mine))
-        ffn_all = lax.all_gather(ffn_mine, "seq", axis=0)
+        ffn_all = lax.all_gather(ffn_mine, "seq", axis=0, axis_index_groups=[ring])
         key_part, held = grow(to_half(jnp.concatenate([key_mine, small_mine])), [], along)
         value_part, held = grow(jnp.concatenate([value_mine[:, :LANES], value_mine[:, LANES:]]), [], along)
         late_mine = to_half(jnp.concatenate([late_mine, output_weight]))
@@ -899,7 +908,7 @@
         late_part, _ = beside_each_other(late_part, late_moved, late_held, along[1])
         links = {}
         for name, low, cut, high in (
-            ("gate", 0, 10 * LANES // 8, 3 * LANES),
+            ("gate", 0, 11 * LANES // 8, 3 * LANES),
             ("output", 3 * LANES, 3 * LANES + 7 * LANES // 8, 5 * LANES),
         ):
             links[name] = [late_part[..., low:cut, :], late_part[..., cut:high, :]]
@@ -936,6 +945,9 @@
     def beside_forward(number, message):
         if not aligned:
             return message
+        if number == 0:
+            beside_scan["normed"] = normed.T
+            message, beside_scan["normed"] = tie((message, beside_scan["normed"]))
         if number == 1:
             message, moved, cot_given[0] = tie((message, gate_moved, cot_given[0]))
             beside_scan["gate"] = second_links(links["gate"], moved)
@@ -957,11 +969,12 @@
         gate_all = beside_scan["gate"]
         queries, gate_values = beside_scan["out"]
         cot_own_moved = beside_scan["cot"]
+        normed_t = beside_scan["normed"]
     else:
         gate_all, output_all = (late_all[:, :, : 3 * LANES], late_all[:, :, 3 * LANES :])
         queries, gate_values = project_late(gate_all)
         cot_own_moved = swap(cot_given[0], *across)
-    cot_other_moved = swap(cot_given[1], *across)
+        normed_t = normed.T
     recurrent, starts, mixed_half = call(
         forward_kernel,
         steps,
@@ -994,11 +1007,8 @@
         [((segment, model_width), half, 0)],
         scratch=[pltpu.VMEM((2, value_width, model_width), jnp.bfloat16)],
     )
-    mixer_part, cot_other_moved = tie((mixer_part, cot_other_moved))
-    mixer_beside = swap(mixer_part, "head", 1)
-    cot_others = (cot_own_moved, cot_other_moved)
-    cot_others_beside = [swap(a, "head", 1) for a in cot_others]
-    mixer_beside, cot_others_beside = tie((mixer_beside, cot_others_beside))
+    mixer_beside, cot_own_beside = (swap(mixer_part, "head", 1), swap(cot_own_moved, "head", 1))
+    mixer_beside, cot_own_beside, mixed_t = tie((mixer_beside, cot_own_beside, mixed_half.T))
     residual, normed_two = call(
         residual_kernel,
         steps,
@@ -1006,70 +1016,81 @@
         [((segment, model_width), full, 0), ((segment, model_width), half, 0)],
     )
 
-    moved = swap(lax.dynamic_slice_in_dim(normed_two, core * half_segment, half_segment, 0), *across)
-
-    def feed_forward(other, mine, beside_mine):
+    def piece_of(rows_of_all, p):
+        return lax.dynamic_slice_in_dim(rows_of_all, core * half_segment + p * TILE, TILE, 0)
+
+    moved = [swap(piece_of(normed_two, p), *across) for p in range(2)]
+    normed_two, cot_given[1] = tie((normed_two, cot_given[1]))
+    cot_other_moved = swap(cot_given[1], *across)
+
+    def feed_forward(piece, mine, beside_mine, cots):
+        other = piece is not None
+        tiles = (4, lambda i: 2 * i + piece) if other else ()
+        width = 2 * TILE if other else segment
         return call(
-            lambda *refs: feed_forward_kernel(other, *refs),
-            steps,
-            [(place, "smem"), mine, beside_mine, (cotangent, 1)]
-            + [(cot_others[other], 0), (cot_beside, 1), (cot_others_beside[other], 0)]
+            lambda *refs: feed_forward_kernel(ring if aligned else range(blocks), other, *refs),
+            width // TILE,
+            [(place, "smem"), mine, beside_mine, (cotangent, 1, *tiles)]
+            + [(cots[0], 0, *tiles), (cot_beside, 1, *tiles), (cots[1], 0, *tiles)]
             + [(ffn_all, None)],
-            [((ffn_padded, segment), half, 1)] * 3
-            + [((2, segment, column_count), half, 1)] * 2
-            + [((segment, model_width), half, 0)] * 2
-            + ([((segment, model_width), half, 0)] if other else [((TILE, model_width), half, None)]),
+            [((ffn_padded, width), half, 1)] * 3
+            + [((2, width, column_count), half, 1)] * 2
+            + [((width, model_width), half, 0)] * 2
+            + ([((width, model_width), half, 0)] if other else [((TILE, model_width), half, None)]),
             scratch=[pltpu.VMEM((3, ffn_padded, model_width), jnp.bfloat16)],
         )
 
-    dummy = (place, "smem")
-    own = feed_forward(False, (normed_two, 0), dummy)
-    moved, own = tie((moved, own))
-    other = feed_forward(True, (moved, 0, 2), (swap(moved, "head", 1), 0, 2))
-    cot_own, cot_other, normed_two_other = (own[6], other[6], other[7])
-    other_rows = other[5].reshape(2, half_segment, model_width)
-    other_sum = to_half(
-        to_float(pick(other_rows, core)) + to_float(swap(pick(other_rows, 1 - core), "head", 1))
-    )
-    home = swap(other_sum, *across)
+    own = feed_forward(None, (normed_two, 0), (place, "smem"), (cot_own_moved, cot_own_beside))
+    moved[0], cot_other_moved, own = tie((moved[0], cot_other_moved, own))
+    cots = (cot_other_moved, swap(cot_other_moved, "head", 1))
+    others, homes = [], []
+    for p in range(2):
+        if p:
+            moved[p], others[0] = tie((moved[p], others[0]))
+        others.append(feed_forward(p, (moved[p], None), (swap(moved[p], "head", 1), None), cots))
+        other_rows = others[p][5].reshape(2, TILE, model_width)
+        other_sum = to_half(
+            to_float(pick(other_rows, core)) + to_float(swap(pick(other_rows, 1 - core), "head", 1))
+        )
+        homes.append(swap(other_sum, *across))
     (ffn_grad,) = call(
         feed_forward_weights_kernel,
         4,
         [
-            (normed_two, 1),
-            (normed_two_other, 1),
-            (cot_own, 1),
-            (cot_other, 1),
-            (own[1], None),
-            (other[1], None),
-            (own[2], None),
-            (other[2], None),
-            (own[0], None),
-            (other[0], None),
+            entry
+            for rows_of_all, group in ((normed_two, own), (others[0][7], others[0]), (others[1][7], others[1]))
+            for entry in (
+                (rows_of_all, 1, blocks, lambda i: ring_block(2 * i)),
+                (rows_of_all, 1, blocks, lambda i: ring_block(2 * i + 1)),
+                (group[6], 1, blocks, lambda i: ring_block(2 * i)),
+                (group[6], 1, blocks, lambda i: ring_block(2 * i + 1)),
+                (group[1], None),
+                (group[2], None),
+                (group[0], None),
+            )
         ],
         [((blocks, 3, ffn_width, LANES), half, 0)],
     )
     own_grad = own[5]
-    own_beside = swap(own_grad, "head", 1)
-    ffn_grad, normed, mixed_half = tie((ffn_grad, normed, mixed_half))
-    home, ffn_grad, own_beside, normed_t, mixed_t = tie(
-        (home, ffn_grad, own_beside, normed.T, mixed_half.T)
-    )
-    out_beside = [swap(give, "head", 1) for give in (own[4], other[4])]
+    beside_own = [swap(a, "head", 1) for a in (own_grad, own[4], others[0][4], others[1][4])]
+    ffn_grad, beside_own = tie((ffn_grad, beside_own))
+    own_beside, out_beside = (beside_own[0], beside_own[1:])
+    homes, ffn_grad = tie((homes, ffn_grad))
+    homes = [a for home in homes for a in (home, swap(home, "head", 1))]
+    by_piece = (2, lambda i: i // 2)
     (
         residual_grad, residual_half, gain_two_grad, recurrent_grad, gate_grad, group_grad, state_in_grad,
         out_give, out_mine,
     ) = call(
-        mixer_backward_kernel,
+        lambda *refs: mixer_backward_kernel(*refs[:5], refs[5:9], *refs[9:18], refs[18:22], *refs[22:]),
         steps,
         [
             (place, "smem"),
             (residual, 0),
-            (cot_own, 0),
+            (own[6], 0),
             (own_grad, 0),
             (own_beside, 0),
-            (home, 0, 2),
-            (swap(home, "head", 1), 0, 2),
+            *[(home, None) for home in homes],
             (gains, None),
             (output_all, None),
             (recurrent, 0),
@@ -1079,8 +1100,7 @@
             (group_weight[None, :], None),
             (own[3], 1),
             (out_beside[0], 1),
-            (other[3], 1),
-            (out_beside[1], 1),
+            *[(a, 1, *by_piece) for a in (others[0][3], others[1][3], out_beside[1], out_beside[2])],
         ],
         [
             ((segment, model_width), full, 0),
@@ -1100,12 +1120,8 @@
         ffn_grad = ffn_grad.reshape(blocks, 3, ffn_width, LANES // rows, rows)
         ffn_grad = ffn_grad.transpose(0, 3, 1, 4, 2).reshape(peers, 3, rows, ffn_width)
     if aligned:
-        ffn_pair = lax.psum_scatter(
-            ffn_grad.reshape((peers // 2, 2) + ffn_grad.shape[1:]),
-            "seq",
-            scatter_dimension=0,
-            tiled=False,
-            axis_index_groups=lines,
+        ffn_sum = lax.psum_scatter(
+            ffn_grad, "seq", scatter_dimension=0, tiled=False, axis_index_groups=[ring]
         )
     else:
         ffn_sum = lax.psum_scatter(ffn_grad, "seq", scatter_dimension=0, tiled=False)
@@ -1156,7 +1172,7 @@
 
     later_grad = scan_blocks(block_decay, state_in_grad, True, beside_backward)
     (query_grad, kept, normed_grad), late_grads = (beside_scan["first"], beside_scan["second"])
-    late_grads, later_grad, out_moved = tie((late_grads, later_grad, out_moved))
+    late_grads, later_grad, out_moved, ffn_sum = tie((late_grads, later_grad, out_moved, ffn_sum))
     back = along[::-1]
     if aligned:
         first_held = seq_bits()
@@ -1247,6 +1263,21 @@
             ((rank_count, model_width), full, None),
         ],
     )
+    once = jnp.where(jnp.arange(8) == 0, (head_index == 0).astype(jnp.float32), 0.25 / peers)
+    share = jnp.broadcast_to(once[:, None], (8, LANES))
+    by_width = lambda a: jnp.moveaxis(a, 0, 2)
+
+    def optimize_early(ffn_sum):
+        return adam_group(
+            share,
+            [ffn_sum],
+            [(lambda g: g[:2], 0), (lambda g: g[2], 0)],
+            [
+                tuple(map(by_width, (ffn_weight, ffn_mean, ffn_square))),
+                (down_weight, down_mean, down_square),
+            ],
+        )
+
     if aligned:
         state_moved, late_moved, gain_one_grad, squeeze_grad, grad_cols = tie(
             (state_moved, late_moved, gain_one_grad, squeeze_grad, grad_cols)
@@ -1272,12 +1303,11 @@
         late_kept, late_gives = next_sides(late_kept, late_moved)
         late_moved = next_moved(late_gives)
         grad_give = to_half(pick(grad_cols, 1 - chip))
-        state_moved, small_moved, grad_give, ffn_pair = tie((state_moved, small_moved, grad_give, ffn_pair))
+        state_moved, small_moved, grad_give = tie((state_moved, small_moved, grad_give))
         state_kept, state_give = split(joined(state_kept, state_moved), along, back[0])
         state_moved = swap(state_give, *back[0])
         small_grad = small_grad + small_moved
         small_moved = swap(small_grad, *beside)
-        ffn_moved = swap(pick(ffn_pair, 1 - side), *beside)
         state_moved, small_moved, late_moved = tie((state_moved, small_moved, late_moved))
         state_kept, state_give = split(to_float(state_kept) + to_float(state_moved), along[:-1], back[1])
         state_moved = swap(state_give, *back[1])
@@ -1285,12 +1315,14 @@
         small_moved = swap(small_grad, *back[0])
         late_kept, late_give = split(joined(late_kept, late_moved), along, back[0])
         late_moved = swap(late_give, *back[0])
-        state_moved, small_moved, late_moved, ffn_moved = tie((state_moved, small_moved, late_moved, ffn_moved))
+        state_moved, small_moved = tie((state_moved, small_moved))
         state_sum = to_float(state_kept) + to_float(state_moved)
         small_grad = small_grad + small_moved
-        small_grad = small_grad + swap(small_grad, *back[1])
+        small_moved = swap(small_grad, *back[1])
+        early, early_squares = optimize_early(ffn_sum)
+        early, early_squares, small_moved, late_moved = tie((early, early_squares, small_moved, late_moved))
+        small_grad = small_grad + small_moved
         late_sum = shrink(to_float(late_kept) + to_float(late_moved), along[:-1], back[1:])[0]
-        ffn_sum = to_float(pick(ffn_pair, side)) + to_float(ffn_moved)
         output_sum_grad = late_sum[3 * LANES :]
     else:
 
@@ -1305,6 +1337,7 @@
         output_sum_grad = scatter_cube(output_grad, [beside, across] + back).T
         grad_give = to_half(pick(grad_cols, 1 - chip))
         small_grad = sum_everywhere(small_grad)
+        early, early_squares = optimize_early(ffn_sum)
     grad_home = to_float(swap(grad_give, *across))
     tokens_grad = jnp.stack(ordered(pick(grad_cols, chip), grad_home, chip))
     out_home = to_float(out_moved)
@@ -1314,33 +1347,23 @@
     expand_total = small_grad[rank_count + 2 :, : 4 * key_width]
     group_total = small_grad[rank_count + 2 : rank_count + 3, 4 * key_width : 4 * key_width + value_width]
 
-    share = jnp.broadcast_to((head_index == 0).astype(jnp.float32), (8, LANES))
-    by_width = lambda a: jnp.moveaxis(a, 0, 2)
-    early, early_squares = adam_group(
-        share,
-        [ffn_sum],
-        [(lambda g: g[:2], False), (lambda g: g[2], False)],
-        [
-            tuple(map(by_width, (ffn_weight, ffn_mean, ffn_square))),
-            (down_weight, down_mean, down_square),
-        ],
-    )
-    early_squares, late_sum = tie((early_squares, late_sum))
     late, late_squares = adam_group(
         share,
-        [late_sum, state_sum, output_sum_grad, mine_grad],
-        [
-            (lambda l, s, o, m: jnp.concatenate([l[:rows], s[:rows]], axis=1), False),
+        [late_sum, state_sum, output_sum_grad, mine_grad, expand_total, group_total],
+        [
+            (lambda l, s, *_: jnp.concatenate([l[:rows], s[:rows]], axis=1), 0),
             (
-                lambda l, s, o, m: jnp.concatenate(
+                lambda l, s, *_: jnp.concatenate(
                     [s[rows : 2 * rows], s[2 * rows : 3 * rows], l[rows : 2 * rows], l[2 * rows : 3 * rows]],
                     axis=1,
                 ),
-                False,
+                0,
             ),
-            (lambda l, s, o, m: o[...], False),
-            (lambda l, s, o, m: m[:rank_count], True),
-            (lambda l, s, o, m: m[rank_count:], True),
+            (lambda l, s, o, *_: o[...], 0),
+            (lambda l, s, o, m, e, g: m[:rank_count], 1),
+            (lambda l, s, o, m, e, g: m[rank_count:], 1),
+            (lambda l, s, o, m, e, g: e[...], 2),
+            (lambda l, s, o, m, e, g: g[...], 2),
         ],
         [
             (query_weight, query_mean, query_square),
@@ -1348,27 +1371,19 @@
             (output_weight, output_mean, output_square),
             (squeeze_weight.T, squeeze_mean.T, squeeze_square.T),
             (norms_weight, norms_mean, norms_square),
-        ],
-    )
-    copied, copied_squares = adam_group(
-        share,
-        [expand_total, group_total],
-        [(lambda e, g: e[...], False), (lambda e, g: g[...], False)],
-        [
             (expand_weight, expand_mean, expand_square),
             tuple(a[None, :] for a in (group_weight, group_mean, group_square)),
         ],
     )
     squares = sum_everywhere(jnp.concatenate([early_squares, late_squares]))
-    squares = jnp.concatenate([squares, copied_squares])
     masters = [
         by_width(ffn_weight), down_weight,
         query_weight, value_weight, output_weight, squeeze_weight.T, norms_weight,
         expand_weight, group_weight[None, :],
     ]
-    moments = early + late + copied
+    moments = early + late
     news = whole_call(
-        lambda *refs: trust_kernel([0, 1, 16, 17, 18, 19, 20, 32, 33], *refs),
+        lambda *refs: trust_kernel([0, 1, 16, 17, 18, 19, 20, 21, 22], *refs),
         [squares] + masters + [moment[2] for moment in moments],
         [master.shape for master in masters],
     )

time: 425 us -> 409 us (0.962)
  waiting for transfers between devices: 112 us -> 102 us
  other arithmetic: 34.5 us -> 27.8 us
    ppermute x68 -> x73, waiting for transfers between devices: 112 us -> 100 us  [swap(): lax.ppermute(value_entries, axis, [(i, i ^ bit) for i in range(peers)])]
    pallas_call x14 -> x15, Pallas kernels: 138 us -> 143 us  [call(): pl.pallas_call(body, grid=(steps,), in_specs=[spec(entry[0].shape, *entry...]
    ppermute x68 -> x73, starting transfers between devices: 66.5 us -> 63.7 us  [swap(): lax.ppermute(value_entries, axis, [(i, i ^ bit) for i in range(peers)])]
    unnamed x133 -> x141, local copies, waits for them, and re-layouts: 19.7 us -> 18 us
    pallas_call x4 -> x3, Pallas kernels: 14.1 us -> 12.5 us  [whole_call(): pl.pallas_call(body, out_shape=[jax.ShapeDtypeStruct(shape, jnp.float32)...]
  transfers between devices with their start and end apart: 70 -> 75, of which waited for: 31 -> 36; matrix products, arithmetic and copies ran while one was open for 12% -> 11% of each run, Pallas kernels for 31% -> 38%
where the time goes in v4:
time: 409 us; the launch traced here: 404 us
  Pallas kernels  155 us (38%)
  waiting for transfers between devices  102 us (25%)
  starting transfers between devices  63.8 us (16%)
  local copies, waits for them, and re-layouts  39.8 us (10%)
  other arithmetic  27.8 us (7%)
  between operations  16 us (4%)
    pallas_call x15, Pallas kernels, call(): pl.pallas_call(body, grid=(steps,), in_specs=[spec(entry[0].shape, *entry...  143 us
    ppermute x73, waiting for transfers between devices, swap(): lax.ppermute(value_entries, axis, [(i, i ^ bit) for i in range(peers)])  100 us
    ppermute x73, starting transfers between devices, swap(): lax.ppermute(value_entries, axis, [(i, i ^ bit) for i in range(peers)])  63.7 us
    unnamed x141, local copies, waits for them, and re-layouts  18 us
    pallas_call x3, Pallas kernels, whole_call(): pl.pallas_call(body, out_shape=[jax.ShapeDtypeStruct(shape, jnp.float32)...  12.5 us
  transfers between devices with their start and end apart: 75, of which 36 were waited for; matrix products, arithmetic and copies ran while one was open for 11% of the time, Pallas kernels for 38%

profile of v4, /device:TPU:0, one launch (start us, length us, event | category | flops | bytes accessed | tf_op | source)
XLA Modules:
  0.0 404.1 jit_solution(16617661022305718217)
XLA Ops:
  10.9 4.1 %collective-permute-start.3 = (bf16[160,128]{1,0:T(8,128)(2,1)S(1)}, bf16[160,128]{1,0:T(8,128)(2,1)S(1)}, u32[]{:S(2)}, u32[]{:S(2)}) collective-permute-start(bf16[160,128]{1,0:T(8,128)(2,1)S(1)} %maximum_maximum_fusion.7), channel_id=1, source_target_pairs={{0,16},{4,20},{8,24},{12,28},{16,0},{20,4},{24,8},{28,12},{1,17},{... | collective-permute-start | bytes 122888 | tf_op jit(solution)/shard_map/ppermute | solution.py:40
  18.0 1.7 collective-permute-start
  20.1 1.6 collective-permute-start.4
  25.2 2.9 collective-permute-done.6
  29.5 2.2 dynamic-slice_bitcast_fusion.2
  31.7 1.5 collective-permute-start.7
  33.2 1.5 collective-permute-start.10
  36.1 1.8 collective-permute-start.9
  37.9 10.1 %collective-permute-done.10 = bf16[2,2,256,128]{3,2,0,1:T(8,128)(2,1)S(1)} collective-permute-done((bf16[2,2,256,128]{3,2,0,1:T(8,128)(2,1)S(1)}, bf16[2,2,256,128]{3,2,0,1:T(8,128)(2,1)S(1)}, u32[]{:S(2)}, u32[]{:S(2)}) %collective-permute-start.10) | collective-permute-done | bytes 262176 | tf_op jit(solution)/shard_map/ppermute | solution.py:40
  48.1 1.8 collective-permute-start.11
  50.1 11.3 %collective-permute-done.9 = bf16[2,2,2,160,128]{4,3,1,2,0:T(8,128)(2,1)S(1)} collective-permute-done((bf16[2,2,2,160,128]{4,3,1,2,0:T(8,128)(2,1)S(1)}, bf16[2,2,2,160,128]{4,3,1,2,0:T(8,128)(2,1)S(1)}, u32[]{:S(2)}, u32[]{:S(2)}) %collective-permute-start.9) | collective-permute-done | bytes 327712 | tf_op jit(solution)/shard_map/ppermute | solution.py:40
  63.2 10.5 %shard_map.500 = (bf16[1024,1024]{1,0:T(8,128)(2,1)}, bf16[1024,1024]{1,0:T(8,128)(2,1)}, bf16[1024,256]{1,0:T(8,128)(2,1)S(1)}, bf16[1024,512]{1,0:T(8,128)(2,1...) custom-call(s32[3]{0:T(128)S(1)} %pad_add_fusion.place_ref.refs_0_.r, ...), custom_call_target="tpu_custom_call" | custom-call | flops 1 | tf_op jit(solution)/shard_map/pallas_call | solution.py:214
  76.3 4.2 %collective-permute-start.13 = (bf16[2,272,128]{2,1,0:T(8,128)(2,1)}, bf16[2,272,128]{2,1,0:T(8,128)(2,1)S(1)}, u32[]{:S(2)}, u32[]{:S(2)}) collective-permute-start(bf16[2,272,128]{2,1,0:T(8,128)(2,1)} %fusion.26), channel_id=1, source_target_pairs={{0,4},{4,0},{8,12},{12,8},{16,20},{20,16},{24,28},{28,24},{1,5},{5... | collective-permute-start | bytes 417800 | tf_op jit(solution)/shard_map/ppermute | solution.py:40
  80.5 4.0 copy.100
  84.5 1.6 collective-permute-start.15
  87.2 1.9 collective-permute-start.21
  90.0 2.5 collective-permute-done.16
  92.9 1.4 collective-permute-start.18
  95.3 6.1 %collective-permute-done.18 = bf16[2,2,2,176,128]{4,3,1,2,0:T(8,128)(2,1)S(1)} collective-permute-done((bf16[2,2,2,176,128]{4,3,1,2,0:T(8,128)(2,1)S(1)}, bf16[2,2,2,176,128]{4,3,1,2,0:T(8,128)(2,1)S(1)}, u32[]{:S(2)}, u32[]{:S(2)}) %collective-permute-start.18) | collective-permute-done | bytes 360480 | tf_op jit(solution)/shard_map/ppermute | solution.py:40
  103.6 5.2 %shard_map.501 = (bf16[1024,256]{1,0:T(8,128)(2,1)S(1)}, f32[1024,512]{1,0:T(8,128)}) custom-call(bf16[1024,1024]{1,0:T(8,128)(2,1)} %get-tuple-element.257.normed_ref, bf16[2,8,384,128]{3,2,1,0:T(8,128)(2,1)S(1)} %maximum_maximum_fusion.1.weight_ref), custom_call_target="tpu_custom_call" | custom-call | flops 1 | tf_op jit(solution)/shard_map/pallas_call | solution.py:214
  110.9 5.8 %shard_map.502 = (f32[1024,512]{1,0:T(8,128)}, bf16[16,2,256,128]{3,2,1,0:T(8,128)(2,1)}, bf16[1024,512]{1,0:T(8,128)(2,1)S(1)}) custom-call(bf16[1024,256]{1,0:T(8,128)(2,1)S(1)} %get-tuple-element.265.query_ref.refs_13_, bf16[1024,256]{1,0:T(8,128)(2,1)S(1)} %get-tuple-element.266.key_ref, bf16[1024,512]{1,0:T(8,128)(2,1)S(1)} %get-tuple-element.267.value_ref, ...), custom_call_target="tpu_custom_call" | custom-call | flops 1 | tf_op jit(solution)/shard_map/pallas_call | solution.py:214
  116.8 3.2 collective-permute-done.23
  120.3 3.3 shard_map.503.mine_ref
  125.5 3.4 collective-permute-done.26.refs_6_
  129.7 5.5 %shard_map.504 = (f32[1024,1024]{1,0:T(8,128)}, bf16[1024,1024]{1,0:T(8,128)(2,1)S(1)}) custom-call(bf16[1024,1024]{1,0:T(8,128)(2,1)} %get-tuple-element.251.x_ref, bf16[1024,1024]{1,0:T(8,128)(2,1)} %shard_map.503.mine_ref, bf16[1024,1024]{1,0:T(8,128)(2,1)} %collective-permute-done.25.other_ref, f32[8,1024]{1,0:T(8,128)S(1)} %get-tuple-element.281.gain_ref.refs_9_), custom_call_target="tpu_custom_call" | custom-call | flops 1 | tf_op jit(solution)/shard_map/pallas_call | solution.py:214
  136.7 1.8 collective-permute-start.28
  140.6 18.0 %shard_map.505 = (bf16[768,1024]{1,0:T(8,128)(2,1)}, bf16[768,1024]{1,0:T(8,128)(2,1)}, bf16[768,1024]{1,0:T(8,128)(2,1)}, bf16[2,1024,256]{2,1,0:T(8,128)(2,1)S...) custom-call(s32[3]{0:T(128)S(1)} %pad_add_fusion.place_ref.refs_0_.r, ...), custom_call_target="tpu_custom_call" | custom-call | flops 1 | tf_op jit(solution)/shard_map/pallas_call | solution.py:214
  159.6 2.6 collective-permute-done.28.refs_4_
  165.0 11.7 %shard_map.506 = (bf16[768,512]{1,0:T(8,128)(2,1)S(1)}, bf16[768,512]{1,0:T(8,128)(2,1)}, bf16[768,512]{1,0:T(8,128)(2,1)}, bf16[2,512,256]{2,1,0:T(8,128)(2,1)S...) custom-call(s32[3]{0:T(128)S(1)} %pad_add_fusion.place_ref.refs_0_.r, ...), custom_call_target="tpu_custom_call" | custom-call | flops 1 | tf_op jit(solution)/shard_map/pallas_call | solution.py:214
  179.4 11.5 %shard_map.507 = (bf16[768,512]{1,0:T(8,128)(2,1)S(1)}, bf16[768,512]{1,0:T(8,128)(2,1)}, bf16[768,512]{1,0:T(8,128)(2,1)}, bf16[2,512,256]{2,1,0:T(8,128)(2,1)S...) custom-call(s32[3]{0:T(128)S(1)} %pad_add_fusion.place_ref.refs_0_.r, ...), custom_call_target="tpu_custom_call" | custom-call | flops 1 | tf_op jit(solution)/shard_map/pallas_call | solution.py:214
  197.4 1.7 collective-permute-start.41
  199.1 15.3 %shard_map.508 = bf16[8,3,704,128]{3,2,1,0:T(8,128)(2,1)} custom-call(bf16[1024,1024]{1,0:T(8,128)(2,1)} %copy-done, bf16[1024,1024]{1,0:T(8,128)(2,1)} %copy-done, bf16[1024,1024]{1,0:T(8,128)(2,1)} %get-tuple-element.296.refs_2_.refs_3_, bf16[1024,1024]{1,0:T(8,128)(2,1)} %get-tuple-element.296.refs_2_.refs_3_, ...), custom_call_target="tpu_custom_call" | custom-call | flops 1 | tf_op jit(solution)/shard_map/pallas_call | solution.py:214
  214.5 6.3 %collective-permute-done.41.refs_7_ = bf16[256,1024]{1,0:T(8,128)(2,1)} collective-permute-done((bf16[256,1024]{1,0:T(8,128)(2,1)}, bf16[256,1024]{1,0:T(8,128)(2,1)}, u32[]{:S(2)}, u32[]{:S(2)}) %collective-permute-start.41) | collective-permute-done | bytes 524320 | tf_op jit(solution)/shard_map/ppermute | solution.py:40
  224.5 15.7 %shard_map.509 = (f32[1024,1024]{1,0:T(8,128)}, bf16[1024,1024]{1,0:T(8,128)(2,1)}, f32[1,1024]{1,0:T(1,128)S(1)}, bf16[1024,512]{1,0:T(8,128)(2,1)}, bf16[1024,...) custom-call(s32[3]{0:T(128)S(1)} %pad_add_fusion.place_ref.refs_0_.r, ...), custom_call_target="tpu_custom_call" | custom-call | flops 1 | tf_op jit(solution)/shard_map/pallas_call | solution.py:214
  240.5 9.3 %collective-permute-done.44 = bf16[2,272,128]{2,1,0:T(8,128)(2,1)S(1)} collective-permute-done((bf16[2,272,128]{2,1,0:T(8,128)(2,1)S(1)}, bf16[2,272,128]{2,1,0:T(8,128)(2,1)S(1)}, u32[]{:S(2)}, u32[]{:S(2)}) %collective-permute-start.44) | collective-permute-done | bytes 139296 | tf_op jit(solution)/shard_map/ppermute | solution.py:40
  250.4 7.6 %shard_map.510 = (bf16[1024,256]{1,0:T(8,128)(2,1)S(1)}, f32[1024,256]{1,0:T(8,128)S(1)}, bf16[1024,1024]{1,0:T(8,128)(2,1)}) custom-call(bf16[1024,256]{1,0:T(8,128)(2,1)S(1)} %copy-done.5, bf16[1024,256]{1,0:T(8,128)(2,1)S(1)} %copy-done.7, bf16[1024,512]{1,0:T(8,128)(2,1)S(1)} %get-tuple-element.267.value_ref, ...), custom_call_target="tpu_custom_call" | custom-call | flops 1 | tf_op jit(solution)/shard_map/pallas_call | solution.py:214
  259.6 2.5 collective-permute-start.46
  262.1 6.4 %shard_map.511 = (bf16[8,320,128]{2,1,0:T(8,128)(2,1)S(1)}, bf16[8,320,128]{2,1,0:T(8,128)(2,1)S(1)}, bf16[2,4,320,128]{3,2,1,0:T(8,128)(2,1)S(1)}, bf16[2,4,320,128]{3,2,1,0:T(8,128)(2,1)S(1)}) custom-call(s32[3]{0:T(128)S(1)} %pad_add_fusion.place_ref.refs_0_.refs_2_, bf16[1024,1024]{1,0:T(8,128)(2,1)} %bitcast.227, ...), custom_call_target="tpu_custom_call" | custom-call | flops 1 | tf_op jit(solution)/shard_map/pallas_call | solution.py:214
  272.2 2.9 collective-permute-done.47
  277.6 1.4 collective-permute-start.48
  281.3 15.1 %shard_map.512 = (bf16[1024,256]{1,0:T(8,128)(2,1)S(1)}, bf16[1024,512]{1,0:T(8,128)(2,1)S(1)}, f32[16,1024]{1,0:T(8,128)S(1)}, f32[24,256]{1,0:T(8,128)S(1)}, bf16[1024,1024]{1,0:T(8,128)(2,1)}) custom-call(bf16[1024,256]{1,0:T(8,128)(2,1)S(1)} %copy-done.5, bf16[1024,256]{1,0:T(8,128)(2,1)S(1)} %copy-done.7, bf16[1024,512]{1,0:T(8,128)(2,1)} %copy-done.2, ...), custom_call_target="tpu_custom_call" | custom-call | flops 1 | tf_op jit(solution)/shard_map/pallas_call | solution.py:214
  297.4 4.3 %shard_map.513 = (bf16[8,192,128]{2,1,0:T(8,128)(2,1)S(1)}, bf16[8,192,128]{2,1,0:T(8,128)(2,1)S(1)}, bf16[2,4,192,128]{3,2,1,0:T(8,128)(2,1)S(1)}, bf16[2,4,192,128]{3,2,1,0:T(8,128)(2,1)S(1)}) custom-call(s32[3]{0:T(128)S(1)} %pad_add_fusion.place_ref.refs_0_.refs_2_, bf16[1024,1024]{1,0:T(8,128)(2,1)} %bitcast.228, ...), custom_call_target="tpu_custom_call" | custom-call | flops 1 | tf_op jit(solution)/shard_map/pallas_call | solution.py:214
  307.6 6.6 %shard_map.514 = (f32[2,1024,256]{2,1,0:T(8,128)S(1)}, f32[1,1024]{1,0:T(1,128)S(1)}, f32[16,1024]{1,0:T(8,128)S(1)}) custom-call(s32[3]{0:T(128)S(1)} %pad_add_fusion.place_ref.refs_0_.refs_2_, bf16[1024,1024]{1,0:T(8,128)(2,1)} %get-tuple-element.251.x_ref, f32[1024,1024]{1,0:T(8,128)} %get-tuple-element.384.grad_ref, ...), custom_call_target="tpu_custom_call" | custom-call | flops 1 | tf_op jit(solution)/shard_map/pallas_call | solution.py:214
  316.5 1.4 collective-permute-start.54
  319.1 1.4 collective-permute-start.55
  323.3 1.8 collective-permute-start.62
  326.0 4.0 collective-permute-done.57
  330.8 2.3 collective-permute-start.59
  334.4 2.0 collective-permute-done.62
  336.4 2.2 collective-permute-done.60
  339.7 1.5 collective-permute-start.64
  345.5 4.7 %shard_map.515 = (f32[2,704,128]{2,1,0:T(8,128)}, f32[2,704,128]{2,1,0:T(8,128)}, f32[2,704,128]{2,1,0:T(8,128)}, f32[704,128]{1,0:T(8,128)}, f32[704,128]{1,0:T...) custom-call(bf16[3,704,128]{2,1,0:T(8,128)(2,1)} %bitcast.247, f32[8,128]{1,0:T(8,128)} %broadcast_in_dim.48.refs_1_.refs_6_, ...), custom_call_target="tpu_custom_call" | custom-call | flops 1 | tf_op jit(solution)/shard_map/pallas_call | solution.py:708
  352.1 2.6 collective-permute-start.65
  354.7 1.6 bitcast_add_fusion.5.refs_1_
  356.3 4.4 %collective-permute-done.65 = f32[35,1024]{1,0:T(8,128)S(1)} collective-permute-done((f32[35,1024]{1,0:T(8,128)S(1)}, f32[35,1024]{1,0:T(8,128)S(1)}, u32[]{:S(2)}, u32[]{:S(2)}) %collective-permute-start.65) | collective-permute-done | bytes 143392 | tf_op jit(solution)/shard_map/ppermute | solution.py:40
  364.0 5.6 %collective-permute-done.67 = bf16[640,128]{1,0:T(8,128)(2,1)S(1)} collective-permute-done((bf16[640,128]{1,0:T(8,128)(2,1)S(1)}, bf16[640,128]{1,0:T(8,128)(2,1)S(1)}, u32[]{:S(2)}, u32[]{:S(2)}) %collective-permute-start.67) | collective-permute-done | bytes 163872 | tf_op jit(solution)/shard_map/ppermute | solution.py:40
  370.4 4.2 %shard_map.516 = (f32[128,1,256]{2,1,0:T(1,128)}, f32[128,1,256]{2,1,0:T(1,128)}, f32[128,1,256]{2,1,0:T(1,128)}, f32[128,1,512]{2,1,0:T(1,128)}, f32[128,1,512]...) custom-call(f32[640,128]{1,0:T(8,128)} %copy-done.46, ...), custom_call_target="tpu_custom_call" | custom-call | flops 1 | tf_op jit(solution)/shard_map/pallas_call | solution.py:708
  375.3 1.5 convert_element_type.301
  378.2 2.5 collective-permute-done.69
  382.7 1.7 collective-permute-done.70
  385.6 2.5 collective-permute-done.71
  389.0 1.5 pad_maximum_fusion
  390.4 2.4 collective-permute-done.72
  393.4 3.6 shard_map.517
  (408 shorter events, 92.9 us)
Async XLA Ops:
  7.2 131.2 %all-gather.3.cloned.1.call-start = ((), (), s32[]{:S(2)}) async-start(), calls=%async_computation.2 | async-start | bytes 4866048 | tf_op jit(solution)/shard_map/all_gather | solution.py:827
  10.9 9.1 %collective-permute-start.3 = (bf16[160,128]{1,0:T(8,128)(2,1)S(1)}, bf16[160,128]{1,0:T(8,128)(2,1)S(1)}, u32[]{:S(2)}, u32[]{:S(2)}) collective-permute-start(bf16[160,128]{1,0:T(8,128)(2,1)S(1)} %maximum_maximum_fusion.7), channel_id=1, source_target_pairs={{0,16},{4,20},{8,24},{12,28},{16,0},{20,4},{24,8},{28,12},{1,17},{... | collective-permute-start | bytes 122888 | tf_op jit(solution)/shard_map/ppermute | solution.py:40
  16.9 5.5 %collective-permute-start.5 = (bf16[256,128]{1,0:T(8,128)(2,1)S(1)}, bf16[256,128]{1,0:T(8,128)(2,1)S(1)}, u32[]{:S(2)}, u32[]{:S(2)}) collective-permute-start(bf16[256,128]{1,0:T(8,128)(2,1)S(1)} %pad_maximum_fusion.23), channel_id=1, source_target_pairs={{0,16},{4,20},{8,24},{12,28},{16,0},{20,4},{24,8},{28,12},{1,17},{... | collective-permute-start | bytes 196616 | tf_op jit(solution)/shard_map/ppermute | solution.py:40
  17.0 46.1 %collective-permute-start.1 = (bf16[2,1024,256]{2,1,0:T(8,128)(2,1)S(1)}, bf16[2,1024,256]{2,1,0:T(8,128)(2,1)}, u32[]{:S(2)}, u32[]{:S(2)}) collective-permute-start(bf16[2,1024,256]{2,1,0:T(8,128)(2,1)S(1)} %copy-done.43), channel_id=1, source_target_pairs={{0,1},{1,0},{2,3},{3,2},{4,5},{5,4},{6,7},{7,6},{8,9},{9,8},{10,11... | collective-permute-start | bytes 3145736 | tf_op jit(solution)/shard_map/ppermute | solution.py:40
  18.0 32.0 %collective-permute-start = (bf16[1,1024,256]{2,1,0:T(8,128)(2,1)}, bf16[1,1024,256]{2,1,0:T(8,128)(2,1)S(1)}, u32[]{:S(2)}, u32[]{:S(2)}) collective-permute-start(bf16[1,1024,256]{2,1,0:T(8,128)(2,1)} %constant_dynamic-slice_fusion.4), channel_id=1, source_target_pairs={{0,2},{1,3},{2,0},{3,1},{4,6},{5,7},{6,4},{7,5},{8,10},{9,11},{10,... | collective-permute-start | bytes 1572872 | tf_op jit(solution)/shard_map/ppermute | solution.py:40
  19.7 256.8 %reduce-scatter.2.cloned.1.call-start = ((), (), s32[]{:S(2)}) async-start(), calls=%async_computation.1 | async-start | bytes 4866048 | tf_op jit(solution)/shard_map/reduce_scatter | solution.py:1123
  20.1 5.0 %collective-permute-start.4 = (bf16[2,160,128]{2,1,0:T(8,128)(2,1)S(1)}, bf16[2,160,128]{2,1,0:T(8,128)(2,1)S(1)}, u32[]{:S(2)}, u32[]{:S(2)}) collective-permute-start(bf16[2,160,128]{2,1,0:T(8,128)(2,1)S(1)} %pad_maximum_fusion.22), channel_id=1, source_target_pairs={{0,8},{4,12},{8,0},{12,4},{16,24},{20,28},{24,16},{28,20},{1,9},{5... | collective-permute-start | bytes 245768 | tf_op jit(solution)/shard_map/ppermute | solution.py:40
  22.5 5.5 %collective-permute-start.6 = (bf16[2,256,128]{2,1,0:T(8,128)(2,1)S(1)}, bf16[2,256,128]{2,1,0:T(8,128)(2,1)S(1)}, u32[]{:S(2)}, u32[]{:S(2)}) collective-permute-start(bf16[2,256,128]{2,1,0:T(8,128)(2,1)S(1)} %pad_maximum_fusion.21), channel_id=1, source_target_pairs={{0,8},{4,12},{8,0},{12,4},{16,24},{20,28},{24,16},{28,20},{1,9},{5... | collective-permute-start | bytes 393224 | tf_op jit(solution)/shard_map/ppermute | solution.py:40
  28.1 7.9 %collective-permute-start.8 = (bf16[2,2,160,128]{3,2,0,1:T(8,128)(2,1)S(1)}, bf16[2,2,160,128]{3,2,0,1:T(8,128)(2,1)S(1)}, u32[]{:S(2)}, u32[]{:S(2)}) collective-permute-start(bf16[2,2,160,128]{3,2,0,1:T(8,128)(2,1)S(1)} %pad_maximum_fusion.19), channel_id=1, source_target_pairs={{0,2},{1,3},{2,0},{3,1},{4,6},{5,7},{6,4},{7,5},{8,10},{9,11},{10,... | collective-permute-start | bytes 491528 | tf_op jit(solution)/shard_map/ppermute | solution.py:40
  31.7 18.2 %collective-permute-start.7 = (bf16[640,128]{1,0:T(8,128)(2,1)S(1)}, bf16[640,128]{1,0:T(8,128)(2,1)S(1)}, u32[]{:S(2)}, u32[]{:S(2)}) collective-permute-start(bf16[640,128]{1,0:T(8,128)(2,1)S(1)} %pad_maximum_fusion.18), channel_id=1, source_target_pairs={{0,16},{4,20},{8,24},{12,28},{16,0},{20,4},{24,8},{28,12},{1,17},{... | collective-permute-start | bytes 491528 | tf_op jit(solution)/shard_map/ppermute | solution.py:40
  33.2 14.8 %collective-permute-start.10 = (bf16[2,2,256,128]{3,2,0,1:T(8,128)(2,1)S(1)}, bf16[2,2,256,128]{3,2,0,1:T(8,128)(2,1)S(1)}, u32[]{:S(2)}, u32[]{:S(2)}) collective-permute-start(bf16[2,2,256,128]{3,2,0,1:T(8,128)(2,1)S(1)} %pad_maximum_fusion.12), channel_id=1, source_target_pairs={{0,4},{4,0},{8,12},{12,8},{16,20},{20,16},{24,28},{28,24},{1,5},{5... | collective-permute-start | bytes 786440 | tf_op jit(solution)/shard_map/ppermute | solution.py:40
  36.1 25.2 %collective-permute-start.9 = (bf16[2,2,2,160,128]{4,3,1,2,0:T(8,128)(2,1)S(1)}, bf16[2,2,2,160,128]{4,3,1,2,0:T(8,128)(2,1)S(1)}, u32[]{:S(2)}, u32[]{:S(2)}) collective-permute-start(bf16[2,2,2,160,128]{4,3,1,2,0:T(8,128)(2,1)S(1)} %pad_maximum_fusion.10), channel_id=1, source_target_pairs={{0,4},{4,0},{8,12},{12,8},{16,20},{20,16},{24,28},{28,24},{1,5},{5... | collective-permute-start | bytes 983048 | tf_op jit(solution)/shard_map/ppermute | solution.py:40
  48.1 13.5 %collective-permute-start.11 = (bf16[2,2,2,256,128]{4,3,0,1,2:T(8,128)(2,1)S(1)}, bf16[2,2,2,256,128]{4,3,0,1,2:T(8,128)(2,1)S(1)}, u32[]{:S(2)}, u32[]{:S(2)}) collective-permute-start(bf16[2,2,2,256,128]{4,3,0,1,2:T(8,128)(2,1)S(1)} %pad_maximum_fusion.5), channel_id=1, source_target_pairs={{0,2},{1,3},{2,0},{3,1},{4,6},{5,7},{6,4},{7,5},{8,10},{9,11},{10,... | collective-permute-start | bytes 1572872 | tf_op jit(solution)/shard_map/ppermute | solution.py:40
  50.0 13.2 %collective-permute-start.2 = (bf16[1,1024,256]{2,1,0:T(8,128)(2,1)S(1)}, bf16[1,1024,256]{2,1,0:T(8,128)(2,1)S(1)}, u32[]{:S(2)}, u32[]{:S(2)}) collective-permute-start(bf16[1,1024,256]{2,1,0:T(8,128)(2,1)S(1)} %collective-permute-done.moved_ref), channel_id=1, source_target_pairs={{0,1},{1,0},{2,3},{3,2},{4,5},{5,4},{6,7},{7,6},{8,9},{9,8},{10,11... | collective-permute-start | bytes 1572872 | tf_op jit(solution)/shard_map/ppermute | solution.py:40
  61.5 13.8 %collective-permute-start.12 = (bf16[2,640,128]{2,1,0:T(8,128)(2,1)S(1)}, bf16[2,640,128]{2,1,0:T(8,128)(2,1)S(1)}, u32[]{:S(2)}, u32[]{:S(2)}) collective-permute-start(bf16[2,640,128]{2,1,0:T(8,128)(2,1)S(1)} %pad_maximum_fusion.9), channel_id=1, source_target_pairs={{0,8},{4,12},{8,0},{12,4},{16,24},{20,28},{24,16},{28,20},{1,9},{5... | collective-permute-start | bytes 983048 | tf_op jit(solution)/shard_map/ppermute | solution.py:40
  76.3 9.9 %collective-permute-start.13 = (bf16[2,272,128]{2,1,0:T(8,128)(2,1)}, bf16[2,272,128]{2,1,0:T(8,128)(2,1)S(1)}, u32[]{:S(2)}, u32[]{:S(2)}) collective-permute-start(bf16[2,272,128]{2,1,0:T(8,128)(2,1)} %fusion.26), channel_id=1, source_target_pairs={{0,4},{4,0},{8,12},{12,8},{16,20},{20,16},{24,28},{28,24},{1,5},{5... | collective-permute-start | bytes 417800 | tf_op jit(solution)/shard_map/ppermute | solution.py:40
  84.5 5.5 %collective-permute-start.15 = (bf16[2,2,176,128]{3,2,0,1:T(8,128)(2,1)S(1)}, bf16[2,2,176,128]{3,2,0,1:T(8,128)(2,1)S(1)}, u32[]{:S(2)}, u32[]{:S(2)}) collective-permute-start(bf16[2,2,176,128]{3,2,0,1:T(8,128)(2,1)S(1)} %fusion.22), channel_id=1, source_target_pairs={{0,2},{1,3},{2,0},{3,1},{4,6},{5,7},{6,4},{7,5},{8,10},{9,11},{10,... | collective-permute-start | bytes 540680 | tf_op jit(solution)/shard_map/ppermute | solution.py:40
  86.1 6.3 %collective-permute-start.16 = (bf16[2,2,208,128]{3,2,0,1:T(8,128)(2,1)S(1)}, bf16[2,2,208,128]{3,2,0,1:T(8,128)(2,1)S(1)}, u32[]{:S(2)}, u32[]{:S(2)}) collective-permute-start(bf16[2,2,208,128]{3,2,0,1:T(8,128)(2,1)S(1)} %fusion.18), channel_id=1, source_target_pairs={{0,4},{4,0},{8,12},{12,8},{16,20},{20,16},{24,28},{28,24},{1,5},{5... | collective-permute-start | bytes 638984 | tf_op jit(solution)/shard_map/ppermute | solution.py:40
  86.5 6.0 %collective-permute-start.14 = (bf16[2,272,128]{2,1,0:T(8,128)(2,1)S(1)}, bf16[2,272,128]{2,1,0:T(8,128)(2,1)S(1)}, u32[]{:S(2)}, u32[]{:S(2)}) collective-permute-start(bf16[2,272,128]{2,1,0:T(8,128)(2,1)S(1)} %maximum_maximum_fusion.3), channel_id=1, source_target_pairs={{0,8},{4,12},{8,0},{12,4},{16,24},{20,28},{24,16},{28,20},{1,9},{5... | collective-permute-start | bytes 417800 | tf_op jit(solution)/shard_map/ppermute | solution.py:40
  86.6 22.2 %collective-permute-start.20 = (bf16[2,2,112,128]{3,2,0,1:T(8,128)(2,1)S(1)}, bf16[2,2,112,128]{3,2,0,1:T(8,128)(2,1)S(1)}, u32[]{:S(2)}, u32[]{:S(2)}) collective-permute-start(bf16[2,2,112,128]{3,2,0,1:T(8,128)(2,1)S(1)} %fusion.28), channel_id=1, source_target_pairs={{0,2},{1,3},{2,0},{3,1},{4,6},{5,7},{6,4},{7,5},{8,10},{9,11},{10,... | collective-permute-start | bytes 344072 | tf_op jit(solution)/shard_map/ppermute | solution.py:40
  87.2 21.6 %collective-permute-start.21 = (bf16[2,2,144,128]{3,2,0,1:T(8,128)(2,1)S(1)}, bf16[2,2,144,128]{3,2,0,1:T(8,128)(2,1)S(1)}, u32[]{:S(2)}, u32[]{:S(2)}) collective-permute-start(bf16[2,2,144,128]{3,2,0,1:T(8,128)(2,1)S(1)} %pad_maximum_fusion.20), channel_id=1, source_target_pairs={{0,4},{4,0},{8,12},{12,8},{16,20},{20,16},{24,28},{28,24},{1,5},{5... | collective-permute-start | bytes 442376 | tf_op jit(solution)/shard_map/ppermute | solution.py:40
  92.6 9.0 %collective-permute-start.19 = (bf16[2,2,2,208,128]{4,3,0,1,2:T(8,128)(2,1)S(1)}, bf16[2,2,2,208,128]{4,3,0,1,2:T(8,128)(2,1)S(1)}, u32[]{:S(2)}, u32[]{:S(2)}) collective-permute-start(bf16[2,2,2,208,128]{4,3,0,1,2:T(8,128)(2,1)S(1)} %pad_maximum_fusion.7), channel_id=1, source_target_pairs={{0,2},{1,3},{2,0},{3,1},{4,6},{5,7},{6,4},{7,5},{8,10},{9,11},{10,... | collective-permute-start | bytes 1277960 | tf_op jit(solution)/shard_map/ppermute | solution.py:40
  92.9 8.4 %collective-permute-start.18 = (bf16[2,2,2,176,128]{4,3,1,2,0:T(8,128)(2,1)S(1)}, bf16[2,2,2,176,128]{4,3,1,2,0:T(8,128)(2,1)S(1)}, u32[]{:S(2)}, u32[]{:S(2)}) collective-permute-start(bf16[2,2,2,176,128]{4,3,1,2,0:T(8,128)(2,1)S(1)} %pad_maximum_fusion.8), channel_id=1, source_target_pairs={{0,4},{4,0},{8,12},{12,8},{16,20},{20,16},{24,28},{28,24},{1,5},{5... | collective-permute-start | bytes 1081352 | tf_op jit(solution)/shard_map/ppermute | solution.py:40
  94.6 14.2 %collective-permute-start.17 = (bf16[2,272,128]{2,1,0:T(8,128)(2,1)S(1)}, bf16[2,272,128]{2,1,0:T(8,128)(2,1)S(1)}, u32[]{:S(2)}, u32[]{:S(2)}) collective-permute-start(bf16[2,272,128]{2,1,0:T(8,128)(2,1)S(1)} %maximum_maximum_fusion.4), channel_id=1, source_target_pairs={{0,16},{4,20},{8,24},{12,28},{16,0},{20,4},{24,8},{28,12},{1,17},{... | collective-permute-start | bytes 417800 | tf_op jit(solution)/shard_map/ppermute | solution.py:40
  102.7 14.1 %collective-permute-start.24 = (bf16[1024,256]{1,0:T(8,128)(2,1)S(1)}, bf16[1024,256]{1,0:T(8,128)(2,1)S(1)}, u32[]{:S(2)}, u32[]{:S(2)}) collective-permute-start(bf16[1024,256]{1,0:T(8,128)(2,1)S(1)} %copy-done.55), channel_id=1, source_target_pairs={{0,2},{1,3},{2,0},{3,1},{4,6},{5,7},{6,4},{7,5},{8,10},{9,11},{10,... | collective-permute-start | bytes 1572872 | tf_op jit(solution)/shard_map/ppermute | solution.py:40
  109.0 11.0 %collective-permute-start.23 = (bf16[2,2,2,144,128]{4,3,0,1,2:T(8,128)(2,1)S(1)}, bf16[2,2,2,144,128]{4,3,0,1,2:T(8,128)(2,1)S(1)}, u32[]{:S(2)}, u32[]{:S(2)}) collective-permute-start(bf16[2,2,2,144,128]{4,3,0,1,2:T(8,128)(2,1)S(1)} %pad_maximum_fusion.11), channel_id=1, source_target_pairs={{0,2},{1,3},{2,0},{3,1},{4,6},{5,7},{6,4},{7,5},{8,10},{9,11},{10,... | collective-permute-start | bytes 884744 | tf_op jit(solution)/shard_map/ppermute | solution.py:40
  110.2 6.6 %collective-permute-start.22 = (bf16[2,2,2,112,128]{4,3,1,2,0:T(8,128)(2,1)S(1)}, bf16[2,2,2,112,128]{4,3,1,2,0:T(8,128)(2,1)S(1)}, u32[]{:S(2)}, u32[]{:S(2)}) collective-permute-start(bf16[2,2,2,112,128]{4,3,1,2,0:T(8,128)(2,1)S(1)} %pad_maximum_fusion.13), channel_id=1, source_target_pairs={{0,4},{4,0},{8,12},{12,8},{16,20},{20,16},{24,28},{28,24},{1,5},{5... | collective-permute-start | bytes 688136 | tf_op jit(solution)/shard_map/ppermute | solution.py:40
  123.6 6.1 %collective-permute-start.25 = (bf16[1024,1024]{1,0:T(8,128)(2,1)}, bf16[1024,1024]{1,0:T(8,128)(2,1)}, u32[]{:S(2)}, u32[]{:S(2)}) collective-permute-start(bf16[1024,1024]{1,0:T(8,128)(2,1)} %shard_map.503.mine_ref), channel_id=1, source_target_pairs={{0,1},{1,0},{2,3},{3,2},{4,5},{5,4},{6,7},{7,6},{8,9},{9,8},{10,11... | collective-permute-start | bytes 6291464 | tf_op jit(solution)/shard_map/ppermute | solution.py:40
  123.6 5.3 %collective-permute-start.26 = (bf16[1024,256]{1,0:T(8,128)(2,1)S(1)}, bf16[1024,256]{1,0:T(8,128)(2,1)S(1)}, u32[]{:S(2)}, u32[]{:S(2)}) collective-permute-start(bf16[1024,256]{1,0:T(8,128)(2,1)S(1)} %collective-permute-done.24.refs_4_), channel_id=1, source_target_pairs={{0,1},{1,0},{2,3},{3,2},{4,5},{5,4},{6,7},{7,6},{8,9},{9,8},{10,11... | collective-permute-start | bytes 1572872 | tf_op jit(solution)/shard_map/ppermute | solution.py:40
  124.2 14.3 %collective-permute-start.29 = (bf16[2,1024,256]{2,1,0:T(8,128)(2,1)}, bf16[2,1024,256]{2,1,0:T(8,128)(2,1)}, u32[]{:S(2)}, u32[]{:S(2)}) collective-permute-start(bf16[2,1024,256]{2,1,0:T(8,128)(2,1)} %refs_3_.6), channel_id=1, source_target_pairs={{0,1},{1,0},{2,3},{3,2},{4,5},{5,4},{6,7},{7,6},{8,9},{9,8},{10,11... | collective-permute-start | bytes 3145736 | tf_op jit(solution)/shard_map/ppermute | solution.py:40
  136.4 23.2 %collective-permute-start.27 = (bf16[256,1024]{1,0:T(8,128)(2,1)}, bf16[256,1024]{1,0:T(8,128)(2,1)}, u32[]{:S(2)}, u32[]{:S(2)}) collective-permute-start(bf16[256,1024]{1,0:T(8,128)(2,1)} %get-tuple-element.480), channel_id=1, source_target_pairs={{0,2},{1,3},{2,0},{3,1},{4,6},{5,7},{6,4},{7,5},{8,10},{9,11},{10,... | collective-permute-start | bytes 1572872 | tf_op jit(solution)/shard_map/ppermute | solution.py:40
  136.7 25.5 %collective-permute-start.28 = (bf16[1024,256]{1,0:T(8,128)(2,1)}, bf16[1024,256]{1,0:T(8,128)(2,1)}, u32[]{:S(2)}, u32[]{:S(2)}) collective-permute-start(bf16[1024,256]{1,0:T(8,128)(2,1)} %get-tuple-element.285), channel_id=1, source_target_pairs={{0,2},{1,3},{2,0},{3,1},{4,6},{5,7},{6,4},{7,5},{8,10},{9,11},{10,... | collective-permute-start | bytes 1572872 | tf_op jit(solution)/shard_map/ppermute | solution.py:40
  162.7 14.8 %collective-permute-start.30 = (bf16[256,1024]{1,0:T(8,128)(2,1)S(1)}, bf16[256,1024]{1,0:T(8,128)(2,1)S(1)}, u32[]{:S(2)}, u32[]{:S(2)}) collective-permute-start(bf16[256,1024]{1,0:T(8,128)(2,1)S(1)} %copy-done.56), channel_id=1, source_target_pairs={{0,2},{1,3},{2,0},{3,1},{4,6},{5,7},{6,4},{7,5},{8,10},{9,11},{10,... | collective-permute-start | bytes 1572872 | tf_op jit(solution)/shard_map/ppermute | solution.py:40
  163.0 51.5 %collective-permute-start.34 = (bf16[1024,1024]{1,0:T(8,128)(2,1)}, bf16[1024,1024]{1,0:T(8,128)(2,1)}, u32[]{:S(2)}, u32[]{:S(2)}) collective-permute-start(bf16[1024,1024]{1,0:T(8,128)(2,1)} %get-tuple-element.297.refs_3_), channel_id=1, source_target_pairs={{0,1},{1,0},{2,3},{3,2},{4,5},{5,4},{6,7},{7,6},{8,9},{9,8},{10,11... | collective-permute-start | bytes 6291464 | tf_op jit(solution)/shard_map/ppermute | solution.py:40
  177.6 18.8 %collective-permute-start.35 = (bf16[2,1024,256]{2,1,0:T(8,128)(2,1)}, bf16[2,1024,256]{2,1,0:T(8,128)(2,1)S(1)}, u32[]{:S(2)}, u32[]{:S(2)}) collective-permute-start(bf16[2,1024,256]{2,1,0:T(8,128)(2,1)} %copy-done.38), channel_id=1, source_target_pairs={{0,1},{1,0},{2,3},{3,2},{4,5},{5,4},{6,7},{7,6},{8,9},{9,8},{10,11... | collective-permute-start | bytes 3145736 | tf_op jit(solution)/shard_map/ppermute | solution.py:40
  179.1 14.6 %collective-permute-start.38 = (bf16[256,1024]{1,0:T(8,128)(2,1)S(1)}, bf16[256,1024]{1,0:T(8,128)(2,1)S(1)}, u32[]{:S(2)}, u32[]{:S(2)}) collective-permute-start(bf16[256,1024]{1,0:T(8,128)(2,1)S(1)} %dynamic-slice_bitcast_fusion.1), channel_id=1, source_target_pairs={{0,1},{1,0},{2,3},{3,2},{4,5},{5,4},{6,7},{7,6},{8,9},{9,8},{10,11... | collective-permute-start | bytes 1572872 | tf_op jit(solution)/shard_map/ppermute | solution.py:40
  193.5 21.0 %collective-permute-start.36 = (bf16[2,512,256]{2,1,0:T(8,128)(2,1)}, bf16[2,512,256]{2,1,0:T(8,128)(2,1)}, u32[]{:S(2)}, u32[]{:S(2)}) collective-permute-start(bf16[2,512,256]{2,1,0:T(8,128)(2,1)} %get-tuple-element.323), channel_id=1, source_target_pairs={{0,1},{1,0},{2,3},{3,2},{4,5},{5,4},{6,7},{7,6},{8,9},{9,8},{10,11... | collective-permute-start | bytes 1572872 | tf_op jit(solution)/shard_map/ppermute | solution.py:40
  193.7 20.8 %collective-permute-start.37 = (bf16[2,512,256]{2,1,0:T(8,128)(2,1)}, bf16[2,512,256]{2,1,0:T(8,128)(2,1)}, u32[]{:S(2)}, u32[]{:S(2)}) collective-permute-start(bf16[2,512,256]{2,1,0:T(8,128)(2,1)} %get-tuple-element.324), channel_id=1, source_target_pairs={{0,1},{1,0},{2,3},{3,2},{4,5},{5,4},{6,7},{7,6},{8,9},{9,8},{10,11... | collective-permute-start | bytes 1572872 | tf_op jit(solution)/shard_map/ppermute | solution.py:40
  195.1 19.4 %collective-permute-start.39 = (bf16[256,1024]{1,0:T(8,128)(2,1)}, bf16[256,1024]{1,0:T(8,128)(2,1)S(1)}, u32[]{:S(2)}, u32[]{:S(2)}) collective-permute-start(bf16[256,1024]{1,0:T(8,128)(2,1)} %fusion.3), channel_id=1, source_target_pairs={{0,2},{1,3},{2,0},{3,1},{4,6},{5,7},{6,4},{7,5},{8,10},{9,11},{10,... | collective-permute-start | bytes 1572872 | tf_op jit(solution)/shard_map/ppermute | solution.py:40
  197.4 23.4 %collective-permute-start.41 = (bf16[256,1024]{1,0:T(8,128)(2,1)}, bf16[256,1024]{1,0:T(8,128)(2,1)}, u32[]{:S(2)}, u32[]{:S(2)}) collective-permute-start(bf16[256,1024]{1,0:T(8,128)(2,1)} %fusion.2), channel_id=1, source_target_pairs={{0,2},{1,3},{2,0},{3,1},{4,6},{5,7},{6,4},{7,5},{8,10},{9,11},{10,... | collective-permute-start | bytes 1572872 | tf_op jit(solution)/shard_map/ppermute | solution.py:40
  240.4 9.4 %collective-permute-start.44 = (bf16[2,272,128]{2,1,0:T(8,128)(2,1)S(1)}, bf16[2,272,128]{2,1,0:T(8,128)(2,1)S(1)}, u32[]{:S(2)}, u32[]{:S(2)}) collective-permute-start(bf16[2,272,128]{2,1,0:T(8,128)(2,1)S(1)} %fusion.27), channel_id=1, source_target_pairs={{0,4},{4,0},{8,12},{12,8},{16,20},{20,16},{24,28},{28,24},{1,5},{5... | collective-permute-start | bytes 417800 | tf_op jit(solution)/shard_map/ppermute | solution.py:40
  250.0 9.3 %collective-permute-start.45 = (bf16[2,272,128]{2,1,0:T(8,128)(2,1)S(1)}, bf16[2,272,128]{2,1,0:T(8,128)(2,1)S(1)}, u32[]{:S(2)}, u32[]{:S(2)}) collective-permute-start(bf16[2,272,128]{2,1,0:T(8,128)(2,1)S(1)} %maximum_maximum_fusion.5), channel_id=1, source_target_pairs={{0,8},{4,12},{8,0},{12,4},{16,24},{20,28},{24,16},{28,20},{1,9},{5... | collective-permute-start | bytes 417800 | tf_op jit(solution)/shard_map/ppermute | solution.py:40
  250.1 25.0 %collective-permute-start.47 = (bf16[2,1024,256]{2,1,0:T(8,128)(2,1)}, bf16[2,1024,256]{2,1,0:T(8,128)(2,1)}, u32[]{:S(2)}, u32[]{:S(2)}) collective-permute-start(bf16[2,1024,256]{2,1,0:T(8,128)(2,1)} %get-tuple-element.358), channel_id=1, source_target_pairs={{0,2},{1,3},{2,0},{3,1},{4,6},{5,7},{6,4},{7,5},{8,10},{9,11},{10,... | collective-permute-start | bytes 3145736 | tf_op jit(solution)/shard_map/ppermute | solution.py:40
  259.6 12.5 %collective-permute-start.46 = (bf16[2,272,128]{2,1,0:T(8,128)(2,1)S(1)}, bf16[2,272,128]{2,1,0:T(8,128)(2,1)S(1)}, u32[]{:S(2)}, u32[]{:S(2)}) collective-permute-start(bf16[2,272,128]{2,1,0:T(8,128)(2,1)S(1)} %maximum_maximum_fusion.6), channel_id=1, source_target_pairs={{0,16},{4,20},{8,24},{12,28},{16,0},{20,4},{24,8},{28,12},{1,17},{... | collective-permute-start | bytes 417800 | tf_op jit(solution)/shard_map/ppermute | solution.py:40
  277.6 18.8 %collective-permute-start.48 = (bf16[2,2,2,320,128]{4,3,0,1,2:T(8,128)(2,1)S(1)}, bf16[2,2,2,320,128]{4,3,0,1,2:T(8,128)(2,1)S(1)}, u32[]{:S(2)}, u32[]{:S(2)}) collective-permute-start(bf16[2,2,2,320,128]{4,3,0,1,2:T(8,128)(2,1)S(1)} %copy.108), channel_id=1, source_target_pairs={{0,2},{1,3},{2,0},{3,1},{4,6},{5,7},{6,4},{7,5},{8,10},{9,11},{10,... | collective-permute-start | bytes 1966088 | tf_op jit(solution)/shard_map/ppermute | solution.py:40
  279.1 17.3 %collective-permute-start.49 = (bf16[2,2,2,320,128]{4,3,1,2,0:T(8,128)(2,1)S(1)}, bf16[2,2,2,320,128]{4,3,1,2,0:T(8,128)(2,1)S(1)}, u32[]{:S(2)}, u32[]{:S(2)}) collective-permute-start(bf16[2,2,2,320,128]{4,3,1,2,0:T(8,128)(2,1)S(1)} %copy.109), channel_id=1, source_target_pairs={{0,4},{4,0},{8,12},{12,8},{16,20},{20,16},{24,28},{28,24},{1,5},{5... | collective-permute-start | bytes 1966088 | tf_op jit(solution)/shard_map/ppermute | solution.py:40
  296.4 5.4 %collective-permute-start.50 = (bf16[1024,1024]{1,0:T(8,128)(2,1)}, bf16[1024,1024]{1,0:T(8,128)(2,1)S(1)}, u32[]{:S(2)}, u32[]{:S(2)}) collective-permute-start(bf16[1024,1024]{1,0:T(8,128)(2,1)} %get-tuple-element.372.mine_ref), channel_id=1, source_target_pairs={{0,1},{1,0},{2,3},{3,2},{4,5},{5,4},{6,7},{7,6},{8,9},{9,8},{10,11... | collective-permute-start | bytes 6291464 | tf_op jit(solution)/shard_map/ppermute | solution.py:40
  297.4 4.4 %collective-permute-start.51 = (f32[16,1024]{1,0:T(8,128)S(1)}, f32[16,1024]{1,0:T(8,128)S(1)}, u32[]{:S(2)}, u32[]{:S(2)}) collective-permute-start(f32[16,1024]{1,0:T(8,128)S(1)} %get-tuple-element.373), channel_id=1, source_target_pairs={{0,1},{1,0},{2,3},{3,2},{4,5},{5,4},{6,7},{7,6},{8,9},{9,8},{10,11... | collective-permute-start | bytes 196616 | tf_op jit(solution)/shard_map/ppermute | solution.py:40
  302.7 11.8 %collective-permute-start.52 = (bf16[2,2,2,192,128]{4,3,0,1,2:T(8,128)(2,1)}, bf16[2,2,2,192,128]{4,3,0,1,2:T(8,128)(2,1)}, u32[]{:S(2)}, u32[]{:S(2)}) collective-permute-start(bf16[2,2,2,192,128]{4,3,0,1,2:T(8,128)(2,1)} %copy.110), channel_id=1, source_target_pairs={{0,2},{1,3},{2,0},{3,1},{4,6},{5,7},{6,4},{7,5},{8,10},{9,11},{10,... | collective-permute-start | bytes 1179656 | tf_op jit(solution)/shard_map/ppermute | solution.py:40
  303.7 11.6 %collective-permute-start.53 = (bf16[2,2,2,192,128]{4,3,1,2,0:T(8,128)(2,1)}, bf16[2,2,2,192,128]{4,3,1,2,0:T(8,128)(2,1)}, u32[]{:S(2)}, u32[]{:S(2)}) collective-permute-start(bf16[2,2,2,192,128]{4,3,1,2,0:T(8,128)(2,1)} %copy.111), channel_id=1, source_target_pairs={{0,4},{4,0},{8,12},{12,8},{16,20},{20,16},{24,28},{28,24},{1,5},{5... | collective-permute-start | bytes 1179656 | tf_op jit(solution)/shard_map/ppermute | solution.py:40
  316.5 9.5 %collective-permute-start.54 = (bf16[2,2,192,128]{3,2,0,1:T(8,128)(2,1)S(1)}, bf16[2,2,192,128]{3,2,0,1:T(8,128)(2,1)S(1)}, u32[]{:S(2)}, u32[]{:S(2)}) collective-permute-start(bf16[2,2,192,128]{3,2,0,1:T(8,128)(2,1)S(1)} %fusion.19), channel_id=1, source_target_pairs={{0,4},{4,0},{8,12},{12,8},{16,20},{20,16},{24,28},{28,24},{1,5},{5... | collective-permute-start | bytes 589832 | tf_op jit(solution)/shard_map/ppermute | solution.py:40
  319.1 6.9 %collective-permute-start.55 = (bf16[2,2,192,128]{3,2,0,1:T(8,128)(2,1)S(1)}, bf16[2,2,192,128]{3,2,0,1:T(8,128)(2,1)S(1)}, u32[]{:S(2)}, u32[]{:S(2)}) collective-permute-start(bf16[2,2,192,128]{3,2,0,1:T(8,128)(2,1)S(1)} %fusion.20), channel_id=1, source_target_pairs={{0,2},{1,3},{2,0},{3,1},{4,6},{5,7},{6,4},{7,5},{8,10},{9,11},{10,... | collective-permute-start | bytes 589832 | tf_op jit(solution)/shard_map/ppermute | solution.py:40
  321.7 12.8 %collective-permute-start.61 = (bf16[2,2,320,128]{3,2,0,1:T(8,128)(2,1)}, bf16[2,2,320,128]{3,2,0,1:T(8,128)(2,1)}, u32[]{:S(2)}, u32[]{:S(2)}) collective-permute-start(bf16[2,2,320,128]{3,2,0,1:T(8,128)(2,1)} %fusion.15), channel_id=1, source_target_pairs={{0,4},{4,0},{8,12},{12,8},{16,20},{20,16},{24,28},{28,24},{1,5},{5... | collective-permute-start | bytes 983048 | tf_op jit(solution)/shard_map/ppermute | solution.py:40
  322.9 7.1 %collective-permute-start.57 = (f32[35,1024]{1,0:T(8,128)S(1)}, f32[35,1024]{1,0:T(8,128)S(1)}, u32[]{:S(2)}, u32[]{:S(2)}) collective-permute-start(f32[35,1024]{1,0:T(8,128)S(1)} %fusion.33), channel_id=1, source_target_pairs={{0,2},{1,3},{2,0},{3,1},{4,6},{5,7},{6,4},{7,5},{8,10},{9,11},{10,... | collective-permute-start | bytes 430088 | tf_op jit(solution)/shard_map/ppermute | solution.py:40
  323.3 13.1 %collective-permute-start.62 = (bf16[2,2,320,128]{3,2,0,1:T(8,128)(2,1)S(1)}, bf16[2,2,320,128]{3,2,0,1:T(8,128)(2,1)}, u32[]{:S(2)}, u32[]{:S(2)}) collective-permute-start(bf16[2,2,320,128]{3,2,0,1:T(8,128)(2,1)S(1)} %fusion.16), channel_id=1, source_target_pairs={{0,2},{1,3},{2,0},{3,1},{4,6},{5,7},{6,4},{7,5},{8,10},{9,11},{10,... | collective-permute-start | bytes 983048 | tf_op jit(solution)/shard_map/ppermute | solution.py:40
  330.8 7.7 %collective-permute-start.59 = (bf16[2,384,128]{2,1,0:T(8,128)(2,1)}, bf16[2,384,128]{2,1,0:T(8,128)(2,1)}, u32[]{:S(2)}, u32[]{:S(2)}) collective-permute-start(bf16[2,384,128]{2,1,0:T(8,128)(2,1)} %fusion.21), channel_id=1, source_target_pairs={{0,8},{4,12},{8,0},{12,4},{16,24},{20,28},{24,16},{28,20},{1,9},{5... | collective-permute-start | bytes 589832 | tf_op jit(solution)/shard_map/ppermute | solution.py:40
  333.2 5.4 %collective-permute-start.60 = (f32[35,1024]{1,0:T(8,128)S(1)}, f32[35,1024]{1,0:T(8,128)S(1)}, u32[]{:S(2)}, u32[]{:S(2)}) collective-permute-start(f32[35,1024]{1,0:T(8,128)S(1)} %add.317), channel_id=1, source_target_pairs={{0,4},{4,0},{8,12},{12,8},{16,20},{20,16},{24,28},{28,24},{1,5},{5... | collective-permute-start | bytes 430088 | tf_op jit(solution)/shard_map/ppermute | solution.py:40
  339.6 11.6 %collective-permute-start.63 = (bf16[384,128]{1,0:T(8,128)(2,1)S(1)}, bf16[384,128]{1,0:T(8,128)(2,1)}, u32[]{:S(2)}, u32[]{:S(2)}) collective-permute-start(bf16[384,128]{1,0:T(8,128)(2,1)S(1)} %fusion.29), channel_id=1, source_target_pairs={{0,16},{4,20},{8,24},{12,28},{16,0},{20,4},{24,8},{28,12},{1,17},{... | collective-permute-start | bytes 294920 | tf_op jit(solution)/shard_map/ppermute | solution.py:40
  339.7 11.5 %collective-permute-start.64 = (f32[35,1024]{1,0:T(8,128)S(1)}, f32[35,1024]{1,0:T(8,128)}, u32[]{:S(2)}, u32[]{:S(2)}) collective-permute-start(f32[35,1024]{1,0:T(8,128)S(1)} %add.325), channel_id=1, source_target_pairs={{0,8},{4,12},{8,0},{12,4},{16,24},{20,28},{24,16},{28,20},{1,9},{5... | collective-permute-start | bytes 430088 | tf_op jit(solution)/shard_map/ppermute | solution.py:40
  344.2 16.4 %collective-permute-start.66 = (bf16[2,640,128]{2,1,0:T(8,128)(2,1)}, bf16[2,640,128]{2,1,0:T(8,128)(2,1)}, u32[]{:S(2)}, u32[]{:S(2)}) collective-permute-start(bf16[2,640,128]{2,1,0:T(8,128)(2,1)} %fusion.17), channel_id=1, source_target_pairs={{0,8},{4,12},{8,0},{12,4},{16,24},{20,28},{24,16},{28,20},{1,9},{5... | collective-permute-start | bytes 983048 | tf_op jit(solution)/shard_map/ppermute | solution.py:40
  350.2 34.3 %collective-permute-start.58 = (bf16[1024,256]{1,0:T(8,128)(2,1)}, bf16[1024,256]{1,0:T(8,128)(2,1)}, u32[]{:S(2)}, u32[]{:S(2)}) collective-permute-start(bf16[1024,256]{1,0:T(8,128)(2,1)} %fusion.9), channel_id=1, source_target_pairs={{0,2},{1,3},{2,0},{3,1},{4,6},{5,7},{6,4},{7,5},{8,10},{9,11},{10,... | collective-permute-start | bytes 1572872 | tf_op jit(solution)/shard_map/ppermute | solution.py:40
  352.1 8.6 %collective-permute-start.65 = (f32[35,1024]{1,0:T(8,128)S(1)}, f32[35,1024]{1,0:T(8,128)S(1)}, u32[]{:S(2)}, u32[]{:S(2)}) collective-permute-start(f32[35,1024]{1,0:T(8,128)S(1)} %add.329), channel_id=1, source_target_pairs={{0,16},{4,20},{8,24},{12,28},{16,0},{20,4},{24,8},{28,12},{1,17},{... | collective-permute-start | bytes 430088 | tf_op jit(solution)/shard_map/ppermute | solution.py:40
  361.8 7.8 %collective-permute-start.67 = (bf16[640,128]{1,0:T(8,128)(2,1)S(1)}, bf16[640,128]{1,0:T(8,128)(2,1)S(1)}, u32[]{:S(2)}, u32[]{:S(2)}) collective-permute-start(bf16[640,128]{1,0:T(8,128)(2,1)S(1)} %fusion.23), channel_id=1, source_target_pairs={{0,16},{4,20},{8,24},{12,28},{16,0},{20,4},{24,8},{28,12},{1,17},{... | collective-permute-start | bytes 491528 | tf_op jit(solution)/shard_map/ppermute | solution.py:40
  388.2 4.6 %collective-permute-start.72 = (f32[32,128]{1,0:T(8,128)S(1)}, f32[32,128]{1,0:T(8,128)S(1)}, u32[]{:S(2)}, u32[]{:S(2)}) collective-permute-start(f32[32,128]{1,0:T(8,128)S(1)} %add.341), channel_id=1, source_target_pairs={{0,16},{4,20},{8,24},{12,28},{16,0},{20,4},{24,8},{28,12},{1,17},{... | collective-permute-start | bytes 49160 | tf_op jit(solution)/shard_map/ppermute | solution.py:40
  (79 other events, 759.0 us)
Sparse Core Ops, SparseCore 0:
  19.8 64.2 all-gather.2
  220.9 55.5 reduce-scatter.1

commit v5 on v4

--- a/solution.py
+++ b/solution.py
@@ -145,7 +145,7 @@
 TILE = 256
 LANES = 128
 VALUES = 256
-VMEM_LIMIT = 50 * 1024 * 1024
+VMEM_LIMIT = 47 * 1024 * 1024
 WHOLE_LIMIT = 60 * 1024 * 1024
 
 
@@ -325,8 +325,9 @@
         state_ref[h] = state_ref[h] * decay[:, k] + mul(values[h], rest[:, k], 0, 0)
 
 
-def project_late_kernel(normed_ref, weight_ref, query_ref, gate_ref):
+def project_late_kernel(normed_ref, weight_ref, query_ref, gate_ref, normed_t_ref):
     normed = normed_ref[...]
+    normed_t_ref[...] = normed.T
     for h, (k, v) in enumerate(zip(heads(LANES), heads(VALUES))):
         query_ref[:, k] = to_half(mul(normed, model_rows(weight_ref, h, 0)))
         gate_ref[:, v] = mul(normed, model_rows(weight_ref, h, LANES, 2))
@@ -371,25 +372,37 @@
         mixed_ref[:, v] = mixed
 
 
-def mix_kernel(mixed_ref, weight_ref, part_ref, output_ref):
+def mix_kernel(mixed_ref, weight_ref, part_ref, mixed_t_ref, output_ref):
     @first_step
     def _():
         load_output(weight_ref, output_ref)
 
-    part_ref[...] = to_half(mul(mixed_ref[...], output_ref[...].reshape(2 * VALUES, -1)))
-
-
-def residual_kernel(x_ref, mine_ref, other_ref, gain_ref, residual_ref, normed_ref):
+    mixed = mixed_ref[...]
+    mixed_t_ref[...] = mixed.T
+    part_ref[...] = to_half(mul(mixed, output_ref[...].reshape(2 * VALUES, -1)))
+
+
+def residual_kernel(place_ref, x_ref, mine_ref, other_ref, gain_ref, residual_ref, normed_ref, *piece_refs):
     residual = to_float(x_ref[...]) + (to_float(mine_ref[...]) + to_float(other_ref[...]))
     scale = lax.rsqrt(jnp.mean(residual * residual, axis=1, keepdims=True) + eps_norm)
     residual_ref[...] = residual
-    normed_ref[...] = to_half(residual * scale * gain_ref[1:2])
+    normed = to_half(residual * scale * gain_ref[1:2])
+    normed_ref[...] = normed
+    for p, piece_ref in enumerate(piece_refs):
+
+        @pl.when(pl.program_id(0) == 2 * place_ref[1] + p)
+        def _(piece_ref=piece_ref):
+            piece_ref[...] = normed
 
 
 def feed_forward_kernel(
     ring, other, place_ref, normed_ref, beside_normed_ref, cot_ref, moved_ref, beside_ref, beside_moved_ref, weight_ref,
-    hidden_ref, gate_grad_ref, up_grad_ref, keep_ref, give_ref, rows_grad_ref, cot_out_ref, normed_out_ref, all_ref,
+    hidden_ref, gate_grad_ref, up_grad_ref, keep_ref, give_ref, *refs,
 ):
+    if other:
+        keep_rows_ref, give_rows_ref, cot_out_ref, normed_out_ref, all_ref = refs
+    else:
+        rows_grad_ref, cot_out_ref, all_ref = refs
     width = weight_ref.shape[2]
 
     @first_step
@@ -418,7 +431,19 @@
     gate_grad_ref[...] = gate_grad.T
     up_grad = to_half(hidden_grad * silu)
     up_grad_ref[...] = up_grad.T
-    rows_grad_ref[...] = to_half(mul(gate_grad, all_ref[0]) + mul(up_grad, all_ref[1]))
+    rows_grad = to_half(mul(gate_grad, all_ref[0]) + mul(up_grad, all_ref[1]))
+    if other:
+
+        @pl.when(pl.program_id(0) == place_ref[1])
+        def _():
+            keep_rows_ref[...] = rows_grad
+
+        @pl.when(pl.program_id(0) != place_ref[1])
+        def _():
+            give_rows_ref[...] = rows_grad
+
+    else:
+        rows_grad_ref[...] = rows_grad
     out = to_half(mul(hidden, all_ref[2]))
     columns = keep_ref.shape[2]
     for b in range(2):
@@ -937,7 +962,11 @@
             project_late_kernel,
             steps,
             [(normed, 0), (gate_all, None)],
-            [((segment, 2 * key_width), half, 0), ((segment, 2 * value_width), full, 0)],
+            [
+                ((segment, 2 * key_width), half, 0),
+                ((segment, 2 * value_width), full, 0),
+                ((model_width, segment), half, 1),
+            ],
         )
 
     beside_scan = {}
@@ -946,9 +975,6 @@
         if not aligned:
             return message
         if number == 0:
-            beside_scan["normed"] = normed.T
-            message, beside_scan["normed"] = tie((message, beside_scan["normed"]))
-        if number == 1:
             message, moved, cot_given[0] = tie((message, gate_moved, cot_given[0]))
             beside_scan["gate"] = second_links(links["gate"], moved)
             beside_scan["output"] = first_links(links["output"])
@@ -967,14 +993,12 @@
     state_in = scan_blocks(block_decay, block_state, False, beside_forward)
     if aligned:
         gate_all = beside_scan["gate"]
-        queries, gate_values = beside_scan["out"]
+        queries, gate_values, normed_t = beside_scan["out"]
         cot_own_moved = beside_scan["cot"]
-        normed_t = beside_scan["normed"]
     else:
         gate_all, output_all = (late_all[:, :, : 3 * LANES], late_all[:, :, 3 * LANES :])
-        queries, gate_values = project_late(gate_all)
+        queries, gate_values, normed_t = project_late(gate_all)
         cot_own_moved = swap(cot_given[0], *across)
-        normed_t = normed.T
     recurrent, starts, mixed_half = call(
         forward_kernel,
         steps,
@@ -1000,26 +1024,24 @@
             (recurrent, mixed_half, output_moved, cot_own_moved)
         )
         output_all = whole_links(output_sides, output_moved)
-    (mixer_part,) = call(
+    mixer_part, mixed_t = call(
         mix_kernel,
         steps,
         [(mixed_half, 0), (output_all, None)],
-        [((segment, model_width), half, 0)],
+        [((segment, model_width), half, 0), ((2 * value_width, segment), half, 1)],
         scratch=[pltpu.VMEM((2, value_width, model_width), jnp.bfloat16)],
     )
     mixer_beside, cot_own_beside = (swap(mixer_part, "head", 1), swap(cot_own_moved, "head", 1))
-    mixer_beside, cot_own_beside, mixed_t = tie((mixer_beside, cot_own_beside, mixed_half.T))
-    residual, normed_two = call(
+    mixer_beside, cot_own_beside = tie((mixer_beside, cot_own_beside))
+    residual, normed_two, *pieces = call(
         residual_kernel,
         steps,
-        [(input_half, 0), (mixer_part, 0), (mixer_beside, 0), (gains, None)],
-        [((segment, model_width), full, 0), ((segment, model_width), half, 0)],
-    )
-
-    def piece_of(rows_of_all, p):
-        return lax.dynamic_slice_in_dim(rows_of_all, core * half_segment + p * TILE, TILE, 0)
-
-    moved = [swap(piece_of(normed_two, p), *across) for p in range(2)]
+        [(place, "smem"), (input_half, 0), (mixer_part, 0), (mixer_beside, 0), (gains, None)],
+        [((segment, model_width), full, 0), ((segment, model_width), half, 0)]
+        + [((TILE, model_width), half, None)] * 2,
+    )
+
+    moved = [swap(piece, *across) for piece in pieces]
     normed_two, cot_given[1] = tie((normed_two, cot_given[1]))
     cot_other_moved = swap(cot_given[1], *across)
 
@@ -1035,35 +1057,38 @@
             + [(ffn_all, None)],
             [((ffn_padded, width), half, 1)] * 3
             + [((2, width, column_count), half, 1)] * 2
-            + [((width, model_width), half, 0)] * 2
-            + ([((width, model_width), half, 0)] if other else [((TILE, model_width), half, None)]),
+            + ([((TILE, model_width), half, None)] * 2 if other else [((width, model_width), half, 0)])
+            + [((width, model_width), half, 0)] * (2 if other else 1),
             scratch=[pltpu.VMEM((3, ffn_padded, model_width), jnp.bfloat16)],
         )
 
     own = feed_forward(None, (normed_two, 0), (place, "smem"), (cot_own_moved, cot_own_beside))
     moved[0], cot_other_moved, own = tie((moved[0], cot_other_moved, own))
     cots = (cot_other_moved, swap(cot_other_moved, "head", 1))
-    others, homes = [], []
+    others, sums, homes = [], [], []
     for p in range(2):
         if p:
-            moved[p], others[0] = tie((moved[p], others[0]))
+            moved[p], sums[0] = tie((moved[p], sums[0]))
+            homes.append(swap(sums[0], *across))
         others.append(feed_forward(p, (moved[p], None), (swap(moved[p], "head", 1), None), cots))
-        other_rows = others[p][5].reshape(2, TILE, model_width)
-        other_sum = to_half(
-            to_float(pick(other_rows, core)) + to_float(swap(pick(other_rows, 1 - core), "head", 1))
-        )
-        homes.append(swap(other_sum, *across))
+        if not p:
+            moved[1], others[0] = tie((moved[1], others[0]))
+        sums.append(to_half(to_float(others[p][5]) + to_float(swap(others[p][6], "head", 1))))
+    homes[0], others[1] = tie((homes[0], others[1]))
+    homes.append(swap(sums[1], *across))
     (ffn_grad,) = call(
         feed_forward_weights_kernel,
         4,
         [
             entry
-            for rows_of_all, group in ((normed_two, own), (others[0][7], others[0]), (others[1][7], others[1]))
+            for rows_of_all, cot_of_all, group in (
+                (normed_two, own[6], own), (others[0][8], others[0][7], others[0]), (others[1][8], others[1][7], others[1])
+            )
             for entry in (
                 (rows_of_all, 1, blocks, lambda i: ring_block(2 * i)),
                 (rows_of_all, 1, blocks, lambda i: ring_block(2 * i + 1)),
-                (group[6], 1, blocks, lambda i: ring_block(2 * i)),
-                (group[6], 1, blocks, lambda i: ring_block(2 * i + 1)),
+                (cot_of_all, 1, blocks, lambda i: ring_block(2 * i)),
+                (cot_of_all, 1, blocks, lambda i: ring_block(2 * i + 1)),
                 (group[1], None),
                 (group[2], None),
                 (group[0], None),

time: 409 us -> 406 us (level)
  starting transfers between devices: 63.8 us -> 72.2 us
  Pallas kernels: 155 us -> 150 us
    ppermute x73, starting transfers between devices: 63.7 us -> 72.1 us  [swap(): lax.ppermute(value_entries, axis, [(i, i ^ bit) for i in range(peers)])]
    pallas_call x15, Pallas kernels: 143 us -> 137 us  [call(): pl.pallas_call(body, grid=(steps,), in_specs=[spec(entry[0].shape, *entry...]
    unnamed x141 -> x165, local copies, waits for them, and re-layouts: 18 us -> 22.9 us
  transfers between devices with their start and end apart: 75 -> 75, of which waited for: 36 -> 36; matrix products, arithmetic and copies ran while one was open for 11% -> 8% of each run, Pallas kernels for 38% -> 36%
where the time goes in v5:
time: 406 us; the launch traced here: 402 us
  Pallas kernels  150 us (37%)
  waiting for transfers between devices  100 us (25%)
  starting transfers between devices  72.2 us (18%)
  local copies, waits for them, and re-layouts  36.4 us (9%)
  other arithmetic  27.1 us (7%)
  between operations  16.2 us (4%)
    pallas_call x15, Pallas kernels, call(): pl.pallas_call(body, grid=(steps,), in_specs=[spec(entry[0].shape, *entry...  137 us
    ppermute x73, waiting for transfers between devices, swap(): lax.ppermute(value_entries, axis, [(i, i ^ bit) for i in range(peers)])  96.6 us
    ppermute x73, starting transfers between devices, swap(): lax.ppermute(value_entries, axis, [(i, i ^ bit) for i in range(peers)])  72.1 us
    unnamed x165, local copies, waits for them, and re-layouts  22.9 us
    pallas_call x3, Pallas kernels, whole_call(): pl.pallas_call(body, out_shape=[jax.ShapeDtypeStruct(shape, jnp.float32)...  12.4 us
  transfers between devices with their start and end apart: 75, of which 36 were waited for; matrix products, arithmetic and copies ran while one was open for 8% of the time, Pallas kernels for 36%

profile of v5, /device:TPU:0, one launch (start us, length us, event | category | flops | bytes accessed | tf_op | source)
XLA Modules:
  0.0 401.6 jit_solution(11025378491940095080)
XLA Ops:
  11.5 4.0 %collective-permute-start.3 = (bf16[160,128]{1,0:T(8,128)(2,1)}, bf16[160,128]{1,0:T(8,128)(2,1)S(1)}, u32[]{:S(2)}, u32[]{:S(2)}) collective-permute-start(bf16[160,128]{1,0:T(8,128)(2,1)} %maximum_maximum_fusion.7), channel_id=1, source_target_pairs={{0,16},{4,20},{8,24},{12,28},{16,0},{20,4},{24,8},{28,12},{1,17},{... | collective-permute-start | bytes 122888 | tf_op jit(solution)/shard_map/ppermute | solution.py:40
  18.5 1.7 collective-permute-start
  20.6 1.6 collective-permute-start.4
  25.7 2.9 collective-permute-done.6
  30.9 1.5 collective-permute-start.7
  32.4 1.5 collective-permute-start.10
  33.9 2.7 collective-permute-done.8
  36.6 1.8 collective-permute-start.9
  38.4 8.7 %collective-permute-done.10 = bf16[2,2,256,128]{3,2,0,1:T(8,128)(2,1)S(1)} collective-permute-done((bf16[2,2,256,128]{3,2,0,1:T(8,128)(2,1)S(1)}, bf16[2,2,256,128]{3,2,0,1:T(8,128)(2,1)S(1)}, u32[]{:S(2)}, u32[]{:S(2)}) %collective-permute-start.10) | collective-permute-done | bytes 262176 | tf_op jit(solution)/shard_map/ppermute | solution.py:40
  47.3 1.8 collective-permute-start.11
  49.2 11.3 %collective-permute-done.9 = bf16[2,2,2,160,128]{4,3,1,2,0:T(8,128)(2,1)S(1)} collective-permute-done((bf16[2,2,2,160,128]{4,3,1,2,0:T(8,128)(2,1)S(1)}, bf16[2,2,2,160,128]{4,3,1,2,0:T(8,128)(2,1)S(1)}, u32[]{:S(2)}, u32[]{:S(2)}) %collective-permute-start.9) | collective-permute-done | bytes 327712 | tf_op jit(solution)/shard_map/ppermute | solution.py:40
  62.5 10.0 %shard_map.500 = (bf16[1024,1024]{1,0:T(8,128)(2,1)}, bf16[1024,1024]{1,0:T(8,128)(2,1)}, bf16[1024,256]{1,0:T(8,128)(2,1)S(1)}, bf16[1024,512]{1,0:T(8,128)(2,1...) custom-call(s32[3]{0:T(128)S(1)} %pad_add_fusion.place_ref.refs_0_.r, ...), custom_call_target="tpu_custom_call" | custom-call | flops 1 | tf_op jit(solution)/shard_map/pallas_call | solution.py:214
  72.5 2.0 collective-permute-done.12
  74.8 4.4 %collective-permute-start.13 = (bf16[2,272,128]{2,1,0:T(8,128)(2,1)S(1)}, bf16[2,272,128]{2,1,0:T(8,128)(2,1)S(1)}, u32[]{:S(2)}, u32[]{:S(2)}) collective-permute-start(bf16[2,272,128]{2,1,0:T(8,128)(2,1)S(1)} %fusion.24), channel_id=1, source_target_pairs={{0,4},{4,0},{8,12},{12,8},{16,20},{20,16},{24,28},{28,24},{1,5},{5... | collective-permute-start | bytes 417800 | tf_op jit(solution)/shard_map/ppermute | solution.py:40
  79.2 1.6 collective-permute-start.14
  81.4 2.0 collective-permute-start.21
  83.5 2.5 collective-permute-done.13
  86.0 4.6 %collective-permute-done.15 = bf16[2,2,208,128]{3,2,0,1:T(8,128)(2,1)S(1)} collective-permute-done((bf16[2,2,208,128]{3,2,0,1:T(8,128)(2,1)S(1)}, bf16[2,2,208,128]{3,2,0,1:T(8,128)(2,1)S(1)}, u32[]{:S(2)}, u32[]{:S(2)}) %collective-permute-start.15) | collective-permute-done | bytes 213024 | tf_op jit(solution)/shard_map/ppermute | solution.py:40
  91.0 1.6 collective-permute-start.19
  93.2 2.7 collective-permute-done.16
  95.9 1.6 collective-permute-start.24
  97.8 2.6 collective-permute-done.18
  100.4 4.2 %collective-permute-start.17 = (bf16[2,272,128]{2,1,0:T(8,128)(2,1)S(1)}, bf16[2,272,128]{2,1,0:T(8,128)(2,1)S(1)}, u32[]{:S(2)}, u32[]{:S(2)}) collective-permute-start(bf16[2,272,128]{2,1,0:T(8,128)(2,1)S(1)} %maximum_maximum_fusion.4), channel_id=1, source_target_pairs={{0,16},{4,20},{8,24},{12,28},{16,0},{20,4},{24,8},{28,12},{1,17},{... | collective-permute-start | bytes 417800 | tf_op jit(solution)/shard_map/ppermute | solution.py:40
  105.1 4.9 %shard_map.501 = (bf16[1024,256]{1,0:T(8,128)(2,1)S(1)}, f32[1024,512]{1,0:T(8,128)S(1)}, bf16[1024,1024]{1,0:T(8,128)(2,1)S(1)}) custom-call(bf16[1024,1024]{1,0:T(8,128)(2,1)} %get-tuple-element.276.normed_ref, bf16[2,8,384,128]{3,2,1,0:T(8,128)(2,1)S(1)} %maximum_maximum_fusion.1.weight_ref), custom_call_target="tpu_custom_call" | custom-call | flops 1 | tf_op jit(solution)/shard_map/pallas_call | solution.py:214
  114.2 5.3 %shard_map.502 = (f32[1024,512]{1,0:T(8,128)S(1)}, bf16[16,2,256,128]{3,2,1,0:T(8,128)(2,1)}, bf16[1024,512]{1,0:T(8,128)(2,1)S(1)}) custom-call(bf16[1024,256]{1,0:T(8,128)(2,1)S(1)} %get-tuple-element.282.query_ref.refs_13_, bf16[1024,256]{1,0:T(8,128)(2,1)S(1)} %get-tuple-element.283.key_ref, bf16[1024,512]{1,0:T(8,128)(2,1)S(1)} %get-tuple-element.284.value_ref, ...), custom_call_target="tpu_custom_call" | custom-call | flops 1 | tf_op jit(solution)/shard_map/pallas_call | solution.py:214
  121.0 2.3 shard_map.503
  124.9 4.3 %collective-permute-done.26.refs_6_ = bf16[1024,256]{1,0:T(8,128)(2,1)S(1)} collective-permute-done((bf16[1024,256]{1,0:T(8,128)(2,1)S(1)}, bf16[1024,256]{1,0:T(8,128)(2,1)S(1)}, u32[]{:S(2)}, u32[]{:S(2)}) %collective-permute-start.26) | collective-permute-done | bytes 524320 | tf_op jit(solution)/shard_map/ppermute | solution.py:40
  130.0 1.4 copy-done.61
  131.5 5.5 %shard_map.504 = (f32[1024,1024]{1,0:T(8,128)}, bf16[1024,1024]{1,0:T(8,128)(2,1)S(1)}, bf16[256,1024]{1,0:T(8,128)(2,1)}, bf16[256,1024]{1,0:T(8,128)(2,1)S(1)}) custom-call(s32[3]{0:T(128)S(1)} %pad_add_fusion.place_ref.refs_0_.refs_2_, bf16[1024,1024]{1,0:T(8,128)(2,1)S(1)} %copy-done.7, bf16[1024,1024]{1,0:T(8,128)(2,1)} %copy-done.23, ...), custom_call_target="tpu_custom_call" | custom-call | flops 1 | tf_op jit(solution)/shard_map/pallas_call | solution.py:214
  143.6 17.8 %shard_map.505 = (bf16[768,1024]{1,0:T(8,128)(2,1)S(1)}, bf16[768,1024]{1,0:T(8,128)(2,1)}, bf16[768,1024]{1,0:T(8,128)(2,1)}, bf16[2,1024,256]{2,1,0:T(8,128)(2...) custom-call(s32[3]{0:T(128)S(1)} %pad_add_fusion.place_ref.refs_0_.refs_2_, ...), custom_call_target="tpu_custom_call" | custom-call | flops 1 | tf_op jit(solution)/shard_map/pallas_call | solution.py:214
  167.5 12.7 %shard_map.506 = (bf16[768,512]{1,0:T(8,128)(2,1)S(1)}, bf16[768,512]{1,0:T(8,128)(2,1)S(1)}, bf16[768,512]{1,0:T(8,128)(2,1)S(1)}, bf16[2,512,256]{2,1,0:T(8,12...) custom-call(s32[3]{0:T(128)S(1)} %pad_add_fusion.place_ref.refs_0_.r, ...), custom_call_target="tpu_custom_call" | custom-call | flops 1 | tf_op jit(solution)/shard_map/pallas_call | solution.py:214
  180.8 1.4 collective-permute-done.33
  184.0 2.0 collective-permute-done.35.refs_2_
  186.0 12.5 %shard_map.507 = (bf16[768,512]{1,0:T(8,128)(2,1)S(1)}, bf16[768,512]{1,0:T(8,128)(2,1)S(1)}, bf16[768,512]{1,0:T(8,128)(2,1)S(1)}, bf16[2,512,256]{2,1,0:T(8,12...) custom-call(s32[3]{0:T(128)S(1)} %pad_add_fusion.place_ref.refs_0_.r, ...), custom_call_target="tpu_custom_call" | custom-call | flops 1 | tf_op jit(solution)/shard_map/pallas_call | solution.py:214
  202.8 14.9 %shard_map.508 = bf16[8,3,704,128]{3,2,1,0:T(8,128)(2,1)} custom-call(bf16[1024,1024]{1,0:T(8,128)(2,1)} %copy-done, bf16[1024,1024]{1,0:T(8,128)(2,1)} %copy-done, bf16[1024,1024]{1,0:T(8,128)(2,1)} %get-tuple-element.315.refs_2_.refs_3_, bf16[1024,1024]{1,0:T(8,128)(2,1)} %get-tuple-element.315.refs_2_.refs_3_, ...), custom_call_target="tpu_custom_call" | custom-call | flops 1 | tf_op jit(solution)/shard_map/pallas_call | solution.py:214
  220.8 14.8 %shard_map.509 = (f32[1024,1024]{1,0:T(8,128)}, bf16[1024,1024]{1,0:T(8,128)(2,1)}, f32[1,1024]{1,0:T(1,128)S(1)}, bf16[1024,512]{1,0:T(8,128)(2,1)S(1)}, bf16[1...) custom-call(s32[3]{0:T(128)S(1)} %pad_add_fusion.place_ref.refs_0_.r, ...), custom_call_target="tpu_custom_call" | custom-call | flops 1 | tf_op jit(solution)/shard_map/pallas_call | solution.py:214
  235.8 1.7 collective-permute-start.44
  237.5 7.7 %collective-permute-done.44 = bf16[2,272,128]{2,1,0:T(8,128)(2,1)S(1)} collective-permute-done((bf16[2,272,128]{2,1,0:T(8,128)(2,1)S(1)}, bf16[2,272,128]{2,1,0:T(8,128)(2,1)S(1)}, u32[]{:S(2)}, u32[]{:S(2)}) %collective-permute-start.44) | collective-permute-done | bytes 139296 | tf_op jit(solution)/shard_map/ppermute | solution.py:40
  245.9 6.9 %shard_map.510 = (bf16[1024,256]{1,0:T(8,128)(2,1)S(1)}, f32[1024,256]{1,0:T(8,128)S(1)}, bf16[1024,1024]{1,0:T(8,128)(2,1)}) custom-call(bf16[1024,256]{1,0:T(8,128)(2,1)S(1)} %copy-done.13, bf16[1024,256]{1,0:T(8,128)(2,1)S(1)} %copy-done.15, bf16[1024,512]{1,0:T(8,128)(2,1)S(1)} %get-tuple-element.284.value_ref, f32[1024,256]{1,0:T(8,128)S(1)} %copy-done.3, ...), custom_call_target="tpu_custom_call" | custom-call | flops 1 | tf_op jit(solution)/shard_map/pallas_call | solution.py:214
  252.8 1.9 collective-permute-done.45
  255.0 1.7 collective-permute-start.46
  256.7 5.5 %shard_map.511 = (bf16[8,320,128]{2,1,0:T(8,128)(2,1)S(1)}, bf16[8,320,128]{2,1,0:T(8,128)(2,1)S(1)}, bf16[2,4,320,128]{3,2,1,0:T(8,128)(2,1)S(1)}, bf16[2,4,320,128]{3,2,1,0:T(8,128)(2,1)S(1)}) custom-call(s32[3]{0:T(128)S(1)} %pad_add_fusion.place_ref.refs_0_.refs_2_, bf16[1024,1024]{1,0:T(8,128)(2,1)} %copy-done.9, ...), custom_call_target="tpu_custom_call" | custom-call | flops 1 | tf_op jit(solution)/shard_map/pallas_call | solution.py:214
  265.6 1.7 collective-permute-done.46
  267.3 3.2 collective-permute-done.47
  270.5 3.4 reduce-scatter.2.cloned.1.call-done
  278.5 14.9 %shard_map.512 = (bf16[1024,256]{1,0:T(8,128)(2,1)S(1)}, bf16[1024,512]{1,0:T(8,128)(2,1)S(1)}, f32[16,1024]{1,0:T(8,128)S(1)}, f32[24,256]{1,0:T(8,128)S(1)}, bf16[1024,1024]{1,0:T(8,128)(2,1)}) custom-call(bf16[1024,256]{1,0:T(8,128)(2,1)S(1)} %copy-done.13, bf16[1024,256]{1,0:T(8,128)(2,1)S(1)} %copy-done.15, ...), custom_call_target="tpu_custom_call" | custom-call | flops 1 | tf_op jit(solution)/shard_map/pallas_call | solution.py:214
  295.1 3.5 shard_map.513
  304.5 1.6 copy-done.22
  306.0 5.8 %shard_map.514 = (f32[2,1024,256]{2,1,0:T(8,128)S(1)}, f32[1,1024]{1,0:T(1,128)S(1)}, f32[16,1024]{1,0:T(8,128)S(1)}) custom-call(s32[3]{0:T(128)S(1)} %pad_add_fusion.place_ref.refs_0_.refs_2_, bf16[1024,1024]{1,0:T(8,128)(2,1)S(1)} %copy-done.8, f32[1024,1024]{1,0:T(8,128)} %get-tuple-element.418.grad_ref, bf16[1024,1024]{1,0:T(8,128)(2,1)S(1)} %copy-done.22, ...), custom_call_target="tpu_custom_call" | custom-call | flops 1 | tf_op jit(solution)/shard_map/pallas_call | solution.py:214
  323.4 3.4 collective-permute-done.57
  327.7 2.7 collective-permute-start.59
  331.5 1.7 collective-permute-done.62
  333.2 2.7 collective-permute-done.60
  338.0 1.5 collective-permute-start.64
  342.9 4.6 %shard_map.515 = (f32[2,704,128]{2,1,0:T(8,128)}, f32[2,704,128]{2,1,0:T(8,128)}, f32[2,704,128]{2,1,0:T(8,128)}, f32[704,128]{1,0:T(8,128)}, f32[704,128]{1,0:T...) custom-call(bf16[3,704,128]{2,1,0:T(8,128)(2,1)} %bitcast.226, f32[8,128]{1,0:T(8,128)} %broadcast_in_dim.48.refs_1_.refs_6_, ...), custom_call_target="tpu_custom_call" | custom-call | flops 1 | tf_op jit(solution)/shard_map/pallas_call | solution.py:733
  349.3 2.9 collective-permute-start.65
  352.9 4.8 %collective-permute-done.65 = f32[35,1024]{1,0:T(8,128)S(1)} collective-permute-done((f32[35,1024]{1,0:T(8,128)S(1)}, f32[35,1024]{1,0:T(8,128)S(1)}, u32[]{:S(2)}, u32[]{:S(2)}) %collective-permute-start.65) | collective-permute-done | bytes 143392 | tf_op jit(solution)/shard_map/ppermute | solution.py:40
  362.3 5.0 %collective-permute-done.67 = bf16[640,128]{1,0:T(8,128)(2,1)S(1)} collective-permute-done((bf16[640,128]{1,0:T(8,128)(2,1)S(1)}, bf16[640,128]{1,0:T(8,128)(2,1)S(1)}, u32[]{:S(2)}, u32[]{:S(2)}) %collective-permute-start.67) | collective-permute-done | bytes 163872 | tf_op jit(solution)/shard_map/ppermute | solution.py:40
  368.0 4.2 %shard_map.516 = (f32[128,1,256]{2,1,0:T(1,128)}, f32[128,1,256]{2,1,0:T(1,128)}, f32[128,1,256]{2,1,0:T(1,128)}, f32[128,1,512]{2,1,0:T(1,128)}, f32[128,1,512]...) custom-call(f32[640,128]{1,0:T(8,128)} %copy-done.62, ...), custom_call_target="tpu_custom_call" | custom-call | flops 1 | tf_op jit(solution)/shard_map/pallas_call | solution.py:733
  375.7 1.8 select_convert_fusion.1
  382.1 3.6 collective-permute-done.71
  386.3 1.5 pad_maximum_fusion
  387.7 2.6 collective-permute-done.72
  390.9 3.6 shard_map.517
  (427 shorter events, 100.2 us)
Async XLA Ops:
  7.2 133.9 %all-gather.3.cloned.1.call-start = ((), (), s32[]{:S(2)}) async-start(), calls=%async_computation.2 | async-start | bytes 4866048 | tf_op jit(solution)/shard_map/all_gather | solution.py:852
  11.5 9.0 %collective-permute-start.3 = (bf16[160,128]{1,0:T(8,128)(2,1)}, bf16[160,128]{1,0:T(8,128)(2,1)S(1)}, u32[]{:S(2)}, u32[]{:S(2)}) collective-permute-start(bf16[160,128]{1,0:T(8,128)(2,1)} %maximum_maximum_fusion.7), channel_id=1, source_target_pairs={{0,16},{4,20},{8,24},{12,28},{16,0},{20,4},{24,8},{28,12},{1,17},{... | collective-permute-start | bytes 122888 | tf_op jit(solution)/shard_map/ppermute | solution.py:40
  17.5 5.5 %collective-permute-start.5 = (bf16[256,128]{1,0:T(8,128)(2,1)S(1)}, bf16[256,128]{1,0:T(8,128)(2,1)S(1)}, u32[]{:S(2)}, u32[]{:S(2)}) collective-permute-start(bf16[256,128]{1,0:T(8,128)(2,1)S(1)} %pad_maximum_fusion.23), channel_id=1, source_target_pairs={{0,16},{4,20},{8,24},{12,28},{16,0},{20,4},{24,8},{28,12},{1,17},{... | collective-permute-start | bytes 196616 | tf_op jit(solution)/shard_map/ppermute | solution.py:40
  17.6 44.7 %collective-permute-start.1 = (bf16[2,1024,256]{2,1,0:T(8,128)(2,1)S(1)}, bf16[2,1024,256]{2,1,0:T(8,128)(2,1)}, u32[]{:S(2)}, u32[]{:S(2)}) collective-permute-start(bf16[2,1024,256]{2,1,0:T(8,128)(2,1)S(1)} %copy-done.20), channel_id=1, source_target_pairs={{0,1},{1,0},{2,3},{3,2},{4,5},{5,4},{6,7},{7,6},{8,9},{9,8},{10,11... | collective-permute-start | bytes 3145736 | tf_op jit(solution)/shard_map/ppermute | solution.py:40
  18.5 30.6 %collective-permute-start = (bf16[1,1024,256]{2,1,0:T(8,128)(2,1)}, bf16[1,1024,256]{2,1,0:T(8,128)(2,1)S(1)}, u32[]{:S(2)}, u32[]{:S(2)}) collective-permute-start(bf16[1,1024,256]{2,1,0:T(8,128)(2,1)} %constant_dynamic-slice_fusion.2), channel_id=1, source_target_pairs={{0,2},{1,3},{2,0},{3,1},{4,6},{5,7},{6,4},{7,5},{8,10},{9,11},{10,... | collective-permute-start | bytes 1572872 | tf_op jit(solution)/shard_map/ppermute | solution.py:40
  20.3 253.7 %reduce-scatter.2.cloned.1.call-start = ((), (), s32[]{:S(2)}) async-start(), calls=%async_computation.1 | async-start | bytes 4866048 | tf_op jit(solution)/shard_map/reduce_scatter | solution.py:1148
  20.6 5.0 %collective-permute-start.4 = (bf16[2,160,128]{2,1,0:T(8,128)(2,1)S(1)}, bf16[2,160,128]{2,1,0:T(8,128)(2,1)S(1)}, u32[]{:S(2)}, u32[]{:S(2)}) collective-permute-start(bf16[2,160,128]{2,1,0:T(8,128)(2,1)S(1)} %pad_maximum_fusion.22), channel_id=1, source_target_pairs={{0,8},{4,12},{8,0},{12,4},{16,24},{20,28},{24,16},{28,20},{1,9},{5... | collective-permute-start | bytes 245768 | tf_op jit(solution)/shard_map/ppermute | solution.py:40
  23.1 5.5 %collective-permute-start.6 = (bf16[2,256,128]{2,1,0:T(8,128)(2,1)S(1)}, bf16[2,256,128]{2,1,0:T(8,128)(2,1)S(1)}, u32[]{:S(2)}, u32[]{:S(2)}) collective-permute-start(bf16[2,256,128]{2,1,0:T(8,128)(2,1)S(1)} %pad_maximum_fusion.21), channel_id=1, source_target_pairs={{0,8},{4,12},{8,0},{12,4},{16,24},{20,28},{24,16},{28,20},{1,9},{5... | collective-permute-start | bytes 393224 | tf_op jit(solution)/shard_map/ppermute | solution.py:40
  28.6 7.9 %collective-permute-start.8 = (bf16[2,2,160,128]{3,2,0,1:T(8,128)(2,1)S(1)}, bf16[2,2,160,128]{3,2,0,1:T(8,128)(2,1)S(1)}, u32[]{:S(2)}, u32[]{:S(2)}) collective-permute-start(bf16[2,2,160,128]{3,2,0,1:T(8,128)(2,1)S(1)} %pad_maximum_fusion.19), channel_id=1, source_target_pairs={{0,2},{1,3},{2,0},{3,1},{4,6},{5,7},{6,4},{7,5},{8,10},{9,11},{10,... | collective-permute-start | bytes 491528 | tf_op jit(solution)/shard_map/ppermute | solution.py:40
  30.9 18.2 %collective-permute-start.7 = (bf16[640,128]{1,0:T(8,128)(2,1)S(1)}, bf16[640,128]{1,0:T(8,128)(2,1)S(1)}, u32[]{:S(2)}, u32[]{:S(2)}) collective-permute-start(bf16[640,128]{1,0:T(8,128)(2,1)S(1)} %pad_maximum_fusion.18), channel_id=1, source_target_pairs={{0,16},{4,20},{8,24},{12,28},{16,0},{20,4},{24,8},{28,12},{1,17},{... | collective-permute-start | bytes 491528 | tf_op jit(solution)/shard_map/ppermute | solution.py:40
  32.4 14.8 %collective-permute-start.10 = (bf16[2,2,256,128]{3,2,0,1:T(8,128)(2,1)S(1)}, bf16[2,2,256,128]{3,2,0,1:T(8,128)(2,1)S(1)}, u32[]{:S(2)}, u32[]{:S(2)}) collective-permute-start(bf16[2,2,256,128]{3,2,0,1:T(8,128)(2,1)S(1)} %pad_maximum_fusion.12), channel_id=1, source_target_pairs={{0,4},{4,0},{8,12},{12,8},{16,20},{20,16},{24,28},{28,24},{1,5},{5... | collective-permute-start | bytes 786440 | tf_op jit(solution)/shard_map/ppermute | solution.py:40
  36.6 23.9 %collective-permute-start.9 = (bf16[2,2,2,160,128]{4,3,1,2,0:T(8,128)(2,1)S(1)}, bf16[2,2,2,160,128]{4,3,1,2,0:T(8,128)(2,1)S(1)}, u32[]{:S(2)}, u32[]{:S(2)}) collective-permute-start(bf16[2,2,2,160,128]{4,3,1,2,0:T(8,128)(2,1)S(1)} %pad_maximum_fusion.10), channel_id=1, source_target_pairs={{0,4},{4,0},{8,12},{12,8},{16,20},{20,16},{24,28},{28,24},{1,5},{5... | collective-permute-start | bytes 983048 | tf_op jit(solution)/shard_map/ppermute | solution.py:40
  47.3 13.5 %collective-permute-start.11 = (bf16[2,2,2,256,128]{4,3,0,1,2:T(8,128)(2,1)S(1)}, bf16[2,2,2,256,128]{4,3,0,1,2:T(8,128)(2,1)S(1)}, u32[]{:S(2)}, u32[]{:S(2)}) collective-permute-start(bf16[2,2,2,256,128]{4,3,0,1,2:T(8,128)(2,1)S(1)} %pad_maximum_fusion.5), channel_id=1, source_target_pairs={{0,2},{1,3},{2,0},{3,1},{4,6},{5,7},{6,4},{7,5},{8,10},{9,11},{10,... | collective-permute-start | bytes 1572872 | tf_op jit(solution)/shard_map/ppermute | solution.py:40
  49.2 13.1 %collective-permute-start.2 = (bf16[1,1024,256]{2,1,0:T(8,128)(2,1)S(1)}, bf16[1,1024,256]{2,1,0:T(8,128)(2,1)S(1)}, u32[]{:S(2)}, u32[]{:S(2)}) collective-permute-start(bf16[1,1024,256]{2,1,0:T(8,128)(2,1)S(1)} %collective-permute-done.moved_ref), channel_id=1, source_target_pairs={{0,1},{1,0},{2,3},{3,2},{4,5},{5,4},{6,7},{7,6},{8,9},{9,8},{10,11... | collective-permute-start | bytes 1572872 | tf_op jit(solution)/shard_map/ppermute | solution.py:40
  60.7 13.8 %collective-permute-start.12 = (bf16[2,640,128]{2,1,0:T(8,128)(2,1)S(1)}, bf16[2,640,128]{2,1,0:T(8,128)(2,1)S(1)}, u32[]{:S(2)}, u32[]{:S(2)}) collective-permute-start(bf16[2,640,128]{2,1,0:T(8,128)(2,1)S(1)} %pad_maximum_fusion.9), channel_id=1, source_target_pairs={{0,8},{4,12},{8,0},{12,4},{16,24},{20,28},{24,16},{28,20},{1,9},{5... | collective-permute-start | bytes 983048 | tf_op jit(solution)/shard_map/ppermute | solution.py:40
  74.8 11.2 %collective-permute-start.13 = (bf16[2,272,128]{2,1,0:T(8,128)(2,1)S(1)}, bf16[2,272,128]{2,1,0:T(8,128)(2,1)S(1)}, u32[]{:S(2)}, u32[]{:S(2)}) collective-permute-start(bf16[2,272,128]{2,1,0:T(8,128)(2,1)S(1)} %fusion.24), channel_id=1, source_target_pairs={{0,4},{4,0},{8,12},{12,8},{16,20},{20,16},{24,28},{28,24},{1,5},{5... | collective-permute-start | bytes 417800 | tf_op jit(solution)/shard_map/ppermute | solution.py:40
  79.2 6.8 %collective-permute-start.14 = (bf16[2,2,176,128]{3,2,0,1:T(8,128)(2,1)S(1)}, bf16[2,2,176,128]{3,2,0,1:T(8,128)(2,1)S(1)}, u32[]{:S(2)}, u32[]{:S(2)}) collective-permute-start(bf16[2,2,176,128]{3,2,0,1:T(8,128)(2,1)S(1)} %fusion.20), channel_id=1, source_target_pairs={{0,2},{1,3},{2,0},{3,1},{4,6},{5,7},{6,4},{7,5},{8,10},{9,11},{10,... | collective-permute-start | bytes 540680 | tf_op jit(solution)/shard_map/ppermute | solution.py:40
  80.8 9.8 %collective-permute-start.15 = (bf16[2,2,208,128]{3,2,0,1:T(8,128)(2,1)S(1)}, bf16[2,2,208,128]{3,2,0,1:T(8,128)(2,1)S(1)}, u32[]{:S(2)}, u32[]{:S(2)}) collective-permute-start(bf16[2,2,208,128]{3,2,0,1:T(8,128)(2,1)S(1)} %fusion.16), channel_id=1, source_target_pairs={{0,4},{4,0},{8,12},{12,8},{16,20},{20,16},{24,28},{28,24},{1,5},{5... | collective-permute-start | bytes 638984 | tf_op jit(solution)/shard_map/ppermute | solution.py:40
  80.9 31.8 %collective-permute-start.20 = (bf16[2,2,112,128]{3,2,0,1:T(8,128)(2,1)S(1)}, bf16[2,2,112,128]{3,2,0,1:T(8,128)(2,1)S(1)}, u32[]{:S(2)}, u32[]{:S(2)}) collective-permute-start(bf16[2,2,112,128]{3,2,0,1:T(8,128)(2,1)S(1)} %fusion.26), channel_id=1, source_target_pairs={{0,2},{1,3},{2,0},{3,1},{4,6},{5,7},{6,4},{7,5},{8,10},{9,11},{10,... | collective-permute-start | bytes 344072 | tf_op jit(solution)/shard_map/ppermute | solution.py:40
  81.4 31.3 %collective-permute-start.21 = (bf16[2,2,144,128]{3,2,0,1:T(8,128)(2,1)S(1)}, bf16[2,2,144,128]{3,2,0,1:T(8,128)(2,1)S(1)}, u32[]{:S(2)}, u32[]{:S(2)}) collective-permute-start(bf16[2,2,144,128]{3,2,0,1:T(8,128)(2,1)S(1)} %pad_maximum_fusion.20), channel_id=1, source_target_pairs={{0,4},{4,0},{8,12},{12,8},{16,20},{20,16},{24,28},{28,24},{1,5},{5... | collective-permute-start | bytes 442376 | tf_op jit(solution)/shard_map/ppermute | solution.py:40
  90.8 5.1 %collective-permute-start.16 = (bf16[2,272,128]{2,1,0:T(8,128)(2,1)S(1)}, bf16[2,272,128]{2,1,0:T(8,128)(2,1)S(1)}, u32[]{:S(2)}, u32[]{:S(2)}) collective-permute-start(bf16[2,272,128]{2,1,0:T(8,128)(2,1)S(1)} %maximum_maximum_fusion.3), channel_id=1, source_target_pairs={{0,8},{4,12},{8,0},{12,4},{16,24},{20,28},{24,16},{28,20},{1,9},{5... | collective-permute-start | bytes 417800 | tf_op jit(solution)/shard_map/ppermute | solution.py:40
  91.0 13.9 %collective-permute-start.19 = (bf16[2,2,2,208,128]{4,3,0,1,2:T(8,128)(2,1)S(1)}, bf16[2,2,2,208,128]{4,3,0,1,2:T(8,128)(2,1)S(1)}, u32[]{:S(2)}, u32[]{:S(2)}) collective-permute-start(bf16[2,2,2,208,128]{4,3,0,1,2:T(8,128)(2,1)S(1)} %pad_maximum_fusion.7), channel_id=1, source_target_pairs={{0,2},{1,3},{2,0},{3,1},{4,6},{5,7},{6,4},{7,5},{8,10},{9,11},{10,... | collective-permute-start | bytes 1277960 | tf_op jit(solution)/shard_map/ppermute | solution.py:40
  92.7 7.7 %collective-permute-start.18 = (bf16[2,2,2,176,128]{4,3,1,2,0:T(8,128)(2,1)S(1)}, bf16[2,2,2,176,128]{4,3,1,2,0:T(8,128)(2,1)S(1)}, u32[]{:S(2)}, u32[]{:S(2)}) collective-permute-start(bf16[2,2,2,176,128]{4,3,1,2,0:T(8,128)(2,1)S(1)} %pad_maximum_fusion.8), channel_id=1, source_target_pairs={{0,4},{4,0},{8,12},{12,8},{16,20},{20,16},{24,28},{28,24},{1,5},{5... | collective-permute-start | bytes 1081352 | tf_op jit(solution)/shard_map/ppermute | solution.py:40
  95.9 23.7 %collective-permute-start.24 = (bf16[1024,256]{1,0:T(8,128)(2,1)S(1)}, bf16[1024,256]{1,0:T(8,128)(2,1)S(1)}, u32[]{:S(2)}, u32[]{:S(2)}) collective-permute-start(bf16[1024,256]{1,0:T(8,128)(2,1)S(1)} %get-tuple-element.292), channel_id=1, source_target_pairs={{0,2},{1,3},{2,0},{3,1},{4,6},{5,7},{6,4},{7,5},{8,10},{9,11},{10,... | collective-permute-start | bytes 1572872 | tf_op jit(solution)/shard_map/ppermute | solution.py:40
  100.4 12.3 %collective-permute-start.17 = (bf16[2,272,128]{2,1,0:T(8,128)(2,1)S(1)}, bf16[2,272,128]{2,1,0:T(8,128)(2,1)S(1)}, u32[]{:S(2)}, u32[]{:S(2)}) collective-permute-start(bf16[2,272,128]{2,1,0:T(8,128)(2,1)S(1)} %maximum_maximum_fusion.4), channel_id=1, source_target_pairs={{0,16},{4,20},{8,24},{12,28},{16,0},{20,4},{24,8},{28,12},{1,17},{... | collective-permute-start | bytes 417800 | tf_op jit(solution)/shard_map/ppermute | solution.py:40
  112.8 6.8 %collective-permute-start.23 = (bf16[2,2,2,144,128]{4,3,0,1,2:T(8,128)(2,1)S(1)}, bf16[2,2,2,144,128]{4,3,0,1,2:T(8,128)(2,1)S(1)}, u32[]{:S(2)}, u32[]{:S(2)}) collective-permute-start(bf16[2,2,2,144,128]{4,3,0,1,2:T(8,128)(2,1)S(1)} %pad_maximum_fusion.11), channel_id=1, source_target_pairs={{0,2},{1,3},{2,0},{3,1},{4,6},{5,7},{6,4},{7,5},{8,10},{9,11},{10,... | collective-permute-start | bytes 884744 | tf_op jit(solution)/shard_map/ppermute | solution.py:40
  113.5 6.1 %collective-permute-start.22 = (bf16[2,2,2,112,128]{4,3,1,2,0:T(8,128)(2,1)S(1)}, bf16[2,2,2,112,128]{4,3,1,2,0:T(8,128)(2,1)S(1)}, u32[]{:S(2)}, u32[]{:S(2)}) collective-permute-start(bf16[2,2,2,112,128]{4,3,1,2,0:T(8,128)(2,1)S(1)} %pad_maximum_fusion.13), channel_id=1, source_target_pairs={{0,4},{4,0},{8,12},{12,8},{16,20},{20,16},{24,28},{28,24},{1,5},{5... | collective-permute-start | bytes 688136 | tf_op jit(solution)/shard_map/ppermute | solution.py:40
  124.3 5.7 %collective-permute-start.25 = (bf16[1024,1024]{1,0:T(8,128)(2,1)S(1)}, bf16[1024,1024]{1,0:T(8,128)(2,1)S(1)}, u32[]{:S(2)}, u32[]{:S(2)}) collective-permute-start(bf16[1024,1024]{1,0:T(8,128)(2,1)S(1)} %get-tuple-element.296.mine_ref), channel_id=1, source_target_pairs={{0,1},{1,0},{2,3},{3,2},{4,5},{5,4},{6,7},{7,6},{8,9},{9,8},{10,11... | collective-permute-start | bytes 6291464 | tf_op jit(solution)/shard_map/ppermute | solution.py:40
  124.3 4.9 %collective-permute-start.26 = (bf16[1024,256]{1,0:T(8,128)(2,1)S(1)}, bf16[1024,256]{1,0:T(8,128)(2,1)S(1)}, u32[]{:S(2)}, u32[]{:S(2)}) collective-permute-start(bf16[1024,256]{1,0:T(8,128)(2,1)S(1)} %collective-permute-done.24.refs_4_), channel_id=1, source_target_pairs={{0,1},{1,0},{2,3},{3,2},{4,5},{5,4},{6,7},{7,6},{8,9},{9,8},{10,11... | collective-permute-start | bytes 1572872 | tf_op jit(solution)/shard_map/ppermute | solution.py:40
  124.8 16.3 %collective-permute-start.29 = (bf16[2,1024,256]{2,1,0:T(8,128)(2,1)S(1)}, bf16[2,1024,256]{2,1,0:T(8,128)(2,1)S(1)}, u32[]{:S(2)}, u32[]{:S(2)}) collective-permute-start(bf16[2,1024,256]{2,1,0:T(8,128)(2,1)S(1)} %copy-done.1), channel_id=1, source_target_pairs={{0,1},{1,0},{2,3},{3,2},{4,5},{5,4},{6,7},{7,6},{8,9},{9,8},{10,11... | collective-permute-start | bytes 3145736 | tf_op jit(solution)/shard_map/ppermute | solution.py:40
  139.1 24.4 %collective-permute-start.27 = (bf16[256,1024]{1,0:T(8,128)(2,1)}, bf16[256,1024]{1,0:T(8,128)(2,1)}, u32[]{:S(2)}, u32[]{:S(2)}) collective-permute-start(bf16[256,1024]{1,0:T(8,128)(2,1)} %get-tuple-element.301), channel_id=1, source_target_pairs={{0,2},{1,3},{2,0},{3,1},{4,6},{5,7},{6,4},{7,5},{8,10},{9,11},{10,... | collective-permute-start | bytes 1572872 | tf_op jit(solution)/shard_map/ppermute | solution.py:40
  140.5 24.2 %collective-permute-start.28 = (bf16[1024,256]{1,0:T(8,128)(2,1)}, bf16[1024,256]{1,0:T(8,128)(2,1)}, u32[]{:S(2)}, u32[]{:S(2)}) collective-permute-start(bf16[1024,256]{1,0:T(8,128)(2,1)} %get-tuple-element.304), channel_id=1, source_target_pairs={{0,2},{1,3},{2,0},{3,1},{4,6},{5,7},{6,4},{7,5},{8,10},{9,11},{10,... | collective-permute-start | bytes 1572872 | tf_op jit(solution)/shard_map/ppermute | solution.py:40
  165.2 15.1 %collective-permute-start.30 = (bf16[256,1024]{1,0:T(8,128)(2,1)S(1)}, bf16[256,1024]{1,0:T(8,128)(2,1)S(1)}, u32[]{:S(2)}, u32[]{:S(2)}) collective-permute-start(bf16[256,1024]{1,0:T(8,128)(2,1)S(1)} %copy-done.55), channel_id=1, source_target_pairs={{0,2},{1,3},{2,0},{3,1},{4,6},{5,7},{6,4},{7,5},{8,10},{9,11},{10,... | collective-permute-start | bytes 1572872 | tf_op jit(solution)/shard_map/ppermute | solution.py:40
  180.5 37.3 %collective-permute-start.36 = (bf16[1024,1024]{1,0:T(8,128)(2,1)}, bf16[1024,1024]{1,0:T(8,128)(2,1)}, u32[]{:S(2)}, u32[]{:S(2)}) collective-permute-start(bf16[1024,1024]{1,0:T(8,128)(2,1)} %get-tuple-element.316.refs_3_), channel_id=1, source_target_pairs={{0,1},{1,0},{2,3},{3,2},{4,5},{5,4},{6,7},{7,6},{8,9},{9,8},{10,11... | collective-permute-start | bytes 6291464 | tf_op jit(solution)/shard_map/ppermute | solution.py:40
  182.6 16.6 %collective-permute-start.34 = (bf16[256,1024]{1,0:T(8,128)(2,1)S(1)}, bf16[256,1024]{1,0:T(8,128)(2,1)S(1)}, u32[]{:S(2)}, u32[]{:S(2)}) collective-permute-start(bf16[256,1024]{1,0:T(8,128)(2,1)S(1)} %add_convert_fusion.1), channel_id=1, source_target_pairs={{0,2},{1,3},{2,0},{3,1},{4,6},{5,7},{6,4},{7,5},{8,10},{9,11},{10,... | collective-permute-start | bytes 1572872 | tf_op jit(solution)/shard_map/ppermute | solution.py:40
  198.7 19.1 %collective-permute-start.37 = (bf16[2,1024,256]{2,1,0:T(8,128)(2,1)}, bf16[2,1024,256]{2,1,0:T(8,128)(2,1)}, u32[]{:S(2)}, u32[]{:S(2)}) collective-permute-start(bf16[2,1024,256]{2,1,0:T(8,128)(2,1)} %get-tuple-element.356), channel_id=1, source_target_pairs={{0,1},{1,0},{2,3},{3,2},{4,5},{5,4},{6,7},{7,6},{8,9},{9,8},{10,11... | collective-permute-start | bytes 3145736 | tf_op jit(solution)/shard_map/ppermute | solution.py:40
  199.1 18.7 %collective-permute-start.38 = (bf16[2,512,256]{2,1,0:T(8,128)(2,1)}, bf16[2,512,256]{2,1,0:T(8,128)(2,1)}, u32[]{:S(2)}, u32[]{:S(2)}) collective-permute-start(bf16[2,512,256]{2,1,0:T(8,128)(2,1)} %get-tuple-element.357), channel_id=1, source_target_pairs={{0,1},{1,0},{2,3},{3,2},{4,5},{5,4},{6,7},{7,6},{8,9},{9,8},{10,11... | collective-permute-start | bytes 1572872 | tf_op jit(solution)/shard_map/ppermute | solution.py:40
  199.2 18.6 %collective-permute-start.39 = (bf16[2,512,256]{2,1,0:T(8,128)(2,1)}, bf16[2,512,256]{2,1,0:T(8,128)(2,1)}, u32[]{:S(2)}, u32[]{:S(2)}) collective-permute-start(bf16[2,512,256]{2,1,0:T(8,128)(2,1)} %get-tuple-element.358), channel_id=1, source_target_pairs={{0,1},{1,0},{2,3},{3,2},{4,5},{5,4},{6,7},{7,6},{8,9},{9,8},{10,11... | collective-permute-start | bytes 1572872 | tf_op jit(solution)/shard_map/ppermute | solution.py:40
  201.5 16.3 %collective-permute-start.41 = (bf16[256,1024]{1,0:T(8,128)(2,1)}, bf16[256,1024]{1,0:T(8,128)(2,1)}, u32[]{:S(2)}, u32[]{:S(2)}) collective-permute-start(bf16[256,1024]{1,0:T(8,128)(2,1)} %add_convert_fusion), channel_id=1, source_target_pairs={{0,2},{1,3},{2,0},{3,1},{4,6},{5,7},{6,4},{7,5},{8,10},{9,11},{10,... | collective-permute-start | bytes 1572872 | tf_op jit(solution)/shard_map/ppermute | solution.py:40
  235.8 9.4 %collective-permute-start.44 = (bf16[2,272,128]{2,1,0:T(8,128)(2,1)S(1)}, bf16[2,272,128]{2,1,0:T(8,128)(2,1)S(1)}, u32[]{:S(2)}, u32[]{:S(2)}) collective-permute-start(bf16[2,272,128]{2,1,0:T(8,128)(2,1)S(1)} %fusion.25), channel_id=1, source_target_pairs={{0,4},{4,0},{8,12},{12,8},{16,20},{20,16},{24,28},{28,24},{1,5},{5... | collective-permute-start | bytes 417800 | tf_op jit(solution)/shard_map/ppermute | solution.py:40
  245.4 9.3 %collective-permute-start.45 = (bf16[2,272,128]{2,1,0:T(8,128)(2,1)S(1)}, bf16[2,272,128]{2,1,0:T(8,128)(2,1)S(1)}, u32[]{:S(2)}, u32[]{:S(2)}) collective-permute-start(bf16[2,272,128]{2,1,0:T(8,128)(2,1)S(1)} %maximum_maximum_fusion.5), channel_id=1, source_target_pairs={{0,8},{4,12},{8,0},{12,4},{16,24},{20,28},{24,16},{28,20},{1,9},{5... | collective-permute-start | bytes 417800 | tf_op jit(solution)/shard_map/ppermute | solution.py:40
  245.5 25.0 %collective-permute-start.47 = (bf16[2,1024,256]{2,1,0:T(8,128)(2,1)}, bf16[2,1024,256]{2,1,0:T(8,128)(2,1)}, u32[]{:S(2)}, u32[]{:S(2)}) collective-permute-start(bf16[2,1024,256]{2,1,0:T(8,128)(2,1)} %get-tuple-element.392), channel_id=1, source_target_pairs={{0,2},{1,3},{2,0},{3,1},{4,6},{5,7},{6,4},{7,5},{8,10},{9,11},{10,... | collective-permute-start | bytes 3145736 | tf_op jit(solution)/shard_map/ppermute | solution.py:40
  255.0 12.2 %collective-permute-start.46 = (bf16[2,272,128]{2,1,0:T(8,128)(2,1)S(1)}, bf16[2,272,128]{2,1,0:T(8,128)(2,1)S(1)}, u32[]{:S(2)}, u32[]{:S(2)}) collective-permute-start(bf16[2,272,128]{2,1,0:T(8,128)(2,1)S(1)} %maximum_maximum_fusion.6), channel_id=1, source_target_pairs={{0,16},{4,20},{8,24},{12,28},{16,0},{20,4},{24,8},{28,12},{1,17},{... | collective-permute-start | bytes 417800 | tf_op jit(solution)/shard_map/ppermute | solution.py:40
  275.2 18.3 %collective-permute-start.48 = (bf16[2,2,2,320,128]{4,3,0,1,2:T(8,128)(2,1)S(1)}, bf16[2,2,2,320,128]{4,3,0,1,2:T(8,128)(2,1)S(1)}, u32[]{:S(2)}, u32[]{:S(2)}) collective-permute-start(bf16[2,2,2,320,128]{4,3,0,1,2:T(8,128)(2,1)S(1)} %copy.102), channel_id=1, source_target_pairs={{0,2},{1,3},{2,0},{3,1},{4,6},{5,7},{6,4},{7,5},{8,10},{9,11},{10,... | collective-permute-start | bytes 1966088 | tf_op jit(solution)/shard_map/ppermute | solution.py:40
  277.5 16.0 %collective-permute-start.49 = (bf16[2,2,2,320,128]{4,3,1,2,0:T(8,128)(2,1)S(1)}, bf16[2,2,2,320,128]{4,3,1,2,0:T(8,128)(2,1)S(1)}, u32[]{:S(2)}, u32[]{:S(2)}) collective-permute-start(bf16[2,2,2,320,128]{4,3,1,2,0:T(8,128)(2,1)S(1)} %copy.103), channel_id=1, source_target_pairs={{0,4},{4,0},{8,12},{12,8},{16,20},{20,16},{24,28},{28,24},{1,5},{5... | collective-permute-start | bytes 1966088 | tf_op jit(solution)/shard_map/ppermute | solution.py:40
  294.6 4.5 %collective-permute-start.50 = (bf16[1024,1024]{1,0:T(8,128)(2,1)}, bf16[1024,1024]{1,0:T(8,128)(2,1)S(1)}, u32[]{:S(2)}, u32[]{:S(2)}) collective-permute-start(bf16[1024,1024]{1,0:T(8,128)(2,1)} %get-tuple-element.406.mine_ref), channel_id=1, source_target_pairs={{0,1},{1,0},{2,3},{3,2},{4,5},{5,4},{6,7},{7,6},{8,9},{9,8},{10,11... | collective-permute-start | bytes 6291464 | tf_op jit(solution)/shard_map/ppermute | solution.py:40
  294.6 4.0 collective-permute-start.51
  299.9 12.0 %collective-permute-start.52 = (bf16[2,2,2,192,128]{4,3,0,1,2:T(8,128)(2,1)}, bf16[2,2,2,192,128]{4,3,0,1,2:T(8,128)(2,1)}, u32[]{:S(2)}, u32[]{:S(2)}) collective-permute-start(bf16[2,2,2,192,128]{4,3,0,1,2:T(8,128)(2,1)} %copy.104), channel_id=1, source_target_pairs={{0,2},{1,3},{2,0},{3,1},{4,6},{5,7},{6,4},{7,5},{8,10},{9,11},{10,... | collective-permute-start | bytes 1179656 | tf_op jit(solution)/shard_map/ppermute | solution.py:40
  301.5 11.2 %collective-permute-start.53 = (bf16[2,2,2,192,128]{4,3,1,2,0:T(8,128)(2,1)}, bf16[2,2,2,192,128]{4,3,1,2,0:T(8,128)(2,1)}, u32[]{:S(2)}, u32[]{:S(2)}) collective-permute-start(bf16[2,2,2,192,128]{4,3,1,2,0:T(8,128)(2,1)} %copy.105), channel_id=1, source_target_pairs={{0,4},{4,0},{8,12},{12,8},{16,20},{20,16},{24,28},{28,24},{1,5},{5... | collective-permute-start | bytes 1179656 | tf_op jit(solution)/shard_map/ppermute | solution.py:40
  313.9 9.5 %collective-permute-start.54 = (bf16[2,2,192,128]{3,2,0,1:T(8,128)(2,1)S(1)}, bf16[2,2,192,128]{3,2,0,1:T(8,128)(2,1)S(1)}, u32[]{:S(2)}, u32[]{:S(2)}) collective-permute-start(bf16[2,2,192,128]{3,2,0,1:T(8,128)(2,1)S(1)} %fusion.17), channel_id=1, source_target_pairs={{0,4},{4,0},{8,12},{12,8},{16,20},{20,16},{24,28},{28,24},{1,5},{5... | collective-permute-start | bytes 589832 | tf_op jit(solution)/shard_map/ppermute | solution.py:40
  316.3 7.2 %collective-permute-start.55 = (bf16[2,2,192,128]{3,2,0,1:T(8,128)(2,1)S(1)}, bf16[2,2,192,128]{3,2,0,1:T(8,128)(2,1)S(1)}, u32[]{:S(2)}, u32[]{:S(2)}) collective-permute-start(bf16[2,2,192,128]{3,2,0,1:T(8,128)(2,1)S(1)} %fusion.18), channel_id=1, source_target_pairs={{0,2},{1,3},{2,0},{3,1},{4,6},{5,7},{6,4},{7,5},{8,10},{9,11},{10,... | collective-permute-start | bytes 589832 | tf_op jit(solution)/shard_map/ppermute | solution.py:40
  318.5 12.9 %collective-permute-start.61 = (bf16[2,2,320,128]{3,2,0,1:T(8,128)(2,1)}, bf16[2,2,320,128]{3,2,0,1:T(8,128)(2,1)}, u32[]{:S(2)}, u32[]{:S(2)}) collective-permute-start(bf16[2,2,320,128]{3,2,0,1:T(8,128)(2,1)} %fusion.13), channel_id=1, source_target_pairs={{0,4},{4,0},{8,12},{12,8},{16,20},{20,16},{24,28},{28,24},{1,5},{5... | collective-permute-start | bytes 983048 | tf_op jit(solution)/shard_map/ppermute | solution.py:40
  319.7 7.1 %collective-permute-start.57 = (f32[35,1024]{1,0:T(8,128)S(1)}, f32[35,1024]{1,0:T(8,128)S(1)}, u32[]{:S(2)}, u32[]{:S(2)}) collective-permute-start(f32[35,1024]{1,0:T(8,128)S(1)} %fusion.31), channel_id=1, source_target_pairs={{0,2},{1,3},{2,0},{3,1},{4,6},{5,7},{6,4},{7,5},{8,10},{9,11},{10,... | collective-permute-start | bytes 430088 | tf_op jit(solution)/shard_map/ppermute | solution.py:40
  321.4 11.8 %collective-permute-start.62 = (bf16[2,2,320,128]{3,2,0,1:T(8,128)(2,1)}, bf16[2,2,320,128]{3,2,0,1:T(8,128)(2,1)}, u32[]{:S(2)}, u32[]{:S(2)}) collective-permute-start(bf16[2,2,320,128]{3,2,0,1:T(8,128)(2,1)} %fusion.14), channel_id=1, source_target_pairs={{0,2},{1,3},{2,0},{3,1},{4,6},{5,7},{6,4},{7,5},{8,10},{9,11},{10,... | collective-permute-start | bytes 983048 | tf_op jit(solution)/shard_map/ppermute | solution.py:40
  327.7 8.2 %collective-permute-start.59 = (bf16[2,384,128]{2,1,0:T(8,128)(2,1)}, bf16[2,384,128]{2,1,0:T(8,128)(2,1)S(1)}, u32[]{:S(2)}, u32[]{:S(2)}) collective-permute-start(bf16[2,384,128]{2,1,0:T(8,128)(2,1)} %fusion.19), channel_id=1, source_target_pairs={{0,8},{4,12},{8,0},{12,4},{16,24},{20,28},{24,16},{28,20},{1,9},{5... | collective-permute-start | bytes 589832 | tf_op jit(solution)/shard_map/ppermute | solution.py:40
  330.5 5.5 %collective-permute-start.60 = (f32[35,1024]{1,0:T(8,128)S(1)}, f32[35,1024]{1,0:T(8,128)}, u32[]{:S(2)}, u32[]{:S(2)}) collective-permute-start(f32[35,1024]{1,0:T(8,128)S(1)} %add.294), channel_id=1, source_target_pairs={{0,4},{4,0},{8,12},{12,8},{16,20},{20,16},{24,28},{28,24},{1,5},{5... | collective-permute-start | bytes 430088 | tf_op jit(solution)/shard_map/ppermute | solution.py:40
  337.9 10.5 %collective-permute-start.63 = (bf16[384,128]{1,0:T(8,128)(2,1)S(1)}, bf16[384,128]{1,0:T(8,128)(2,1)S(1)}, u32[]{:S(2)}, u32[]{:S(2)}) collective-permute-start(bf16[384,128]{1,0:T(8,128)(2,1)S(1)} %fusion.27), channel_id=1, source_target_pairs={{0,16},{4,20},{8,24},{12,28},{16,0},{20,4},{24,8},{28,12},{1,17},{... | collective-permute-start | bytes 294920 | tf_op jit(solution)/shard_map/ppermute | solution.py:40
  338.0 10.4 %collective-permute-start.64 = (f32[35,1024]{1,0:T(8,128)S(1)}, f32[35,1024]{1,0:T(8,128)}, u32[]{:S(2)}, u32[]{:S(2)}) collective-permute-start(f32[35,1024]{1,0:T(8,128)S(1)} %add.302), channel_id=1, source_target_pairs={{0,8},{4,12},{8,0},{12,4},{16,24},{20,28},{24,16},{28,20},{1,9},{5... | collective-permute-start | bytes 430088 | tf_op jit(solution)/shard_map/ppermute | solution.py:40
  341.6 16.1 %collective-permute-start.66 = (bf16[2,640,128]{2,1,0:T(8,128)(2,1)S(1)}, bf16[2,640,128]{2,1,0:T(8,128)(2,1)S(1)}, u32[]{:S(2)}, u32[]{:S(2)}) collective-permute-start(bf16[2,640,128]{2,1,0:T(8,128)(2,1)S(1)} %fusion.15), channel_id=1, source_target_pairs={{0,8},{4,12},{8,0},{12,4},{16,24},{20,28},{24,16},{28,20},{1,9},{5... | collective-permute-start | bytes 983048 | tf_op jit(solution)/shard_map/ppermute | solution.py:40
  347.6 34.3 %collective-permute-start.58 = (bf16[1024,256]{1,0:T(8,128)(2,1)S(1)}, bf16[1024,256]{1,0:T(8,128)(2,1)S(1)}, u32[]{:S(2)}, u32[]{:S(2)}) collective-permute-start(bf16[1024,256]{1,0:T(8,128)(2,1)S(1)} %copy-done.68), channel_id=1, source_target_pairs={{0,2},{1,3},{2,0},{3,1},{4,6},{5,7},{6,4},{7,5},{8,10},{9,11},{10,... | collective-permute-start | bytes 1572872 | tf_op jit(solution)/shard_map/ppermute | solution.py:40
  349.3 8.4 %collective-permute-start.65 = (f32[35,1024]{1,0:T(8,128)S(1)}, f32[35,1024]{1,0:T(8,128)S(1)}, u32[]{:S(2)}, u32[]{:S(2)}) collective-permute-start(f32[35,1024]{1,0:T(8,128)S(1)} %add.306), channel_id=1, source_target_pairs={{0,16},{4,20},{8,24},{12,28},{16,0},{20,4},{24,8},{28,12},{1,17},{... | collective-permute-start | bytes 430088 | tf_op jit(solution)/shard_map/ppermute | solution.py:40
  359.5 7.7 %collective-permute-start.67 = (bf16[640,128]{1,0:T(8,128)(2,1)S(1)}, bf16[640,128]{1,0:T(8,128)(2,1)S(1)}, u32[]{:S(2)}, u32[]{:S(2)}) collective-permute-start(bf16[640,128]{1,0:T(8,128)(2,1)S(1)} %fusion.21), channel_id=1, source_target_pairs={{0,16},{4,20},{8,24},{12,28},{16,0},{20,4},{24,8},{28,12},{1,17},{... | collective-permute-start | bytes 491528 | tf_op jit(solution)/shard_map/ppermute | solution.py:40
  374.4 3.8 collective-permute-start.69
  385.7 4.6 %collective-permute-start.72 = (f32[32,128]{1,0:T(8,128)S(1)}, f32[32,128]{1,0:T(8,128)S(1)}, u32[]{:S(2)}, u32[]{:S(2)}) collective-permute-start(f32[32,128]{1,0:T(8,128)S(1)} %add.318), channel_id=1, source_target_pairs={{0,16},{4,20},{8,24},{12,28},{16,0},{20,4},{24,8},{28,12},{1,17},{... | collective-permute-start | bytes 49160 | tf_op jit(solution)/shard_map/ppermute | solution.py:40
  (91 other events, 732.5 us)
Sparse Core Ops, SparseCore 0:
  20.4 65.7 all-gather.2
  218.0 55.9 reduce-scatter.1
